TPU v7x, 32 devices: a whole 2x2x4 slice. The times are simulated.
32 devices in a mesh: scan: 2 (over x), tile: 8 (over z, y), row: 2 (over core).
Axes of the slice: x: 2, y: 2, z: 4, core: 2. Of those that a mesh axis runs over, the one named last changes fastest.
Arguments:
- object_tiles: float32 [16, 2, 256, 256], P(('scan', 'tile')), parts along dimension 0, may hold values from -6 to 6
- probe_modes: float32 [4, 2, 256, 256], P('row'), may hold values from -6 to 6
- amplitude: float32 [32, 256, 256], P(('scan', 'tile')), parts along dimension 0, may hold values from 0 to 4
- offsets: int32 [32, 2], P(('scan', 'tile')), parts along dimension 0, may hold values from 0 to 1792, as said below
- counts: int32 [16], P(('scan', 'tile')), parts along dimension 0, may hold values from 1 to 2, as said below
Outputs:
- new_object: float32 [16, 2, 256, 256], P(('scan', 'tile')), parts along dimension 0
- new_probe: float32 [8, 2, 256, 256], P(('scan', 'row')), parts along dimension 0
There are 2 independent parts, one for each index of `scan`. A program takes and returns all parts, laid end to end along the dimension named above; an argument that names none is the same for every part. Nothing has to cross between parts.
Inputs may be any that keep to these rules, and one draw needn't show every extreme that they name: The patch of slot p lies inside the object, and its centre, offsets[p] + 128 in both coordinates, lies in tile p // 2. The first slot's patch sits at the object's top-left corner and the last tile's first slot's patch at its bottom-right corner. `counts`: at least one tile holds 2 live slots; a tile's live slots are its first ones.
All inputs are finite; a program needn't handle non-finite values.
Results may differ from a plain program's by a relative error of at most 0.0001.
Values sent between devices are 32-bit elements; how exact they have to be, the bound alone decides.
No kernel may reach another device: no remote copies, remote signals or barrier semaphores. Data moves between devices by JAX's collectives and lax.ppermute only.
A program may use at most 64 MiB of HBM per device.

v0:
```python
import math

import jax
import jax.numpy as jnp
from jax import lax
from jax.sharding import PartitionSpec as P

MODES = 4
GX = 8
ITERS = 2


precise = lax.Precision.HIGHEST


def from_behind(value, axis, steps):
    count = lax.axis_size(axis)
    initial, last = (max(0, -steps), min(count, count - steps))
    return lax.ppermute(value, axis, [(source, source + steps) for source in range(initial, last)])


def dft_tables(length):
    steps_axis = jnp.arange(length, dtype=jnp.int32)
    product = steps_axis[:, None] * steps_axis[None, :] % length
    angle = product.astype(jnp.float32) * (2.0 * math.pi / length)
    scaling = 1.0 / math.sqrt(length)
    return (jnp.cos(angle) * scaling, -jnp.sin(angle) * scaling)


def transform(real_part, imag_part, cosine, sine):
    left_real = jnp.einsum("ij,bjk->bik", cosine, real_part, precision=precise) - jnp.einsum(
        "ij,bjk->bik", sine, imag_part, precision=precise
    )
    left_imag = jnp.einsum("ij,bjk->bik", cosine, imag_part, precision=precise) + jnp.einsum(
        "ij,bjk->bik", sine, real_part, precision=precise
    )
    out_real = jnp.einsum("bij,jk->bik", left_real, cosine, precision=precise) - jnp.einsum(
        "bij,jk->bik", left_imag, sine, precision=precise
    )
    out_imag = jnp.einsum("bij,jk->bik", left_real, sine, precision=precise) + jnp.einsum(
        "bij,jk->bik", left_imag, cosine, precision=precise
    )
    return (out_real, out_imag)


def source_span(grid_step, tile_size, half_width):
    if grid_step < 0:
        return (tile_size - half_width, half_width)
    if grid_step == 0:
        return (0, tile_size)
    return (0, half_width)


def margin_span(grid_step, tile_size, half_width):
    if grid_step < 0:
        return 0
    if grid_step == 0:
        return half_width
    return half_width + tile_size


def neighbour_steps():
    return [
        (row_step, col_step)
        for row_step in (-1, 0, 1)
        for col_step in (-1, 0, 1)
        if row_step != 0 or col_step != 0
    ]


def extend_direct(own_tile, half_width):
    tile_size = own_tile.shape[-1]
    full_size = tile_size + 2 * half_width
    extended = jnp.zeros((2, full_size, full_size), own_tile.dtype)
    extended = extended.at[
        :, half_width : half_width + tile_size, half_width : half_width + tile_size
    ].set(own_tile)
    for row_step, col_step in neighbour_steps():
        row_first, row_count = source_span(row_step, tile_size, half_width)
        col_first, col_count = source_span(col_step, tile_size, half_width)
        strip_piece = own_tile[
            :, row_first : row_first + row_count, col_first : col_first + col_count
        ]
        received = from_behind(strip_piece, "tile", -(row_step * GX + col_step))
        row_place = margin_span(row_step, tile_size, half_width)
        col_place = margin_span(col_step, tile_size, half_width)
        extended = extended.at[
            :, row_place : row_place + row_count, col_place : col_place + col_count
        ].set(received)
    return extended


def return_direct(gradient, half_width, tile_size):
    tile_grad = gradient[
        :, half_width : half_width + tile_size, half_width : half_width + tile_size
    ]
    for row_step, col_step in neighbour_steps():
        row_first, row_count = source_span(row_step, tile_size, half_width)
        col_first, col_count = source_span(col_step, tile_size, half_width)
        row_place = margin_span(row_step, tile_size, half_width)
        col_place = margin_span(col_step, tile_size, half_width)
        strip_piece = gradient[
            :, row_place : row_place + row_count, col_place : col_place + col_count
        ]
        received = from_behind(strip_piece, "tile", row_step * GX + col_step)
        tile_grad = tile_grad.at[
            :, row_first : row_first + row_count, col_first : col_first + col_count
        ].add(received)
    return tile_grad


def per_device(object_tiles, probe_modes, amplitude, offsets, counts):
    own_tile = object_tiles[0]
    tile_size = own_tile.shape[-1]
    frame = probe_modes.shape[-1]
    half_width = frame // 2
    position = lax.axis_index("tile")
    grid_row = position // GX
    grid_col = position % GX
    slot_total = offsets.shape[0]
    total_slots = slot_total * lax.axis_size("tile")
    cosine, sine = dft_tables(frame)
    live_count = counts[0]
    probe_now = probe_modes
    for iteration in range(ITERS):
        extended = extend_direct(own_tile, half_width)
        probe_real = probe_now[:, 0]
        probe_imag = probe_now[:, 1]

        def visit(slot_index, state):
            object_grad, probe_grad = state
            weight = (slot_index < live_count).astype(jnp.float32)
            row_start = offsets[slot_index, 0] - grid_row * tile_size + half_width
            col_start = offsets[slot_index, 1] - grid_col * tile_size + half_width
            object_patch = lax.dynamic_slice(extended, (0, row_start, col_start), (2, frame, frame))
            exit_real = probe_real * object_patch[0] - probe_imag * object_patch[1]
            exit_imag = probe_real * object_patch[1] + probe_imag * object_patch[0]
            far_real, far_imag = transform(exit_real, exit_imag, cosine, sine)
            power_part = jnp.sum(far_real * far_real + far_imag * far_imag, axis=0)
            power_sum = lax.psum(power_part, "row")
            factor = amplitude[slot_index] / (jnp.sqrt(power_sum) + 0.5)
            back_real, back_imag = transform(far_real * factor, far_imag * factor, cosine, -sine)
            diff_real = (back_real - exit_real) * weight
            diff_imag = (back_imag - exit_imag) * weight
            grad_real = jnp.sum(probe_real * diff_real + probe_imag * diff_imag, axis=0)
            grad_imag = jnp.sum(probe_real * diff_imag - probe_imag * diff_real, axis=0)
            current = lax.dynamic_slice(object_grad, (0, row_start, col_start), (2, frame, frame))
            object_grad = lax.dynamic_update_slice(
                object_grad, current + jnp.stack([grad_real, grad_imag]), (0, row_start, col_start)
            )
            probe_step = jnp.stack(
                [
                    object_patch[0] * diff_real + object_patch[1] * diff_imag,
                    object_patch[0] * diff_imag - object_patch[1] * diff_real,
                ],
                axis=1,
            )
            return (object_grad, probe_grad + probe_step)

        start = (jnp.zeros_like(extended), jnp.zeros_like(probe_now))
        object_grad, probe_grad = lax.fori_loop(0, slot_total, visit, start)
        tile_grad = return_direct(object_grad, half_width, tile_size)
        tile_grad = lax.psum(tile_grad, "row")
        own_tile = own_tile + tile_grad / MODES
        probe_sum = lax.psum(probe_grad, "tile")
        probe_now = probe_now + 4.0 / total_slots * probe_sum
    return (own_tile[None], probe_now)


def solution(mesh):
    return jax.shard_map(
        per_device,
        mesh=mesh,
        in_specs=(
            P(("scan", "tile"), None, None, None),
            P("row", None, None, None),
            P(("scan", "tile"), None, None),
            P(("scan", "tile"), None),
            P(("scan", "tile")),
        ),
        out_specs=(P(("scan", "tile"), None, None, None), P(("scan", "row"), None, None, None)),
        check_vma=False,
    )
```

profile of v0, /device:TPU:0, one launch (start us, length us, event | category | flops | bytes accessed | tf_op | source)
XLA Modules:
  0.0 623.5 jit_solution(10288354850254224243)
XLA Ops:
  13.2 7.9 %collective-permute-start.2 = (f32[2,128,128]{2,1,0:T(8,128)}, f32[2,128,128]{2,1,0:T(8,128)S(1)}, u32[]{:S(2)}, u32[]{:S(2)}) collective-permute-start(f32[2,128,128]{2,1,0:T(8,128)} %get-tuple-element.1498), channel_id=1, source_target_pairs={{0,14},{1,15},{16,30},{17,31}} | collective-permute-start | bytes 393224 | tf_op jit(solution)/shard_map/ppermute | solution.py:19
  34.9 4.7 scatter.64
  43.1 3.8 scatter.65
  53.1 136.9 %while.74 = (s32[]{:T(128)}, f32[2,512,512]{2,1,0:T(8,128)}, f32[2,2,256,256]{3,2,0,1:T(8,128)}, s32[2,2]{1,0:T(2,128)S(1)}, s32[]{:T(128)}, /*index=5*/s32[]{:T...) while((s32[]{:T(128)}, f32[2,512,512]{2,1,0:T(8,128)}, ...), condition=%wide.region_7.8_spmd.clone.clone, body=%wide.region_2.0_spmd.clone.clone.sunk | while | flops 6465257472 | bytes 45089252 | solution.py:161
  69.6 3.4 add_reduce_fusion.6
  73.7 20.5 %all-reduce.17.cloned.1.call-done = f32[256,256]{1,0:T(8,128)} async-done(((f32[256,256]{1,0:T(8,128)}), f32[256,256]{1,0:T(8,128)}) %all-reduce.17.cloned.1.call-update) | async-done | bytes 262160 | tf_op jit(solution)/shard_map/while/body/eval_jaxpr/psum | solution.py:140
  108.3 3.1 add_bitcast_fusion.5
  112.9 5.5 dynamic_update_slice.28
  135.7 3.4 add_reduce_fusion.6
  139.8 18.9 %all-reduce.17.cloned.1.call-done = f32[256,256]{1,0:T(8,128)} async-done(((f32[256,256]{1,0:T(8,128)}), f32[256,256]{1,0:T(8,128)}) %all-reduce.17.cloned.1.call-update) | async-done | bytes 262160 | tf_op jit(solution)/shard_map/while/body/eval_jaxpr/psum | solution.py:140
  172.9 3.1 add_bitcast_fusion.5
  177.5 6.3 %dynamic_update_slice.28 = f32[2,512,512]{2,1,0:T(8,128)} dynamic-update-slice(f32[2,512,512]{2,1,0:T(8,128)} %get-tuple-element.1707, f32[2,256,256]{2,1,0:T(8,128)S(1)} %maximum_add_fusion.8, s32[]{:T(128)} %constant.1022.clone.1..sunk, s32[]{:T(128)S(6)} %select_n.362, s32[]{:T(128)S(6)} %select_n.363) | dynamic-update-slice | bytes 1048580 | tf_op jit(solution)/shard_map/while/body/eval_jaxpr/dynamic_update_slice | solution.py:148
  196.5 4.6 collective-permute-start.12
  201.1 4.0 collective-permute-start.13
  217.3 18.6 %all-reduce.9.cloned.1.call-done = f32[2,256,256]{2,1,0:T(8,128)} async-done(((f32[2,256,256]{2,1,0:T(8,128)}), f32[2,256,256]{2,1,0:T(8,128)}) %all-reduce.9.cloned.1.call-update) | async-done | bytes 524304 | tf_op jit(solution)/shard_map/psum | solution.py:163
  240.2 6.4 %collective-permute-start.18 = (f32[2,128,128]{2,1,0:T(8,128)S(1)}, f32[2,128,128]{2,1,0:T(8,128)S(1)}, u32[]{:S(2)}, u32[]{:S(2)}) collective-permute-start(f32[2,128,128]{2,1,0:T(8,128)S(1)} %get-tuple-element.1490), channel_id=1, source_target_pairs={{0,14},{1,15},{16,30},{17,31}} | collective-permute-start | bytes 393224 | tf_op jit(solution)/shard_map/ppermute | solution.py:19
  255.0 4.7 scatter.79
  263.2 3.8 scatter.80
  267.1 59.6 %all-reduce.11.cloned.1.call-done = f32[2,2,256,256]{3,2,1,0:T(8,128)} async-done(((f32[2,2,256,256]{3,2,1,0:T(8,128)}), f32[2,2,256,256]{3,2,1,0:T(8,128)}) %all-reduce.11.cloned.1.call-update) | async-done | bytes 1048592 | tf_op jit(solution)/shard_map/psum | solution.py:165
  333.6 150.9 %while.75 = (s32[]{:T(128)}, f32[2,512,512]{2,1,0:T(8,128)}, f32[2,2,256,256]{3,2,0,1:T(8,128)}, s32[2,2]{1,0:T(2,128)S(1)}, s32[]{:T(128)}, /*index=5*/s32[]{:T...) while((s32[]{:T(128)}, f32[2,512,512]{2,1,0:T(8,128)}, ...), condition=%wide.region_16.17_spmd.clone.clone, body=%wide.region_11.16_spmd.clone.clone.sunk | while | flops 6465257472 | bytes 45089252 | solution.py:161
  371.0 3.4 add_reduce_fusion.7
  375.1 17.3 %all-reduce.19.cloned.1.call-done = f32[256,256]{1,0:T(8,128)} async-done(((f32[256,256]{1,0:T(8,128)}), f32[256,256]{1,0:T(8,128)}) %all-reduce.19.cloned.1.call-update) | async-done | bytes 262160 | tf_op jit(solution)/shard_map/while/body/eval_jaxpr/psum | solution.py:140
  406.5 3.1 add_bitcast_fusion.6
  411.1 5.5 dynamic_update_slice.29
  434.0 3.4 add_reduce_fusion.7
  438.0 18.9 %all-reduce.19.cloned.1.call-done = f32[256,256]{1,0:T(8,128)} async-done(((f32[256,256]{1,0:T(8,128)}), f32[256,256]{1,0:T(8,128)}) %all-reduce.19.cloned.1.call-update) | async-done | bytes 262160 | tf_op jit(solution)/shard_map/while/body/eval_jaxpr/psum | solution.py:140
  471.1 3.1 add_bitcast_fusion.6
  475.7 6.3 %dynamic_update_slice.29 = f32[2,512,512]{2,1,0:T(8,128)} dynamic-update-slice(f32[2,512,512]{2,1,0:T(8,128)} %get-tuple-element.1755, f32[2,256,256]{2,1,0:T(8,128)S(1)} %maximum_add_fusion.10, s32[]{:T(128)} %constant.1022.clone.1..sunk.1, s32[]{:T(128)S(6)} %select_n.380, s32[]{:T(128)S(6)} %select_n.381) | dynamic-update-slice | bytes 1048580 | tf_op jit(solution)/shard_map/while/body/eval_jaxpr/dynamic_update_slice | solution.py:148
  491.0 4.6 collective-permute-start.28
  495.6 4.0 collective-permute-start.29
  511.9 18.5 %all-reduce.13.cloned.1.call-done = f32[2,256,256]{2,1,0:T(8,128)} async-done(((f32[2,256,256]{2,1,0:T(8,128)}), f32[2,256,256]{2,1,0:T(8,128)}) %all-reduce.13.cloned.1.call-update) | async-done | bytes 524304 | tf_op jit(solution)/shard_map/psum | solution.py:163
  532.3 81.1 %all-reduce.15.cloned.1.call-done = f32[2,2,256,256]{3,2,1,0:T(8,128)} async-done(((f32[2,2,256,256]{3,2,1,0:T(8,128)}), f32[2,2,256,256]{3,2,1,0:T(8,128)}) %all-reduce.15.cloned.1.call-update) | async-done | bytes 1048592 | tf_op jit(solution)/shard_map/psum | solution.py:165
  (282 shorter events, 221.5 us)
Async XLA Ops:
  10.0 18.3 %collective-permute-start = (f32[2,128,128]{2,1,0:T(8,128)}, f32[2,128,128]{2,1,0:T(8,128)}, u32[]{:S(2)}, u32[]{:S(2)}) collective-permute-start(f32[2,128,128]{2,1,0:T(8,128)} %get-tuple-element.1499), channel_id=1, source_target_pairs={} | collective-permute-start | bytes 393224 | tf_op jit(solution)/shard_map/ppermute | solution.py:19
  12.5 18.7 %collective-permute-start.1 = (f32[2,128,256]{2,1,0:T(8,128)S(1)}, f32[2,128,256]{2,1,0:T(8,128)S(1)}, u32[]{:S(2)}, u32[]{:S(2)}) collective-permute-start(f32[2,128,256]{2,1,0:T(8,128)S(1)} %get-tuple-element.1501), channel_id=1, source_target_pairs={} | collective-permute-start | bytes 786440 | tf_op jit(solution)/shard_map/ppermute | solution.py:19
  13.2 26.4 %collective-permute-start.2 = (f32[2,128,128]{2,1,0:T(8,128)}, f32[2,128,128]{2,1,0:T(8,128)S(1)}, u32[]{:S(2)}, u32[]{:S(2)}) collective-permute-start(f32[2,128,128]{2,1,0:T(8,128)} %get-tuple-element.1498), channel_id=1, source_target_pairs={{0,14},{1,15},{16,30},{17,31}} | collective-permute-start | bytes 393224 | tf_op jit(solution)/shard_map/ppermute | solution.py:19
  21.2 25.7 %collective-permute-start.3 = (f32[2,256,128]{2,1,0:T(8,128)S(1)}, f32[2,256,128]{2,1,0:T(8,128)S(1)}, u32[]{:S(2)}, u32[]{:S(2)}) collective-permute-start(f32[2,256,128]{2,1,0:T(8,128)S(1)} %get-tuple-element.1503), channel_id=1, source_target_pairs={{0,2},{2,4},{4,6},{6,8},{8,10},{10,12},{12,14},{1,3},{3,5},{5,7},{... | collective-permute-start | bytes 786440 | tf_op jit(solution)/shard_map/ppermute | solution.py:19
  22.5 25.1 %collective-permute-start.4 = (f32[2,256,128]{2,1,0:T(8,128)S(1)}, f32[2,256,128]{2,1,0:T(8,128)S(1)}, u32[]{:S(2)}, u32[]{:S(2)}) collective-permute-start(f32[2,256,128]{2,1,0:T(8,128)S(1)} %get-tuple-element.1502), channel_id=1, source_target_pairs={{2,0},{4,2},{6,4},{8,6},{10,8},{12,10},{14,12},{3,1},{5,3},{7,5},{... | collective-permute-start | bytes 786440 | tf_op jit(solution)/shard_map/ppermute | solution.py:19
  28.3 20.1 %collective-permute-start.5 = (f32[2,128,128]{2,1,0:T(8,128)}, f32[2,128,128]{2,1,0:T(8,128)}, u32[]{:S(2)}, u32[]{:S(2)}) collective-permute-start(f32[2,128,128]{2,1,0:T(8,128)} %get-tuple-element.1497), channel_id=1, source_target_pairs={{14,0},{15,1},{30,16},{31,17}} | collective-permute-start | bytes 393224 | tf_op jit(solution)/shard_map/ppermute | solution.py:19
  31.2 18.8 %collective-permute-start.6 = (f32[2,128,256]{2,1,0:T(8,128)S(1)}, f32[2,128,256]{2,1,0:T(8,128)S(1)}, u32[]{:S(2)}, u32[]{:S(2)}) collective-permute-start(f32[2,128,256]{2,1,0:T(8,128)S(1)} %get-tuple-element.1500), channel_id=1, source_target_pairs={} | collective-permute-start | bytes 786440 | tf_op jit(solution)/shard_map/ppermute | solution.py:19
  39.6 11.2 %collective-permute-start.7 = (f32[2,128,128]{2,1,0:T(8,128)}, f32[2,128,128]{2,1,0:T(8,128)S(1)}, u32[]{:S(2)}, u32[]{:S(2)}) collective-permute-start(f32[2,128,128]{2,1,0:T(8,128)} %get-tuple-element.1496), channel_id=1, source_target_pairs={} | collective-permute-start | bytes 393224 | tf_op jit(solution)/shard_map/ppermute | solution.py:19
  53.4 40.8 %all-reduce.17.cloned.1.call-start = ((), (), s32[]{:S(2)}) async-start(), calls=%async_computation.4 | async-start | bytes 524288 | tf_op jit(solution)/shard_map/while/body/eval_jaxpr/psum | solution.py:140
  119.5 39.2 %all-reduce.17.cloned.1.call-start = ((), (), s32[]{:S(2)}) async-start(), calls=%async_computation.4 | async-start | bytes 524288 | tf_op jit(solution)/shard_map/while/body/eval_jaxpr/psum | solution.py:140
  190.0 45.8 %all-reduce.9.cloned.1.call-start = ((), (), s32[]{:S(2)}) async-start(), calls=%async_computation | async-start | bytes 1048576 | tf_op jit(solution)/shard_map/psum | solution.py:163
  193.1 12.0 %collective-permute-start.9 = (f32[2,128,256]{2,1,0:T(8,128)S(1)}, f32[2,128,256]{2,1,0:T(8,128)S(1)}, u32[]{:S(2)}, u32[]{:S(2)}) collective-permute-start(f32[2,128,256]{2,1,0:T(8,128)S(1)} %get-tuple-element.1481), channel_id=1, source_target_pairs={} | collective-permute-start | bytes 786440 | tf_op jit(solution)/shard_map/ppermute | solution.py:19
  193.9 12.0 %collective-permute-start.10 = (f32[2,128,128]{2,1,0:T(8,128)S(1)}, f32[2,128,128]{2,1,0:T(8,128)S(1)}, u32[]{:S(2)}, u32[]{:S(2)}) collective-permute-start(f32[2,128,128]{2,1,0:T(8,128)S(1)} %get-tuple-element.1477), channel_id=1, source_target_pairs={{14,0},{15,1},{30,16},{31,17}} | collective-permute-start | bytes 393224 | tf_op jit(solution)/shard_map/ppermute | solution.py:19
  195.2 13.1 %collective-permute-start.11 = (f32[2,256,128]{2,1,0:T(8,128)S(1)}, f32[2,256,128]{2,1,0:T(8,128)S(1)}, u32[]{:S(2)}, u32[]{:S(2)}) collective-permute-start(f32[2,256,128]{2,1,0:T(8,128)S(1)} %get-tuple-element.1483), channel_id=1, source_target_pairs={{2,0},{4,2},{6,4},{8,6},{10,8},{12,10},{14,12},{3,1},{5,3},{7,5},{... | collective-permute-start | bytes 786440 | tf_op jit(solution)/shard_map/ppermute | solution.py:19
  196.5 14.2 %collective-permute-start.12 = (f32[2,256,128]{2,1,0:T(8,128)S(1)}, f32[2,256,128]{2,1,0:T(8,128)S(1)}, u32[]{:S(2)}, u32[]{:S(2)}) collective-permute-start(f32[2,256,128]{2,1,0:T(8,128)S(1)} %get-tuple-element.1482), channel_id=1, source_target_pairs={{0,2},{2,4},{4,6},{6,8},{8,10},{10,12},{12,14},{1,3},{3,5},{5,7},{... | collective-permute-start | bytes 786440 | tf_op jit(solution)/shard_map/ppermute | solution.py:19
  216.1 110.6 %all-reduce.11.cloned.1.call-start = ((), (), s32[]{:S(2)}) async-start(), calls=%async_computation.1 | async-start | bytes 2097152 | tf_op jit(solution)/shard_map/psum | solution.py:165
  238.6 10.6 %collective-permute-start.16 = (f32[2,128,128]{2,1,0:T(8,128)S(1)}, f32[2,128,128]{2,1,0:T(8,128)S(1)}, u32[]{:S(2)}, u32[]{:S(2)}) collective-permute-start(f32[2,128,128]{2,1,0:T(8,128)S(1)} %get-tuple-element.1491), channel_id=1, source_target_pairs={} | collective-permute-start | bytes 393224 | tf_op jit(solution)/shard_map/ppermute | solution.py:19
  239.5 11.8 %collective-permute-start.17 = (f32[2,128,256]{2,1,0:T(8,128)S(1)}, f32[2,128,256]{2,1,0:T(8,128)S(1)}, u32[]{:S(2)}, u32[]{:S(2)}) collective-permute-start(f32[2,128,256]{2,1,0:T(8,128)S(1)} %get-tuple-element.1493), channel_id=1, source_target_pairs={} | collective-permute-start | bytes 786440 | tf_op jit(solution)/shard_map/ppermute | solution.py:19
  240.2 19.6 %collective-permute-start.18 = (f32[2,128,128]{2,1,0:T(8,128)S(1)}, f32[2,128,128]{2,1,0:T(8,128)S(1)}, u32[]{:S(2)}, u32[]{:S(2)}) collective-permute-start(f32[2,128,128]{2,1,0:T(8,128)S(1)} %get-tuple-element.1490), channel_id=1, source_target_pairs={{0,14},{1,15},{16,30},{17,31}} | collective-permute-start | bytes 393224 | tf_op jit(solution)/shard_map/ppermute | solution.py:19
  246.7 81.5 %collective-permute-start.19 = (f32[2,256,128]{2,1,0:T(8,128)S(1)}, f32[2,256,128]{2,1,0:T(8,128)S(1)}, u32[]{:S(2)}, u32[]{:S(2)}) collective-permute-start(f32[2,256,128]{2,1,0:T(8,128)S(1)} %get-tuple-element.1495), channel_id=1, source_target_pairs={{0,2},{2,4},{4,6},{6,8},{8,10},{10,12},{12,14},{1,3},{3,5},{5,7},{... | collective-permute-start | bytes 786440 | tf_op jit(solution)/shard_map/ppermute | solution.py:19
  248.0 81.1 %collective-permute-start.20 = (f32[2,256,128]{2,1,0:T(8,128)S(1)}, f32[2,256,128]{2,1,0:T(8,128)S(1)}, u32[]{:S(2)}, u32[]{:S(2)}) collective-permute-start(f32[2,256,128]{2,1,0:T(8,128)S(1)} %get-tuple-element.1494), channel_id=1, source_target_pairs={{2,0},{4,2},{6,4},{8,6},{10,8},{12,10},{14,12},{3,1},{5,3},{7,5},{... | collective-permute-start | bytes 786440 | tf_op jit(solution)/shard_map/ppermute | solution.py:19
  249.3 80.6 %collective-permute-start.21 = (f32[2,128,128]{2,1,0:T(8,128)S(1)}, f32[2,128,128]{2,1,0:T(8,128)S(1)}, u32[]{:S(2)}, u32[]{:S(2)}) collective-permute-start(f32[2,128,128]{2,1,0:T(8,128)S(1)} %get-tuple-element.1489), channel_id=1, source_target_pairs={{14,0},{15,1},{30,16},{31,17}} | collective-permute-start | bytes 393224 | tf_op jit(solution)/shard_map/ppermute | solution.py:19
  251.3 79.3 %collective-permute-start.22 = (f32[2,128,256]{2,1,0:T(8,128)S(1)}, f32[2,128,256]{2,1,0:T(8,128)S(1)}, u32[]{:S(2)}, u32[]{:S(2)}) collective-permute-start(f32[2,128,256]{2,1,0:T(8,128)S(1)} %get-tuple-element.1492), channel_id=1, source_target_pairs={} | collective-permute-start | bytes 786440 | tf_op jit(solution)/shard_map/ppermute | solution.py:19
  259.7 71.6 %collective-permute-start.23 = (f32[2,128,128]{2,1,0:T(8,128)S(1)}, f32[2,128,128]{2,1,0:T(8,128)S(1)}, u32[]{:S(2)}, u32[]{:S(2)}) collective-permute-start(f32[2,128,128]{2,1,0:T(8,128)S(1)} %get-tuple-element.1488), channel_id=1, source_target_pairs={} | collective-permute-start | bytes 393224 | tf_op jit(solution)/shard_map/ppermute | solution.py:19
  354.8 37.6 %all-reduce.19.cloned.1.call-start = ((), (), s32[]{:S(2)}) async-start(), calls=%async_computation.5 | async-start | bytes 524288 | tf_op jit(solution)/shard_map/while/body/eval_jaxpr/psum | solution.py:140
  417.8 39.1 %all-reduce.19.cloned.1.call-start = ((), (), s32[]{:S(2)}) async-start(), calls=%async_computation.5 | async-start | bytes 524288 | tf_op jit(solution)/shard_map/while/body/eval_jaxpr/psum | solution.py:140
  484.6 45.8 %all-reduce.13.cloned.1.call-start = ((), (), s32[]{:S(2)}) async-start(), calls=%async_computation.2 | async-start | bytes 1048576 | tf_op jit(solution)/shard_map/psum | solution.py:163
  487.7 12.0 %collective-permute-start.25 = (f32[2,128,256]{2,1,0:T(8,128)S(1)}, f32[2,128,256]{2,1,0:T(8,128)S(1)}, u32[]{:S(2)}, u32[]{:S(2)}) collective-permute-start(f32[2,128,256]{2,1,0:T(8,128)S(1)} %get-tuple-element.1473), channel_id=1, source_target_pairs={} | collective-permute-start | bytes 786440 | tf_op jit(solution)/shard_map/ppermute | solution.py:19
  488.4 12.0 %collective-permute-start.26 = (f32[2,128,128]{2,1,0:T(8,128)S(1)}, f32[2,128,128]{2,1,0:T(8,128)S(1)}, u32[]{:S(2)}, u32[]{:S(2)}) collective-permute-start(f32[2,128,128]{2,1,0:T(8,128)S(1)} %get-tuple-element.1469), channel_id=1, source_target_pairs={{14,0},{15,1},{30,16},{31,17}} | collective-permute-start | bytes 393224 | tf_op jit(solution)/shard_map/ppermute | solution.py:19
  489.7 13.1 %collective-permute-start.27 = (f32[2,256,128]{2,1,0:T(8,128)S(1)}, f32[2,256,128]{2,1,0:T(8,128)S(1)}, u32[]{:S(2)}, u32[]{:S(2)}) collective-permute-start(f32[2,256,128]{2,1,0:T(8,128)S(1)} %get-tuple-element.1475), channel_id=1, source_target_pairs={{2,0},{4,2},{6,4},{8,6},{10,8},{12,10},{14,12},{3,1},{5,3},{7,5},{... | collective-permute-start | bytes 786440 | tf_op jit(solution)/shard_map/ppermute | solution.py:19
  491.0 14.2 %collective-permute-start.28 = (f32[2,256,128]{2,1,0:T(8,128)S(1)}, f32[2,256,128]{2,1,0:T(8,128)S(1)}, u32[]{:S(2)}, u32[]{:S(2)}) collective-permute-start(f32[2,256,128]{2,1,0:T(8,128)S(1)} %get-tuple-element.1474), channel_id=1, source_target_pairs={{0,2},{2,4},{4,6},{6,8},{8,10},{10,12},{12,14},{1,3},{3,5},{5,7},{... | collective-permute-start | bytes 786440 | tf_op jit(solution)/shard_map/ppermute | solution.py:19
  510.7 102.7 %all-reduce.15.cloned.1.call-start = ((), (), s32[]{:S(2)}) async-start(), calls=%async_computation.3 | async-start | bytes 2097152 | tf_op jit(solution)/shard_map/psum | solution.py:165
  (38 other events, 477.1 us)
Sparse Core Ops, SparseCore 0:
  73.1 20.9 all-reduce.16
  139.2 19.4 all-reduce.16
  374.5 17.7 all-reduce.18
  437.5 19.4 all-reduce.18
Sparse Core Ops, SparseCore 1:
  216.2 19.5 all-reduce.8
  240.2 86.4 all-reduce.10
  510.8 19.6 all-reduce.12
  534.3 79.1 all-reduce.14
where the time goes:
time: 628 us; the launch traced here: 624 us
  waiting for transfers between devices  262 us (42%)
  matrix products  129 us (21%)
  local copies, waits for them, and re-layouts  83.9 us (13%)
  starting transfers between devices  56.2 us (9%)
  other arithmetic  42.5 us (7%)
  loops' own time  33.7 us (5%)
  between operations  16.6 us (3%)
    psum x2, waiting for transfers between devices, per_device(): probe_sum = lax.psum(probe_grad, 'tile')  141 us
    psum x4, waiting for transfers between devices, visit(): power_sum = lax.psum(power_part, 'row')  75.6 us
    ppermute x32, starting transfers between devices, from_behind(): lax.ppermute(value, axis, [(source, source + steps) for source in range(i...  55.9 us
    psum x2, waiting for transfers between devices, per_device(): tile_grad = lax.psum(tile_grad, 'row')  37.1 us
    another operation x2, loops' own time, per_device(): object_grad, probe_grad = lax.fori_loop(0, slot_total, visit, start)  33.7 us
    scatter x16, local copies, waits for them, and re-layouts, extend_direct(): extended = extended.at[:, row_place:row_place + row_count, col_place:col_...  27.7 us
    dynamic_update_slice x4, local copies, waits for them, and re-layouts, visit(): lax.dynamic_update_slice(object_grad, current + jnp.stack([grad_real, gra...  23.7 us
    dot_general x8, matrix products, transform(): jnp.einsum('bij,jk->bik', left_imag, cosine, precision=precise)  20.9 us
  transfers between devices with their start and end apart: 40, of which 12 were waited for; matrix products, arithmetic and copies ran while one was open for 10% of the time, Pallas kernels for 0%

commit v1 on v0

v1 whole, which is shorter than its diff:
```python
import functools
import math

import jax
import jax.numpy as jnp
import numpy as np
from jax import lax
from jax.experimental import pallas as pl
from jax.experimental.pallas import tpu as pltpu
from jax.sharding import PartitionSpec as P

MODES = 4
GX = 8
ITERS = 2
CHUNK_BITS = 3
CHUNKS = 1 << CHUNK_BITS
ORDERS = ((0, 1, 2), (1, 0, 2))

f32 = jnp.float32
bf16 = jnp.bfloat16


def tables(length):
    half = length // 2
    n = np.arange(half)
    out = []
    for odd in (0, 1):
        angle = 2.0 * math.pi * np.outer(2 * n + odd, n) / length
        c, s = np.cos(angle) / math.sqrt(length), np.sin(angle) / math.sqrt(length)
        out.append(np.block([[c, s], [-s, c]]))
    forward = np.stack(out)
    both = np.stack([forward, np.transpose(forward, (0, 2, 1))]).astype(np.float32)
    high = both.astype(bf16)
    low = (both - high.astype(np.float32)).astype(bf16)
    return np.stack([high, low], axis=2)


def deinterleave(length):
    half = length // 2
    out = np.zeros((length, length), np.float32)
    out[2 * np.arange(half), np.arange(half)] = 1.0
    out[2 * np.arange(half) + 1, half + np.arange(half)] = 1.0
    return np.stack([out, out.T]).astype(bf16)


def split(x):
    high = x.astype(bf16)
    return high, (x - high.astype(f32)).astype(bf16)


def dot(a, b):
    return jnp.dot(a, b, preferred_element_type=f32)


def mul_left(table, x):
    high, low = split(x)
    return dot(table[0], high) + (dot(table[1], high) + dot(table[0], low))


def mul_right(x, table):
    high, low = split(x)
    return dot(high, table[0]) + (dot(high, table[1]) + dot(low, table[0]))


def forward(xr, xi, tab):
    h = xr.shape[0] // 2
    even = jnp.concatenate([xr[:h] + xr[h:], xi[:h] + xi[h:]], 0)
    odd = jnp.concatenate([xr[:h] - xr[h:], xi[:h] - xi[h:]], 0)
    ye = mul_left((tab[0, 0, 0], tab[0, 0, 1]), even)
    yo = mul_left((tab[0, 1, 0], tab[0, 1, 1]), odd)
    yr = jnp.concatenate([ye[:h], yo[:h]], 0)
    yi = jnp.concatenate([ye[h:], yo[h:]], 0)
    even = jnp.concatenate([yr[:, :h] + yr[:, h:], yi[:, :h] + yi[:, h:]], 1)
    odd = jnp.concatenate([yr[:, :h] - yr[:, h:], yi[:, :h] - yi[:, h:]], 1)
    fe = mul_right(even, (tab[1, 0, 0], tab[1, 0, 1]))
    fo = mul_right(odd, (tab[1, 1, 0], tab[1, 1, 1]))
    return fe, fo


def inverse(fe, fo, tab):
    h = fe.shape[0] // 2
    he = mul_right(fe, (tab[0, 0, 0], tab[0, 0, 1]))
    ho = mul_right(fo, (tab[0, 1, 0], tab[0, 1, 1]))
    yr = jnp.concatenate([he[:, :h] + ho[:, :h], he[:, :h] - ho[:, :h]], 1)
    yi = jnp.concatenate([he[:, h:] + ho[:, h:], he[:, h:] - ho[:, h:]], 1)
    xe = mul_left((tab[1, 0, 0], tab[1, 0, 1]), jnp.concatenate([yr[:h], yi[:h]], 0))
    xo = mul_left((tab[1, 1, 0], tab[1, 1, 1]), jnp.concatenate([yr[h:], yi[h:]], 0))
    xr = jnp.concatenate([xe[:h] + xo[:h], xe[:h] - xo[:h]], 0)
    xi = jnp.concatenate([xe[h:] + xo[h:], xe[h:] - xo[h:]], 0)
    return xr, xi


def exact(x):
    high = x.astype(bf16)
    rest = x - high.astype(f32)
    mid = rest.astype(bf16)
    return high, mid, (rest - mid.astype(f32)).astype(bf16)


def amplitude_kernel(amp, perm, out):
    for s in range(amp.shape[0]):
        high, mid, low = exact(amp[s])
        rows = dot(perm[1], high) + (dot(perm[1], mid) + dot(perm[1], low))
        high, mid, low = exact(rows)
        out[s] = dot(high, perm[0]) + (dot(mid, perm[0]) + dot(low, perm[0]))


def update_probe(sm, old, pieces, coef, out):
    rows = old.shape[2] // CHUNKS
    for mode in range(len(pieces)):
        rel = 0
        for piece in pieces[mode]:
            for k in range(piece.shape[0]):
                start = pl.multiple_of((rel ^ sm[4 + mode]) * rows, rows)
                here = pl.ds(start, rows)
                out[mode, :, here, :] = old[mode, :, here, :] + coef * piece[k]
                rel += 1


def forward_kernel(slot, n_pieces, coef, tall, *refs):
    refs = list(refs)
    sm, near, far_half, probe, tab = refs[:5]
    refs = refs[5:]
    if n_pieces:
        modes = probe.shape[0]
        pieces = [refs[m * n_pieces : (m + 1) * n_pieces] for m in range(modes)]
        refs = refs[modes * n_pieces :]
        new_probe = refs.pop(3)
        update_probe(sm, probe, pieces, coef, new_probe)
        probe = new_probe
    far, power, patch, window = refs
    frame = probe.shape[-1]
    core = sm[6]
    window[core] = near[...]
    window[1 - core] = far_half[...]
    cols = window.shape[-1]
    for c in range(2):
        whole = jnp.concatenate([window[0, c], window[1, c]], 0)
        moved = pltpu.roll(whole, lax.rem(cols - sm[slot], cols), 1)[:, :frame]
        if tall:
            rows = whole.shape[0]
            moved = pltpu.roll(moved, lax.rem(rows - sm[2 + slot], rows), 0)[:frame]
        patch[c] = moved
    total = None
    for m in range(probe.shape[0]):
        pr, pi = probe[m, 0], probe[m, 1]
        exit_real = pr * patch[0] - pi * patch[1]
        exit_imag = pr * patch[1] + pi * patch[0]
        fe, fo = forward(exit_real, exit_imag, tab)
        far[m, 0] = fe
        far[m, 1] = fo
        h = frame // 2
        sq = jnp.concatenate(
            [fe[:, :h] * fe[:, :h] + fe[:, h:] * fe[:, h:], fo[:, :h] * fo[:, :h] + fo[:, h:] * fo[:, h:]], 1
        )
        total = sq if total is None else total + sq
    power[...] = total


def inverse_kernel(mode, last, tall, *refs):
    refs = list(refs)
    sm, tab, amp, probe = refs[:4]
    refs = refs[4:]
    slots = amp.shape[0]
    fars, powers, others, patches = (refs[i * slots : (i + 1) * slots] for i in range(4))
    refs = refs[4 * slots :]
    if mode:
        before = refs.pop(0)
    send, keep = refs[:2]
    refs = refs[2:]
    frame = probe.shape[-1]
    h = frame // 2
    pr, pi = probe[mode, 0], probe[mode, 1]
    probe_real = probe_imag = None
    windows = [None, None]
    for s in range(slots):
        live = (s < sm[7]).astype(f32)
        factor = amp[s] / (jnp.sqrt(powers[s][...] + others[s][...]) + 0.5)
        even = jnp.concatenate([factor[:, :h]] * 2, 1)
        odd = jnp.concatenate([factor[:, h:]] * 2, 1)
        xr, xi = inverse(fars[s][mode, 0] * even, fars[s][mode, 1] * odd, tab)
        ar, ai = patches[s][0], patches[s][1]
        ur = (xr - (pr * ar - pi * ai)) * live
        ui = (xi - (pr * ai + pi * ar)) * live
        gr = pr * ur + pi * ui
        gi = pr * ui - pi * ur
        qr = ar * ur + ai * ui
        qi = ar * ui - ai * ur
        probe_real = qr if probe_real is None else probe_real + qr
        probe_imag = qi if probe_imag is None else probe_imag + qi
        if mode:
            gr = gr + before[s, 0]
            gi = gi + before[s, 1]
        if not last:
            refs[0][s, 0] = gr
            refs[0][s, 1] = gi
        else:
            near, away = refs[0], refs[1]
            cols, rows = near.shape[-1], 2 * near.shape[1]
            for c, g in enumerate((gr, gi)):
                if tall:
                    g = jnp.concatenate([g, jnp.zeros((rows - frame, frame), f32)], 0)
                    g = pltpu.roll(g, sm[2 + s], 0)
                g = jnp.concatenate([g, jnp.zeros((rows, cols - frame), f32)], 1)
                g = pltpu.roll(g, sm[s], 1)
                windows[c] = g if windows[c] is None else windows[c] + g
    if last:
        near, away, both = refs
        core = sm[6]
        hr = near.shape[1]
        for c in range(2):
            both[0, c] = windows[c][:hr]
            both[1, c] = windows[c][hr:]
        near[...] = both[core]
        away[...] = both[1 - core]
    work = refs[-1] if not last else None
    rows = frame // CHUNKS
    quarter = CHUNKS // 2
    for c in range(CHUNKS):
        rel = c ^ sm[4 + mode]
        upper = rel >= quarter
        for k, q in enumerate((probe_real, probe_imag)):
            piece = q[c * rows : (c + 1) * rows]

            @pl.when(upper)
            def _():
                send[rel - quarter, k] = piece

            @pl.when(jnp.logical_not(upper))
            def _():
                keep[rel, k] = piece


def finish_kernel(n_pieces, coef, *refs):
    refs = list(refs)
    sm, near, away, probe = refs[:4]
    modes = probe.shape[0]
    pieces = [refs[4 + m * n_pieces : 4 + (m + 1) * n_pieces] for m in range(modes)]
    tile, new_probe = refs[-2:]
    update_probe(sm, probe, pieces, coef, new_probe)
    hr = near.shape[1]
    core = sm[6]
    tile[:, pl.ds(pl.multiple_of(core * hr, hr), hr), :] = near[...]
    tile[:, pl.ds(pl.multiple_of((1 - core) * hr, hr), hr), :] = away[...]


def vmem():
    return pl.BlockSpec(memory_space=pltpu.VMEM)


def call(kernel, outs, args, scratch=(), flops=0):
    size = sum(math.prod(a.shape) * a.dtype.itemsize for a in args)
    size += sum(math.prod(o) * 4 for o in outs)
    return pl.pallas_call(
        kernel,
        out_shape=[jax.ShapeDtypeStruct(o, f32) for o in outs],
        in_specs=[
            pl.BlockSpec(memory_space=pltpu.SMEM) if a.ndim == 1 else vmem() for a in args
        ],
        out_specs=[vmem() for _ in outs],
        scratch_shapes=list(scratch),
        cost_estimate=pl.CostEstimate(flops=flops, bytes_accessed=size, transcendentals=0),
        compiler_params=pltpu.CompilerParams(vmem_limit_bytes=40 * 1024 * 1024),
    )(*args)


def swap_rows(x):
    return lax.ppermute(x, "row", [(0, 1), (1, 0)])


def shift_cols(x, step, tiles):
    pairs = [(s, s + step) for s in range(tiles) if 0 <= s % GX + step < GX]
    return lax.ppermute(x, "tile", pairs)


def swap_vertical(x, tiles):
    pairs = [(2 * t, 2 * (t - GX) + 1) for t in range(GX, tiles)]
    pairs += [(2 * t + 1, 2 * (t + GX)) for t in range(tiles - GX)]
    return lax.ppermute(x, ("tile", "row"), pairs)


def exchange(x, bit, tiles):
    return lax.ppermute(x, "tile", [(s, s ^ (1 << bit)) for s in range(tiles)])


def reduce_chunks(send, keep, order, tiles):
    bits = int(math.log2(tiles))
    for i, bit in enumerate(order):
        got = exchange(send, bit, tiles)
        if i + 1 < len(order):
            n = keep.shape[0] // 2
            send, keep = keep[n:] + got[n:], keep[:n] + got[:n]
        else:
            keep = keep + got
    for bit in range(CHUNK_BITS, bits):
        keep = keep + exchange(keep, bit, tiles)
    pieces = [keep]
    for bit in reversed(order):
        block = pieces[0] if len(pieces) == 1 else jnp.concatenate(pieces, 0)
        pieces.append(exchange(block, bit, tiles))
    return pieces


def per_device(object_tiles, probe_modes, amplitude, offsets, counts):
    own_tile = object_tiles[0]
    size = own_tile.shape[-1]
    frame = probe_modes.shape[-1]
    half = frame // 2
    tiles = lax.axis_size("tile")
    tall = tiles > GX
    slots = offsets.shape[0]
    modes = probe_modes.shape[0]
    t = lax.axis_index("tile")
    core = lax.axis_index("row")
    hr = size // 2
    col0 = (t % GX) * size - half
    row0 = (t // GX) * size - (half if tall else 0)

    def key(order):
        return sum(((t >> bit) & 1) << (len(order) - 1 - i) for i, bit in enumerate(order))

    scalars = jnp.stack(
        [offsets[0, 1] - col0, offsets[1, 1] - col0, offsets[0, 0] - row0, offsets[1, 0] - row0]
        + [key(o) for o in ORDERS]
        + [core, counts[0]]
    ).astype(jnp.int32)
    tab = jnp.asarray(tables(frame))
    perm = jnp.asarray(deinterleave(frame))
    coef = 4.0 / (slots * tiles)

    mine = lax.dynamic_slice(own_tile, (0, core * hr, 0), (2, hr, size))
    from_left = shift_cols(mine[:, :, size - half :], 1, tiles)
    from_right = shift_cols(mine[:, :, :half], -1, tiles)
    near = jnp.concatenate([from_left, mine, from_right], 2)
    if tall:
        other = swap_vertical(near, tiles)
        near = jnp.where(core == 0, jnp.concatenate([other, near], 1), jnp.concatenate([near, other], 1))
    away = swap_rows(near)
    (amp,) = call(amplitude_kernel, [amplitude.shape], [amplitude, perm])

    matmul = 2 * 3 * 4 * frame**3
    probe = probe_modes
    pieces = None
    for iteration in range(ITERS):
        fars, powers, others, patches = [], [], [], []
        for s in range(slots):
            args = [scalars, near, away, probe, tab]
            outs = [(modes, 2, frame, frame), (frame, frame), (2, frame, frame)]
            count = 0
            if pieces is not None:
                count = len(pieces[0])
                args += [p for group in pieces for p in group]
                outs.append(probe.shape)
                pieces = None
            got = call(
                functools.partial(forward_kernel, s, count, coef, tall),
                outs,
                args,
                [pltpu.VMEM((2,) + near.shape, f32)],
                matmul * modes,
            )
            if count:
                probe = got[3]
            fars.append(got[0])
            powers.append(got[1])
            patches.append(got[2])
            others.append(swap_rows(got[1]))
        before = None
        pieces = []
        for m in range(modes):
            last = m == modes - 1
            args = [scalars, tab, amp, probe] + fars + powers + others + patches
            if m:
                args.append(before)
            part = (CHUNKS // 2, 2, frame // CHUNKS, frame)
            outs = [part, part]
            outs += [near.shape, near.shape] if last else [(slots, 2, frame, frame)]
            scratch = [pltpu.VMEM((2,) + near.shape, f32)] if last else []
            got = call(
                functools.partial(inverse_kernel, m, last, tall), outs, args, scratch, matmul * slots
            )
            before = got[2]
            pieces.append((got[0], got[1]))
        grad = got[2] + swap_rows(got[3])
        pieces = [reduce_chunks(a, b, o, tiles) for (a, b), o in zip(pieces, ORDERS)]
        if iteration + 1 < ITERS or tall:
            left, right = grad[:, :, :size], grad[:, :, size:]
            left = left + shift_cols(right, 1, tiles)
            right = right + shift_cols(grad[:, :, :size], -1, tiles)
            total = jnp.concatenate([left, right], 2)
            if tall:
                total = total + swap_vertical(total, tiles)
            near = near + total / MODES
            if iteration + 1 < ITERS:
                away = swap_rows(near)
            else:
                near = near[:, :, half : half + size]
                near = jnp.where(core == 0, near[:, half:], near[:, : size - half])
        else:
            got_left = shift_cols(grad[:, :, half + size :], 1, tiles)
            got_right = shift_cols(grad[:, :, :half], -1, tiles)
            total = grad[:, :, half : half + size] + jnp.concatenate([got_left, got_right], 2)
            near = near[:, :, half : half + size] + total / MODES
    away = swap_rows(near)
    args = [scalars, near, away, probe] + [p for group in pieces for p in group]
    tile, probe = call(
        functools.partial(finish_kernel, len(pieces[0]), coef), [own_tile.shape, probe.shape], args
    )
    return (tile[None], probe)


def solution(mesh):
    return jax.shard_map(
        per_device,
        mesh=mesh,
        in_specs=(
            P(("scan", "tile"), None, None, None),
            P("row", None, None, None),
            P(("scan", "tile"), None, None),
            P(("scan", "tile"), None),
            P(("scan", "tile")),
        ),
        out_specs=(P(("scan", "tile"), None, None, None), P(("scan", "row"), None, None, None)),
        check_vma=False,
    )
```

time: 628 us -> 142 us (0.23)
  waiting for transfers between devices: 262 us -> 52.7 us
  matrix products: 129 us -> 0 us
  local copies, waits for them, and re-layouts: 83.9 us -> 3.19 us
  other arithmetic: 42.5 us -> 0.77 us
  loops' own time: 33.7 us -> 0 us
  Pallas kernels: 0 us -> 23.5 us
  between operations: 16.6 us -> 4.3 us
    psum x8 -> x0, waiting for transfers between devices: 253 us -> none  [the longest x2 141 us: per_device(): probe_sum = lax.psum(probe_grad, 'tile')]
    dot_general x64 -> x0, matrix products: 129 us -> none  [the longest x8 20.9 us: transform(): jnp.einsum('bij,jk->bik', left_imag, cosine, precision=precise)]
    ppermute x32 -> x39, waiting for transfers between devices: 8.21 us -> 52.7 us  [the longest x24 40.6 us: exchange(): return lax.ppermute(x, 'tile', [(s, s ^ 1 << bit) for s in range(tiles)])]
    another operation x2 -> x0, loops' own time: 33.7 us -> none  [per_device(): object_grad, probe_grad = lax.fori_loop(0, slot_total, visit, start)]
    scatter x18 -> x0, local copies, waits for them, and re-layouts: 31 us -> none  [the longest x16 27.7 us: extend_direct(): extended = extended.at[:, row_place:row_place + row_count, col_place:col_...]
    dynamic_update_slice x4 -> x0, local copies, waits for them, and re-layouts: 23.7 us -> none  [visit(): lax.dynamic_update_slice(object_grad, current + jnp.stack([grad_real, gra...]
    pallas_call x0 -> x10, Pallas kernels: none -> 23.5 us  [call(): pl.pallas_call(kernel, out_shape=[jax.ShapeDtypeStruct(o, f32) for o in o...]
    another operation x10 -> x0, other arithmetic: 17.1 us -> none
  transfers between devices with their start and end apart: 40 -> 39, of which waited for: 12 -> 21; matrix products, arithmetic and copies ran while one was open for 10% -> 1% of each run, Pallas kernels for 0% -> 4%
where the time goes in v1:
time: 142 us
  starting transfers between devices  57.7 us (41%)
  waiting for transfers between devices  52.7 us (37%)
  Pallas kernels  23.5 us (17%)
  between operations  4.3 us (3%)
  local copies, waits for them, and re-layouts  3.19 us (2%)
    ppermute x24, waiting for transfers between devices, exchange(): return lax.ppermute(x, 'tile', [(s, s ^ 1 << bit) for s in range(tiles)])  40.6 us
    ppermute x24, starting transfers between devices, exchange(): return lax.ppermute(x, 'tile', [(s, s ^ 1 << bit) for s in range(tiles)])  40.5 us
    pallas_call x10, Pallas kernels, call(): pl.pallas_call(kernel, out_shape=[jax.ShapeDtypeStruct(o, f32) for o in o...  23.5 us
    ppermute x6, starting transfers between devices, shift_cols(): return lax.ppermute(x, 'tile', pairs)  15.7 us
    ppermute x6, waiting for transfers between devices, shift_cols(): return lax.ppermute(x, 'tile', pairs)  10.3 us
  transfers between devices with their start and end apart: 39, of which 21 were waited for; matrix products, arithmetic and copies ran while one was open for 1% of the time, Pallas kernels for 4%

profile of v1, /device:TPU:0, one launch (start us, length us, event | category | flops | bytes accessed | tf_op | source)
XLA Modules:
  0.0 142.1 jit_solution(12247232597937491589)
XLA Ops:
  1.7 5.0 %collective-permute-start = (f32[2,128,128]{2,1,0:T(8,128)S(1)}, f32[2,128,128]{2,1,0:T(8,128)S(1)}, u32[]{:S(2)}, u32[]{:S(2)}) collective-permute-start(f32[2,128,128]{2,1,0:T(8,128)S(1)} %get-tuple-element.74), channel_id=1, source_target_pairs={{0,2},{2,4},{4,6},{6,8},{8,10},{10,12},{12,14},{1,3},{3,5},{5,7},{... | collective-permute-start | bytes 393224 | tf_op jit(solution)/shard_map/ppermute | solution.py:273
  9.5 4.1 %collective-permute-done.1 = f32[2,128,128]{2,1,0:T(8,128)S(1)} collective-permute-done((f32[2,128,128]{2,1,0:T(8,128)S(1)}, f32[2,128,128]{2,1,0:T(8,128)S(1)}, u32[]{:S(2)}, u32[]{:S(2)}) %collective-permute-start.1) | collective-permute-done | bytes 131104 | tf_op jit(solution)/shard_map/ppermute | solution.py:273
  19.0 2.7 %shard_map.88 = (f32[2,2,256,256]{3,2,1,0:T(8,128)S(1)}, f32[256,256]{1,0:T(8,128)S(1)}, f32[2,256,256]{2,1,0:T(8,128)S(1)}) custom-call(s32[8]{0:T(128)S(1)} %stack.31.refs_0_, f32[2,128,512]{2,1,0:T(8,128)S(1)} %pad_maximum_fusion.refs_1_, f32[2,128,512]{2,1,0:T(8,128)} %collective-permute-done.2.refs_2_, f32[2,2,256,256]{3,2,1,0:T(8,128)S(1)} %copy-done.2, ...), custom_call_target="tpu_custom_call" | custom-call | flops 805306368 | bytes 4980768 | tf_op jit(solution)/shard_map/pallas_call | solution.py:254
  22.3 2.7 %shard_map.87 = (f32[2,2,256,256]{3,2,1,0:T(8,128)S(1)}, f32[256,256]{1,0:T(8,128)S(1)}, f32[2,256,256]{2,1,0:T(8,128)S(1)}) custom-call(s32[8]{0:T(128)S(1)} %stack.31.refs_0_, f32[2,128,512]{2,1,0:T(8,128)S(1)} %pad_maximum_fusion.refs_1_, f32[2,128,512]{2,1,0:T(8,128)} %collective-permute-done.2.refs_2_, f32[2,2,256,256]{3,2,1,0:T(8,128)S(1)} %copy-done.2, ...), custom_call_target="tpu_custom_call" | custom-call | flops 805306368 | bytes 4980768 | tf_op jit(solution)/shard_map/pallas_call | solution.py:254
  26.6 2.6 %shard_map.89 = (f32[4,2,32,256]{3,2,1,0:T(8,128)S(1)}, f32[4,2,32,256]{3,2,1,0:T(8,128)S(1)}, f32[2,2,256,256]{3,2,1,0:T(8,128)S(1)}) custom-call(s32[8]{0:T(128)S(1)} %stack.31.refs_0_, bf16[2,2,2,256,256]{4,3,2,1,0:T(8,128)(2,1)S(1)} %copy-done.1, f32[2,256,256]{2,1,0:T(8,128)S(1)} %shard_map.86.refs_2_, f32[2,2,256,256]{3,2,1,0:T(8,128)S(1)} %copy-done.2, ...), custom_call_target="tpu_custom_call" | custom-call | flops 805306368 | bytes 8388640 | tf_op jit(solution)/shard_map/pallas_call | solution.py:254
  29.2 2.9 %shard_map.90 = (f32[4,2,32,256]{3,2,1,0:T(8,128)S(1)}, f32[4,2,32,256]{3,2,1,0:T(8,128)S(1)}, f32[2,128,512]{2,1,0:T(8,128)S(1)}, f32[2,128,512]{2,1,0:T(8,128)S(1)}) custom-call(s32[8]{0:T(128)S(1)} %stack.31.refs_0_, bf16[2,2,2,256,256]{4,3,2,1,0:T(8,128)(2,1)S(1)} %copy-done.1, f32[2,256,256]{2,1,0:T(8,128)S(1)} %shard_map.86.refs_2_, ...), custom_call_target="tpu_custom_call" | custom-call | flops 805306368 | bytes 9437216 | tf_op jit(solution)/shard_map/pallas_call | solution.py:254
  32.1 2.2 %collective-permute-start.15 = (f32[4,2,32,256]{3,2,1,0:T(8,128)S(1)}, f32[4,2,32,256]{3,2,1,0:T(8,128)S(1)}, u32[]{:S(2)}, u32[]{:S(2)}) collective-permute-start(f32[4,2,32,256]{3,2,1,0:T(8,128)S(1)} %get-tuple-element.43), channel_id=1, source_target_pairs={{0,4},{2,6},{4,0},{6,2},{8,12},{10,14},{12,8},{14,10},{1,5},{3,7},... | collective-permute-start | bytes 786440 | tf_op jit(solution)/shard_map/ppermute | solution.py:283
  34.3 1.9 %collective-permute-start.9 = (f32[4,2,32,256]{3,2,1,0:T(8,128)S(1)}, f32[4,2,32,256]{3,2,1,0:T(8,128)S(1)}, u32[]{:S(2)}, u32[]{:S(2)}) collective-permute-start(f32[4,2,32,256]{3,2,1,0:T(8,128)S(1)} %get-tuple-element.41), channel_id=1, source_target_pairs={{0,2},{2,0},{4,6},{6,4},{8,10},{10,8},{12,14},{14,12},{1,3},{3,1},... | collective-permute-start | bytes 786440 | tf_op jit(solution)/shard_map/ppermute | solution.py:283
  36.2 4.7 %collective-permute-done.15 = f32[4,2,32,256]{3,2,1,0:T(8,128)S(1)} collective-permute-done((f32[4,2,32,256]{3,2,1,0:T(8,128)S(1)}, f32[4,2,32,256]{3,2,1,0:T(8,128)S(1)}, u32[]{:S(2)}, u32[]{:S(2)}) %collective-permute-start.15) | collective-permute-done | bytes 262176 | tf_op jit(solution)/shard_map/ppermute | solution.py:283
  40.9 2.1 %collective-permute-start.16 = (f32[2,2,32,256]{3,2,1,0:T(8,128)S(1)}, f32[2,2,32,256]{3,2,1,0:T(8,128)S(1)}, u32[]{:S(2)}, u32[]{:S(2)}) collective-permute-start(f32[2,2,32,256]{3,2,1,0:T(8,128)S(1)} %get-tuple-element.67), channel_id=1, source_target_pairs={{0,2},{2,0},{4,6},{6,4},{8,10},{10,8},{12,14},{14,12},{1,3},{3,1},... | collective-permute-start | bytes 393224 | tf_op jit(solution)/shard_map/ppermute | solution.py:283
  46.0 2.8 %collective-permute-start.17 = (f32[1,2,32,256]{3,2,1,0:T(8,128)S(1)}, f32[1,2,32,256]{3,2,1,0:T(8,128)S(1)}, u32[]{:S(2)}, u32[]{:S(2)}) collective-permute-start(f32[1,2,32,256]{3,2,1,0:T(8,128)S(1)} %slice_add_fusion.13), channel_id=1, source_target_pairs={{0,8},{2,10},{4,12},{6,14},{8,0},{10,2},{12,4},{14,6},{1,9},{3,11}... | collective-permute-start | bytes 196616 | tf_op jit(solution)/shard_map/ppermute | solution.py:283
  48.8 2.7 %collective-permute-start.11 = (f32[1,2,32,256]{3,2,1,0:T(8,128)S(1)}, f32[1,2,32,256]{3,2,1,0:T(8,128)S(1)}, u32[]{:S(2)}, u32[]{:S(2)}) collective-permute-start(f32[1,2,32,256]{3,2,1,0:T(8,128)S(1)} %slice_add_fusion.15), channel_id=1, source_target_pairs={{0,8},{2,10},{4,12},{6,14},{8,0},{10,2},{12,4},{14,6},{1,9},{3,11}... | collective-permute-start | bytes 196616 | tf_op jit(solution)/shard_map/ppermute | solution.py:283
  51.5 1.9 %collective-permute-done.17 = f32[1,2,32,256]{3,2,1,0:T(8,128)S(1)} collective-permute-done((f32[1,2,32,256]{3,2,1,0:T(8,128)S(1)}, f32[1,2,32,256]{3,2,1,0:T(8,128)S(1)}, u32[]{:S(2)}, u32[]{:S(2)}) %collective-permute-start.17) | collective-permute-done | bytes 65568 | tf_op jit(solution)/shard_map/ppermute | solution.py:283
  54.2 4.6 %collective-permute-start.6 = (f32[2,128,256]{2,1,0:T(8,128)S(1)}, f32[2,128,256]{2,1,0:T(8,128)S(1)}, u32[]{:S(2)}, u32[]{:S(2)}) collective-permute-start(f32[2,128,256]{2,1,0:T(8,128)S(1)} %get-tuple-element.72), channel_id=1, source_target_pairs={{0,2},{2,4},{4,6},{6,8},{8,10},{10,12},{12,14},{1,3},{3,5},{5,7},{... | collective-permute-start | bytes 786440 | tf_op jit(solution)/shard_map/ppermute | solution.py:273
  60.3 3.7 %collective-permute-start.12 = (f32[1,2,32,256]{3,2,1,0:T(8,128)S(1)}, f32[1,2,32,256]{3,2,1,0:T(8,128)S(1)}, u32[]{:S(2)}, u32[]{:S(2)}) collective-permute-start(f32[1,2,32,256]{3,2,1,0:T(8,128)S(1)} %fusion.6.refs_5_), channel_id=1, source_target_pairs={{0,8},{2,10},{4,12},{6,14},{8,0},{10,2},{12,4},{14,6},{1,9},{3,11}... | collective-permute-start | bytes 196616 | tf_op jit(solution)/shard_map/ppermute | solution.py:283
  64.1 1.9 %collective-permute-start.19 = (f32[2,2,32,256]{3,2,1,0:T(8,128)S(1)}, f32[2,2,32,256]{3,2,1,0:T(8,128)S(1)}, u32[]{:S(2)}, u32[]{:S(2)}) collective-permute-start(f32[2,2,32,256]{3,2,1,0:T(8,128)S(1)} %pad_maximum_fusion.6), channel_id=1, source_target_pairs={{0,2},{2,0},{4,6},{6,4},{8,10},{10,8},{12,14},{14,12},{1,3},{3,1},... | collective-permute-start | bytes 393224 | tf_op jit(solution)/shard_map/ppermute | solution.py:283
  66.0 3.0 %collective-permute-done.6 = f32[2,128,256]{2,1,0:T(8,128)S(1)} collective-permute-done((f32[2,128,256]{2,1,0:T(8,128)S(1)}, f32[2,128,256]{2,1,0:T(8,128)S(1)}, u32[]{:S(2)}, u32[]{:S(2)}) %collective-permute-start.6) | collective-permute-done | bytes 262176 | tf_op jit(solution)/shard_map/ppermute | solution.py:273
  69.3 3.0 %collective-permute-start.13 = (f32[2,2,32,256]{3,2,1,0:T(8,128)S(1)}, f32[2,2,32,256]{3,2,1,0:T(8,128)S(1)}, u32[]{:S(2)}, u32[]{:S(2)}) collective-permute-start(f32[2,2,32,256]{3,2,1,0:T(8,128)S(1)} %pad_maximum_fusion.5), channel_id=1, source_target_pairs={{0,4},{2,6},{4,0},{6,2},{8,12},{10,14},{12,8},{14,10},{1,5},{3,7},... | collective-permute-start | bytes 393224 | tf_op jit(solution)/shard_map/ppermute | solution.py:283
  73.4 3.2 %collective-permute-done.13.refs_7_ = f32[2,2,32,256]{3,2,1,0:T(8,128)S(1)} collective-permute-done((f32[2,2,32,256]{3,2,1,0:T(8,128)S(1)}, f32[2,2,32,256]{3,2,1,0:T(8,128)S(1)}, u32[]{:S(2)}, u32[]{:S(2)}) %collective-permute-start.13) | collective-permute-done | bytes 131104 | tf_op jit(solution)/shard_map/ppermute | solution.py:283
  78.2 3.8 %collective-permute-done.20.refs_12_ = f32[4,2,32,256]{3,2,1,0:T(8,128)S(1)} collective-permute-done((f32[4,2,32,256]{3,2,1,0:T(8,128)S(1)}, f32[4,2,32,256]{3,2,1,0:T(8,128)S(1)}, u32[]{:S(2)}, u32[]{:S(2)}) %collective-permute-start.20) | collective-permute-done | bytes 262176 | tf_op jit(solution)/shard_map/ppermute | solution.py:283
  82.0 2.6 %collective-permute-done.14.refs_8_ = f32[4,2,32,256]{3,2,1,0:T(8,128)S(1)} collective-permute-done((f32[4,2,32,256]{3,2,1,0:T(8,128)S(1)}, f32[4,2,32,256]{3,2,1,0:T(8,128)S(1)}, u32[]{:S(2)}, u32[]{:S(2)}) %collective-permute-start.14) | collective-permute-done | bytes 262176 | tf_op jit(solution)/shard_map/ppermute | solution.py:283
  84.6 2.3 %shard_map.91 = (f32[2,2,256,256]{3,2,1,0:T(8,128)S(1)}, f32[256,256]{1,0:T(8,128)S(1)}, f32[2,256,256]{2,1,0:T(8,128)S(1)}, f32[2,2,256,256]{3,2,1,0:T(8,128)S(1)}) custom-call(s32[8]{0:T(128)S(1)} %stack.31.refs_0_, f32[2,128,512]{2,1,0:T(8,128)S(1)} %fusion.refs_1_, f32[2,128,512]{2,1,0:T(8,128)S(1)} %collective-permute-done.8.refs_2_, ...), custom_call_target="tpu_custom_call" | custom-call | flops 805306368 | bytes 7077920 | tf_op jit(solution)/shard_map/pallas_call | solution.py:254
  86.9 2.2 %shard_map.92 = (f32[2,2,256,256]{3,2,1,0:T(8,128)S(1)}, f32[256,256]{1,0:T(8,128)S(1)}, f32[2,256,256]{2,1,0:T(8,128)S(1)}) custom-call(s32[8]{0:T(128)S(1)} %stack.31.refs_0_, f32[2,128,512]{2,1,0:T(8,128)S(1)} %fusion.refs_1_, f32[2,128,512]{2,1,0:T(8,128)S(1)} %collective-permute-done.8.refs_2_, f32[2,2,256,256]{3,2,1,0:T(8,128)S(1)} %get-tuple-element.44.refs_3_, ...), custom_call_target="tpu_custom_call" | custom-call | flops 805306368 | bytes 4980768 | tf_op jit(solution)/shard_map/pallas_call | solution.py:254
  90.9 2.5 %shard_map.93 = (f32[4,2,32,256]{3,2,1,0:T(8,128)S(1)}, f32[4,2,32,256]{3,2,1,0:T(8,128)S(1)}, f32[2,2,256,256]{3,2,1,0:T(8,128)S(1)}) custom-call(s32[8]{0:T(128)S(1)} %stack.31.refs_0_, bf16[2,2,2,256,256]{4,3,2,1,0:T(8,128)(2,1)S(1)} %copy-done.1, f32[2,256,256]{2,1,0:T(8,128)S(1)} %shard_map.86.refs_2_, ...), custom_call_target="tpu_custom_call" | custom-call | flops 805306368 | bytes 8388640 | tf_op jit(solution)/shard_map/pallas_call | solution.py:254
  93.4 2.9 %shard_map.94 = (f32[4,2,32,256]{3,2,1,0:T(8,128)S(1)}, f32[4,2,32,256]{3,2,1,0:T(8,128)S(1)}, f32[2,128,512]{2,1,0:T(8,128)S(1)}, f32[2,128,512]{2,1,0:T(8,128)S(1)}) custom-call(s32[8]{0:T(128)S(1)} %stack.31.refs_0_, bf16[2,2,2,256,256]{4,3,2,1,0:T(8,128)(2,1)S(1)} %copy-done.1, f32[2,256,256]{2,1,0:T(8,128)S(1)} %shard_map.86.refs_2_, ...), custom_call_target="tpu_custom_call" | custom-call | flops 805306368 | bytes 9437216 | tf_op jit(solution)/shard_map/pallas_call | solution.py:254
  98.3 6.7 %collective-permute-done.33 = f32[4,2,32,256]{3,2,1,0:T(8,128)S(1)} collective-permute-done((f32[4,2,32,256]{3,2,1,0:T(8,128)S(1)}, f32[4,2,32,256]{3,2,1,0:T(8,128)S(1)}, u32[]{:S(2)}, u32[]{:S(2)}) %collective-permute-start.33) | collective-permute-done | bytes 262176 | tf_op jit(solution)/shard_map/ppermute | solution.py:283
  107.1 3.0 %collective-permute-done.34 = f32[2,2,32,256]{3,2,1,0:T(8,128)S(1)} collective-permute-done((f32[2,2,32,256]{3,2,1,0:T(8,128)S(1)}, f32[2,2,32,256]{3,2,1,0:T(8,128)S(1)}, u32[]{:S(2)}, u32[]{:S(2)}) %collective-permute-start.34) | collective-permute-done | bytes 131104 | tf_op jit(solution)/shard_map/ppermute | solution.py:283
  113.1 4.9 %collective-permute-done.35 = f32[1,2,32,256]{3,2,1,0:T(8,128)S(1)} collective-permute-done((f32[1,2,32,256]{3,2,1,0:T(8,128)S(1)}, f32[1,2,32,256]{3,2,1,0:T(8,128)S(1)}, u32[]{:S(2)}, u32[]{:S(2)}) %collective-permute-start.35) | collective-permute-done | bytes 65568 | tf_op jit(solution)/shard_map/ppermute | solution.py:283
  121.1 2.2 %collective-permute-done.36.refs_9_ = f32[1,2,32,256]{3,2,1,0:T(8,128)S(1)} collective-permute-done((f32[1,2,32,256]{3,2,1,0:T(8,128)S(1)}, f32[1,2,32,256]{3,2,1,0:T(8,128)S(1)}, u32[]{:S(2)}, u32[]{:S(2)}) %collective-permute-start.36) | collective-permute-done | bytes 65568 | tf_op jit(solution)/shard_map/ppermute | solution.py:283
  126.0 1.9 %collective-permute-start.24 = (f32[2,128,128]{2,1,0:T(8,128)S(1)}, f32[2,128,128]{2,1,0:T(8,128)S(1)}, u32[]{:S(2)}, u32[]{:S(2)}) collective-permute-start(f32[2,128,128]{2,1,0:T(8,128)S(1)} %get-tuple-element.64), channel_id=1, source_target_pairs={{0,2},{2,4},{4,6},{6,8},{8,10},{10,12},{12,14},{1,3},{3,5},{5,7},{... | collective-permute-start | bytes 393224 | tf_op jit(solution)/shard_map/ppermute | solution.py:273
  129.3 4.4 %collective-permute-start.38 = (f32[4,2,32,256]{3,2,1,0:T(8,128)S(1)}, f32[4,2,32,256]{3,2,1,0:T(8,128)S(1)}, u32[]{:S(2)}, u32[]{:S(2)}) collective-permute-start(f32[4,2,32,256]{3,2,1,0:T(8,128)S(1)} %pad_maximum_fusion.4), channel_id=1, source_target_pairs={{0,4},{2,6},{4,0},{6,2},{8,12},{10,14},{12,8},{14,10},{1,5},{3,7},... | collective-permute-start | bytes 786440 | tf_op jit(solution)/shard_map/ppermute | solution.py:283
  136.6 2.8 %collective-permute-done.38.refs_11_ = f32[4,2,32,256]{3,2,1,0:T(8,128)S(1)} collective-permute-done((f32[4,2,32,256]{3,2,1,0:T(8,128)S(1)}, f32[4,2,32,256]{3,2,1,0:T(8,128)S(1)}, u32[]{:S(2)}, u32[]{:S(2)}) %collective-permute-start.38) | collective-permute-done | bytes 262176 | tf_op jit(solution)/shard_map/ppermute | solution.py:283
  (104 shorter events, 37.9 us)
Async XLA Ops:
  1.7 7.7 %collective-permute-start = (f32[2,128,128]{2,1,0:T(8,128)S(1)}, f32[2,128,128]{2,1,0:T(8,128)S(1)}, u32[]{:S(2)}, u32[]{:S(2)}) collective-permute-start(f32[2,128,128]{2,1,0:T(8,128)S(1)} %get-tuple-element.74), channel_id=1, source_target_pairs={{0,2},{2,4},{4,6},{6,8},{8,10},{10,12},{12,14},{1,3},{3,5},{5,7},{... | collective-permute-start | bytes 393224 | tf_op jit(solution)/shard_map/ppermute | solution.py:273
  6.7 6.9 %collective-permute-start.1 = (f32[2,128,128]{2,1,0:T(8,128)S(1)}, f32[2,128,128]{2,1,0:T(8,128)S(1)}, u32[]{:S(2)}, u32[]{:S(2)}) collective-permute-start(f32[2,128,128]{2,1,0:T(8,128)S(1)} %get-tuple-element.75), channel_id=1, source_target_pairs={{2,0},{4,2},{6,4},{8,6},{10,8},{12,10},{14,12},{3,1},{5,3},{7,5},{... | collective-permute-start | bytes 393224 | tf_op jit(solution)/shard_map/ppermute | solution.py:273
  32.1 8.8 %collective-permute-start.15 = (f32[4,2,32,256]{3,2,1,0:T(8,128)S(1)}, f32[4,2,32,256]{3,2,1,0:T(8,128)S(1)}, u32[]{:S(2)}, u32[]{:S(2)}) collective-permute-start(f32[4,2,32,256]{3,2,1,0:T(8,128)S(1)} %get-tuple-element.43), channel_id=1, source_target_pairs={{0,4},{2,6},{4,0},{6,2},{8,12},{10,14},{12,8},{14,10},{1,5},{3,7},... | collective-permute-start | bytes 786440 | tf_op jit(solution)/shard_map/ppermute | solution.py:283
  34.3 8.8 %collective-permute-start.9 = (f32[4,2,32,256]{3,2,1,0:T(8,128)S(1)}, f32[4,2,32,256]{3,2,1,0:T(8,128)S(1)}, u32[]{:S(2)}, u32[]{:S(2)}) collective-permute-start(f32[4,2,32,256]{3,2,1,0:T(8,128)S(1)} %get-tuple-element.41), channel_id=1, source_target_pairs={{0,2},{2,0},{4,6},{6,4},{8,10},{10,8},{12,14},{14,12},{1,3},{3,1},... | collective-permute-start | bytes 786440 | tf_op jit(solution)/shard_map/ppermute | solution.py:283
  36.2 17.9 %collective-permute-start.5 = (f32[2,128,512]{2,1,0:T(8,128)S(1)}, f32[2,128,512]{2,1,0:T(8,128)S(1)}, u32[]{:S(2)}, u32[]{:S(2)}) collective-permute-start(f32[2,128,512]{2,1,0:T(8,128)S(1)} %get-tuple-element.39), channel_id=1, source_target_pairs={{0,1},{1,0},{2,3},{3,2},{4,5},{5,4},{6,7},{7,6},{8,9},{9,8},{10,11... | collective-permute-start | bytes 1572872 | tf_op jit(solution)/shard_map/ppermute | solution.py:268
  40.9 5.1 %collective-permute-start.16 = (f32[2,2,32,256]{3,2,1,0:T(8,128)S(1)}, f32[2,2,32,256]{3,2,1,0:T(8,128)S(1)}, u32[]{:S(2)}, u32[]{:S(2)}) collective-permute-start(f32[2,2,32,256]{3,2,1,0:T(8,128)S(1)} %get-tuple-element.67), channel_id=1, source_target_pairs={{0,2},{2,0},{4,6},{6,4},{8,10},{10,8},{12,14},{14,12},{1,3},{3,1},... | collective-permute-start | bytes 393224 | tf_op jit(solution)/shard_map/ppermute | solution.py:283
  43.1 5.7 %collective-permute-start.10 = (f32[2,2,32,256]{3,2,1,0:T(8,128)S(1)}, f32[2,2,32,256]{3,2,1,0:T(8,128)S(1)}, u32[]{:S(2)}, u32[]{:S(2)}) collective-permute-start(f32[2,2,32,256]{3,2,1,0:T(8,128)S(1)} %get-tuple-element.69), channel_id=1, source_target_pairs={{0,4},{2,6},{4,0},{6,2},{8,12},{10,14},{12,8},{14,10},{1,5},{3,7},... | collective-permute-start | bytes 393224 | tf_op jit(solution)/shard_map/ppermute | solution.py:283
  46.0 7.3 %collective-permute-start.17 = (f32[1,2,32,256]{3,2,1,0:T(8,128)S(1)}, f32[1,2,32,256]{3,2,1,0:T(8,128)S(1)}, u32[]{:S(2)}, u32[]{:S(2)}) collective-permute-start(f32[1,2,32,256]{3,2,1,0:T(8,128)S(1)} %slice_add_fusion.13), channel_id=1, source_target_pairs={{0,8},{2,10},{4,12},{6,14},{8,0},{10,2},{12,4},{14,6},{1,9},{3,11}... | collective-permute-start | bytes 196616 | tf_op jit(solution)/shard_map/ppermute | solution.py:283
  48.8 11.5 %collective-permute-start.11 = (f32[1,2,32,256]{3,2,1,0:T(8,128)S(1)}, f32[1,2,32,256]{3,2,1,0:T(8,128)S(1)}, u32[]{:S(2)}, u32[]{:S(2)}) collective-permute-start(f32[1,2,32,256]{3,2,1,0:T(8,128)S(1)} %slice_add_fusion.15), channel_id=1, source_target_pairs={{0,8},{2,10},{4,12},{6,14},{8,0},{10,2},{12,4},{14,6},{1,9},{3,11}... | collective-permute-start | bytes 196616 | tf_op jit(solution)/shard_map/ppermute | solution.py:283
  53.4 10.7 %collective-permute-start.18 = (f32[1,2,32,256]{3,2,1,0:T(8,128)S(1)}, f32[1,2,32,256]{3,2,1,0:T(8,128)S(1)}, u32[]{:S(2)}, u32[]{:S(2)}) collective-permute-start(f32[1,2,32,256]{3,2,1,0:T(8,128)S(1)} %fusion.5.refs_9_), channel_id=1, source_target_pairs={{0,8},{2,10},{4,12},{6,14},{8,0},{10,2},{12,4},{14,6},{1,9},{3,11}... | collective-permute-start | bytes 196616 | tf_op jit(solution)/shard_map/ppermute | solution.py:283
  54.2 14.8 %collective-permute-start.6 = (f32[2,128,256]{2,1,0:T(8,128)S(1)}, f32[2,128,256]{2,1,0:T(8,128)S(1)}, u32[]{:S(2)}, u32[]{:S(2)}) collective-permute-start(f32[2,128,256]{2,1,0:T(8,128)S(1)} %get-tuple-element.72), channel_id=1, source_target_pairs={{0,2},{2,4},{4,6},{6,8},{8,10},{10,12},{12,14},{1,3},{3,5},{5,7},{... | collective-permute-start | bytes 786440 | tf_op jit(solution)/shard_map/ppermute | solution.py:273
  58.8 10.2 %collective-permute-start.7 = (f32[2,128,256]{2,1,0:T(8,128)S(1)}, f32[2,128,256]{2,1,0:T(8,128)S(1)}, u32[]{:S(2)}, u32[]{:S(2)}) collective-permute-start(f32[2,128,256]{2,1,0:T(8,128)S(1)} %get-tuple-element.73), channel_id=1, source_target_pairs={{2,0},{4,2},{6,4},{8,6},{10,8},{12,10},{14,12},{3,1},{5,3},{7,5},{... | collective-permute-start | bytes 786440 | tf_op jit(solution)/shard_map/ppermute | solution.py:273
  60.3 8.9 %collective-permute-start.12 = (f32[1,2,32,256]{3,2,1,0:T(8,128)S(1)}, f32[1,2,32,256]{3,2,1,0:T(8,128)S(1)}, u32[]{:S(2)}, u32[]{:S(2)}) collective-permute-start(f32[1,2,32,256]{3,2,1,0:T(8,128)S(1)} %fusion.6.refs_5_), channel_id=1, source_target_pairs={{0,8},{2,10},{4,12},{6,14},{8,0},{10,2},{12,4},{14,6},{1,9},{3,11}... | collective-permute-start | bytes 196616 | tf_op jit(solution)/shard_map/ppermute | solution.py:283
  64.1 8.1 %collective-permute-start.19 = (f32[2,2,32,256]{3,2,1,0:T(8,128)S(1)}, f32[2,2,32,256]{3,2,1,0:T(8,128)S(1)}, u32[]{:S(2)}, u32[]{:S(2)}) collective-permute-start(f32[2,2,32,256]{3,2,1,0:T(8,128)S(1)} %pad_maximum_fusion.6), channel_id=1, source_target_pairs={{0,2},{2,0},{4,6},{6,4},{8,10},{10,8},{12,14},{14,12},{1,3},{3,1},... | collective-permute-start | bytes 393224 | tf_op jit(solution)/shard_map/ppermute | solution.py:283
  69.2 15.4 %collective-permute-start.8 = (f32[2,128,512]{2,1,0:T(8,128)S(1)}, f32[2,128,512]{2,1,0:T(8,128)S(1)}, u32[]{:S(2)}, u32[]{:S(2)}) collective-permute-start(f32[2,128,512]{2,1,0:T(8,128)S(1)} %fusion.refs_1_), channel_id=1, source_target_pairs={{0,1},{1,0},{2,3},{3,2},{4,5},{5,4},{6,7},{7,6},{8,9},{9,8},{10,11... | collective-permute-start | bytes 1572872 | tf_op jit(solution)/shard_map/ppermute | solution.py:268
  69.3 7.3 %collective-permute-start.13 = (f32[2,2,32,256]{3,2,1,0:T(8,128)S(1)}, f32[2,2,32,256]{3,2,1,0:T(8,128)S(1)}, u32[]{:S(2)}, u32[]{:S(2)}) collective-permute-start(f32[2,2,32,256]{3,2,1,0:T(8,128)S(1)} %pad_maximum_fusion.5), channel_id=1, source_target_pairs={{0,4},{2,6},{4,0},{6,2},{8,12},{10,14},{12,8},{14,10},{1,5},{3,7},... | collective-permute-start | bytes 393224 | tf_op jit(solution)/shard_map/ppermute | solution.py:283
  72.3 9.7 %collective-permute-start.20 = (f32[4,2,32,256]{3,2,1,0:T(8,128)S(1)}, f32[4,2,32,256]{3,2,1,0:T(8,128)S(1)}, u32[]{:S(2)}, u32[]{:S(2)}) collective-permute-start(f32[4,2,32,256]{3,2,1,0:T(8,128)S(1)} %pad_maximum_fusion.2), channel_id=1, source_target_pairs={{0,4},{2,6},{4,0},{6,2},{8,12},{10,14},{12,8},{14,10},{1,5},{3,7},... | collective-permute-start | bytes 786440 | tf_op jit(solution)/shard_map/ppermute | solution.py:283
  76.6 8.0 %collective-permute-start.14 = (f32[4,2,32,256]{3,2,1,0:T(8,128)S(1)}, f32[4,2,32,256]{3,2,1,0:T(8,128)S(1)}, u32[]{:S(2)}, u32[]{:S(2)}) collective-permute-start(f32[4,2,32,256]{3,2,1,0:T(8,128)S(1)} %pad_maximum_fusion.1), channel_id=1, source_target_pairs={{0,2},{2,0},{4,6},{6,4},{8,10},{10,8},{12,14},{14,12},{1,3},{3,1},... | collective-permute-start | bytes 786440 | tf_op jit(solution)/shard_map/ppermute | solution.py:283
  96.3 8.7 %collective-permute-start.33 = (f32[4,2,32,256]{3,2,1,0:T(8,128)S(1)}, f32[4,2,32,256]{3,2,1,0:T(8,128)S(1)}, u32[]{:S(2)}, u32[]{:S(2)}) collective-permute-start(f32[4,2,32,256]{3,2,1,0:T(8,128)S(1)} %get-tuple-element.57), channel_id=1, source_target_pairs={{0,4},{2,6},{4,0},{6,2},{8,12},{10,14},{12,8},{14,10},{1,5},{3,7},... | collective-permute-start | bytes 786440 | tf_op jit(solution)/shard_map/ppermute | solution.py:283
  98.0 8.3 %collective-permute-start.27 = (f32[4,2,32,256]{3,2,1,0:T(8,128)S(1)}, f32[4,2,32,256]{3,2,1,0:T(8,128)S(1)}, u32[]{:S(2)}, u32[]{:S(2)}) collective-permute-start(f32[4,2,32,256]{3,2,1,0:T(8,128)S(1)} %get-tuple-element.55), channel_id=1, source_target_pairs={{0,2},{2,0},{4,6},{6,4},{8,10},{10,8},{12,14},{14,12},{1,3},{3,1},... | collective-permute-start | bytes 786440 | tf_op jit(solution)/shard_map/ppermute | solution.py:283
  98.3 27.6 %collective-permute-start.23 = (f32[2,128,512]{2,1,0:T(8,128)S(1)}, f32[2,128,512]{2,1,0:T(8,128)S(1)}, u32[]{:S(2)}, u32[]{:S(2)}) collective-permute-start(f32[2,128,512]{2,1,0:T(8,128)S(1)} %get-tuple-element.53), channel_id=1, source_target_pairs={{0,1},{1,0},{2,3},{3,2},{4,5},{5,4},{6,7},{7,6},{8,9},{9,8},{10,11... | collective-permute-start | bytes 1572872 | tf_op jit(solution)/shard_map/ppermute | solution.py:268
  105.0 5.0 %collective-permute-start.34 = (f32[2,2,32,256]{3,2,1,0:T(8,128)S(1)}, f32[2,2,32,256]{3,2,1,0:T(8,128)S(1)}, u32[]{:S(2)}, u32[]{:S(2)}) collective-permute-start(f32[2,2,32,256]{3,2,1,0:T(8,128)S(1)} %get-tuple-element.61), channel_id=1, source_target_pairs={{0,2},{2,0},{4,6},{6,4},{8,10},{10,8},{12,14},{14,12},{1,3},{3,1},... | collective-permute-start | bytes 393224 | tf_op jit(solution)/shard_map/ppermute | solution.py:283
  110.1 7.9 %collective-permute-start.35 = (f32[1,2,32,256]{3,2,1,0:T(8,128)S(1)}, f32[1,2,32,256]{3,2,1,0:T(8,128)S(1)}, u32[]{:S(2)}, u32[]{:S(2)}) collective-permute-start(f32[1,2,32,256]{3,2,1,0:T(8,128)S(1)} %slice_add_fusion.9), channel_id=1, source_target_pairs={{0,8},{2,10},{4,12},{6,14},{8,0},{10,2},{12,4},{14,6},{1,9},{3,11}... | collective-permute-start | bytes 196616 | tf_op jit(solution)/shard_map/ppermute | solution.py:283
  111.3 8.0 %collective-permute-start.29 = (f32[1,2,32,256]{3,2,1,0:T(8,128)S(1)}, f32[1,2,32,256]{3,2,1,0:T(8,128)S(1)}, u32[]{:S(2)}, u32[]{:S(2)}) collective-permute-start(f32[1,2,32,256]{3,2,1,0:T(8,128)S(1)} %slice_add_fusion.11), channel_id=1, source_target_pairs={{0,8},{2,10},{4,12},{6,14},{8,0},{10,2},{12,4},{14,6},{1,9},{3,11}... | collective-permute-start | bytes 196616 | tf_op jit(solution)/shard_map/ppermute | solution.py:283
  118.0 5.2 %collective-permute-start.36 = (f32[1,2,32,256]{3,2,1,0:T(8,128)S(1)}, f32[1,2,32,256]{3,2,1,0:T(8,128)S(1)}, u32[]{:S(2)}, u32[]{:S(2)}) collective-permute-start(f32[1,2,32,256]{3,2,1,0:T(8,128)S(1)} %fusion.3.refs_8_), channel_id=1, source_target_pairs={{0,8},{2,10},{4,12},{6,14},{8,0},{10,2},{12,4},{14,6},{1,9},{3,11}... | collective-permute-start | bytes 196616 | tf_op jit(solution)/shard_map/ppermute | solution.py:283
  119.4 5.3 %collective-permute-start.30 = (f32[1,2,32,256]{3,2,1,0:T(8,128)S(1)}, f32[1,2,32,256]{3,2,1,0:T(8,128)S(1)}, u32[]{:S(2)}, u32[]{:S(2)}) collective-permute-start(f32[1,2,32,256]{3,2,1,0:T(8,128)S(1)} %fusion.4.refs_4_), channel_id=1, source_target_pairs={{0,8},{2,10},{4,12},{6,14},{8,0},{10,2},{12,4},{14,6},{1,9},{3,11}... | collective-permute-start | bytes 196616 | tf_op jit(solution)/shard_map/ppermute | solution.py:283
  123.3 6.0 %collective-permute-start.37 = (f32[2,2,32,256]{3,2,1,0:T(8,128)S(1)}, f32[2,2,32,256]{3,2,1,0:T(8,128)S(1)}, u32[]{:S(2)}, u32[]{:S(2)}) collective-permute-start(f32[2,2,32,256]{3,2,1,0:T(8,128)S(1)} %pad_maximum_fusion.8), channel_id=1, source_target_pairs={{0,2},{2,0},{4,6},{6,4},{8,10},{10,8},{12,14},{14,12},{1,3},{3,1},... | collective-permute-start | bytes 393224 | tf_op jit(solution)/shard_map/ppermute | solution.py:283
  124.7 9.1 %collective-permute-start.31 = (f32[2,2,32,256]{3,2,1,0:T(8,128)S(1)}, f32[2,2,32,256]{3,2,1,0:T(8,128)S(1)}, u32[]{:S(2)}, u32[]{:S(2)}) collective-permute-start(f32[2,2,32,256]{3,2,1,0:T(8,128)S(1)} %pad_maximum_fusion.7), channel_id=1, source_target_pairs={{0,4},{2,6},{4,0},{6,2},{8,12},{10,14},{12,8},{14,10},{1,5},{3,7},... | collective-permute-start | bytes 393224 | tf_op jit(solution)/shard_map/ppermute | solution.py:283
  126.0 8.7 %collective-permute-start.24 = (f32[2,128,128]{2,1,0:T(8,128)S(1)}, f32[2,128,128]{2,1,0:T(8,128)S(1)}, u32[]{:S(2)}, u32[]{:S(2)}) collective-permute-start(f32[2,128,128]{2,1,0:T(8,128)S(1)} %get-tuple-element.64), channel_id=1, source_target_pairs={{0,2},{2,4},{4,6},{6,8},{8,10},{10,12},{12,14},{1,3},{3,5},{5,7},{... | collective-permute-start | bytes 393224 | tf_op jit(solution)/shard_map/ppermute | solution.py:273
  128.0 8.5 %collective-permute-start.25 = (f32[2,128,128]{2,1,0:T(8,128)S(1)}, f32[2,128,128]{2,1,0:T(8,128)S(1)}, u32[]{:S(2)}, u32[]{:S(2)}) collective-permute-start(f32[2,128,128]{2,1,0:T(8,128)S(1)} %get-tuple-element.65), channel_id=1, source_target_pairs={{2,0},{4,2},{6,4},{8,6},{10,8},{12,10},{14,12},{3,1},{5,3},{7,5},{... | collective-permute-start | bytes 393224 | tf_op jit(solution)/shard_map/ppermute | solution.py:273
  129.3 10.1 %collective-permute-start.38 = (f32[4,2,32,256]{3,2,1,0:T(8,128)S(1)}, f32[4,2,32,256]{3,2,1,0:T(8,128)S(1)}, u32[]{:S(2)}, u32[]{:S(2)}) collective-permute-start(f32[4,2,32,256]{3,2,1,0:T(8,128)S(1)} %pad_maximum_fusion.4), channel_id=1, source_target_pairs={{0,4},{2,6},{4,0},{6,2},{8,12},{10,14},{12,8},{14,10},{1,5},{3,7},... | collective-permute-start | bytes 786440 | tf_op jit(solution)/shard_map/ppermute | solution.py:283
  133.8 6.4 %collective-permute-start.32 = (f32[4,2,32,256]{3,2,1,0:T(8,128)S(1)}, f32[4,2,32,256]{3,2,1,0:T(8,128)S(1)}, u32[]{:S(2)}, u32[]{:S(2)}) collective-permute-start(f32[4,2,32,256]{3,2,1,0:T(8,128)S(1)} %pad_maximum_fusion.3), channel_id=1, source_target_pairs={{0,2},{2,0},{4,6},{6,4},{8,10},{10,8},{12,14},{14,12},{1,3},{3,1},... | collective-permute-start | bytes 786440 | tf_op jit(solution)/shard_map/ppermute | solution.py:283
  (15 other events, 72.8 us)

commit v2 on v1

v2 whole, which is shorter than its diff:
```python
import functools
import math

import jax
import jax.numpy as jnp
import numpy as np
from jax import lax
from jax.experimental import pallas as pl
from jax.experimental.pallas import tpu as pltpu
from jax.sharding import PartitionSpec as P

MODES = 4
GX = 8
ITERS = 2
HALVINGS = 2
CHUNKS = 1 << HALVINGS
ORDERS = ((0, 1, 2), (1, 0, 2))

f32 = jnp.float32
bf16 = jnp.bfloat16


def tables(length):
    half = length // 2
    n = np.arange(half)
    left, right = [], []
    for transposed in (False, True):
        for odd in (0, 1):
            angle = 2.0 * math.pi * np.outer(2 * n + odd, n) / length
            c, s = np.cos(angle) / math.sqrt(length), np.sin(angle) / math.sqrt(length)
            matrix = np.block([[c, s], [-s, c]])
            matrix = (matrix.T if transposed else matrix).astype(np.float32)
            high = matrix.astype(bf16)
            low = (matrix - high.astype(np.float32)).astype(bf16)
            left.append(np.concatenate([high, low, high], 1))
            right.append(np.concatenate([high, high, low], 0))
    return np.stack(left).reshape(2, 2, length, -1), np.stack(right).reshape(2, 2, -1, length)


def deinterleave(length):
    half = length // 2
    out = np.zeros((length, length), np.float32)
    out[2 * np.arange(half), np.arange(half)] = 1.0
    out[2 * np.arange(half) + 1, half + np.arange(half)] = 1.0
    return np.stack([out, out.T]).astype(bf16)


def split(x):
    high = x.astype(bf16)
    return high, (x - high.astype(f32)).astype(bf16)


def dot(a, b):
    return jnp.dot(a, b, preferred_element_type=f32)


def mul_left(table, x):
    high, low = split(x)
    return dot(table, jnp.concatenate([high, high, low], 0))


def mul_right(x, table):
    high, low = split(x)
    return dot(jnp.concatenate([high, low, high], 1), table)


def forward(fields, left, right):
    h = fields[0][0].shape[0] // 2
    width = 2 * h
    even = [jnp.concatenate([x[:h] + x[h:] for x in f], 0) for f in fields]
    odd = [jnp.concatenate([x[:h] - x[h:] for x in f], 0) for f in fields]
    ye = mul_left(left[0, 0], jnp.concatenate(even, 1))
    yo = mul_left(left[0, 1], jnp.concatenate(odd, 1))
    even, odd = [], []
    for i in range(len(fields)):
        at = slice(i * width, (i + 1) * width)
        parts = [jnp.concatenate([y[k * h : (k + 1) * h, at] for y in (ye, yo)], 0) for k in range(2)]
        even.append(jnp.concatenate([y[:, :h] + y[:, h:] for y in parts], 1))
        odd.append(jnp.concatenate([y[:, :h] - y[:, h:] for y in parts], 1))
    fe = mul_right(jnp.concatenate(even, 0), right[1, 0])
    fo = mul_right(jnp.concatenate(odd, 0), right[1, 1])
    return [(fe[i * width : (i + 1) * width], fo[i * width : (i + 1) * width]) for i in range(len(fields))]


def inverse(fields, left, right):
    h = fields[0][0].shape[0] // 2
    width = 2 * h
    he = mul_right(jnp.concatenate([f[0] for f in fields], 0), right[0, 0])
    ho = mul_right(jnp.concatenate([f[1] for f in fields], 0), right[0, 1])
    ys = [
        jnp.concatenate([he[:, k] + ho[:, k], he[:, k] - ho[:, k]], 1) for k in (slice(0, h), slice(h, width))
    ]
    even, odd = [], []
    for i in range(len(fields)):
        even.append(jnp.concatenate([y[i * width : i * width + h] for y in ys], 0))
        odd.append(jnp.concatenate([y[i * width + h : (i + 1) * width] for y in ys], 0))
    xe = mul_left(left[1, 0], jnp.concatenate(even, 1))
    xo = mul_left(left[1, 1], jnp.concatenate(odd, 1))
    parts = [
        jnp.concatenate([xe[k] + xo[k], xe[k] - xo[k]], 0) for k in (slice(0, h), slice(h, width))
    ]
    return [[x[:, i * width : (i + 1) * width] for x in parts] for i in range(len(fields))]


def exact(x):
    high = x.astype(bf16)
    rest = x - high.astype(f32)
    mid = rest.astype(bf16)
    return high, mid, (rest - mid.astype(f32)).astype(bf16)


def amplitude_kernel(amp, perm, out):
    for s in range(amp.shape[0]):
        high, mid, low = exact(amp[s])
        rows = dot(perm[1], high) + (dot(perm[1], mid) + dot(perm[1], low))
        high, mid, low = exact(rows)
        out[s] = dot(high, perm[0]) + (dot(mid, perm[0]) + dot(low, perm[0]))


def chunk_key(order):
    t = lax.axis_index("tile")
    return sum(((t >> order[i]) & 1) << (HALVINGS - 1 - i) for i in range(HALVINGS))


def corner(offsets, slot, dim, size, margin):
    t = lax.axis_index("tile")
    along = lax.rem(t, GX) if dim else lax.div(t, GX)
    return offsets[slot, dim] - along * size + margin


def update_probe(old, pieces, coef, out):
    rows = old.shape[2] // CHUNKS
    for mode in range(len(pieces)):
        key = chunk_key(ORDERS[mode])
        rel = 0
        for piece in pieces[mode]:
            for k in range(piece.shape[0]):
                here = pl.ds(pl.multiple_of((rel ^ key) * rows, rows), rows)
                out[mode, :, here, :] = old[mode, :, here, :] + coef * piece[k]
                rel += 1


def forward_kernel(slot, n_pieces, coef, tall, *refs):
    refs = list(refs)
    offsets, near, away, probe, left, right = refs[:6]
    refs = refs[6:]
    modes = probe.shape[0]
    if n_pieces:
        pieces = [refs[m * n_pieces : (m + 1) * n_pieces] for m in range(modes)]
        refs = refs[modes * n_pieces :]
        new_probe = refs.pop(3)
        update_probe(probe, pieces, coef, new_probe)
        probe = new_probe
    far, power, patch, window = refs
    frame = probe.shape[-1]
    h = frame // 2
    core = lax.axis_index("row")
    window[core] = near[...]
    window[1 - core] = away[...]
    cols = window.shape[-1]
    size = cols - 2 * h
    for c in range(2):
        whole = jnp.concatenate([window[0, c], window[1, c]], 0)
        moved = pltpu.roll(whole, lax.rem(cols - corner(offsets, slot, 1, size, h), cols), 1)[:, :frame]
        if tall:
            rows = whole.shape[0]
            moved = pltpu.roll(moved, lax.rem(rows - corner(offsets, slot, 0, size, h), rows), 0)[:frame]
        patch[c] = moved
    ar, ai = patch[0], patch[1]
    exits = [
        (probe[m, 0] * ar - probe[m, 1] * ai, probe[m, 0] * ai + probe[m, 1] * ar) for m in range(modes)
    ]
    total = None
    for m, pair in enumerate(forward(exits, left, right)):
        for k in range(2):
            far[m, k] = pair[k]
        sq = jnp.concatenate([f[:, :h] * f[:, :h] + f[:, h:] * f[:, h:] for f in pair], 1)
        total = sq if total is None else total + sq
    power[...] = total


def inverse_kernel(mode, last, tall, *refs):
    refs = list(refs)
    offsets, counts, left, right, amp, probe = refs[:6]
    refs = refs[6:]
    slots = amp.shape[0]
    fars, powers, others, patches = (refs[i * slots : (i + 1) * slots] for i in range(4))
    refs = refs[4 * slots :]
    before = refs.pop(0) if mode else None
    send, keep = refs[:2]
    refs = refs[2:]
    frame = probe.shape[-1]
    h = frame // 2
    pr, pi = probe[mode, 0], probe[mode, 1]
    fields = []
    for s in range(slots):
        factor = amp[s] / (jnp.sqrt(powers[s][...] + others[s][...]) + 0.5)
        fields.append(
            [fars[s][mode, k] * jnp.concatenate([factor[:, k * h : (k + 1) * h]] * 2, 1) for k in range(2)]
        )
    probe_grad = None
    windows = [None, None]
    for s, (xr, xi) in enumerate(inverse(fields, left, right)):
        live = (s < counts[0]).astype(f32)
        ar, ai = patches[s][0], patches[s][1]
        ur = (xr - (pr * ar - pi * ai)) * live
        ui = (xi - (pr * ai + pi * ar)) * live
        grad = [pr * ur + pi * ui, pr * ui - pi * ur]
        step = [ar * ur + ai * ui, ar * ui - ai * ur]
        probe_grad = step if s == 0 else [a + b for a, b in zip(probe_grad, step)]
        for c, g in enumerate(grad):
            if mode:
                g = g + before[s, c]
            if not last:
                refs[0][s, c] = g
                continue
            cols, rows = refs[0].shape[-1], 2 * refs[0].shape[1]
            size = cols - 2 * h
            if tall:
                g = jnp.concatenate([g, jnp.zeros((rows - frame, frame), f32)], 0)
                g = pltpu.roll(g, corner(offsets, s, 0, size, h), 0)
            g = jnp.concatenate([g, jnp.zeros((rows, cols - frame), f32)], 1)
            g = pltpu.roll(g, corner(offsets, s, 1, size, h), 1)
            windows[c] = g if s == 0 else windows[c] + g
    if last:
        near, away, both = refs
        core = lax.axis_index("row")
        hr = near.shape[1]
        for c in range(2):
            for k in range(2):
                both[k, c] = windows[c][k * hr : (k + 1) * hr]
        near[...] = both[core]
        away[...] = both[1 - core]
    rows = frame // CHUNKS
    part = CHUNKS // 2
    key = chunk_key(ORDERS[mode])
    for c in range(CHUNKS):
        rel = c ^ key
        for k in range(2):
            piece = probe_grad[k][c * rows : (c + 1) * rows]

            @pl.when(rel >= part)
            def _():
                send[rel - part, k] = piece

            @pl.when(rel < part)
            def _():
                keep[rel, k] = piece


def finish_kernel(n_pieces, coef, *refs):
    refs = list(refs)
    near, away, probe = refs[:3]
    pieces = [refs[3 + m * n_pieces : 3 + (m + 1) * n_pieces] for m in range(probe.shape[0])]
    tile, new_probe = refs[-2:]
    update_probe(probe, pieces, coef, new_probe)
    hr = near.shape[1]
    core = lax.axis_index("row")
    tile[:, pl.ds(pl.multiple_of(core * hr, hr), hr), :] = near[...]
    tile[:, pl.ds(pl.multiple_of((1 - core) * hr, hr), hr), :] = away[...]


def vmem():
    return pl.BlockSpec(memory_space=pltpu.VMEM)


def call(kernel, outs, args, scratch=(), flops=0):
    size = sum(math.prod(a.shape) * a.dtype.itemsize for a in args)
    size += sum(math.prod(o) * 4 for o in outs)
    return pl.pallas_call(
        kernel,
        out_shape=[jax.ShapeDtypeStruct(o, f32) for o in outs],
        in_specs=[
            pl.BlockSpec(memory_space=pltpu.SMEM) if a.dtype == jnp.int32 else vmem() for a in args
        ],
        out_specs=[vmem() for _ in outs],
        scratch_shapes=list(scratch),
        cost_estimate=pl.CostEstimate(flops=flops, bytes_accessed=size, transcendentals=0),
        compiler_params=pltpu.CompilerParams(vmem_limit_bytes=40 * 1024 * 1024),
    )(*args)


def swap_rows(x):
    return lax.ppermute(x, "row", [(0, 1), (1, 0)])


def shift_cols(x, step, tiles):
    pairs = [(s, s + step) for s in range(tiles) if 0 <= s % GX + step < GX]
    return lax.ppermute(x, "tile", pairs)


def swap_vertical(x, tiles):
    pairs = [(2 * t, 2 * (t - GX) + 1) for t in range(GX, tiles)]
    pairs += [(2 * t + 1, 2 * (t + GX)) for t in range(tiles - GX)]
    return lax.ppermute(x, ("tile", "row"), pairs)


def exchange(x, bit, tiles):
    return lax.ppermute(x, "tile", [(s, s ^ (1 << bit)) for s in range(tiles)])


def together(*groups):
    return lax.optimization_barrier(groups)


def window_sum(grad, size, half, tiles, tall, wide):
    if wide:
        left, right = grad[:, :, :size], grad[:, :, size:]
        right_side = shift_cols(left, -1, tiles)
        left_side = shift_cols(right, 1, tiles)
        total = jnp.concatenate([left + left_side, right + right_side], 2)
        return total + swap_vertical(total, tiles) if tall else total
    got_left = shift_cols(grad[:, :, half + size :], 1, tiles)
    got_right = shift_cols(grad[:, :, :half], -1, tiles)
    return grad[:, :, half : half + size] + jnp.concatenate([got_left, got_right], 2)


def reduce_all(parts, grad, tiles, window):
    bits = int(math.log2(tiles))
    parts = [list(p) for p in parts]
    for i in range(HALVINGS):
        got = [exchange(p[0], o[i], tiles) for p, o in zip(parts, ORDERS)]
        for p, g in zip(parts, got):
            if i + 1 < HALVINGS:
                n = g.shape[0] // 2
                p[:] = p[1][n:] + g[n:], p[1][:n] + g[:n]
            else:
                p[:] = [p[1] + g]
    held = [p[0] for p in parts]
    held, grad = together(held, grad)
    got = [exchange(h, o[-1], tiles) for h, o in zip(held, ORDERS)]
    near = window(grad)
    held = [h + g for h, g in zip(held, got)]
    for bit in range(len(ORDERS[0]), bits):
        held = [h + exchange(h, bit, tiles) for h in held]
    pieces = [[h] for h in held]
    for i in reversed(range(HALVINGS)):
        for p, o in zip(pieces, ORDERS):
            p.append(exchange(p[0] if len(p) == 1 else jnp.concatenate(p, 0), o[i], tiles))
    return pieces, near


def per_device(object_tiles, probe_modes, amplitude, offsets, counts):
    own_tile = object_tiles[0]
    size = own_tile.shape[-1]
    frame = probe_modes.shape[-1]
    half = frame // 2
    tiles = lax.axis_size("tile")
    tall = tiles > GX
    slots = offsets.shape[0]
    modes = probe_modes.shape[0]
    core = lax.axis_index("row")
    hr = size // 2
    left, right = (jnp.asarray(x) for x in tables(frame))
    perm = jnp.asarray(deinterleave(frame))
    coef = 4.0 / (slots * tiles)

    mine = lax.dynamic_slice(own_tile, (0, core * hr, 0), (2, hr, size))
    from_left = shift_cols(mine[:, :, size - half :], 1, tiles)
    from_right = shift_cols(mine[:, :, :half], -1, tiles)
    near = jnp.concatenate([from_left, mine, from_right], 2)
    if tall:
        other = swap_vertical(near, tiles)
        near = jnp.where(core == 0, jnp.concatenate([other, near], 1), jnp.concatenate([near, other], 1))
    (amp,) = call(amplitude_kernel, [amplitude.shape], [amplitude, perm])
    away = swap_rows(near)
    near, away, amp = together(near, away, amp)

    matmul = 4 * 2 * 3 * 4 * frame**3
    probe = probe_modes
    pieces = None
    for iteration in range(ITERS):
        final = iteration + 1 == ITERS
        fars, powers, others, patches = [], [], [], []
        for s in range(slots):
            args = [offsets, near, away, probe, left, right]
            outs = [(modes, 2, frame, frame), (frame, frame), (2, frame, frame)]
            count = 0
            if pieces is not None:
                count = len(pieces[0])
                args += [p for group in pieces for p in group]
                outs.append(probe.shape)
                pieces = None
            got = call(
                functools.partial(forward_kernel, s, count, coef, tall),
                outs,
                args,
                [pltpu.VMEM((2,) + near.shape, f32)],
                matmul * modes,
            )
            if count:
                probe = got[3]
            fars.append(got[0])
            powers.append(got[1])
            patches.append(got[2])
            others.append(swap_rows(got[1]))
        before = None
        parts = []
        for m in range(modes):
            last = m == modes - 1
            args = [offsets, counts, left, right, amp, probe] + fars + powers + others + patches
            if m:
                args.append(before)
            part = (CHUNKS // 2, 2, frame // CHUNKS, frame)
            outs = [part, part]
            outs += [near.shape, near.shape] if last else [(slots, 2, frame, frame)]
            scratch = [pltpu.VMEM((2,) + near.shape, f32)] if last else []
            got = call(
                functools.partial(inverse_kernel, m, last, tall), outs, args, scratch, matmul * slots
            )
            before = got[2]
            parts.append((got[0], got[1]))
        grad = got[2] + swap_rows(got[3])
        wide = tall or not final
        pieces, total = reduce_all(
            parts, grad, tiles, lambda g: window_sum(g, size, half, tiles, tall, wide)
        )
        if wide:
            near = near + total / MODES
        else:
            near = near[:, :, half : half + size] + total / MODES
        if tall and final:
            near = near[:, :, half : half + size]
            near = jnp.where(core == 0, near[:, half:], near[:, : size - half])
        away = swap_rows(near)
    args = [near, away, probe] + [p for group in pieces for p in group]
    tile, probe = call(
        functools.partial(finish_kernel, len(pieces[0]), coef), [own_tile.shape, probe.shape], args
    )
    return (tile[None], probe)


def solution(mesh):
    return jax.shard_map(
        per_device,
        mesh=mesh,
        in_specs=(
            P(("scan", "tile"), None, None, None),
            P("row", None, None, None),
            P(("scan", "tile"), None, None),
            P(("scan", "tile"), None),
            P(("scan", "tile")),
        ),
        out_specs=(P(("scan", "tile"), None, None, None), P(("scan", "row"), None, None, None)),
        check_vma=False,
    )
```

time: 142 us -> 136 us (0.958)
  starting transfers between devices: 57.7 us -> 42.7 us
  waiting for transfers between devices: 52.7 us -> 66.8 us
  between operations: 4.3 us -> 1.73 us
  Pallas kernels: 23.5 us -> 21.2 us
    ppermute x24 -> x20, waiting for transfers between devices: 40.6 us -> 59.3 us  [exchange(): return lax.ppermute(x, 'tile', [(s, s ^ 1 << bit) for s in range(tiles)])]
    ppermute x24 -> x20, starting transfers between devices: 40.5 us -> 24.8 us  [exchange(): return lax.ppermute(x, 'tile', [(s, s ^ 1 << bit) for s in range(tiles)])]
    ppermute x6, waiting for transfers between devices: 10.3 us -> 4.52 us  [shift_cols(): return lax.ppermute(x, 'tile', pairs)]
    pallas_call x10, Pallas kernels: 23.5 us -> 21.2 us  [call(): pl.pallas_call(kernel, out_shape=[jax.ShapeDtypeStruct(o, f32) for o in o...]
  transfers between devices with their start and end apart: 39 -> 35, of which waited for: 21 -> 26; matrix products, arithmetic and copies ran while one was open for 1% -> 0% of each run, Pallas kernels for 4% -> 6%
where the time goes in v2:
time: 136 us
  waiting for transfers between devices  66.8 us (49%)
  starting transfers between devices  42.7 us (31%)
  Pallas kernels  21.2 us (16%)
  local copies, waits for them, and re-layouts  2.55 us (2%)
  between operations  1.73 us (1%)
    ppermute x20, waiting for transfers between devices, exchange(): return lax.ppermute(x, 'tile', [(s, s ^ 1 << bit) for s in range(tiles)])  59.3 us
    ppermute x20, starting transfers between devices, exchange(): return lax.ppermute(x, 'tile', [(s, s ^ 1 << bit) for s in range(tiles)])  24.8 us
    pallas_call x10, Pallas kernels, call(): pl.pallas_call(kernel, out_shape=[jax.ShapeDtypeStruct(o, f32) for o in o...  21.2 us
    ppermute x6, starting transfers between devices, shift_cols(): return lax.ppermute(x, 'tile', pairs)  16.4 us
    ppermute x6, waiting for transfers between devices, shift_cols(): return lax.ppermute(x, 'tile', pairs)  4.52 us
    ppermute x9, waiting for transfers between devices, swap_rows(): return lax.ppermute(x, 'row', [(0, 1), (1, 0)])  2.96 us
  transfers between devices with their start and end apart: 35, of which 26 were waited for; matrix products, arithmetic and copies ran while one was open for 0% of the time, Pallas kernels for 6%

profile of v2, /device:TPU:0, one launch (start us, length us, event | category | flops | bytes accessed | tf_op | source)
XLA Modules:
  0.0 135.7 jit_solution(14757283766422663580)
XLA Ops:
  3.2 5.5 %collective-permute-start = (f32[2,128,128]{2,1,0:T(8,128)S(1)}, f32[2,128,128]{2,1,0:T(8,128)S(1)}, u32[]{:S(2)}, u32[]{:S(2)}) collective-permute-start(f32[2,128,128]{2,1,0:T(8,128)S(1)} %get-tuple-element.84), channel_id=1, source_target_pairs={{0,2},{2,4},{4,6},{6,8},{8,10},{10,12},{12,14},{1,3},{3,5},{5,7},{... | collective-permute-start | bytes 393224 | tf_op jit(solution)/shard_map/ppermute | solution.py:289
  10.3 3.0 %collective-permute-done = f32[2,128,128]{2,1,0:T(8,128)S(1)} collective-permute-done((f32[2,128,128]{2,1,0:T(8,128)S(1)}, f32[2,128,128]{2,1,0:T(8,128)S(1)}, u32[]{:S(2)}, u32[]{:S(2)}) %collective-permute-start) | collective-permute-done | bytes 131104 | tf_op jit(solution)/shard_map/ppermute | solution.py:289
  16.7 2.2 %shard_map.96 = (f32[2,2,256,256]{3,2,1,0:T(8,128)S(1)}, f32[256,256]{1,0:T(8,128)S(1)}, f32[2,256,256]{2,1,0:T(8,128)S(1)}) custom-call(s32[2,2]{1,0:T(2,128)S(1)} %copy-done.4, f32[2,128,512]{2,1,0:T(8,128)S(1)} %pad_maximum_fusion.refs_1_, f32[2,128,512]{2,1,0:T(8,128)S(1)} %collective-permute-done.2.refs_2_, f32[2,2,256,256]{3,2,1,0:T(8,128)S(1)} %copy-done.3, ...), custom_call_target="tpu_custom_call" | custom-call | flops 3221225472 | bytes 7077904 | tf_op jit(solution)/shard_map/pallas_call | solution.py:270
  18.9 2.2 %shard_map.97 = (f32[2,2,256,256]{3,2,1,0:T(8,128)S(1)}, f32[256,256]{1,0:T(8,128)S(1)}, f32[2,256,256]{2,1,0:T(8,128)S(1)}) custom-call(s32[2,2]{1,0:T(2,128)S(1)} %copy-done.4, f32[2,128,512]{2,1,0:T(8,128)S(1)} %pad_maximum_fusion.refs_1_, f32[2,128,512]{2,1,0:T(8,128)S(1)} %collective-permute-done.2.refs_2_, f32[2,2,256,256]{3,2,1,0:T(8,128)S(1)} %copy-done.3, ...), custom_call_target="tpu_custom_call" | custom-call | flops 3221225472 | bytes 7077904 | tf_op jit(solution)/shard_map/pallas_call | solution.py:270
  23.1 2.4 %shard_map.98 = (f32[2,2,64,256]{3,2,1,0:T(8,128)S(1)}, f32[2,2,64,256]{3,2,1,0:T(8,128)S(1)}, f32[2,2,256,256]{3,2,1,0:T(8,128)S(1)}) custom-call(s32[2,2]{1,0:T(2,128)S(1)} %copy-done.4, s32[1]{0:T(128)S(6)} %copy.10.refs_1_, bf16[2,2,256,768]{3,2,1,0:T(8,128)(2,1)S(1)} %copy-done.5, bf16[2,2,768,256]{3,2,1,0:T(8,128)(2,1)S(1)} %copy-done.6, ...), custom_call_target="tpu_custom_call" | custom-call | flops 3221225472 | bytes 10485780 | tf_op jit(solution)/shard_map/pallas_call | solution.py:270
  25.5 2.5 %collective-permute-start.5 = (f32[2,2,64,256]{3,2,1,0:T(8,128)S(1)}, f32[2,2,64,256]{3,2,1,0:T(8,128)S(1)}, u32[]{:S(2)}, u32[]{:S(2)}) collective-permute-start(f32[2,2,64,256]{3,2,1,0:T(8,128)S(1)} %get-tuple-element.50), channel_id=1, source_target_pairs={{0,2},{2,0},{4,6},{6,4},{8,10},{10,8},{12,14},{14,12},{1,3},{3,1},... | collective-permute-start | bytes 786440 | tf_op jit(solution)/shard_map/ppermute | solution.py:299
  28.0 2.8 %shard_map.99 = (f32[2,2,64,256]{3,2,1,0:T(8,128)S(1)}, f32[2,2,64,256]{3,2,1,0:T(8,128)S(1)}, f32[2,128,512]{2,1,0:T(8,128)S(1)}, f32[2,128,512]{2,1,0:T(8,128)S(1)}) custom-call(s32[2,2]{1,0:T(2,128)S(1)} %copy-done.4, s32[1]{0:T(128)S(6)} %copy.10.refs_1_, bf16[2,2,256,768]{3,2,1,0:T(8,128)(2,1)S(1)} %copy-done.5, bf16[2,2,768,256]{3,2,1,0:T(8,128)(2,1)S(1)} %copy-done.6, ...), custom_call_target="tpu_custom_call" | custom-call | flops 3221225472 | bytes 11534356 | tf_op jit(solution)/shard_map/pallas_call | solution.py:270
  32.5 2.2 %collective-permute-done.5 = f32[2,2,64,256]{3,2,1,0:T(8,128)S(1)} collective-permute-done((f32[2,2,64,256]{3,2,1,0:T(8,128)S(1)}, f32[2,2,64,256]{3,2,1,0:T(8,128)S(1)}, u32[]{:S(2)}, u32[]{:S(2)}) %collective-permute-start.5) | collective-permute-done | bytes 262176 | tf_op jit(solution)/shard_map/ppermute | solution.py:299
  34.6 2.1 %collective-permute-start.6 = (f32[1,2,64,256]{3,2,1,0:T(8,128)S(1)}, f32[1,2,64,256]{3,2,1,0:T(8,128)S(1)}, u32[]{:S(2)}, u32[]{:S(2)}) collective-permute-start(f32[1,2,64,256]{3,2,1,0:T(8,128)S(1)} %slice_add_fusion.7), channel_id=1, source_target_pairs={{0,4},{2,6},{4,0},{6,2},{8,12},{10,14},{12,8},{14,10},{1,5},{3,7},... | collective-permute-start | bytes 393224 | tf_op jit(solution)/shard_map/ppermute | solution.py:299
  36.8 3.3 %collective-permute-done.7 = f32[2,2,64,256]{3,2,1,0:T(8,128)S(1)} collective-permute-done((f32[2,2,64,256]{3,2,1,0:T(8,128)S(1)}, f32[2,2,64,256]{3,2,1,0:T(8,128)S(1)}, u32[]{:S(2)}, u32[]{:S(2)}) %collective-permute-start.7) | collective-permute-done | bytes 262176 | tf_op jit(solution)/shard_map/ppermute | solution.py:299
  41.8 3.3 %collective-permute-done.8 = f32[1,2,64,256]{3,2,1,0:T(8,128)S(1)} collective-permute-done((f32[1,2,64,256]{3,2,1,0:T(8,128)S(1)}, f32[1,2,64,256]{3,2,1,0:T(8,128)S(1)}, u32[]{:S(2)}, u32[]{:S(2)}) %collective-permute-start.8) | collective-permute-done | bytes 131104 | tf_op jit(solution)/shard_map/ppermute | solution.py:299
  45.3 2.2 %collective-permute-start.10 = (f32[2,128,256]{2,1,0:T(8,128)S(1)}, f32[2,128,256]{2,1,0:T(8,128)S(1)}, u32[]{:S(2)}, u32[]{:S(2)}) collective-permute-start(f32[2,128,256]{2,1,0:T(8,128)S(1)} %get-tuple-element.82), channel_id=1, source_target_pairs={{0,2},{2,4},{4,6},{6,8},{8,10},{10,12},{12,14},{1,3},{3,5},{5,7},{... | collective-permute-start | bytes 786440 | tf_op jit(solution)/shard_map/ppermute | solution.py:289
  49.0 5.9 %collective-permute-start.13 = (f32[1,2,64,256]{3,2,1,0:T(8,128)S(1)}, f32[1,2,64,256]{3,2,1,0:T(8,128)S(1)}, u32[]{:S(2)}, u32[]{:S(2)}) collective-permute-start(f32[1,2,64,256]{3,2,1,0:T(8,128)S(1)} %fusion.5), channel_id=1, source_target_pairs={{0,8},{2,10},{4,12},{6,14},{8,0},{10,2},{12,4},{14,6},{1,9},{3,11}... | collective-permute-start | bytes 393224 | tf_op jit(solution)/shard_map/ppermute | solution.py:299
  55.0 12.2 %collective-permute-done.13 = f32[1,2,64,256]{3,2,1,0:T(8,128)S(1)} collective-permute-done((f32[1,2,64,256]{3,2,1,0:T(8,128)S(1)}, f32[1,2,64,256]{3,2,1,0:T(8,128)S(1)}, u32[]{:S(2)}, u32[]{:S(2)}) %collective-permute-start.13) | collective-permute-done | bytes 131104 | tf_op jit(solution)/shard_map/ppermute | solution.py:299
  68.7 3.5 %collective-permute-done.14.refs_7_ = f32[1,2,64,256]{3,2,1,0:T(8,128)S(1)} collective-permute-done((f32[1,2,64,256]{3,2,1,0:T(8,128)S(1)}, f32[1,2,64,256]{3,2,1,0:T(8,128)S(1)}, u32[]{:S(2)}, u32[]{:S(2)}) %collective-permute-start.14) | collective-permute-done | bytes 131104 | tf_op jit(solution)/shard_map/ppermute | solution.py:299
  72.3 2.8 %collective-permute-done.17.refs_10_ = f32[1,2,64,256]{3,2,1,0:T(8,128)S(1)} collective-permute-done((f32[1,2,64,256]{3,2,1,0:T(8,128)S(1)}, f32[1,2,64,256]{3,2,1,0:T(8,128)S(1)}, u32[]{:S(2)}, u32[]{:S(2)}) %collective-permute-start.17) | collective-permute-done | bytes 131104 | tf_op jit(solution)/shard_map/ppermute | solution.py:299
  76.0 3.1 %collective-permute-done.15.refs_8_ = f32[2,2,64,256]{3,2,1,0:T(8,128)S(1)} collective-permute-done((f32[2,2,64,256]{3,2,1,0:T(8,128)S(1)}, f32[2,2,64,256]{3,2,1,0:T(8,128)S(1)}, u32[]{:S(2)}, u32[]{:S(2)}) %collective-permute-start.15) | collective-permute-done | bytes 262176 | tf_op jit(solution)/shard_map/ppermute | solution.py:299
  79.1 2.6 %collective-permute-done.18.refs_11_ = f32[2,2,64,256]{3,2,1,0:T(8,128)S(1)} collective-permute-done((f32[2,2,64,256]{3,2,1,0:T(8,128)S(1)}, f32[2,2,64,256]{3,2,1,0:T(8,128)S(1)}, u32[]{:S(2)}, u32[]{:S(2)}) %collective-permute-start.18) | collective-permute-done | bytes 262176 | tf_op jit(solution)/shard_map/ppermute | solution.py:299
  81.8 2.2 %shard_map.100 = (f32[2,2,256,256]{3,2,1,0:T(8,128)S(1)}, f32[256,256]{1,0:T(8,128)S(1)}, f32[2,256,256]{2,1,0:T(8,128)S(1)}, f32[2,2,256,256]{3,2,1,0:T(8,128)S(1)}) custom-call(s32[2,2]{1,0:T(2,128)S(1)} %copy-done.4, f32[2,128,512]{2,1,0:T(8,128)S(1)} %fusion.refs_1_, f32[2,128,512]{2,1,0:T(8,128)S(1)} %collective-permute-done.12.refs_2_, ...), custom_call_target="tpu_custom_call" | custom-call | flops 3221225472 | bytes 9175056 | tf_op jit(solution)/shard_map/pallas_call | solution.py:270
  84.1 2.2 %shard_map.101 = (f32[2,2,256,256]{3,2,1,0:T(8,128)S(1)}, f32[256,256]{1,0:T(8,128)S(1)}, f32[2,256,256]{2,1,0:T(8,128)S(1)}) custom-call(s32[2,2]{1,0:T(2,128)S(1)} %copy-done.4, f32[2,128,512]{2,1,0:T(8,128)S(1)} %fusion.refs_1_, f32[2,128,512]{2,1,0:T(8,128)S(1)} %collective-permute-done.12.refs_2_, ...), custom_call_target="tpu_custom_call" | custom-call | flops 3221225472 | bytes 7077904 | tf_op jit(solution)/shard_map/pallas_call | solution.py:270
  88.0 2.3 %shard_map.102 = (f32[2,2,64,256]{3,2,1,0:T(8,128)S(1)}, f32[2,2,64,256]{3,2,1,0:T(8,128)S(1)}, f32[2,2,256,256]{3,2,1,0:T(8,128)S(1)}) custom-call(s32[2,2]{1,0:T(2,128)S(1)} %copy-done.4, s32[1]{0:T(128)S(6)} %copy.10.refs_1_, bf16[2,2,256,768]{3,2,1,0:T(8,128)(2,1)S(1)} %copy-done.5, bf16[2,2,768,256]{3,2,1,0:T(8,128)(2,1)S(1)} %copy-done.7, ...), custom_call_target="tpu_custom_call" | custom-call | flops 3221225472 | bytes 10485780 | tf_op jit(solution)/shard_map/pallas_call | solution.py:270
  90.9 2.8 %shard_map.103 = (f32[2,2,64,256]{3,2,1,0:T(8,128)S(1)}, f32[2,2,64,256]{3,2,1,0:T(8,128)S(1)}, f32[2,128,512]{2,1,0:T(8,128)S(1)}, f32[2,128,512]{2,1,0:T(8,128)S(1)}) custom-call(s32[2,2]{1,0:T(2,128)S(1)} %copy-done.4, s32[1]{0:T(128)S(6)} %copy.10.refs_1_, bf16[2,2,256,768]{3,2,1,0:T(8,128)(2,1)S(1)} %copy-done.5, ...), custom_call_target="tpu_custom_call" | custom-call | flops 3221225472 | bytes 11534356 | tf_op jit(solution)/shard_map/pallas_call | solution.py:270
  95.5 3.5 %collective-permute-done.21 = f32[2,2,64,256]{3,2,1,0:T(8,128)S(1)} collective-permute-done((f32[2,2,64,256]{3,2,1,0:T(8,128)S(1)}, f32[2,2,64,256]{3,2,1,0:T(8,128)S(1)}, u32[]{:S(2)}, u32[]{:S(2)}) %collective-permute-start.21) | collective-permute-done | bytes 262176 | tf_op jit(solution)/shard_map/ppermute | solution.py:299
  100.8 2.0 %collective-permute-done.23 = f32[2,2,64,256]{3,2,1,0:T(8,128)S(1)} collective-permute-done((f32[2,2,64,256]{3,2,1,0:T(8,128)S(1)}, f32[2,2,64,256]{3,2,1,0:T(8,128)S(1)}, u32[]{:S(2)}, u32[]{:S(2)}) %collective-permute-start.23) | collective-permute-done | bytes 262176 | tf_op jit(solution)/shard_map/ppermute | solution.py:299
  104.9 3.0 %collective-permute-done.24 = f32[1,2,64,256]{3,2,1,0:T(8,128)S(1)} collective-permute-done((f32[1,2,64,256]{3,2,1,0:T(8,128)S(1)}, f32[1,2,64,256]{3,2,1,0:T(8,128)S(1)}, u32[]{:S(2)}, u32[]{:S(2)}) %collective-permute-start.24) | collective-permute-done | bytes 131104 | tf_op jit(solution)/shard_map/ppermute | solution.py:299
  108.8 2.3 %collective-permute-start.32 = (f32[1,2,64,256]{3,2,1,0:T(8,128)S(1)}, f32[1,2,64,256]{3,2,1,0:T(8,128)S(1)}, u32[]{:S(2)}, u32[]{:S(2)}) collective-permute-start(f32[1,2,64,256]{3,2,1,0:T(8,128)S(1)} %fusion.2), channel_id=1, source_target_pairs={{0,8},{2,10},{4,12},{6,14},{8,0},{10,2},{12,4},{14,6},{1,9},{3,11}... | collective-permute-start | bytes 393224 | tf_op jit(solution)/shard_map/ppermute | solution.py:299
  112.4 4.6 %collective-permute-start.26 = (f32[2,128,128]{2,1,0:T(8,128)S(1)}, f32[2,128,128]{2,1,0:T(8,128)S(1)}, u32[]{:S(2)}, u32[]{:S(2)}) collective-permute-start(f32[2,128,128]{2,1,0:T(8,128)S(1)} %get-tuple-element.78), channel_id=1, source_target_pairs={{0,2},{2,4},{4,6},{6,8},{8,10},{10,12},{12,14},{1,3},{3,5},{5,7},{... | collective-permute-start | bytes 393224 | tf_op jit(solution)/shard_map/ppermute | solution.py:289
  116.9 1.9 %collective-permute-done.29 = f32[1,2,64,256]{3,2,1,0:T(8,128)S(1)} collective-permute-done((f32[1,2,64,256]{3,2,1,0:T(8,128)S(1)}, f32[1,2,64,256]{3,2,1,0:T(8,128)S(1)}, u32[]{:S(2)}, u32[]{:S(2)}) %collective-permute-start.29) | collective-permute-done | bytes 131104 | tf_op jit(solution)/shard_map/ppermute | solution.py:299
  118.9 2.7 %collective-permute-done.32 = f32[1,2,64,256]{3,2,1,0:T(8,128)S(1)} collective-permute-done((f32[1,2,64,256]{3,2,1,0:T(8,128)S(1)}, f32[1,2,64,256]{3,2,1,0:T(8,128)S(1)}, u32[]{:S(2)}, u32[]{:S(2)}) %collective-permute-start.32) | collective-permute-done | bytes 131104 | tf_op jit(solution)/shard_map/ppermute | solution.py:299
  125.5 2.5 %collective-permute-done.33.refs_7_ = f32[1,2,64,256]{3,2,1,0:T(8,128)S(1)} collective-permute-done((f32[1,2,64,256]{3,2,1,0:T(8,128)S(1)}, f32[1,2,64,256]{3,2,1,0:T(8,128)S(1)}, u32[]{:S(2)}, u32[]{:S(2)}) %collective-permute-start.33) | collective-permute-done | bytes 131104 | tf_op jit(solution)/shard_map/ppermute | solution.py:299
  128.0 4.2 %collective-permute-done.31.refs_5_ = f32[2,2,64,256]{3,2,1,0:T(8,128)S(1)} collective-permute-done((f32[2,2,64,256]{3,2,1,0:T(8,128)S(1)}, f32[2,2,64,256]{3,2,1,0:T(8,128)S(1)}, u32[]{:S(2)}, u32[]{:S(2)}) %collective-permute-start.31) | collective-permute-done | bytes 262176 | tf_op jit(solution)/shard_map/ppermute | solution.py:299
  132.2 2.2 %collective-permute-done.34.refs_8_ = f32[2,2,64,256]{3,2,1,0:T(8,128)S(1)} collective-permute-done((f32[2,2,64,256]{3,2,1,0:T(8,128)S(1)}, f32[2,2,64,256]{3,2,1,0:T(8,128)S(1)}, u32[]{:S(2)}, u32[]{:S(2)}) %collective-permute-start.34) | collective-permute-done | bytes 262176 | tf_op jit(solution)/shard_map/ppermute | solution.py:299
  (90 shorter events, 31.9 us)
Async XLA Ops:
  1.8 8.5 %collective-permute-start.1 = (f32[2,128,128]{2,1,0:T(8,128)S(1)}, f32[2,128,128]{2,1,0:T(8,128)S(1)}, u32[]{:S(2)}, u32[]{:S(2)}) collective-permute-start(f32[2,128,128]{2,1,0:T(8,128)S(1)} %get-tuple-element.85), channel_id=1, source_target_pairs={{2,0},{4,2},{6,4},{8,6},{10,8},{12,10},{14,12},{3,1},{5,3},{7,5},{... | collective-permute-start | bytes 393224 | tf_op jit(solution)/shard_map/ppermute | solution.py:289
  3.2 10.0 %collective-permute-start = (f32[2,128,128]{2,1,0:T(8,128)S(1)}, f32[2,128,128]{2,1,0:T(8,128)S(1)}, u32[]{:S(2)}, u32[]{:S(2)}) collective-permute-start(f32[2,128,128]{2,1,0:T(8,128)S(1)} %get-tuple-element.84), channel_id=1, source_target_pairs={{0,2},{2,4},{4,6},{6,8},{8,10},{10,12},{12,14},{1,3},{3,5},{5,7},{... | collective-permute-start | bytes 393224 | tf_op jit(solution)/shard_map/ppermute | solution.py:289
  13.3 2.0 %collective-permute-start.2 = (f32[2,128,512]{2,1,0:T(8,128)S(1)}, f32[2,128,512]{2,1,0:T(8,128)S(1)}, u32[]{:S(2)}, u32[]{:S(2)}) collective-permute-start(f32[2,128,512]{2,1,0:T(8,128)S(1)} %pad_maximum_fusion.refs_1_), channel_id=1, source_target_pairs={{0,1},{1,0},{2,3},{3,2},{4,5},{5,4},{6,7},{7,6},{8,9},{9,8},{10,11... | collective-permute-start | bytes 1572872 | tf_op jit(solution)/shard_map/ppermute | solution.py:284
  25.5 9.2 %collective-permute-start.5 = (f32[2,2,64,256]{3,2,1,0:T(8,128)S(1)}, f32[2,2,64,256]{3,2,1,0:T(8,128)S(1)}, u32[]{:S(2)}, u32[]{:S(2)}) collective-permute-start(f32[2,2,64,256]{3,2,1,0:T(8,128)S(1)} %get-tuple-element.50), channel_id=1, source_target_pairs={{0,2},{2,0},{4,6},{6,4},{8,10},{10,8},{12,14},{14,12},{1,3},{3,1},... | collective-permute-start | bytes 786440 | tf_op jit(solution)/shard_map/ppermute | solution.py:299
  30.8 9.3 %collective-permute-start.7 = (f32[2,2,64,256]{3,2,1,0:T(8,128)S(1)}, f32[2,2,64,256]{3,2,1,0:T(8,128)S(1)}, u32[]{:S(2)}, u32[]{:S(2)}) collective-permute-start(f32[2,2,64,256]{3,2,1,0:T(8,128)S(1)} %get-tuple-element.53), channel_id=1, source_target_pairs={{0,4},{2,6},{4,0},{6,2},{8,12},{10,14},{12,8},{14,10},{1,5},{3,7},... | collective-permute-start | bytes 786440 | tf_op jit(solution)/shard_map/ppermute | solution.py:299
  32.5 12.7 %collective-permute-start.9 = (f32[2,128,512]{2,1,0:T(8,128)S(1)}, f32[2,128,512]{2,1,0:T(8,128)S(1)}, u32[]{:S(2)}, u32[]{:S(2)}) collective-permute-start(f32[2,128,512]{2,1,0:T(8,128)S(1)} %get-tuple-element.55), channel_id=1, source_target_pairs={{0,1},{1,0},{2,3},{3,2},{4,5},{5,4},{6,7},{7,6},{8,9},{9,8},{10,11... | collective-permute-start | bytes 1572872 | tf_op jit(solution)/shard_map/ppermute | solution.py:284
  34.6 7.1 %collective-permute-start.6 = (f32[1,2,64,256]{3,2,1,0:T(8,128)S(1)}, f32[1,2,64,256]{3,2,1,0:T(8,128)S(1)}, u32[]{:S(2)}, u32[]{:S(2)}) collective-permute-start(f32[1,2,64,256]{3,2,1,0:T(8,128)S(1)} %slice_add_fusion.7), channel_id=1, source_target_pairs={{0,4},{2,6},{4,0},{6,2},{8,12},{10,14},{12,8},{14,10},{1,5},{3,7},... | collective-permute-start | bytes 393224 | tf_op jit(solution)/shard_map/ppermute | solution.py:299
  40.1 5.0 %collective-permute-start.8 = (f32[1,2,64,256]{3,2,1,0:T(8,128)S(1)}, f32[1,2,64,256]{3,2,1,0:T(8,128)S(1)}, u32[]{:S(2)}, u32[]{:S(2)}) collective-permute-start(f32[1,2,64,256]{3,2,1,0:T(8,128)S(1)} %slice_add_fusion.5), channel_id=1, source_target_pairs={{0,2},{2,0},{4,6},{6,4},{8,10},{10,8},{12,14},{14,12},{1,3},{3,1},... | collective-permute-start | bytes 393224 | tf_op jit(solution)/shard_map/ppermute | solution.py:299
  45.3 22.0 %collective-permute-start.10 = (f32[2,128,256]{2,1,0:T(8,128)S(1)}, f32[2,128,256]{2,1,0:T(8,128)S(1)}, u32[]{:S(2)}, u32[]{:S(2)}) collective-permute-start(f32[2,128,256]{2,1,0:T(8,128)S(1)} %get-tuple-element.82), channel_id=1, source_target_pairs={{0,2},{2,4},{4,6},{6,8},{8,10},{10,12},{12,14},{1,3},{3,5},{5,7},{... | collective-permute-start | bytes 786440 | tf_op jit(solution)/shard_map/ppermute | solution.py:289
  47.5 19.8 %collective-permute-start.11 = (f32[2,128,256]{2,1,0:T(8,128)S(1)}, f32[2,128,256]{2,1,0:T(8,128)S(1)}, u32[]{:S(2)}, u32[]{:S(2)}) collective-permute-start(f32[2,128,256]{2,1,0:T(8,128)S(1)} %get-tuple-element.83), channel_id=1, source_target_pairs={{2,0},{4,2},{6,4},{8,6},{10,8},{12,10},{14,12},{3,1},{5,3},{7,5},{... | collective-permute-start | bytes 786440 | tf_op jit(solution)/shard_map/ppermute | solution.py:289
  49.0 18.2 %collective-permute-start.13 = (f32[1,2,64,256]{3,2,1,0:T(8,128)S(1)}, f32[1,2,64,256]{3,2,1,0:T(8,128)S(1)}, u32[]{:S(2)}, u32[]{:S(2)}) collective-permute-start(f32[1,2,64,256]{3,2,1,0:T(8,128)S(1)} %fusion.5), channel_id=1, source_target_pairs={{0,8},{2,10},{4,12},{6,14},{8,0},{10,2},{12,4},{14,6},{1,9},{3,11}... | collective-permute-start | bytes 393224 | tf_op jit(solution)/shard_map/ppermute | solution.py:299
  54.9 13.7 %collective-permute-start.16 = (f32[1,2,64,256]{3,2,1,0:T(8,128)S(1)}, f32[1,2,64,256]{3,2,1,0:T(8,128)S(1)}, u32[]{:S(2)}, u32[]{:S(2)}) collective-permute-start(f32[1,2,64,256]{3,2,1,0:T(8,128)S(1)} %fusion.4), channel_id=1, source_target_pairs={{0,8},{2,10},{4,12},{6,14},{8,0},{10,2},{12,4},{14,6},{1,9},{3,11}... | collective-permute-start | bytes 393224 | tf_op jit(solution)/shard_map/ppermute | solution.py:299
  67.2 5.0 %collective-permute-start.14 = (f32[1,2,64,256]{3,2,1,0:T(8,128)S(1)}, f32[1,2,64,256]{3,2,1,0:T(8,128)S(1)}, u32[]{:S(2)}, u32[]{:S(2)}) collective-permute-start(f32[1,2,64,256]{3,2,1,0:T(8,128)S(1)} %add.83.refs_6_), channel_id=1, source_target_pairs={{0,4},{2,6},{4,0},{6,2},{8,12},{10,14},{12,8},{14,10},{1,5},{3,7},... | collective-permute-start | bytes 393224 | tf_op jit(solution)/shard_map/ppermute | solution.py:299
  67.5 14.3 %collective-permute-start.12 = (f32[2,128,512]{2,1,0:T(8,128)S(1)}, f32[2,128,512]{2,1,0:T(8,128)S(1)}, u32[]{:S(2)}, u32[]{:S(2)}) collective-permute-start(f32[2,128,512]{2,1,0:T(8,128)S(1)} %fusion.refs_1_), channel_id=1, source_target_pairs={{0,1},{1,0},{2,3},{3,2},{4,5},{5,4},{6,7},{7,6},{8,9},{9,8},{10,11... | collective-permute-start | bytes 1572872 | tf_op jit(solution)/shard_map/ppermute | solution.py:284
  68.6 6.5 %collective-permute-start.17 = (f32[1,2,64,256]{3,2,1,0:T(8,128)S(1)}, f32[1,2,64,256]{3,2,1,0:T(8,128)S(1)}, u32[]{:S(2)}, u32[]{:S(2)}) collective-permute-start(f32[1,2,64,256]{3,2,1,0:T(8,128)S(1)} %add.84.refs_9_), channel_id=1, source_target_pairs={{0,2},{2,0},{4,6},{6,4},{8,10},{10,8},{12,14},{14,12},{1,3},{3,1},... | collective-permute-start | bytes 393224 | tf_op jit(solution)/shard_map/ppermute | solution.py:299
  72.2 6.9 %collective-permute-start.15 = (f32[2,2,64,256]{3,2,1,0:T(8,128)S(1)}, f32[2,2,64,256]{3,2,1,0:T(8,128)S(1)}, u32[]{:S(2)}, u32[]{:S(2)}) collective-permute-start(f32[2,2,64,256]{3,2,1,0:T(8,128)S(1)} %pad_maximum_fusion.1), channel_id=1, source_target_pairs={{0,2},{2,0},{4,6},{6,4},{8,10},{10,8},{12,14},{14,12},{1,3},{3,1},... | collective-permute-start | bytes 786440 | tf_op jit(solution)/shard_map/ppermute | solution.py:299
  75.1 6.7 %collective-permute-start.18 = (f32[2,2,64,256]{3,2,1,0:T(8,128)S(1)}, f32[2,2,64,256]{3,2,1,0:T(8,128)S(1)}, u32[]{:S(2)}, u32[]{:S(2)}) collective-permute-start(f32[2,2,64,256]{3,2,1,0:T(8,128)S(1)} %pad_maximum_fusion.2), channel_id=1, source_target_pairs={{0,4},{2,6},{4,0},{6,2},{8,12},{10,14},{12,8},{14,10},{1,5},{3,7},... | collective-permute-start | bytes 786440 | tf_op jit(solution)/shard_map/ppermute | solution.py:299
  84.0 2.9 %collective-permute-start.19 = (f32[256,256]{1,0:T(8,128)S(1)}, f32[256,256]{1,0:T(8,128)S(1)}, u32[]{:S(2)}, u32[]{:S(2)}) collective-permute-start(f32[256,256]{1,0:T(8,128)S(1)} %get-tuple-element.62.refs_8_), channel_id=1, source_target_pairs={{0,1},{1,0},{2,3},{3,2},{4,5},{5,4},{6,7},{7,6},{8,9},{9,8},{10,11... | collective-permute-start | bytes 786440 | tf_op jit(solution)/shard_map/ppermute | solution.py:284
  90.4 8.6 %collective-permute-start.21 = (f32[2,2,64,256]{3,2,1,0:T(8,128)S(1)}, f32[2,2,64,256]{3,2,1,0:T(8,128)S(1)}, u32[]{:S(2)}, u32[]{:S(2)}) collective-permute-start(f32[2,2,64,256]{3,2,1,0:T(8,128)S(1)} %get-tuple-element.67), channel_id=1, source_target_pairs={{0,2},{2,0},{4,6},{6,4},{8,10},{10,8},{12,14},{14,12},{1,3},{3,1},... | collective-permute-start | bytes 786440 | tf_op jit(solution)/shard_map/ppermute | solution.py:299
  93.7 9.1 %collective-permute-start.23 = (f32[2,2,64,256]{3,2,1,0:T(8,128)S(1)}, f32[2,2,64,256]{3,2,1,0:T(8,128)S(1)}, u32[]{:S(2)}, u32[]{:S(2)}) collective-permute-start(f32[2,2,64,256]{3,2,1,0:T(8,128)S(1)} %get-tuple-element.70), channel_id=1, source_target_pairs={{0,4},{2,6},{4,0},{6,2},{8,12},{10,14},{12,8},{14,10},{1,5},{3,7},... | collective-permute-start | bytes 786440 | tf_op jit(solution)/shard_map/ppermute | solution.py:299
  95.5 12.4 %collective-permute-start.25 = (f32[2,128,512]{2,1,0:T(8,128)S(1)}, f32[2,128,512]{2,1,0:T(8,128)S(1)}, u32[]{:S(2)}, u32[]{:S(2)}) collective-permute-start(f32[2,128,512]{2,1,0:T(8,128)S(1)} %get-tuple-element.72), channel_id=1, source_target_pairs={{0,1},{1,0},{2,3},{3,2},{4,5},{5,4},{6,7},{7,6},{8,9},{9,8},{10,11... | collective-permute-start | bytes 1572872 | tf_op jit(solution)/shard_map/ppermute | solution.py:284
  99.0 5.8 %collective-permute-start.22 = (f32[1,2,64,256]{3,2,1,0:T(8,128)S(1)}, f32[1,2,64,256]{3,2,1,0:T(8,128)S(1)}, u32[]{:S(2)}, u32[]{:S(2)}) collective-permute-start(f32[1,2,64,256]{3,2,1,0:T(8,128)S(1)} %slice_add_fusion.3), channel_id=1, source_target_pairs={{0,4},{2,6},{4,0},{6,2},{8,12},{10,14},{12,8},{14,10},{1,5},{3,7},... | collective-permute-start | bytes 393224 | tf_op jit(solution)/shard_map/ppermute | solution.py:299
  102.8 5.0 %collective-permute-start.24 = (f32[1,2,64,256]{3,2,1,0:T(8,128)S(1)}, f32[1,2,64,256]{3,2,1,0:T(8,128)S(1)}, u32[]{:S(2)}, u32[]{:S(2)}) collective-permute-start(f32[1,2,64,256]{3,2,1,0:T(8,128)S(1)} %slice_add_fusion.1), channel_id=1, source_target_pairs={{0,2},{2,0},{4,6},{6,4},{8,10},{10,8},{12,14},{14,12},{1,3},{3,1},... | collective-permute-start | bytes 393224 | tf_op jit(solution)/shard_map/ppermute | solution.py:299
  108.0 10.8 %collective-permute-start.29 = (f32[1,2,64,256]{3,2,1,0:T(8,128)S(1)}, f32[1,2,64,256]{3,2,1,0:T(8,128)S(1)}, u32[]{:S(2)}, u32[]{:S(2)}) collective-permute-start(f32[1,2,64,256]{3,2,1,0:T(8,128)S(1)} %fusion.3), channel_id=1, source_target_pairs={{0,8},{2,10},{4,12},{6,14},{8,0},{10,2},{12,4},{14,6},{1,9},{3,11}... | collective-permute-start | bytes 393224 | tf_op jit(solution)/shard_map/ppermute | solution.py:299
  108.8 12.7 %collective-permute-start.32 = (f32[1,2,64,256]{3,2,1,0:T(8,128)S(1)}, f32[1,2,64,256]{3,2,1,0:T(8,128)S(1)}, u32[]{:S(2)}, u32[]{:S(2)}) collective-permute-start(f32[1,2,64,256]{3,2,1,0:T(8,128)S(1)} %fusion.2), channel_id=1, source_target_pairs={{0,8},{2,10},{4,12},{6,14},{8,0},{10,2},{12,4},{14,6},{1,9},{3,11}... | collective-permute-start | bytes 393224 | tf_op jit(solution)/shard_map/ppermute | solution.py:299
  111.1 10.8 %collective-permute-start.27 = (f32[2,128,128]{2,1,0:T(8,128)S(1)}, f32[2,128,128]{2,1,0:T(8,128)S(1)}, u32[]{:S(2)}, u32[]{:S(2)}) collective-permute-start(f32[2,128,128]{2,1,0:T(8,128)S(1)} %get-tuple-element.79), channel_id=1, source_target_pairs={{2,0},{4,2},{6,4},{8,6},{10,8},{12,10},{14,12},{3,1},{5,3},{7,5},{... | collective-permute-start | bytes 393224 | tf_op jit(solution)/shard_map/ppermute | solution.py:289
  112.4 9.5 %collective-permute-start.26 = (f32[2,128,128]{2,1,0:T(8,128)S(1)}, f32[2,128,128]{2,1,0:T(8,128)S(1)}, u32[]{:S(2)}, u32[]{:S(2)}) collective-permute-start(f32[2,128,128]{2,1,0:T(8,128)S(1)} %get-tuple-element.78), channel_id=1, source_target_pairs={{0,2},{2,4},{4,6},{6,8},{8,10},{10,12},{12,14},{1,3},{3,5},{5,7},{... | collective-permute-start | bytes 393224 | tf_op jit(solution)/shard_map/ppermute | solution.py:289
  118.8 5.0 %collective-permute-start.30 = (f32[1,2,64,256]{3,2,1,0:T(8,128)S(1)}, f32[1,2,64,256]{3,2,1,0:T(8,128)S(1)}, u32[]{:S(2)}, u32[]{:S(2)}) collective-permute-start(f32[1,2,64,256]{3,2,1,0:T(8,128)S(1)} %add.94.refs_3_), channel_id=1, source_target_pairs={{0,4},{2,6},{4,0},{6,2},{8,12},{10,14},{12,8},{14,10},{1,5},{3,7},... | collective-permute-start | bytes 393224 | tf_op jit(solution)/shard_map/ppermute | solution.py:299
  121.5 6.4 %collective-permute-start.33 = (f32[1,2,64,256]{3,2,1,0:T(8,128)S(1)}, f32[1,2,64,256]{3,2,1,0:T(8,128)S(1)}, u32[]{:S(2)}, u32[]{:S(2)}) collective-permute-start(f32[1,2,64,256]{3,2,1,0:T(8,128)S(1)} %add.95.refs_6_), channel_id=1, source_target_pairs={{0,2},{2,0},{4,6},{6,4},{8,10},{10,8},{12,14},{14,12},{1,3},{3,1},... | collective-permute-start | bytes 393224 | tf_op jit(solution)/shard_map/ppermute | solution.py:299
  121.9 6.1 %collective-permute-start.28 = (f32[2,128,256]{2,1,0:T(8,128)S(1)}, f32[2,128,256]{2,1,0:T(8,128)S(1)}, u32[]{:S(2)}, u32[]{:S(2)}) collective-permute-start(f32[2,128,256]{2,1,0:T(8,128)S(1)} %slice_add_fusion.refs_0_), channel_id=1, source_target_pairs={{0,1},{1,0},{2,3},{3,2},{4,5},{5,4},{6,7},{7,6},{8,9},{9,8},{10,11... | collective-permute-start | bytes 786440 | tf_op jit(solution)/shard_map/ppermute | solution.py:284
  123.9 8.3 %collective-permute-start.31 = (f32[2,2,64,256]{3,2,1,0:T(8,128)S(1)}, f32[2,2,64,256]{3,2,1,0:T(8,128)S(1)}, u32[]{:S(2)}, u32[]{:S(2)}) collective-permute-start(f32[2,2,64,256]{3,2,1,0:T(8,128)S(1)} %pad_maximum_fusion.3), channel_id=1, source_target_pairs={{0,2},{2,0},{4,6},{6,4},{8,10},{10,8},{12,14},{14,12},{1,3},{3,1},... | collective-permute-start | bytes 786440 | tf_op jit(solution)/shard_map/ppermute | solution.py:299
  127.9 6.4 %collective-permute-start.34 = (f32[2,2,64,256]{3,2,1,0:T(8,128)S(1)}, f32[2,2,64,256]{3,2,1,0:T(8,128)S(1)}, u32[]{:S(2)}, u32[]{:S(2)}) collective-permute-start(f32[2,2,64,256]{3,2,1,0:T(8,128)S(1)} %pad_maximum_fusion.4), channel_id=1, source_target_pairs={{0,4},{2,6},{4,0},{6,2},{8,12},{10,14},{12,8},{14,10},{1,5},{3,7},... | collective-permute-start | bytes 786440 | tf_op jit(solution)/shard_map/ppermute | solution.py:299
  (11 other events, 88.0 us)

commit v3 on v2

v3 whole, which is shorter than its diff:
```python
import functools
import math

import jax
import jax.numpy as jnp
import numpy as np
from jax import lax
from jax.experimental import pallas as pl
from jax.experimental.pallas import tpu as pltpu
from jax.sharding import PartitionSpec as P

MODES = 4
GX = 8
ITERS = 2
HALVINGS = 2
CHUNKS = 1 << HALVINGS
STRIP = 16
ORDERS = ((0, 1, 2), (1, 0, 2))

f32 = jnp.float32
bf16 = jnp.bfloat16


def tables(length):
    half = length // 2
    n = np.arange(half)
    out = []
    for odd in (0, 1):
        angle = 2.0 * math.pi * np.outer(2 * n + odd, n) / length
        c, s = np.cos(angle) / math.sqrt(length), np.sin(angle) / math.sqrt(length)
        out.append(np.block([[c, s], [-s, c]]))
    both = np.stack([np.stack(out), np.stack([m.T for m in out])]).astype(np.float32)
    high = both.astype(bf16)
    return np.stack([high, (both - high.astype(np.float32)).astype(bf16)], axis=2)


def deinterleave(length):
    half = length // 2
    out = np.zeros((length, length), np.float32)
    out[2 * np.arange(half), np.arange(half)] = 1.0
    out[2 * np.arange(half) + 1, half + np.arange(half)] = 1.0
    return np.stack([out, out.T]).astype(bf16)


def split(x):
    high = x.astype(bf16)
    return high, (x - high.astype(f32)).astype(bf16)


def dot(a, b):
    return jnp.dot(a, b, preferred_element_type=f32)


def mul_left(table, x):
    return dot(jnp.concatenate([table[0], table[1], table[0]], 1), jnp.concatenate([x[0], x[0], x[1]], 0))


def mul_right(x, table):
    return dot(jnp.concatenate([x[0], x[1], x[0]], 1), jnp.concatenate([table[0], table[0], table[1]], 0))


def put(ref, where, rows, cols, x):
    for k, part in enumerate(split(x)):
        ref[where, k, rows, cols] = part


def strips(count, body):
    lax.fori_loop(0, count, lambda i, c: (body(i), c)[1], 0)


def at(start, length=STRIP):
    return pl.ds(pl.multiple_of(start, STRIP), length)


def exact(x):
    high = x.astype(bf16)
    rest = x - high.astype(f32)
    mid = rest.astype(bf16)
    return high, mid, (rest - mid.astype(f32)).astype(bf16)


def amplitude_kernel(amp, perm, out):
    for s in range(amp.shape[0]):
        high, mid, low = exact(amp[s])
        rows = dot(perm[1], high) + (dot(perm[1], mid) + dot(perm[1], low))
        high, mid, low = exact(rows)
        out[s] = dot(high, perm[0]) + (dot(mid, perm[0]) + dot(low, perm[0]))


def chunk_key(order):
    t = lax.axis_index("tile")
    return sum(((t >> order[i]) & 1) << (HALVINGS - 1 - i) for i in range(HALVINGS))


def corner(offsets, slot, dim, size, margin):
    t = lax.axis_index("tile")
    along = lax.rem(t, GX) if dim else lax.div(t, GX)
    return offsets[slot, dim] - along * size + margin


def update_probe(old, pieces, coef, out):
    rows = old.shape[2] // CHUNKS
    for mode in range(len(pieces)):
        key = chunk_key(ORDERS[mode])
        rel = 0
        for piece in pieces[mode]:
            for k in range(piece.shape[0]):
                here = pl.ds(pl.multiple_of((rel ^ key) * rows, rows), rows)
                out[mode, :, here, :] = old[mode, :, here, :] + coef * piece[k]
                rel += 1


def shift_in(offsets, slot, near, away, patch, tall):
    frame = patch.shape[-1]
    h = frame // 2
    cols, hr = near.shape[-1], near.shape[1]
    size = cols - 2 * h
    core = lax.axis_index("row")
    across = lax.rem(cols - corner(offsets, slot, 1, size, h), cols)
    if tall:
        down = lax.rem(2 * hr - corner(offsets, slot, 0, size, h), 2 * hr)
        for c in range(2):
            both = [jnp.where(core == k, near[c], away[c]) for k in range(2)]
            moved = pltpu.roll(jnp.concatenate(both, 0), across, 1)[:, :frame]
            patch[c] = pltpu.roll(moved, down, 0)[:frame]
        return

    def body(j):
        for ref, half in ((near, core), (away, 1 - core)):
            for c in range(2):
                x = pltpu.roll(ref[c, at(j * STRIP), :], across, 1)
                patch[c, at(half * hr + j * STRIP), :] = x[:, :frame]

    strips(hr // STRIP, body)


def forward_kernel(slot, n_pieces, coef, tall, *refs):
    refs = list(refs)
    offsets, near, away, probe, tab = refs[:5]
    refs = refs[5:]
    modes = probe.shape[0]
    if n_pieces:
        pieces = [refs[m * n_pieces : (m + 1) * n_pieces] for m in range(modes)]
        refs = refs[modes * n_pieces :]
        new_probe = refs.pop(3)
        update_probe(probe, pieces, coef, new_probe)
        probe = new_probe
    far, power, patch, tall_parts, wide_parts, product = refs
    frame = probe.shape[-1]
    h = frame // 2
    shift_in(offsets, slot, near, away, patch, tall)

    def exits(j):
        for m in range(modes):
            pair = []
            for start in (j * STRIP, h + j * STRIP):
                rows = at(start)
                pr, pi = probe[m, 0, rows, :], probe[m, 1, rows, :]
                ar, ai = patch[0, rows, :], patch[1, rows, :]
                pair.append((pr * ar - pi * ai, pr * ai + pi * ar))
            cols = slice(m * frame, (m + 1) * frame)
            for k in range(2):
                put(tall_parts, 0, at(k * h + j * STRIP), cols, pair[0][k] + pair[1][k])
                put(tall_parts, 1, at(k * h + j * STRIP), cols, pair[0][k] - pair[1][k])

    strips(h // STRIP, exits)
    for p in range(2):
        product[p] = mul_left(tab[0, p], tall_parts[p])

    def columns(j):
        for p in range(2):
            for m in range(modes):
                cols = slice(m * frame, (m + 1) * frame)
                y = [product[p, at(k * h + j * STRIP), cols] for k in range(2)]
                rows = at(m * frame + p * h + j * STRIP)
                put(wide_parts, 0, rows, slice(None), jnp.concatenate([v[:, :h] + v[:, h:] for v in y], 1))
                put(wide_parts, 1, rows, slice(None), jnp.concatenate([v[:, :h] - v[:, h:] for v in y], 1))

    strips(h // STRIP, columns)
    for q in range(2):
        out = mul_right(wide_parts[q], tab[1, q])
        for m in range(modes):
            far[m, q] = out[m * frame : (m + 1) * frame]

    def powers(j):
        rows = at(j * STRIP)
        for q in range(2):
            total = None
            for m in range(modes):
                f = far[m, q, rows, :]
                f = f * f
                f = f[:, :h] + f[:, h:]
                total = f if m == 0 else total + f
            power[rows, slice(q * h, (q + 1) * h)] = total

    strips(frame // STRIP, powers)


def inverse_kernel(mode, last, tall, *refs):
    refs = list(refs)
    offsets, counts, tab, amp, probe = refs[:5]
    refs = refs[5:]
    slots = amp.shape[0]
    fars, powers, others, patches = (refs[i * slots : (i + 1) * slots] for i in range(4))
    refs = refs[4 * slots :]
    before = refs.pop(0) if mode else None
    probe_grad, grads, tall_parts, wide_parts, product_wide, product_tall = refs[:6]
    frame = probe.shape[-1]
    h = frame // 2

    def factors(j):
        rows = at(j * STRIP)
        for s in range(slots):
            factor = amp[s, rows, :] / (jnp.sqrt(powers[s][rows, :] + others[s][rows, :]) + 0.5)
            for q in range(2):
                f = factor[:, q * h : (q + 1) * h]
                put(
                    wide_parts,
                    q,
                    at(s * frame + j * STRIP),
                    slice(None),
                    fars[s][mode, q, rows, :] * jnp.concatenate([f, f], 1),
                )

    strips(frame // STRIP, factors)
    for q in range(2):
        product_wide[q] = mul_right(wide_parts[q], tab[0, q])

    def columns(j):
        for p in range(2):
            for s in range(slots):
                rows = at(s * frame + p * h + j * STRIP)
                he, ho = product_wide[0, rows, :], product_wide[1, rows, :]
                cols = slice(s * frame, (s + 1) * frame)
                for k in range(2):
                    a, b = he[:, k * h : (k + 1) * h], ho[:, k * h : (k + 1) * h]
                    put(tall_parts, p, at(k * h + j * STRIP), cols, jnp.concatenate([a + b, a - b], 1))

    strips(h // STRIP, columns)
    for p in range(2):
        product_tall[p] = mul_left(tab[1, p], tall_parts[p])
    key = chunk_key(ORDERS[mode])
    chunk = frame // CHUNKS
    core = lax.axis_index("row")

    def results(j):
        x = [[product_tall[p, at(k * h + j * STRIP), :] for k in range(2)] for p in range(2)]
        for lower in range(2):
            rows = at(lower * h + j * STRIP)
            pr, pi = probe[mode, 0, rows, :], probe[mode, 1, rows, :]
            step = [None, None]
            window = [None, None]
            for s in range(slots):
                cols = slice(s * frame, (s + 1) * frame)
                xr, xi = (
                    x[0][k][:, cols] - x[1][k][:, cols] if lower else x[0][k][:, cols] + x[1][k][:, cols]
                    for k in range(2)
                )
                live = (s < counts[0]).astype(f32)
                ar, ai = patches[s][0, rows, :], patches[s][1, rows, :]
                ur = (xr - (pr * ar - pi * ai)) * live
                ui = (xi - (pr * ai + pi * ar)) * live
                for k, g in enumerate((ar * ur + ai * ui, ar * ui - ai * ur)):
                    step[k] = g if s == 0 else step[k] + g
                for k, g in enumerate((pr * ur + pi * ui, pr * ui - pi * ur)):
                    if mode:
                        g = g + before[s, k, rows, :]
                    if not last or tall:
                        grads[s, k, rows, :] = g
                        continue
                    wide = grads.shape[-1]
                    g = jnp.concatenate([g, jnp.zeros((STRIP, wide - frame), f32)], 1)
                    g = pltpu.roll(g, corner(offsets, s, 1, wide - 2 * h, h), 1)
                    window[k] = g if s == 0 else window[k] + g
            start = lower * h + j * STRIP
            rel = lax.div(start, chunk) ^ key
            for k in range(2):
                probe_grad[rel, k, at(lax.rem(start, chunk)), :] = step[k]
                if last and not tall:
                    grads[lower ^ core, k, at(j * STRIP), :] = window[k]

    strips(h // STRIP, results)


def place_kernel(offsets, grads, out):
    slots, _, frame, _ = grads.shape
    _, _, hr, cols = out.shape
    h = frame // 2
    size = cols - 2 * h
    core = lax.axis_index("row")
    for c in range(2):
        total = None
        for s in range(slots):
            g = jnp.concatenate([grads[s, c], jnp.zeros((2 * hr - frame, frame), f32)], 0)
            g = pltpu.roll(g, corner(offsets, s, 0, size, h), 0)
            g = jnp.concatenate([g, jnp.zeros((2 * hr, cols - frame), f32)], 1)
            g = pltpu.roll(g, corner(offsets, s, 1, size, h), 1)
            total = g if s == 0 else total + g
        for k in range(2):
            out[k ^ core, c] = total[k * hr : (k + 1) * hr]


def finish_kernel(n_pieces, coef, *refs):
    refs = list(refs)
    near, away, probe = refs[:3]
    pieces = [refs[3 + m * n_pieces : 3 + (m + 1) * n_pieces] for m in range(probe.shape[0])]
    tile, new_probe = refs[-2:]
    update_probe(probe, pieces, coef, new_probe)
    hr = near.shape[1]
    core = lax.axis_index("row")
    tile[:, pl.ds(pl.multiple_of(core * hr, hr), hr), :] = near[...]
    tile[:, pl.ds(pl.multiple_of((1 - core) * hr, hr), hr), :] = away[...]


def vmem():
    return pl.BlockSpec(memory_space=pltpu.VMEM)


def call(kernel, outs, args, scratch=(), flops=0):
    size = sum(math.prod(a.shape) * a.dtype.itemsize for a in args)
    size += sum(math.prod(o) * 4 for o in outs)
    return pl.pallas_call(
        kernel,
        out_shape=[jax.ShapeDtypeStruct(o, f32) for o in outs],
        in_specs=[
            pl.BlockSpec(memory_space=pltpu.SMEM) if a.dtype == jnp.int32 else vmem() for a in args
        ],
        out_specs=[vmem() for _ in outs],
        scratch_shapes=list(scratch),
        cost_estimate=pl.CostEstimate(flops=flops, bytes_accessed=size, transcendentals=0),
        compiler_params=pltpu.CompilerParams(vmem_limit_bytes=40 * 1024 * 1024),
    )(*args)


def swap_rows(x):
    return lax.ppermute(x, "row", [(0, 1), (1, 0)])


def shift_cols(x, step, tiles):
    pairs = [(s, s + step) for s in range(tiles) if 0 <= s % GX + step < GX]
    return lax.ppermute(x, "tile", pairs)


def swap_vertical(x, tiles):
    pairs = [(2 * t, 2 * (t - GX) + 1) for t in range(GX, tiles)]
    pairs += [(2 * t + 1, 2 * (t + GX)) for t in range(tiles - GX)]
    return lax.ppermute(x, ("tile", "row"), pairs)


def exchange(x, bit, tiles):
    return lax.ppermute(x, "tile", [(s, s ^ (1 << bit)) for s in range(tiles)])


def together(*groups):
    return lax.optimization_barrier(groups)


def window_sum(grad, size, half, tiles, tall, wide):
    if wide:
        left, right = grad[:, :, :size], grad[:, :, size:]
        right_side = shift_cols(left, -1, tiles)
        left_side = shift_cols(right, 1, tiles)
        total = jnp.concatenate([left + left_side, right + right_side], 2)
        return total + swap_vertical(total, tiles) if tall else total
    got_left = shift_cols(grad[:, :, half + size :], 1, tiles)
    got_right = shift_cols(grad[:, :, :half], -1, tiles)
    return grad[:, :, half : half + size] + jnp.concatenate([got_left, got_right], 2)


def reduce_all(parts, grad, tiles, window):
    bits = int(math.log2(tiles))
    held = list(parts)
    for i in range(HALVINGS):
        n = held[0].shape[0] // 2
        got = [exchange(h[n:], o[i], tiles) for h, o in zip(held, ORDERS)]
        held = [h[:n] + g for h, g in zip(held, got)]
    held, grad = together(held, grad)
    got = [exchange(h, o[-1], tiles) for h, o in zip(held, ORDERS)]
    near = window(grad)
    held = [h + g for h, g in zip(held, got)]
    for bit in range(len(ORDERS[0]), bits):
        held = [h + exchange(h, bit, tiles) for h in held]
    pieces = [[h] for h in held]
    for i in reversed(range(HALVINGS)):
        for p, o in zip(pieces, ORDERS):
            p.append(exchange(p[0] if len(p) == 1 else jnp.concatenate(p, 0), o[i], tiles))
    return pieces, near


def per_device(object_tiles, probe_modes, amplitude, offsets, counts):
    own_tile = object_tiles[0]
    size = own_tile.shape[-1]
    frame = probe_modes.shape[-1]
    half = frame // 2
    tiles = lax.axis_size("tile")
    tall = tiles > GX
    slots = offsets.shape[0]
    modes = probe_modes.shape[0]
    core = lax.axis_index("row")
    hr = size // 2
    tab = jnp.asarray(tables(frame))
    perm = jnp.asarray(deinterleave(frame))
    coef = 4.0 / (slots * tiles)

    mine = lax.dynamic_slice(own_tile, (0, core * hr, 0), (2, hr, size))
    from_left = shift_cols(mine[:, :, size - half :], 1, tiles)
    from_right = shift_cols(mine[:, :, :half], -1, tiles)
    near = jnp.concatenate([from_left, mine, from_right], 2)
    if tall:
        other = swap_vertical(near, tiles)
        near = jnp.where(core == 0, jnp.concatenate([other, near], 1), jnp.concatenate([near, other], 1))
    (amp,) = call(amplitude_kernel, [amplitude.shape], [amplitude, perm])
    away = swap_rows(near)
    near, away, amp = together(near, away, amp)

    def scratch(count):
        return [
            pltpu.VMEM((2, 2, frame, count * frame), bf16),
            pltpu.VMEM((2, 2, count * frame, frame), bf16),
        ]

    matmul = 4 * 2 * 3 * 4 * frame**3
    probe = probe_modes
    pieces = None
    for iteration in range(ITERS):
        final = iteration + 1 == ITERS
        fars, powers, others, patches = [], [], [], []
        for s in range(slots):
            args = [offsets, near, away, probe, tab]
            outs = [(modes, 2, frame, frame), (frame, frame), (2, frame, frame)]
            count = 0
            if pieces is not None:
                count = len(pieces[0])
                args += [p for group in pieces for p in group]
                outs.append(probe.shape)
                pieces = None
            got = call(
                functools.partial(forward_kernel, s, count, coef, tall),
                outs,
                args,
                scratch(modes) + [pltpu.VMEM((2, frame, modes * frame), f32)],
                matmul * modes,
            )
            if count:
                probe = got[3]
            fars.append(got[0])
            powers.append(got[1])
            patches.append(got[2])
            others.append(swap_rows(got[1]))
        before = None
        parts = []
        for m in range(modes):
            last = m == modes - 1
            args = [offsets, counts, tab, amp, probe] + fars + powers + others + patches
            if m:
                args.append(before)
            grads = (2,) + near.shape if last and not tall else (slots, 2, frame, frame)
            got = call(
                functools.partial(inverse_kernel, m, last, tall),
                [(CHUNKS, 2, frame // CHUNKS, frame), grads],
                args,
                scratch(slots)
                + [pltpu.VMEM((2, slots * frame, frame), f32), pltpu.VMEM((2, frame, slots * frame), f32)],
                matmul * slots,
            )
            parts.append(got[0])
            before = got[1]
        if tall:
            (before,) = call(place_kernel, [(2,) + near.shape], [offsets, before])
        grad = before[0] + swap_rows(before[1])
        wide = tall or not final
        pieces, total = reduce_all(
            parts, grad, tiles, lambda g: window_sum(g, size, half, tiles, tall, wide)
        )
        if wide:
            near = near + total / MODES
        else:
            near = near[:, :, half : half + size] + total / MODES
        if tall and final:
            near = near[:, :, half : half + size]
            near = jnp.where(core == 0, near[:, half:], near[:, : size - half])
        away = swap_rows(near)
    args = [near, away, probe] + [p for group in pieces for p in group]
    tile, probe = call(
        functools.partial(finish_kernel, len(pieces[0]), coef), [own_tile.shape, probe.shape], args
    )
    return (tile[None], probe)


def solution(mesh):
    return jax.shard_map(
        per_device,
        mesh=mesh,
        in_specs=(
            P(("scan", "tile"), None, None, None),
            P("row", None, None, None),
            P(("scan", "tile"), None, None),
            P(("scan", "tile"), None),
            P(("scan", "tile")),
        ),
        out_specs=(P(("scan", "tile"), None, None, None), P(("scan", "row"), None, None, None)),
        check_vma=False,
    )
```

time: 136 us -> 142 us (1.044)
  Pallas kernels: 21.2 us -> 28.2 us
    pallas_call x10, Pallas kernels: 21.2 us -> 28.2 us  [call(): pl.pallas_call(kernel, out_shape=[jax.ShapeDtypeStruct(o, f32) for o in o...]
  transfers between devices with their start and end apart: 35 -> 35, of which waited for: 26 -> 26; matrix products, arithmetic and copies ran while one was open for 0% -> 1% of each run, Pallas kernels for 6% -> 8%
where the time goes in v3:
time: 142 us; the launch traced here: 141 us
  waiting for transfers between devices  66.2 us (47%)
  starting transfers between devices  42.9 us (30%)
  Pallas kernels  28.2 us (20%)
  between operations  1.78 us (1%)
    ppermute x20, waiting for transfers between devices, exchange(): return lax.ppermute(x, 'tile', [(s, s ^ 1 << bit) for s in range(tiles)])  58.9 us
    pallas_call x10, Pallas kernels, call(): pl.pallas_call(kernel, out_shape=[jax.ShapeDtypeStruct(o, f32) for o in o...  28.2 us
    ppermute x20, starting transfers between devices, exchange(): return lax.ppermute(x, 'tile', [(s, s ^ 1 << bit) for s in range(tiles)])  24.8 us
    ppermute x6, starting transfers between devices, shift_cols(): return lax.ppermute(x, 'tile', pairs)  16.5 us
    ppermute x6, waiting for transfers between devices, shift_cols(): return lax.ppermute(x, 'tile', pairs)  4.35 us
    ppermute x9, waiting for transfers between devices, swap_rows(): return lax.ppermute(x, 'row', [(0, 1), (1, 0)])  2.96 us
  transfers between devices with their start and end apart: 35, of which 26 were waited for; matrix products, arithmetic and copies ran while one was open for 1% of the time, Pallas kernels for 8%

profile of v3, /device:TPU:0, one launch (start us, length us, event | category | flops | bytes accessed | tf_op | source)
XLA Modules:
  0.0 141.3 jit_solution(7850828831418727722)
XLA Ops:
  3.2 5.6 %collective-permute-start = (f32[2,128,128]{2,1,0:T(8,128)S(1)}, f32[2,128,128]{2,1,0:T(8,128)S(1)}, u32[]{:S(2)}, u32[]{:S(2)}) collective-permute-start(f32[2,128,128]{2,1,0:T(8,128)S(1)} %get-tuple-element.72), channel_id=1, source_target_pairs={{0,2},{2,4},{4,6},{6,8},{8,10},{10,12},{12,14},{1,3},{3,5},{5,7},{... | collective-permute-start | bytes 393224 | tf_op jit(solution)/shard_map/ppermute | solution.py:341
  10.2 3.0 %collective-permute-done = f32[2,128,128]{2,1,0:T(8,128)S(1)} collective-permute-done((f32[2,128,128]{2,1,0:T(8,128)S(1)}, f32[2,128,128]{2,1,0:T(8,128)S(1)}, u32[]{:S(2)}, u32[]{:S(2)}) %collective-permute-start) | collective-permute-done | bytes 131104 | tf_op jit(solution)/shard_map/ppermute | solution.py:341
  15.2 3.2 %shard_map.87 = (f32[2,2,256,256]{3,2,1,0:T(8,128)S(1)}, f32[256,256]{1,0:T(8,128)S(1)}, f32[2,256,256]{2,1,0:T(8,128)S(1)}) custom-call(s32[2,2]{1,0:T(2,128)S(1)} %copy-done.4, f32[2,128,512]{2,1,0:T(8,128)S(1)} %pad_maximum_fusion.refs_1_, f32[2,128,512]{2,1,0:T(8,128)S(1)} %collective-permute-done.2.refs_2_, f32[2,2,256,256]{3,2,1,0:T(8,128)S(1)} %copy-done.3, ...), custom_call_target="tpu_custom_call" | custom-call | flops 3221225472 | bytes 4980752 | tf_op jit(solution)/shard_map/pallas_call | solution.py:322
  18.5 3.2 %shard_map.88 = (f32[2,2,256,256]{3,2,1,0:T(8,128)S(1)}, f32[256,256]{1,0:T(8,128)S(1)}, f32[2,256,256]{2,1,0:T(8,128)S(1)}) custom-call(s32[2,2]{1,0:T(2,128)S(1)} %copy-done.4, f32[2,128,512]{2,1,0:T(8,128)S(1)} %pad_maximum_fusion.refs_1_, f32[2,128,512]{2,1,0:T(8,128)S(1)} %collective-permute-done.2.refs_2_, f32[2,2,256,256]{3,2,1,0:T(8,128)S(1)} %copy-done.3, ...), custom_call_target="tpu_custom_call" | custom-call | flops 3221225472 | bytes 4980752 | tf_op jit(solution)/shard_map/pallas_call | solution.py:322
  23.7 3.0 %shard_map.89 = (f32[4,2,64,256]{3,2,1,0:T(8,128)S(1)}, f32[2,2,256,256]{3,2,1,0:T(8,128)S(1)}) custom-call(s32[2,2]{1,0:T(2,128)S(1)} %copy-done.4, s32[1]{0:T(128)S(6)} %copy.9.refs_1_, bf16[2,2,2,256,256]{4,3,2,1,0:T(8,128)(2,1)S(1)} %copy-done.5, f32[2,256,256]{2,1,0:T(8,128)S(1)} %shard_map.86.refs_3_, f32[2,2,256,256]{3,2,1,0:T(8,128)S(1)} %copy-done.3, ...), custom_call_target="tpu_custom_call" | custom-call | flops 3221225472 | bytes 8388628 | tf_op jit(solution)/shard_map/pallas_call | solution.py:322
  26.7 2.5 %collective-permute-start.5 = (f32[2,2,64,256]{3,2,1,0:T(8,128)S(1)}, f32[2,2,64,256]{3,2,1,0:T(8,128)S(1)}, u32[]{:S(2)}, u32[]{:S(2)}) collective-permute-start(f32[2,2,64,256]{3,2,1,0:T(8,128)S(1)} %slice.87), channel_id=1, source_target_pairs={{0,2},{2,0},{4,6},{6,4},{8,10},{10,8},{12,14},{14,12},{1,3},{3,1},... | collective-permute-start | bytes 786440 | tf_op jit(solution)/shard_map/ppermute | solution.py:351
  29.2 3.6 %shard_map.90 = (f32[4,2,64,256]{3,2,1,0:T(8,128)S(1)}, f32[2,2,128,512]{3,2,1,0:T(8,128)S(1)}) custom-call(s32[2,2]{1,0:T(2,128)S(1)} %copy-done.4, s32[1]{0:T(128)S(6)} %copy.9.refs_1_, bf16[2,2,2,256,256]{4,3,2,1,0:T(8,128)(2,1)S(1)} %copy-done.5, f32[2,256,256]{2,1,0:T(8,128)S(1)} %shard_map.86.refs_3_, f32[2,2,256,256]{3,2,1,0:T(8,128)S(1)} %copy-done.3, ...), custom_call_target="tpu_custom_call" | custom-call | flops 3221225472 | bytes 9437204 | tf_op jit(solution)/shard_map/pallas_call | solution.py:322
  35.9 2.3 %collective-permute-start.6 = (f32[1,2,64,256]{3,2,1,0:T(8,128)S(1)}, f32[1,2,64,256]{3,2,1,0:T(8,128)S(1)}, u32[]{:S(2)}, u32[]{:S(2)}) collective-permute-start(f32[1,2,64,256]{3,2,1,0:T(8,128)S(1)} %slice.115), channel_id=1, source_target_pairs={{0,4},{2,6},{4,0},{6,2},{8,12},{10,14},{12,8},{14,10},{1,5},{3,7},... | collective-permute-start | bytes 393224 | tf_op jit(solution)/shard_map/ppermute | solution.py:351
  38.2 3.9 %collective-permute-done.7 = f32[2,2,64,256]{3,2,1,0:T(8,128)S(1)} collective-permute-done((f32[2,2,64,256]{3,2,1,0:T(8,128)S(1)}, f32[2,2,64,256]{3,2,1,0:T(8,128)S(1)}, u32[]{:S(2)}, u32[]{:S(2)}) %collective-permute-start.7) | collective-permute-done | bytes 262176 | tf_op jit(solution)/shard_map/ppermute | solution.py:351
  43.8 3.4 %collective-permute-done.8 = f32[1,2,64,256]{3,2,1,0:T(8,128)S(1)} collective-permute-done((f32[1,2,64,256]{3,2,1,0:T(8,128)S(1)}, f32[1,2,64,256]{3,2,1,0:T(8,128)S(1)}, u32[]{:S(2)}, u32[]{:S(2)}) %collective-permute-start.8) | collective-permute-done | bytes 131104 | tf_op jit(solution)/shard_map/ppermute | solution.py:351
  47.3 2.4 %collective-permute-start.10 = (f32[2,128,256]{2,1,0:T(8,128)S(1)}, f32[2,128,256]{2,1,0:T(8,128)S(1)}, u32[]{:S(2)}, u32[]{:S(2)}) collective-permute-start(f32[2,128,256]{2,1,0:T(8,128)S(1)} %get-tuple-element.70), channel_id=1, source_target_pairs={{0,2},{2,4},{4,6},{6,8},{8,10},{10,12},{12,14},{1,3},{3,5},{5,7},{... | collective-permute-start | bytes 786440 | tf_op jit(solution)/shard_map/ppermute | solution.py:341
  51.0 5.7 %collective-permute-start.13 = (f32[1,2,64,256]{3,2,1,0:T(8,128)S(1)}, f32[1,2,64,256]{3,2,1,0:T(8,128)S(1)}, u32[]{:S(2)}, u32[]{:S(2)}) collective-permute-start(f32[1,2,64,256]{3,2,1,0:T(8,128)S(1)} %slice_add_fusion.8), channel_id=1, source_target_pairs={{0,8},{2,10},{4,12},{6,14},{8,0},{10,2},{12,4},{14,6},{1,9},{3,11}... | collective-permute-start | bytes 393224 | tf_op jit(solution)/shard_map/ppermute | solution.py:351
  56.8 12.3 %collective-permute-done.13 = f32[1,2,64,256]{3,2,1,0:T(8,128)S(1)} collective-permute-done((f32[1,2,64,256]{3,2,1,0:T(8,128)S(1)}, f32[1,2,64,256]{3,2,1,0:T(8,128)S(1)}, u32[]{:S(2)}, u32[]{:S(2)}) %collective-permute-start.13) | collective-permute-done | bytes 131104 | tf_op jit(solution)/shard_map/ppermute | solution.py:351
  70.7 3.5 %collective-permute-done.14.refs_6_ = f32[1,2,64,256]{3,2,1,0:T(8,128)S(1)} collective-permute-done((f32[1,2,64,256]{3,2,1,0:T(8,128)S(1)}, f32[1,2,64,256]{3,2,1,0:T(8,128)S(1)}, u32[]{:S(2)}, u32[]{:S(2)}) %collective-permute-start.14) | collective-permute-done | bytes 131104 | tf_op jit(solution)/shard_map/ppermute | solution.py:351
  74.3 2.8 %collective-permute-done.17.refs_9_ = f32[1,2,64,256]{3,2,1,0:T(8,128)S(1)} collective-permute-done((f32[1,2,64,256]{3,2,1,0:T(8,128)S(1)}, f32[1,2,64,256]{3,2,1,0:T(8,128)S(1)}, u32[]{:S(2)}, u32[]{:S(2)}) %collective-permute-start.17) | collective-permute-done | bytes 131104 | tf_op jit(solution)/shard_map/ppermute | solution.py:351
  78.0 3.1 %collective-permute-done.15.refs_7_ = f32[2,2,64,256]{3,2,1,0:T(8,128)S(1)} collective-permute-done((f32[2,2,64,256]{3,2,1,0:T(8,128)S(1)}, f32[2,2,64,256]{3,2,1,0:T(8,128)S(1)}, u32[]{:S(2)}, u32[]{:S(2)}) %collective-permute-start.15) | collective-permute-done | bytes 262176 | tf_op jit(solution)/shard_map/ppermute | solution.py:351
  81.1 2.6 %collective-permute-done.18.refs_10_ = f32[2,2,64,256]{3,2,1,0:T(8,128)S(1)} collective-permute-done((f32[2,2,64,256]{3,2,1,0:T(8,128)S(1)}, f32[2,2,64,256]{3,2,1,0:T(8,128)S(1)}, u32[]{:S(2)}, u32[]{:S(2)}) %collective-permute-start.18) | collective-permute-done | bytes 262176 | tf_op jit(solution)/shard_map/ppermute | solution.py:351
  83.8 3.3 %shard_map.91 = (f32[2,2,256,256]{3,2,1,0:T(8,128)S(1)}, f32[256,256]{1,0:T(8,128)S(1)}, f32[2,256,256]{2,1,0:T(8,128)S(1)}, f32[2,2,256,256]{3,2,1,0:T(8,128)S(1)}) custom-call(s32[2,2]{1,0:T(2,128)S(1)} %copy-done.4, f32[2,128,512]{2,1,0:T(8,128)S(1)} %fusion.refs_1_, f32[2,128,512]{2,1,0:T(8,128)S(1)} %collective-permute-done.12.refs_2_, ...), custom_call_target="tpu_custom_call" | custom-call | flops 3221225472 | bytes 7077904 | tf_op jit(solution)/shard_map/pallas_call | solution.py:322
  87.2 3.2 %shard_map.92 = (f32[2,2,256,256]{3,2,1,0:T(8,128)S(1)}, f32[256,256]{1,0:T(8,128)S(1)}, f32[2,256,256]{2,1,0:T(8,128)S(1)}) custom-call(s32[2,2]{1,0:T(2,128)S(1)} %copy-done.4, f32[2,128,512]{2,1,0:T(8,128)S(1)} %fusion.refs_1_, f32[2,128,512]{2,1,0:T(8,128)S(1)} %collective-permute-done.12.refs_2_, ...), custom_call_target="tpu_custom_call" | custom-call | flops 3221225472 | bytes 4980752 | tf_op jit(solution)/shard_map/pallas_call | solution.py:322
  92.1 3.0 %shard_map.93 = (f32[4,2,64,256]{3,2,1,0:T(8,128)S(1)}, f32[2,2,256,256]{3,2,1,0:T(8,128)S(1)}) custom-call(s32[2,2]{1,0:T(2,128)S(1)} %copy-done.4, s32[1]{0:T(128)S(6)} %copy.9.refs_1_, bf16[2,2,2,256,256]{4,3,2,1,0:T(8,128)(2,1)S(1)} %copy-done.5, f32[2,256,256]{2,1,0:T(8,128)S(1)} %shard_map.86.refs_3_, ...), custom_call_target="tpu_custom_call" | custom-call | flops 3221225472 | bytes 8388628 | tf_op jit(solution)/shard_map/pallas_call | solution.py:322
  95.7 3.6 %shard_map.94 = (f32[4,2,64,256]{3,2,1,0:T(8,128)S(1)}, f32[2,2,128,512]{3,2,1,0:T(8,128)S(1)}) custom-call(s32[2,2]{1,0:T(2,128)S(1)} %copy-done.4, s32[1]{0:T(128)S(6)} %copy.9.refs_1_, bf16[2,2,2,256,256]{4,3,2,1,0:T(8,128)(2,1)S(1)} %copy-done.5, f32[2,256,256]{2,1,0:T(8,128)S(1)} %shard_map.86.refs_3_, ...), custom_call_target="tpu_custom_call" | custom-call | flops 3221225472 | bytes 9437204 | tf_op jit(solution)/shard_map/pallas_call | solution.py:322
  99.3 1.8 %collective-permute-start.23 = (f32[2,2,64,256]{3,2,1,0:T(8,128)S(1)}, f32[2,2,64,256]{3,2,1,0:T(8,128)S(1)}, u32[]{:S(2)}, u32[]{:S(2)}) collective-permute-start(f32[2,2,64,256]{3,2,1,0:T(8,128)S(1)} %slice.104), channel_id=1, source_target_pairs={{0,4},{2,6},{4,0},{6,2},{8,12},{10,14},{12,8},{14,10},{1,5},{3,7},... | collective-permute-start | bytes 786440 | tf_op jit(solution)/shard_map/ppermute | solution.py:351
  101.2 2.5 %collective-permute-done.21 = f32[2,2,64,256]{3,2,1,0:T(8,128)S(1)} collective-permute-done((f32[2,2,64,256]{3,2,1,0:T(8,128)S(1)}, f32[2,2,64,256]{3,2,1,0:T(8,128)S(1)}, u32[]{:S(2)}, u32[]{:S(2)}) %collective-permute-start.21) | collective-permute-done | bytes 262176 | tf_op jit(solution)/shard_map/ppermute | solution.py:351
  103.8 1.8 %collective-permute-start.22 = (f32[1,2,64,256]{3,2,1,0:T(8,128)S(1)}, f32[1,2,64,256]{3,2,1,0:T(8,128)S(1)}, u32[]{:S(2)}, u32[]{:S(2)}) collective-permute-start(f32[1,2,64,256]{3,2,1,0:T(8,128)S(1)} %slice.120), channel_id=1, source_target_pairs={{0,4},{2,6},{4,0},{6,2},{8,12},{10,14},{12,8},{14,10},{1,5},{3,7},... | collective-permute-start | bytes 393224 | tf_op jit(solution)/shard_map/ppermute | solution.py:351
  105.7 2.9 %collective-permute-done.23 = f32[2,2,64,256]{3,2,1,0:T(8,128)S(1)} collective-permute-done((f32[2,2,64,256]{3,2,1,0:T(8,128)S(1)}, f32[2,2,64,256]{3,2,1,0:T(8,128)S(1)}, u32[]{:S(2)}, u32[]{:S(2)}) %collective-permute-start.23) | collective-permute-done | bytes 262176 | tf_op jit(solution)/shard_map/ppermute | solution.py:351
  110.5 3.1 %collective-permute-done.24 = f32[1,2,64,256]{3,2,1,0:T(8,128)S(1)} collective-permute-done((f32[1,2,64,256]{3,2,1,0:T(8,128)S(1)}, f32[1,2,64,256]{3,2,1,0:T(8,128)S(1)}, u32[]{:S(2)}, u32[]{:S(2)}) %collective-permute-start.24) | collective-permute-done | bytes 131104 | tf_op jit(solution)/shard_map/ppermute | solution.py:351
  114.4 2.4 %collective-permute-start.32 = (f32[1,2,64,256]{3,2,1,0:T(8,128)S(1)}, f32[1,2,64,256]{3,2,1,0:T(8,128)S(1)}, u32[]{:S(2)}, u32[]{:S(2)}) collective-permute-start(f32[1,2,64,256]{3,2,1,0:T(8,128)S(1)} %slice_add_fusion.5), channel_id=1, source_target_pairs={{0,8},{2,10},{4,12},{6,14},{8,0},{10,2},{12,4},{14,6},{1,9},{3,11}... | collective-permute-start | bytes 393224 | tf_op jit(solution)/shard_map/ppermute | solution.py:351
  118.1 4.6 %collective-permute-start.26 = (f32[2,128,128]{2,1,0:T(8,128)S(1)}, f32[2,128,128]{2,1,0:T(8,128)S(1)}, u32[]{:S(2)}, u32[]{:S(2)}) collective-permute-start(f32[2,128,128]{2,1,0:T(8,128)S(1)} %get-tuple-element.66), channel_id=1, source_target_pairs={{0,2},{2,4},{4,6},{6,8},{8,10},{10,12},{12,14},{1,3},{3,5},{5,7},{... | collective-permute-start | bytes 393224 | tf_op jit(solution)/shard_map/ppermute | solution.py:341
  124.5 2.6 %collective-permute-done.32 = f32[1,2,64,256]{3,2,1,0:T(8,128)S(1)} collective-permute-done((f32[1,2,64,256]{3,2,1,0:T(8,128)S(1)}, f32[1,2,64,256]{3,2,1,0:T(8,128)S(1)}, u32[]{:S(2)}, u32[]{:S(2)}) %collective-permute-start.32) | collective-permute-done | bytes 131104 | tf_op jit(solution)/shard_map/ppermute | solution.py:351
  131.1 2.5 %collective-permute-done.33.refs_7_ = f32[1,2,64,256]{3,2,1,0:T(8,128)S(1)} collective-permute-done((f32[1,2,64,256]{3,2,1,0:T(8,128)S(1)}, f32[1,2,64,256]{3,2,1,0:T(8,128)S(1)}, u32[]{:S(2)}, u32[]{:S(2)}) %collective-permute-start.33) | collective-permute-done | bytes 131104 | tf_op jit(solution)/shard_map/ppermute | solution.py:351
  133.7 4.2 %collective-permute-done.31.refs_5_ = f32[2,2,64,256]{3,2,1,0:T(8,128)S(1)} collective-permute-done((f32[2,2,64,256]{3,2,1,0:T(8,128)S(1)}, f32[2,2,64,256]{3,2,1,0:T(8,128)S(1)}, u32[]{:S(2)}, u32[]{:S(2)}) %collective-permute-start.31) | collective-permute-done | bytes 262176 | tf_op jit(solution)/shard_map/ppermute | solution.py:351
  137.8 2.2 %collective-permute-done.34.refs_8_ = f32[2,2,64,256]{3,2,1,0:T(8,128)S(1)} collective-permute-done((f32[2,2,64,256]{3,2,1,0:T(8,128)S(1)}, f32[2,2,64,256]{3,2,1,0:T(8,128)S(1)}, u32[]{:S(2)}, u32[]{:S(2)}) %collective-permute-start.34) | collective-permute-done | bytes 262176 | tf_op jit(solution)/shard_map/ppermute | solution.py:351
  (96 shorter events, 29.6 us)
Async XLA Ops:
  1.7 8.5 %collective-permute-start.1 = (f32[2,128,128]{2,1,0:T(8,128)S(1)}, f32[2,128,128]{2,1,0:T(8,128)S(1)}, u32[]{:S(2)}, u32[]{:S(2)}) collective-permute-start(f32[2,128,128]{2,1,0:T(8,128)S(1)} %get-tuple-element.73), channel_id=1, source_target_pairs={{2,0},{4,2},{6,4},{8,6},{10,8},{12,10},{14,12},{3,1},{5,3},{7,5},{... | collective-permute-start | bytes 393224 | tf_op jit(solution)/shard_map/ppermute | solution.py:341
  3.2 10.0 %collective-permute-start = (f32[2,128,128]{2,1,0:T(8,128)S(1)}, f32[2,128,128]{2,1,0:T(8,128)S(1)}, u32[]{:S(2)}, u32[]{:S(2)}) collective-permute-start(f32[2,128,128]{2,1,0:T(8,128)S(1)} %get-tuple-element.72), channel_id=1, source_target_pairs={{0,2},{2,4},{4,6},{6,8},{8,10},{10,12},{12,14},{1,3},{3,5},{5,7},{... | collective-permute-start | bytes 393224 | tf_op jit(solution)/shard_map/ppermute | solution.py:341
  13.2 2.0 %collective-permute-start.2 = (f32[2,128,512]{2,1,0:T(8,128)S(1)}, f32[2,128,512]{2,1,0:T(8,128)S(1)}, u32[]{:S(2)}, u32[]{:S(2)}) collective-permute-start(f32[2,128,512]{2,1,0:T(8,128)S(1)} %pad_maximum_fusion.refs_1_), channel_id=1, source_target_pairs={{0,1},{1,0},{2,3},{3,2},{4,5},{5,4},{6,7},{7,6},{8,9},{9,8},{10,11... | collective-permute-start | bytes 1572872 | tf_op jit(solution)/shard_map/ppermute | solution.py:336
  26.7 9.2 %collective-permute-start.5 = (f32[2,2,64,256]{3,2,1,0:T(8,128)S(1)}, f32[2,2,64,256]{3,2,1,0:T(8,128)S(1)}, u32[]{:S(2)}, u32[]{:S(2)}) collective-permute-start(f32[2,2,64,256]{3,2,1,0:T(8,128)S(1)} %slice.87), channel_id=1, source_target_pairs={{0,2},{2,0},{4,6},{6,4},{8,10},{10,8},{12,14},{14,12},{1,3},{3,1},... | collective-permute-start | bytes 786440 | tf_op jit(solution)/shard_map/ppermute | solution.py:351
  32.8 9.3 %collective-permute-start.7 = (f32[2,2,64,256]{3,2,1,0:T(8,128)S(1)}, f32[2,2,64,256]{3,2,1,0:T(8,128)S(1)}, u32[]{:S(2)}, u32[]{:S(2)}) collective-permute-start(f32[2,2,64,256]{3,2,1,0:T(8,128)S(1)} %slice.91), channel_id=1, source_target_pairs={{0,4},{2,6},{4,0},{6,2},{8,12},{10,14},{12,8},{14,10},{1,5},{3,7},... | collective-permute-start | bytes 786440 | tf_op jit(solution)/shard_map/ppermute | solution.py:351
  34.5 12.7 %collective-permute-start.9 = (f32[2,128,512]{2,1,0:T(8,128)S(1)}, f32[2,128,512]{2,1,0:T(8,128)S(1)}, u32[]{:S(2)}, u32[]{:S(2)}) collective-permute-start(f32[2,128,512]{2,1,0:T(8,128)S(1)} %slice_bitcast_fusion.1), channel_id=1, source_target_pairs={{0,1},{1,0},{2,3},{3,2},{4,5},{5,4},{6,7},{7,6},{8,9},{9,8},{10,11... | collective-permute-start | bytes 1572872 | tf_op jit(solution)/shard_map/ppermute | solution.py:336
  35.9 7.9 %collective-permute-start.6 = (f32[1,2,64,256]{3,2,1,0:T(8,128)S(1)}, f32[1,2,64,256]{3,2,1,0:T(8,128)S(1)}, u32[]{:S(2)}, u32[]{:S(2)}) collective-permute-start(f32[1,2,64,256]{3,2,1,0:T(8,128)S(1)} %slice.115), channel_id=1, source_target_pairs={{0,4},{2,6},{4,0},{6,2},{8,12},{10,14},{12,8},{14,10},{1,5},{3,7},... | collective-permute-start | bytes 393224 | tf_op jit(solution)/shard_map/ppermute | solution.py:351
  42.1 5.0 %collective-permute-start.8 = (f32[1,2,64,256]{3,2,1,0:T(8,128)S(1)}, f32[1,2,64,256]{3,2,1,0:T(8,128)S(1)}, u32[]{:S(2)}, u32[]{:S(2)}) collective-permute-start(f32[1,2,64,256]{3,2,1,0:T(8,128)S(1)} %slice.117), channel_id=1, source_target_pairs={{0,2},{2,0},{4,6},{6,4},{8,10},{10,8},{12,14},{14,12},{1,3},{3,1},... | collective-permute-start | bytes 393224 | tf_op jit(solution)/shard_map/ppermute | solution.py:351
  47.3 21.9 %collective-permute-start.10 = (f32[2,128,256]{2,1,0:T(8,128)S(1)}, f32[2,128,256]{2,1,0:T(8,128)S(1)}, u32[]{:S(2)}, u32[]{:S(2)}) collective-permute-start(f32[2,128,256]{2,1,0:T(8,128)S(1)} %get-tuple-element.70), channel_id=1, source_target_pairs={{0,2},{2,4},{4,6},{6,8},{8,10},{10,12},{12,14},{1,3},{3,5},{5,7},{... | collective-permute-start | bytes 786440 | tf_op jit(solution)/shard_map/ppermute | solution.py:341
  49.7 19.6 %collective-permute-start.11 = (f32[2,128,256]{2,1,0:T(8,128)S(1)}, f32[2,128,256]{2,1,0:T(8,128)S(1)}, u32[]{:S(2)}, u32[]{:S(2)}) collective-permute-start(f32[2,128,256]{2,1,0:T(8,128)S(1)} %get-tuple-element.71), channel_id=1, source_target_pairs={{2,0},{4,2},{6,4},{8,6},{10,8},{12,10},{14,12},{3,1},{5,3},{7,5},{... | collective-permute-start | bytes 786440 | tf_op jit(solution)/shard_map/ppermute | solution.py:341
  51.0 18.2 %collective-permute-start.13 = (f32[1,2,64,256]{3,2,1,0:T(8,128)S(1)}, f32[1,2,64,256]{3,2,1,0:T(8,128)S(1)}, u32[]{:S(2)}, u32[]{:S(2)}) collective-permute-start(f32[1,2,64,256]{3,2,1,0:T(8,128)S(1)} %slice_add_fusion.8), channel_id=1, source_target_pairs={{0,8},{2,10},{4,12},{6,14},{8,0},{10,2},{12,4},{14,6},{1,9},{3,11}... | collective-permute-start | bytes 393224 | tf_op jit(solution)/shard_map/ppermute | solution.py:351
  56.8 13.8 %collective-permute-start.16 = (f32[1,2,64,256]{3,2,1,0:T(8,128)S(1)}, f32[1,2,64,256]{3,2,1,0:T(8,128)S(1)}, u32[]{:S(2)}, u32[]{:S(2)}) collective-permute-start(f32[1,2,64,256]{3,2,1,0:T(8,128)S(1)} %slice_add_fusion.7), channel_id=1, source_target_pairs={{0,8},{2,10},{4,12},{6,14},{8,0},{10,2},{12,4},{14,6},{1,9},{3,11}... | collective-permute-start | bytes 393224 | tf_op jit(solution)/shard_map/ppermute | solution.py:351
  69.2 5.0 %collective-permute-start.14 = (f32[1,2,64,256]{3,2,1,0:T(8,128)S(1)}, f32[1,2,64,256]{3,2,1,0:T(8,128)S(1)}, u32[]{:S(2)}, u32[]{:S(2)}) collective-permute-start(f32[1,2,64,256]{3,2,1,0:T(8,128)S(1)} %add.69.refs_5_), channel_id=1, source_target_pairs={{0,4},{2,6},{4,0},{6,2},{8,12},{10,14},{12,8},{14,10},{1,5},{3,7},... | collective-permute-start | bytes 393224 | tf_op jit(solution)/shard_map/ppermute | solution.py:351
  69.4 14.3 %collective-permute-start.12 = (f32[2,128,512]{2,1,0:T(8,128)S(1)}, f32[2,128,512]{2,1,0:T(8,128)S(1)}, u32[]{:S(2)}, u32[]{:S(2)}) collective-permute-start(f32[2,128,512]{2,1,0:T(8,128)S(1)} %fusion.refs_1_), channel_id=1, source_target_pairs={{0,1},{1,0},{2,3},{3,2},{4,5},{5,4},{6,7},{7,6},{8,9},{9,8},{10,11... | collective-permute-start | bytes 1572872 | tf_op jit(solution)/shard_map/ppermute | solution.py:336
  70.6 6.5 %collective-permute-start.17 = (f32[1,2,64,256]{3,2,1,0:T(8,128)S(1)}, f32[1,2,64,256]{3,2,1,0:T(8,128)S(1)}, u32[]{:S(2)}, u32[]{:S(2)}) collective-permute-start(f32[1,2,64,256]{3,2,1,0:T(8,128)S(1)} %add.70.refs_8_), channel_id=1, source_target_pairs={{0,2},{2,0},{4,6},{6,4},{8,10},{10,8},{12,14},{14,12},{1,3},{3,1},... | collective-permute-start | bytes 393224 | tf_op jit(solution)/shard_map/ppermute | solution.py:351
  74.2 6.9 %collective-permute-start.15 = (f32[2,2,64,256]{3,2,1,0:T(8,128)S(1)}, f32[2,2,64,256]{3,2,1,0:T(8,128)S(1)}, u32[]{:S(2)}, u32[]{:S(2)}) collective-permute-start(f32[2,2,64,256]{3,2,1,0:T(8,128)S(1)} %pad_maximum_fusion.1), channel_id=1, source_target_pairs={{0,2},{2,0},{4,6},{6,4},{8,10},{10,8},{12,14},{14,12},{1,3},{3,1},... | collective-permute-start | bytes 786440 | tf_op jit(solution)/shard_map/ppermute | solution.py:351
  77.1 6.7 %collective-permute-start.18 = (f32[2,2,64,256]{3,2,1,0:T(8,128)S(1)}, f32[2,2,64,256]{3,2,1,0:T(8,128)S(1)}, u32[]{:S(2)}, u32[]{:S(2)}) collective-permute-start(f32[2,2,64,256]{3,2,1,0:T(8,128)S(1)} %pad_maximum_fusion.2), channel_id=1, source_target_pairs={{0,4},{2,6},{4,0},{6,2},{8,12},{10,14},{12,8},{14,10},{1,5},{3,7},... | collective-permute-start | bytes 786440 | tf_op jit(solution)/shard_map/ppermute | solution.py:351
  87.1 3.9 %collective-permute-start.19 = (f32[256,256]{1,0:T(8,128)S(1)}, f32[256,256]{1,0:T(8,128)S(1)}, u32[]{:S(2)}, u32[]{:S(2)}) collective-permute-start(f32[256,256]{1,0:T(8,128)S(1)} %get-tuple-element.53.refs_7_), channel_id=1, source_target_pairs={{0,1},{1,0},{2,3},{3,2},{4,5},{5,4},{6,7},{7,6},{8,9},{9,8},{10,11... | collective-permute-start | bytes 786440 | tf_op jit(solution)/shard_map/ppermute | solution.py:336
  95.1 8.7 %collective-permute-start.21 = (f32[2,2,64,256]{3,2,1,0:T(8,128)S(1)}, f32[2,2,64,256]{3,2,1,0:T(8,128)S(1)}, u32[]{:S(2)}, u32[]{:S(2)}) collective-permute-start(f32[2,2,64,256]{3,2,1,0:T(8,128)S(1)} %slice.100), channel_id=1, source_target_pairs={{0,2},{2,0},{4,6},{6,4},{8,10},{10,8},{12,14},{14,12},{1,3},{3,1},... | collective-permute-start | bytes 786440 | tf_op jit(solution)/shard_map/ppermute | solution.py:351
  99.3 9.2 %collective-permute-start.23 = (f32[2,2,64,256]{3,2,1,0:T(8,128)S(1)}, f32[2,2,64,256]{3,2,1,0:T(8,128)S(1)}, u32[]{:S(2)}, u32[]{:S(2)}) collective-permute-start(f32[2,2,64,256]{3,2,1,0:T(8,128)S(1)} %slice.104), channel_id=1, source_target_pairs={{0,4},{2,6},{4,0},{6,2},{8,12},{10,14},{12,8},{14,10},{1,5},{3,7},... | collective-permute-start | bytes 786440 | tf_op jit(solution)/shard_map/ppermute | solution.py:351
  101.2 12.5 %collective-permute-start.25 = (f32[2,128,512]{2,1,0:T(8,128)S(1)}, f32[2,128,512]{2,1,0:T(8,128)S(1)}, u32[]{:S(2)}, u32[]{:S(2)}) collective-permute-start(f32[2,128,512]{2,1,0:T(8,128)S(1)} %slice_bitcast_fusion), channel_id=1, source_target_pairs={{0,1},{1,0},{2,3},{3,2},{4,5},{5,4},{6,7},{7,6},{8,9},{9,8},{10,11... | collective-permute-start | bytes 1572872 | tf_op jit(solution)/shard_map/ppermute | solution.py:336
  103.8 6.6 %collective-permute-start.22 = (f32[1,2,64,256]{3,2,1,0:T(8,128)S(1)}, f32[1,2,64,256]{3,2,1,0:T(8,128)S(1)}, u32[]{:S(2)}, u32[]{:S(2)}) collective-permute-start(f32[1,2,64,256]{3,2,1,0:T(8,128)S(1)} %slice.120), channel_id=1, source_target_pairs={{0,4},{2,6},{4,0},{6,2},{8,12},{10,14},{12,8},{14,10},{1,5},{3,7},... | collective-permute-start | bytes 393224 | tf_op jit(solution)/shard_map/ppermute | solution.py:351
  108.6 5.0 %collective-permute-start.24 = (f32[1,2,64,256]{3,2,1,0:T(8,128)S(1)}, f32[1,2,64,256]{3,2,1,0:T(8,128)S(1)}, u32[]{:S(2)}, u32[]{:S(2)}) collective-permute-start(f32[1,2,64,256]{3,2,1,0:T(8,128)S(1)} %slice.122), channel_id=1, source_target_pairs={{0,2},{2,0},{4,6},{6,4},{8,10},{10,8},{12,14},{14,12},{1,3},{3,1},... | collective-permute-start | bytes 393224 | tf_op jit(solution)/shard_map/ppermute | solution.py:351
  113.8 10.6 %collective-permute-start.29 = (f32[1,2,64,256]{3,2,1,0:T(8,128)S(1)}, f32[1,2,64,256]{3,2,1,0:T(8,128)S(1)}, u32[]{:S(2)}, u32[]{:S(2)}) collective-permute-start(f32[1,2,64,256]{3,2,1,0:T(8,128)S(1)} %slice_add_fusion.6), channel_id=1, source_target_pairs={{0,8},{2,10},{4,12},{6,14},{8,0},{10,2},{12,4},{14,6},{1,9},{3,11}... | collective-permute-start | bytes 393224 | tf_op jit(solution)/shard_map/ppermute | solution.py:351
  114.4 12.7 %collective-permute-start.32 = (f32[1,2,64,256]{3,2,1,0:T(8,128)S(1)}, f32[1,2,64,256]{3,2,1,0:T(8,128)S(1)}, u32[]{:S(2)}, u32[]{:S(2)}) collective-permute-start(f32[1,2,64,256]{3,2,1,0:T(8,128)S(1)} %slice_add_fusion.5), channel_id=1, source_target_pairs={{0,8},{2,10},{4,12},{6,14},{8,0},{10,2},{12,4},{14,6},{1,9},{3,11}... | collective-permute-start | bytes 393224 | tf_op jit(solution)/shard_map/ppermute | solution.py:351
  116.8 10.7 %collective-permute-start.27 = (f32[2,128,128]{2,1,0:T(8,128)S(1)}, f32[2,128,128]{2,1,0:T(8,128)S(1)}, u32[]{:S(2)}, u32[]{:S(2)}) collective-permute-start(f32[2,128,128]{2,1,0:T(8,128)S(1)} %get-tuple-element.67), channel_id=1, source_target_pairs={{2,0},{4,2},{6,4},{8,6},{10,8},{12,10},{14,12},{3,1},{5,3},{7,5},{... | collective-permute-start | bytes 393224 | tf_op jit(solution)/shard_map/ppermute | solution.py:341
  118.1 9.4 %collective-permute-start.26 = (f32[2,128,128]{2,1,0:T(8,128)S(1)}, f32[2,128,128]{2,1,0:T(8,128)S(1)}, u32[]{:S(2)}, u32[]{:S(2)}) collective-permute-start(f32[2,128,128]{2,1,0:T(8,128)S(1)} %get-tuple-element.66), channel_id=1, source_target_pairs={{0,2},{2,4},{4,6},{6,8},{8,10},{10,12},{12,14},{1,3},{3,5},{5,7},{... | collective-permute-start | bytes 393224 | tf_op jit(solution)/shard_map/ppermute | solution.py:341
  124.4 5.0 %collective-permute-start.30 = (f32[1,2,64,256]{3,2,1,0:T(8,128)S(1)}, f32[1,2,64,256]{3,2,1,0:T(8,128)S(1)}, u32[]{:S(2)}, u32[]{:S(2)}) collective-permute-start(f32[1,2,64,256]{3,2,1,0:T(8,128)S(1)} %add.78.refs_3_), channel_id=1, source_target_pairs={{0,4},{2,6},{4,0},{6,2},{8,12},{10,14},{12,8},{14,10},{1,5},{3,7},... | collective-permute-start | bytes 393224 | tf_op jit(solution)/shard_map/ppermute | solution.py:351
  127.2 6.4 %collective-permute-start.33 = (f32[1,2,64,256]{3,2,1,0:T(8,128)S(1)}, f32[1,2,64,256]{3,2,1,0:T(8,128)S(1)}, u32[]{:S(2)}, u32[]{:S(2)}) collective-permute-start(f32[1,2,64,256]{3,2,1,0:T(8,128)S(1)} %add.79.refs_6_), channel_id=1, source_target_pairs={{0,2},{2,0},{4,6},{6,4},{8,10},{10,8},{12,14},{14,12},{1,3},{3,1},... | collective-permute-start | bytes 393224 | tf_op jit(solution)/shard_map/ppermute | solution.py:351
  127.6 6.1 %collective-permute-start.28 = (f32[2,128,256]{2,1,0:T(8,128)S(1)}, f32[2,128,256]{2,1,0:T(8,128)S(1)}, u32[]{:S(2)}, u32[]{:S(2)}) collective-permute-start(f32[2,128,256]{2,1,0:T(8,128)S(1)} %slice_add_fusion.refs_0_), channel_id=1, source_target_pairs={{0,1},{1,0},{2,3},{3,2},{4,5},{5,4},{6,7},{7,6},{8,9},{9,8},{10,11... | collective-permute-start | bytes 786440 | tf_op jit(solution)/shard_map/ppermute | solution.py:336
  129.5 8.4 %collective-permute-start.31 = (f32[2,2,64,256]{3,2,1,0:T(8,128)S(1)}, f32[2,2,64,256]{3,2,1,0:T(8,128)S(1)}, u32[]{:S(2)}, u32[]{:S(2)}) collective-permute-start(f32[2,2,64,256]{3,2,1,0:T(8,128)S(1)} %pad_maximum_fusion.3), channel_id=1, source_target_pairs={{0,2},{2,0},{4,6},{6,4},{8,10},{10,8},{12,14},{14,12},{1,3},{3,1},... | collective-permute-start | bytes 786440 | tf_op jit(solution)/shard_map/ppermute | solution.py:351
  133.6 6.4 %collective-permute-start.34 = (f32[2,2,64,256]{3,2,1,0:T(8,128)S(1)}, f32[2,2,64,256]{3,2,1,0:T(8,128)S(1)}, u32[]{:S(2)}, u32[]{:S(2)}) collective-permute-start(f32[2,2,64,256]{3,2,1,0:T(8,128)S(1)} %pad_maximum_fusion.4), channel_id=1, source_target_pairs={{0,4},{2,6},{4,0},{6,2},{8,12},{10,14},{12,8},{14,10},{1,5},{3,7},... | collective-permute-start | bytes 786440 | tf_op jit(solution)/shard_map/ppermute | solution.py:351
  (9 other events, 54.1 us)

commit v4 on v3

--- a/solution.py
+++ b/solution.py
@@ -65,11 +65,12 @@
 
 
 def strips(count, body):
-    lax.fori_loop(0, count, lambda i, c: (body(i), c)[1], 0)
+    for i in range(count):
+        body(i)
 
 
 def at(start, length=STRIP):
-    return pl.ds(pl.multiple_of(start, STRIP), length)
+    return pl.ds(start if isinstance(start, int) else pl.multiple_of(start, STRIP), length)
 
 
 def exact(x):
@@ -273,9 +274,9 @@
                     g = pltpu.roll(g, corner(offsets, s, 1, wide - 2 * h, h), 1)
                     window[k] = g if s == 0 else window[k] + g
             start = lower * h + j * STRIP
-            rel = lax.div(start, chunk) ^ key
+            rel = (start // chunk) ^ key
             for k in range(2):
-                probe_grad[rel, k, at(lax.rem(start, chunk)), :] = step[k]
+                probe_grad[rel, k, at(start % chunk), :] = step[k]
                 if last and not tall:
                     grads[lower ^ core, k, at(j * STRIP), :] = window[k]
 

time: 142 us -> 134 us (0.944)
  Pallas kernels: 28.2 us -> 20.1 us
    pallas_call x10, Pallas kernels: 28.2 us -> 20.1 us  [call(): pl.pallas_call(kernel, out_shape=[jax.ShapeDtypeStruct(o, f32) for o in o...]
  transfers between devices with their start and end apart: 35 -> 35, of which waited for: 26 -> 26; matrix products, arithmetic and copies ran while one was open for 1% -> 1% of each run, Pallas kernels for 8% -> 6%
where the time goes in v4:
time: 134 us; the launch traced here: 133 us
  waiting for transfers between devices  65.8 us (49%)
  starting transfers between devices  43.4 us (32%)
  Pallas kernels  20.1 us (15%)
  between operations  1.79 us (1%)
  local copies, waits for them, and re-layouts  1.35 us (1%)
    ppermute x20, waiting for transfers between devices, exchange(): return lax.ppermute(x, 'tile', [(s, s ^ 1 << bit) for s in range(tiles)])  58.5 us
    ppermute x20, starting transfers between devices, exchange(): return lax.ppermute(x, 'tile', [(s, s ^ 1 << bit) for s in range(tiles)])  25.1 us
    pallas_call x10, Pallas kernels, call(): pl.pallas_call(kernel, out_shape=[jax.ShapeDtypeStruct(o, f32) for o in o...  20.1 us
    ppermute x6, starting transfers between devices, shift_cols(): return lax.ppermute(x, 'tile', pairs)  16.7 us
    ppermute x6, waiting for transfers between devices, shift_cols(): return lax.ppermute(x, 'tile', pairs)  4.35 us
    ppermute x9, waiting for transfers between devices, swap_rows(): return lax.ppermute(x, 'row', [(0, 1), (1, 0)])  2.96 us
  transfers between devices with their start and end apart: 35, of which 26 were waited for; matrix products, arithmetic and copies ran while one was open for 1% of the time, Pallas kernels for 6%

profile of v4, /device:TPU:0, one launch (start us, length us, event | category | flops | bytes accessed | tf_op | source)
XLA Modules:
  0.0 133.2 jit_solution(4600585129893454589)
XLA Ops:
  3.2 5.6 %collective-permute-start = (f32[2,128,128]{2,1,0:T(8,128)S(1)}, f32[2,128,128]{2,1,0:T(8,128)S(1)}, u32[]{:S(2)}, u32[]{:S(2)}) collective-permute-start(f32[2,128,128]{2,1,0:T(8,128)S(1)} %get-tuple-element.72), channel_id=1, source_target_pairs={{0,2},{2,4},{4,6},{6,8},{8,10},{10,12},{12,14},{1,3},{3,5},{5,7},{... | collective-permute-start | bytes 393224 | tf_op jit(solution)/shard_map/ppermute | solution.py:342
  10.2 3.0 %collective-permute-done = f32[2,128,128]{2,1,0:T(8,128)S(1)} collective-permute-done((f32[2,128,128]{2,1,0:T(8,128)S(1)}, f32[2,128,128]{2,1,0:T(8,128)S(1)}, u32[]{:S(2)}, u32[]{:S(2)}) %collective-permute-start) | collective-permute-done | bytes 131104 | tf_op jit(solution)/shard_map/ppermute | solution.py:342
  15.2 2.1 %shard_map.87 = (f32[2,2,256,256]{3,2,1,0:T(8,128)S(1)}, f32[256,256]{1,0:T(8,128)S(1)}, f32[2,256,256]{2,1,0:T(8,128)S(1)}) custom-call(s32[2,2]{1,0:T(2,128)S(1)} %copy-done.4, f32[2,128,512]{2,1,0:T(8,128)S(1)} %pad_maximum_fusion.refs_1_, f32[2,128,512]{2,1,0:T(8,128)S(1)} %collective-permute-done.2.refs_2_, f32[2,2,256,256]{3,2,1,0:T(8,128)S(1)} %copy-done.3, ...), custom_call_target="tpu_custom_call" | custom-call | flops 3221225472 | bytes 4980752 | tf_op jit(solution)/shard_map/pallas_call | solution.py:323
  17.3 2.1 %shard_map.88 = (f32[2,2,256,256]{3,2,1,0:T(8,128)S(1)}, f32[256,256]{1,0:T(8,128)S(1)}, f32[2,256,256]{2,1,0:T(8,128)S(1)}) custom-call(s32[2,2]{1,0:T(2,128)S(1)} %copy-done.4, f32[2,128,512]{2,1,0:T(8,128)S(1)} %pad_maximum_fusion.refs_1_, f32[2,128,512]{2,1,0:T(8,128)S(1)} %collective-permute-done.2.refs_2_, f32[2,2,256,256]{3,2,1,0:T(8,128)S(1)} %copy-done.3, ...), custom_call_target="tpu_custom_call" | custom-call | flops 3221225472 | bytes 4980752 | tf_op jit(solution)/shard_map/pallas_call | solution.py:323
  21.3 2.2 %shard_map.89 = (f32[4,2,64,256]{3,2,1,0:T(8,128)S(1)}, f32[2,2,256,256]{3,2,1,0:T(8,128)S(1)}) custom-call(s32[2,2]{1,0:T(2,128)S(1)} %copy-done.4, s32[1]{0:T(128)S(6)} %copy.9.refs_1_, bf16[2,2,2,256,256]{4,3,2,1,0:T(8,128)(2,1)S(1)} %copy-done.5, f32[2,256,256]{2,1,0:T(8,128)S(1)} %shard_map.86.refs_3_, f32[2,2,256,256]{3,2,1,0:T(8,128)S(1)} %copy-done.3, ...), custom_call_target="tpu_custom_call" | custom-call | flops 3221225472 | bytes 8388628 | tf_op jit(solution)/shard_map/pallas_call | solution.py:323
  23.6 2.5 %collective-permute-start.5 = (f32[2,2,64,256]{3,2,1,0:T(8,128)S(1)}, f32[2,2,64,256]{3,2,1,0:T(8,128)S(1)}, u32[]{:S(2)}, u32[]{:S(2)}) collective-permute-start(f32[2,2,64,256]{3,2,1,0:T(8,128)S(1)} %slice.87), channel_id=1, source_target_pairs={{0,2},{2,0},{4,6},{6,4},{8,10},{10,8},{12,14},{14,12},{1,3},{3,1},... | collective-permute-start | bytes 786440 | tf_op jit(solution)/shard_map/ppermute | solution.py:352
  26.2 2.6 %shard_map.90 = (f32[4,2,64,256]{3,2,1,0:T(8,128)S(1)}, f32[2,2,128,512]{3,2,1,0:T(8,128)S(1)}) custom-call(s32[2,2]{1,0:T(2,128)S(1)} %copy-done.4, s32[1]{0:T(128)S(6)} %copy.9.refs_1_, bf16[2,2,2,256,256]{4,3,2,1,0:T(8,128)(2,1)S(1)} %copy-done.5, f32[2,256,256]{2,1,0:T(8,128)S(1)} %shard_map.86.refs_3_, f32[2,2,256,256]{3,2,1,0:T(8,128)S(1)} %copy-done.3, ...), custom_call_target="tpu_custom_call" | custom-call | flops 3221225472 | bytes 9437204 | tf_op jit(solution)/shard_map/pallas_call | solution.py:323
  30.5 2.2 %collective-permute-done.5 = f32[2,2,64,256]{3,2,1,0:T(8,128)S(1)} collective-permute-done((f32[2,2,64,256]{3,2,1,0:T(8,128)S(1)}, f32[2,2,64,256]{3,2,1,0:T(8,128)S(1)}, u32[]{:S(2)}, u32[]{:S(2)}) %collective-permute-start.5) | collective-permute-done | bytes 262176 | tf_op jit(solution)/shard_map/ppermute | solution.py:352
  32.8 2.3 %collective-permute-start.6 = (f32[1,2,64,256]{3,2,1,0:T(8,128)S(1)}, f32[1,2,64,256]{3,2,1,0:T(8,128)S(1)}, u32[]{:S(2)}, u32[]{:S(2)}) collective-permute-start(f32[1,2,64,256]{3,2,1,0:T(8,128)S(1)} %slice.115), channel_id=1, source_target_pairs={{0,4},{2,6},{4,0},{6,2},{8,12},{10,14},{12,8},{14,10},{1,5},{3,7},... | collective-permute-start | bytes 393224 | tf_op jit(solution)/shard_map/ppermute | solution.py:352
  35.1 2.9 %collective-permute-done.7 = f32[2,2,64,256]{3,2,1,0:T(8,128)S(1)} collective-permute-done((f32[2,2,64,256]{3,2,1,0:T(8,128)S(1)}, f32[2,2,64,256]{3,2,1,0:T(8,128)S(1)}, u32[]{:S(2)}, u32[]{:S(2)}) %collective-permute-start.7) | collective-permute-done | bytes 262176 | tf_op jit(solution)/shard_map/ppermute | solution.py:352
  39.7 3.4 %collective-permute-done.8 = f32[1,2,64,256]{3,2,1,0:T(8,128)S(1)} collective-permute-done((f32[1,2,64,256]{3,2,1,0:T(8,128)S(1)}, f32[1,2,64,256]{3,2,1,0:T(8,128)S(1)}, u32[]{:S(2)}, u32[]{:S(2)}) %collective-permute-start.8) | collective-permute-done | bytes 131104 | tf_op jit(solution)/shard_map/ppermute | solution.py:352
  43.3 2.4 %collective-permute-start.10 = (f32[2,128,256]{2,1,0:T(8,128)S(1)}, f32[2,128,256]{2,1,0:T(8,128)S(1)}, u32[]{:S(2)}, u32[]{:S(2)}) collective-permute-start(f32[2,128,256]{2,1,0:T(8,128)S(1)} %get-tuple-element.70), channel_id=1, source_target_pairs={{0,2},{2,4},{4,6},{6,8},{8,10},{10,12},{12,14},{1,3},{3,5},{5,7},{... | collective-permute-start | bytes 786440 | tf_op jit(solution)/shard_map/ppermute | solution.py:342
  47.1 5.7 %collective-permute-start.13 = (f32[1,2,64,256]{3,2,1,0:T(8,128)S(1)}, f32[1,2,64,256]{3,2,1,0:T(8,128)S(1)}, u32[]{:S(2)}, u32[]{:S(2)}) collective-permute-start(f32[1,2,64,256]{3,2,1,0:T(8,128)S(1)} %slice_add_fusion.8), channel_id=1, source_target_pairs={{0,8},{2,10},{4,12},{6,14},{8,0},{10,2},{12,4},{14,6},{1,9},{3,11}... | collective-permute-start | bytes 393224 | tf_op jit(solution)/shard_map/ppermute | solution.py:352
  53.0 12.2 %collective-permute-done.13 = f32[1,2,64,256]{3,2,1,0:T(8,128)S(1)} collective-permute-done((f32[1,2,64,256]{3,2,1,0:T(8,128)S(1)}, f32[1,2,64,256]{3,2,1,0:T(8,128)S(1)}, u32[]{:S(2)}, u32[]{:S(2)}) %collective-permute-start.13) | collective-permute-done | bytes 131104 | tf_op jit(solution)/shard_map/ppermute | solution.py:352
  66.6 3.5 %collective-permute-done.14.refs_6_ = f32[1,2,64,256]{3,2,1,0:T(8,128)S(1)} collective-permute-done((f32[1,2,64,256]{3,2,1,0:T(8,128)S(1)}, f32[1,2,64,256]{3,2,1,0:T(8,128)S(1)}, u32[]{:S(2)}, u32[]{:S(2)}) %collective-permute-start.14) | collective-permute-done | bytes 131104 | tf_op jit(solution)/shard_map/ppermute | solution.py:352
  70.3 2.8 %collective-permute-done.17.refs_9_ = f32[1,2,64,256]{3,2,1,0:T(8,128)S(1)} collective-permute-done((f32[1,2,64,256]{3,2,1,0:T(8,128)S(1)}, f32[1,2,64,256]{3,2,1,0:T(8,128)S(1)}, u32[]{:S(2)}, u32[]{:S(2)}) %collective-permute-start.17) | collective-permute-done | bytes 131104 | tf_op jit(solution)/shard_map/ppermute | solution.py:352
  74.0 3.1 %collective-permute-done.15.refs_7_ = f32[2,2,64,256]{3,2,1,0:T(8,128)S(1)} collective-permute-done((f32[2,2,64,256]{3,2,1,0:T(8,128)S(1)}, f32[2,2,64,256]{3,2,1,0:T(8,128)S(1)}, u32[]{:S(2)}, u32[]{:S(2)}) %collective-permute-start.15) | collective-permute-done | bytes 262176 | tf_op jit(solution)/shard_map/ppermute | solution.py:352
  77.1 2.6 %collective-permute-done.18.refs_10_ = f32[2,2,64,256]{3,2,1,0:T(8,128)S(1)} collective-permute-done((f32[2,2,64,256]{3,2,1,0:T(8,128)S(1)}, f32[2,2,64,256]{3,2,1,0:T(8,128)S(1)}, u32[]{:S(2)}, u32[]{:S(2)}) %collective-permute-start.18) | collective-permute-done | bytes 262176 | tf_op jit(solution)/shard_map/ppermute | solution.py:352
  79.7 2.1 %shard_map.91 = (f32[2,2,256,256]{3,2,1,0:T(8,128)S(1)}, f32[256,256]{1,0:T(8,128)S(1)}, f32[2,256,256]{2,1,0:T(8,128)S(1)}, f32[2,2,256,256]{3,2,1,0:T(8,128)S(1)}) custom-call(s32[2,2]{1,0:T(2,128)S(1)} %copy-done.4, f32[2,128,512]{2,1,0:T(8,128)S(1)} %fusion.refs_1_, f32[2,128,512]{2,1,0:T(8,128)S(1)} %collective-permute-done.12.refs_2_, ...), custom_call_target="tpu_custom_call" | custom-call | flops 3221225472 | bytes 7077904 | tf_op jit(solution)/shard_map/pallas_call | solution.py:323
  81.9 2.1 %shard_map.92 = (f32[2,2,256,256]{3,2,1,0:T(8,128)S(1)}, f32[256,256]{1,0:T(8,128)S(1)}, f32[2,256,256]{2,1,0:T(8,128)S(1)}) custom-call(s32[2,2]{1,0:T(2,128)S(1)} %copy-done.4, f32[2,128,512]{2,1,0:T(8,128)S(1)} %fusion.refs_1_, f32[2,128,512]{2,1,0:T(8,128)S(1)} %collective-permute-done.12.refs_2_, ...), custom_call_target="tpu_custom_call" | custom-call | flops 3221225472 | bytes 4980752 | tf_op jit(solution)/shard_map/pallas_call | solution.py:323
  85.7 2.3 %shard_map.93 = (f32[4,2,64,256]{3,2,1,0:T(8,128)S(1)}, f32[2,2,256,256]{3,2,1,0:T(8,128)S(1)}) custom-call(s32[2,2]{1,0:T(2,128)S(1)} %copy-done.4, s32[1]{0:T(128)S(6)} %copy.9.refs_1_, bf16[2,2,2,256,256]{4,3,2,1,0:T(8,128)(2,1)S(1)} %copy-done.5, f32[2,256,256]{2,1,0:T(8,128)S(1)} %shard_map.86.refs_3_, ...), custom_call_target="tpu_custom_call" | custom-call | flops 3221225472 | bytes 8388628 | tf_op jit(solution)/shard_map/pallas_call | solution.py:323
  88.6 2.6 %shard_map.94 = (f32[4,2,64,256]{3,2,1,0:T(8,128)S(1)}, f32[2,2,128,512]{3,2,1,0:T(8,128)S(1)}) custom-call(s32[2,2]{1,0:T(2,128)S(1)} %copy-done.4, s32[1]{0:T(128)S(6)} %copy.9.refs_1_, bf16[2,2,2,256,256]{4,3,2,1,0:T(8,128)(2,1)S(1)} %copy-done.5, f32[2,256,256]{2,1,0:T(8,128)S(1)} %shard_map.86.refs_3_, ...), custom_call_target="tpu_custom_call" | custom-call | flops 3221225472 | bytes 9437204 | tf_op jit(solution)/shard_map/pallas_call | solution.py:323
  93.2 3.5 %collective-permute-done.21 = f32[2,2,64,256]{3,2,1,0:T(8,128)S(1)} collective-permute-done((f32[2,2,64,256]{3,2,1,0:T(8,128)S(1)}, f32[2,2,64,256]{3,2,1,0:T(8,128)S(1)}, u32[]{:S(2)}, u32[]{:S(2)}) %collective-permute-start.21) | collective-permute-done | bytes 262176 | tf_op jit(solution)/shard_map/ppermute | solution.py:352
  100.2 1.9 %collective-permute-start.24 = (f32[1,2,64,256]{3,2,1,0:T(8,128)S(1)}, f32[1,2,64,256]{3,2,1,0:T(8,128)S(1)}, u32[]{:S(2)}, u32[]{:S(2)}) collective-permute-start(f32[1,2,64,256]{3,2,1,0:T(8,128)S(1)} %slice.122), channel_id=1, source_target_pairs={{0,2},{2,0},{4,6},{6,4},{8,10},{10,8},{12,14},{14,12},{1,3},{3,1},... | collective-permute-start | bytes 393224 | tf_op jit(solution)/shard_map/ppermute | solution.py:352
  102.4 2.8 %collective-permute-done.24 = f32[1,2,64,256]{3,2,1,0:T(8,128)S(1)} collective-permute-done((f32[1,2,64,256]{3,2,1,0:T(8,128)S(1)}, f32[1,2,64,256]{3,2,1,0:T(8,128)S(1)}, u32[]{:S(2)}, u32[]{:S(2)}) %collective-permute-start.24) | collective-permute-done | bytes 131104 | tf_op jit(solution)/shard_map/ppermute | solution.py:352
  106.5 1.9 %collective-permute-start.32 = (f32[1,2,64,256]{3,2,1,0:T(8,128)S(1)}, f32[1,2,64,256]{3,2,1,0:T(8,128)S(1)}, u32[]{:S(2)}, u32[]{:S(2)}) collective-permute-start(f32[1,2,64,256]{3,2,1,0:T(8,128)S(1)} %slice_add_fusion.5), channel_id=1, source_target_pairs={{0,8},{2,10},{4,12},{6,14},{8,0},{10,2},{12,4},{14,6},{1,9},{3,11}... | collective-permute-start | bytes 393224 | tf_op jit(solution)/shard_map/ppermute | solution.py:352
  109.7 4.6 %collective-permute-start.26 = (f32[2,128,128]{2,1,0:T(8,128)S(1)}, f32[2,128,128]{2,1,0:T(8,128)S(1)}, u32[]{:S(2)}, u32[]{:S(2)}) collective-permute-start(f32[2,128,128]{2,1,0:T(8,128)S(1)} %get-tuple-element.66), channel_id=1, source_target_pairs={{0,2},{2,4},{4,6},{6,8},{8,10},{10,12},{12,14},{1,3},{3,5},{5,7},{... | collective-permute-start | bytes 393224 | tf_op jit(solution)/shard_map/ppermute | solution.py:342
  114.3 2.0 %collective-permute-done.29 = f32[1,2,64,256]{3,2,1,0:T(8,128)S(1)} collective-permute-done((f32[1,2,64,256]{3,2,1,0:T(8,128)S(1)}, f32[1,2,64,256]{3,2,1,0:T(8,128)S(1)}, u32[]{:S(2)}, u32[]{:S(2)}) %collective-permute-start.29) | collective-permute-done | bytes 131104 | tf_op jit(solution)/shard_map/ppermute | solution.py:352
  116.4 2.7 %collective-permute-done.32 = f32[1,2,64,256]{3,2,1,0:T(8,128)S(1)} collective-permute-done((f32[1,2,64,256]{3,2,1,0:T(8,128)S(1)}, f32[1,2,64,256]{3,2,1,0:T(8,128)S(1)}, u32[]{:S(2)}, u32[]{:S(2)}) %collective-permute-start.32) | collective-permute-done | bytes 131104 | tf_op jit(solution)/shard_map/ppermute | solution.py:352
  123.0 2.5 %collective-permute-done.33.refs_7_ = f32[1,2,64,256]{3,2,1,0:T(8,128)S(1)} collective-permute-done((f32[1,2,64,256]{3,2,1,0:T(8,128)S(1)}, f32[1,2,64,256]{3,2,1,0:T(8,128)S(1)}, u32[]{:S(2)}, u32[]{:S(2)}) %collective-permute-start.33) | collective-permute-done | bytes 131104 | tf_op jit(solution)/shard_map/ppermute | solution.py:352
  125.6 4.2 %collective-permute-done.31.refs_5_ = f32[2,2,64,256]{3,2,1,0:T(8,128)S(1)} collective-permute-done((f32[2,2,64,256]{3,2,1,0:T(8,128)S(1)}, f32[2,2,64,256]{3,2,1,0:T(8,128)S(1)}, u32[]{:S(2)}, u32[]{:S(2)}) %collective-permute-start.31) | collective-permute-done | bytes 262176 | tf_op jit(solution)/shard_map/ppermute | solution.py:352
  129.7 2.2 %collective-permute-done.34.refs_8_ = f32[2,2,64,256]{3,2,1,0:T(8,128)S(1)} collective-permute-done((f32[2,2,64,256]{3,2,1,0:T(8,128)S(1)}, f32[2,2,64,256]{3,2,1,0:T(8,128)S(1)}, u32[]{:S(2)}, u32[]{:S(2)}) %collective-permute-start.34) | collective-permute-done | bytes 262176 | tf_op jit(solution)/shard_map/ppermute | solution.py:352
  (96 shorter events, 30.9 us)
Async XLA Ops:
  1.7 8.5 %collective-permute-start.1 = (f32[2,128,128]{2,1,0:T(8,128)S(1)}, f32[2,128,128]{2,1,0:T(8,128)S(1)}, u32[]{:S(2)}, u32[]{:S(2)}) collective-permute-start(f32[2,128,128]{2,1,0:T(8,128)S(1)} %get-tuple-element.73), channel_id=1, source_target_pairs={{2,0},{4,2},{6,4},{8,6},{10,8},{12,10},{14,12},{3,1},{5,3},{7,5},{... | collective-permute-start | bytes 393224 | tf_op jit(solution)/shard_map/ppermute | solution.py:342
  3.2 10.0 %collective-permute-start = (f32[2,128,128]{2,1,0:T(8,128)S(1)}, f32[2,128,128]{2,1,0:T(8,128)S(1)}, u32[]{:S(2)}, u32[]{:S(2)}) collective-permute-start(f32[2,128,128]{2,1,0:T(8,128)S(1)} %get-tuple-element.72), channel_id=1, source_target_pairs={{0,2},{2,4},{4,6},{6,8},{8,10},{10,12},{12,14},{1,3},{3,5},{5,7},{... | collective-permute-start | bytes 393224 | tf_op jit(solution)/shard_map/ppermute | solution.py:342
  13.2 2.0 %collective-permute-start.2 = (f32[2,128,512]{2,1,0:T(8,128)S(1)}, f32[2,128,512]{2,1,0:T(8,128)S(1)}, u32[]{:S(2)}, u32[]{:S(2)}) collective-permute-start(f32[2,128,512]{2,1,0:T(8,128)S(1)} %pad_maximum_fusion.refs_1_), channel_id=1, source_target_pairs={{0,1},{1,0},{2,3},{3,2},{4,5},{5,4},{6,7},{7,6},{8,9},{9,8},{10,11... | collective-permute-start | bytes 1572872 | tf_op jit(solution)/shard_map/ppermute | solution.py:337
  23.6 9.2 %collective-permute-start.5 = (f32[2,2,64,256]{3,2,1,0:T(8,128)S(1)}, f32[2,2,64,256]{3,2,1,0:T(8,128)S(1)}, u32[]{:S(2)}, u32[]{:S(2)}) collective-permute-start(f32[2,2,64,256]{3,2,1,0:T(8,128)S(1)} %slice.87), channel_id=1, source_target_pairs={{0,2},{2,0},{4,6},{6,4},{8,10},{10,8},{12,14},{14,12},{1,3},{3,1},... | collective-permute-start | bytes 786440 | tf_op jit(solution)/shard_map/ppermute | solution.py:352
  28.8 9.3 %collective-permute-start.7 = (f32[2,2,64,256]{3,2,1,0:T(8,128)S(1)}, f32[2,2,64,256]{3,2,1,0:T(8,128)S(1)}, u32[]{:S(2)}, u32[]{:S(2)}) collective-permute-start(f32[2,2,64,256]{3,2,1,0:T(8,128)S(1)} %slice.91), channel_id=1, source_target_pairs={{0,4},{2,6},{4,0},{6,2},{8,12},{10,14},{12,8},{14,10},{1,5},{3,7},... | collective-permute-start | bytes 786440 | tf_op jit(solution)/shard_map/ppermute | solution.py:352
  30.5 12.7 %collective-permute-start.9 = (f32[2,128,512]{2,1,0:T(8,128)S(1)}, f32[2,128,512]{2,1,0:T(8,128)S(1)}, u32[]{:S(2)}, u32[]{:S(2)}) collective-permute-start(f32[2,128,512]{2,1,0:T(8,128)S(1)} %slice_bitcast_fusion.1), channel_id=1, source_target_pairs={{0,1},{1,0},{2,3},{3,2},{4,5},{5,4},{6,7},{7,6},{8,9},{9,8},{10,11... | collective-permute-start | bytes 1572872 | tf_op jit(solution)/shard_map/ppermute | solution.py:337
  32.8 6.9 %collective-permute-start.6 = (f32[1,2,64,256]{3,2,1,0:T(8,128)S(1)}, f32[1,2,64,256]{3,2,1,0:T(8,128)S(1)}, u32[]{:S(2)}, u32[]{:S(2)}) collective-permute-start(f32[1,2,64,256]{3,2,1,0:T(8,128)S(1)} %slice.115), channel_id=1, source_target_pairs={{0,4},{2,6},{4,0},{6,2},{8,12},{10,14},{12,8},{14,10},{1,5},{3,7},... | collective-permute-start | bytes 393224 | tf_op jit(solution)/shard_map/ppermute | solution.py:352
  38.1 5.0 %collective-permute-start.8 = (f32[1,2,64,256]{3,2,1,0:T(8,128)S(1)}, f32[1,2,64,256]{3,2,1,0:T(8,128)S(1)}, u32[]{:S(2)}, u32[]{:S(2)}) collective-permute-start(f32[1,2,64,256]{3,2,1,0:T(8,128)S(1)} %slice.117), channel_id=1, source_target_pairs={{0,2},{2,0},{4,6},{6,4},{8,10},{10,8},{12,14},{14,12},{1,3},{3,1},... | collective-permute-start | bytes 393224 | tf_op jit(solution)/shard_map/ppermute | solution.py:352
  43.3 21.9 %collective-permute-start.10 = (f32[2,128,256]{2,1,0:T(8,128)S(1)}, f32[2,128,256]{2,1,0:T(8,128)S(1)}, u32[]{:S(2)}, u32[]{:S(2)}) collective-permute-start(f32[2,128,256]{2,1,0:T(8,128)S(1)} %get-tuple-element.70), channel_id=1, source_target_pairs={{0,2},{2,4},{4,6},{6,8},{8,10},{10,12},{12,14},{1,3},{3,5},{5,7},{... | collective-permute-start | bytes 786440 | tf_op jit(solution)/shard_map/ppermute | solution.py:342
  45.7 19.6 %collective-permute-start.11 = (f32[2,128,256]{2,1,0:T(8,128)S(1)}, f32[2,128,256]{2,1,0:T(8,128)S(1)}, u32[]{:S(2)}, u32[]{:S(2)}) collective-permute-start(f32[2,128,256]{2,1,0:T(8,128)S(1)} %get-tuple-element.71), channel_id=1, source_target_pairs={{2,0},{4,2},{6,4},{8,6},{10,8},{12,10},{14,12},{3,1},{5,3},{7,5},{... | collective-permute-start | bytes 786440 | tf_op jit(solution)/shard_map/ppermute | solution.py:342
  47.1 18.0 %collective-permute-start.13 = (f32[1,2,64,256]{3,2,1,0:T(8,128)S(1)}, f32[1,2,64,256]{3,2,1,0:T(8,128)S(1)}, u32[]{:S(2)}, u32[]{:S(2)}) collective-permute-start(f32[1,2,64,256]{3,2,1,0:T(8,128)S(1)} %slice_add_fusion.8), channel_id=1, source_target_pairs={{0,8},{2,10},{4,12},{6,14},{8,0},{10,2},{12,4},{14,6},{1,9},{3,11}... | collective-permute-start | bytes 393224 | tf_op jit(solution)/shard_map/ppermute | solution.py:352
  52.9 13.6 %collective-permute-start.16 = (f32[1,2,64,256]{3,2,1,0:T(8,128)S(1)}, f32[1,2,64,256]{3,2,1,0:T(8,128)S(1)}, u32[]{:S(2)}, u32[]{:S(2)}) collective-permute-start(f32[1,2,64,256]{3,2,1,0:T(8,128)S(1)} %slice_add_fusion.7), channel_id=1, source_target_pairs={{0,8},{2,10},{4,12},{6,14},{8,0},{10,2},{12,4},{14,6},{1,9},{3,11}... | collective-permute-start | bytes 393224 | tf_op jit(solution)/shard_map/ppermute | solution.py:352
  65.1 5.0 %collective-permute-start.14 = (f32[1,2,64,256]{3,2,1,0:T(8,128)S(1)}, f32[1,2,64,256]{3,2,1,0:T(8,128)S(1)}, u32[]{:S(2)}, u32[]{:S(2)}) collective-permute-start(f32[1,2,64,256]{3,2,1,0:T(8,128)S(1)} %add.69.refs_5_), channel_id=1, source_target_pairs={{0,4},{2,6},{4,0},{6,2},{8,12},{10,14},{12,8},{14,10},{1,5},{3,7},... | collective-permute-start | bytes 393224 | tf_op jit(solution)/shard_map/ppermute | solution.py:352
  65.4 14.3 %collective-permute-start.12 = (f32[2,128,512]{2,1,0:T(8,128)S(1)}, f32[2,128,512]{2,1,0:T(8,128)S(1)}, u32[]{:S(2)}, u32[]{:S(2)}) collective-permute-start(f32[2,128,512]{2,1,0:T(8,128)S(1)} %fusion.refs_1_), channel_id=1, source_target_pairs={{0,1},{1,0},{2,3},{3,2},{4,5},{5,4},{6,7},{7,6},{8,9},{9,8},{10,11... | collective-permute-start | bytes 1572872 | tf_op jit(solution)/shard_map/ppermute | solution.py:337
  66.5 6.5 %collective-permute-start.17 = (f32[1,2,64,256]{3,2,1,0:T(8,128)S(1)}, f32[1,2,64,256]{3,2,1,0:T(8,128)S(1)}, u32[]{:S(2)}, u32[]{:S(2)}) collective-permute-start(f32[1,2,64,256]{3,2,1,0:T(8,128)S(1)} %add.70.refs_8_), channel_id=1, source_target_pairs={{0,2},{2,0},{4,6},{6,4},{8,10},{10,8},{12,14},{14,12},{1,3},{3,1},... | collective-permute-start | bytes 393224 | tf_op jit(solution)/shard_map/ppermute | solution.py:352
  70.2 6.9 %collective-permute-start.15 = (f32[2,2,64,256]{3,2,1,0:T(8,128)S(1)}, f32[2,2,64,256]{3,2,1,0:T(8,128)S(1)}, u32[]{:S(2)}, u32[]{:S(2)}) collective-permute-start(f32[2,2,64,256]{3,2,1,0:T(8,128)S(1)} %pad_maximum_fusion.1), channel_id=1, source_target_pairs={{0,2},{2,0},{4,6},{6,4},{8,10},{10,8},{12,14},{14,12},{1,3},{3,1},... | collective-permute-start | bytes 786440 | tf_op jit(solution)/shard_map/ppermute | solution.py:352
  73.1 6.7 %collective-permute-start.18 = (f32[2,2,64,256]{3,2,1,0:T(8,128)S(1)}, f32[2,2,64,256]{3,2,1,0:T(8,128)S(1)}, u32[]{:S(2)}, u32[]{:S(2)}) collective-permute-start(f32[2,2,64,256]{3,2,1,0:T(8,128)S(1)} %pad_maximum_fusion.2), channel_id=1, source_target_pairs={{0,4},{2,6},{4,0},{6,2},{8,12},{10,14},{12,8},{14,10},{1,5},{3,7},... | collective-permute-start | bytes 786440 | tf_op jit(solution)/shard_map/ppermute | solution.py:352
  81.9 2.7 %collective-permute-start.19 = (f32[256,256]{1,0:T(8,128)S(1)}, f32[256,256]{1,0:T(8,128)S(1)}, u32[]{:S(2)}, u32[]{:S(2)}) collective-permute-start(f32[256,256]{1,0:T(8,128)S(1)} %get-tuple-element.53.refs_7_), channel_id=1, source_target_pairs={{0,1},{1,0},{2,3},{3,2},{4,5},{5,4},{6,7},{7,6},{8,9},{9,8},{10,11... | collective-permute-start | bytes 786440 | tf_op jit(solution)/shard_map/ppermute | solution.py:337
  88.0 8.7 %collective-permute-start.21 = (f32[2,2,64,256]{3,2,1,0:T(8,128)S(1)}, f32[2,2,64,256]{3,2,1,0:T(8,128)S(1)}, u32[]{:S(2)}, u32[]{:S(2)}) collective-permute-start(f32[2,2,64,256]{3,2,1,0:T(8,128)S(1)} %slice.100), channel_id=1, source_target_pairs={{0,2},{2,0},{4,6},{6,4},{8,10},{10,8},{12,14},{14,12},{1,3},{3,1},... | collective-permute-start | bytes 786440 | tf_op jit(solution)/shard_map/ppermute | solution.py:352
  91.2 8.9 %collective-permute-start.23 = (f32[2,2,64,256]{3,2,1,0:T(8,128)S(1)}, f32[2,2,64,256]{3,2,1,0:T(8,128)S(1)}, u32[]{:S(2)}, u32[]{:S(2)}) collective-permute-start(f32[2,2,64,256]{3,2,1,0:T(8,128)S(1)} %slice.104), channel_id=1, source_target_pairs={{0,4},{2,6},{4,0},{6,2},{8,12},{10,14},{12,8},{14,10},{1,5},{3,7},... | collective-permute-start | bytes 786440 | tf_op jit(solution)/shard_map/ppermute | solution.py:352
  93.1 12.2 %collective-permute-start.25 = (f32[2,128,512]{2,1,0:T(8,128)S(1)}, f32[2,128,512]{2,1,0:T(8,128)S(1)}, u32[]{:S(2)}, u32[]{:S(2)}) collective-permute-start(f32[2,128,512]{2,1,0:T(8,128)S(1)} %slice_bitcast_fusion), channel_id=1, source_target_pairs={{0,1},{1,0},{2,3},{3,2},{4,5},{5,4},{6,7},{7,6},{8,9},{9,8},{10,11... | collective-permute-start | bytes 1572872 | tf_op jit(solution)/shard_map/ppermute | solution.py:337
  96.7 5.6 %collective-permute-start.22 = (f32[1,2,64,256]{3,2,1,0:T(8,128)S(1)}, f32[1,2,64,256]{3,2,1,0:T(8,128)S(1)}, u32[]{:S(2)}, u32[]{:S(2)}) collective-permute-start(f32[1,2,64,256]{3,2,1,0:T(8,128)S(1)} %slice.120), channel_id=1, source_target_pairs={{0,4},{2,6},{4,0},{6,2},{8,12},{10,14},{12,8},{14,10},{1,5},{3,7},... | collective-permute-start | bytes 393224 | tf_op jit(solution)/shard_map/ppermute | solution.py:352
  100.2 5.0 %collective-permute-start.24 = (f32[1,2,64,256]{3,2,1,0:T(8,128)S(1)}, f32[1,2,64,256]{3,2,1,0:T(8,128)S(1)}, u32[]{:S(2)}, u32[]{:S(2)}) collective-permute-start(f32[1,2,64,256]{3,2,1,0:T(8,128)S(1)} %slice.122), channel_id=1, source_target_pairs={{0,2},{2,0},{4,6},{6,4},{8,10},{10,8},{12,14},{14,12},{1,3},{3,1},... | collective-permute-start | bytes 393224 | tf_op jit(solution)/shard_map/ppermute | solution.py:352
  105.3 11.0 %collective-permute-start.29 = (f32[1,2,64,256]{3,2,1,0:T(8,128)S(1)}, f32[1,2,64,256]{3,2,1,0:T(8,128)S(1)}, u32[]{:S(2)}, u32[]{:S(2)}) collective-permute-start(f32[1,2,64,256]{3,2,1,0:T(8,128)S(1)} %slice_add_fusion.6), channel_id=1, source_target_pairs={{0,8},{2,10},{4,12},{6,14},{8,0},{10,2},{12,4},{14,6},{1,9},{3,11}... | collective-permute-start | bytes 393224 | tf_op jit(solution)/shard_map/ppermute | solution.py:352
  106.5 12.6 %collective-permute-start.32 = (f32[1,2,64,256]{3,2,1,0:T(8,128)S(1)}, f32[1,2,64,256]{3,2,1,0:T(8,128)S(1)}, u32[]{:S(2)}, u32[]{:S(2)}) collective-permute-start(f32[1,2,64,256]{3,2,1,0:T(8,128)S(1)} %slice_add_fusion.5), channel_id=1, source_target_pairs={{0,8},{2,10},{4,12},{6,14},{8,0},{10,2},{12,4},{14,6},{1,9},{3,11}... | collective-permute-start | bytes 393224 | tf_op jit(solution)/shard_map/ppermute | solution.py:352
  108.4 11.0 %collective-permute-start.27 = (f32[2,128,128]{2,1,0:T(8,128)S(1)}, f32[2,128,128]{2,1,0:T(8,128)S(1)}, u32[]{:S(2)}, u32[]{:S(2)}) collective-permute-start(f32[2,128,128]{2,1,0:T(8,128)S(1)} %get-tuple-element.67), channel_id=1, source_target_pairs={{2,0},{4,2},{6,4},{8,6},{10,8},{12,10},{14,12},{3,1},{5,3},{7,5},{... | collective-permute-start | bytes 393224 | tf_op jit(solution)/shard_map/ppermute | solution.py:342
  109.7 9.7 %collective-permute-start.26 = (f32[2,128,128]{2,1,0:T(8,128)S(1)}, f32[2,128,128]{2,1,0:T(8,128)S(1)}, u32[]{:S(2)}, u32[]{:S(2)}) collective-permute-start(f32[2,128,128]{2,1,0:T(8,128)S(1)} %get-tuple-element.66), channel_id=1, source_target_pairs={{0,2},{2,4},{4,6},{6,8},{8,10},{10,12},{12,14},{1,3},{3,5},{5,7},{... | collective-permute-start | bytes 393224 | tf_op jit(solution)/shard_map/ppermute | solution.py:342
  116.3 5.0 %collective-permute-start.30 = (f32[1,2,64,256]{3,2,1,0:T(8,128)S(1)}, f32[1,2,64,256]{3,2,1,0:T(8,128)S(1)}, u32[]{:S(2)}, u32[]{:S(2)}) collective-permute-start(f32[1,2,64,256]{3,2,1,0:T(8,128)S(1)} %add.78.refs_3_), channel_id=1, source_target_pairs={{0,4},{2,6},{4,0},{6,2},{8,12},{10,14},{12,8},{14,10},{1,5},{3,7},... | collective-permute-start | bytes 393224 | tf_op jit(solution)/shard_map/ppermute | solution.py:352
  119.1 6.4 %collective-permute-start.33 = (f32[1,2,64,256]{3,2,1,0:T(8,128)S(1)}, f32[1,2,64,256]{3,2,1,0:T(8,128)S(1)}, u32[]{:S(2)}, u32[]{:S(2)}) collective-permute-start(f32[1,2,64,256]{3,2,1,0:T(8,128)S(1)} %add.79.refs_6_), channel_id=1, source_target_pairs={{0,2},{2,0},{4,6},{6,4},{8,10},{10,8},{12,14},{14,12},{1,3},{3,1},... | collective-permute-start | bytes 393224 | tf_op jit(solution)/shard_map/ppermute | solution.py:352
  119.5 6.1 %collective-permute-start.28 = (f32[2,128,256]{2,1,0:T(8,128)S(1)}, f32[2,128,256]{2,1,0:T(8,128)S(1)}, u32[]{:S(2)}, u32[]{:S(2)}) collective-permute-start(f32[2,128,256]{2,1,0:T(8,128)S(1)} %slice_add_fusion.refs_0_), channel_id=1, source_target_pairs={{0,1},{1,0},{2,3},{3,2},{4,5},{5,4},{6,7},{7,6},{8,9},{9,8},{10,11... | collective-permute-start | bytes 786440 | tf_op jit(solution)/shard_map/ppermute | solution.py:337
  121.4 8.4 %collective-permute-start.31 = (f32[2,2,64,256]{3,2,1,0:T(8,128)S(1)}, f32[2,2,64,256]{3,2,1,0:T(8,128)S(1)}, u32[]{:S(2)}, u32[]{:S(2)}) collective-permute-start(f32[2,2,64,256]{3,2,1,0:T(8,128)S(1)} %pad_maximum_fusion.3), channel_id=1, source_target_pairs={{0,2},{2,0},{4,6},{6,4},{8,10},{10,8},{12,14},{14,12},{1,3},{3,1},... | collective-permute-start | bytes 786440 | tf_op jit(solution)/shard_map/ppermute | solution.py:352
  125.5 6.4 %collective-permute-start.34 = (f32[2,2,64,256]{3,2,1,0:T(8,128)S(1)}, f32[2,2,64,256]{3,2,1,0:T(8,128)S(1)}, u32[]{:S(2)}, u32[]{:S(2)}) collective-permute-start(f32[2,2,64,256]{3,2,1,0:T(8,128)S(1)} %pad_maximum_fusion.4), channel_id=1, source_target_pairs={{0,4},{2,6},{4,0},{6,2},{8,12},{10,14},{12,8},{14,10},{1,5},{3,7},... | collective-permute-start | bytes 786440 | tf_op jit(solution)/shard_map/ppermute | solution.py:352
  (9 other events, 54.1 us)

commit v5 on v4

--- a/solution.py
+++ b/solution.py
@@ -99,38 +99,52 @@
     return offsets[slot, dim] - along * size + margin
 
 
-def update_probe(old, pieces, coef, out):
+def left_half():
+    return 1 - lax.rem(lax.axis_index("tile"), 2)
+
+
+def update_probe(old, streams, coef, out):
     rows = old.shape[2] // CHUNKS
-    for mode in range(len(pieces)):
-        key = chunk_key(ORDERS[mode])
+    for i, pieces in enumerate(streams):
+        mode, part = divmod(i, 2)
+        key = chunk_key(ORDERS[part])
         rel = 0
-        for piece in pieces[mode]:
+        for piece in pieces:
             for k in range(piece.shape[0]):
                 here = pl.ds(pl.multiple_of((rel ^ key) * rows, rows), rows)
-                out[mode, :, here, :] = old[mode, :, here, :] + coef * piece[k]
+                out[mode, part, here, :] = old[mode, part, here, :] + coef * piece[k]
                 rel += 1
+
+
+def grouped(refs, streams, per_stream):
+    return [refs[i * per_stream : (i + 1) * per_stream] for i in range(streams)]
 
 
 def shift_in(offsets, slot, near, away, patch, tall):
     frame = patch.shape[-1]
     h = frame // 2
-    cols, hr = near.shape[-1], near.shape[1]
+    hr, cols = near.shape[2], 2 * near.shape[3]
     size = cols - 2 * h
     core = lax.axis_index("row")
+    first = left_half()
     across = lax.rem(cols - corner(offsets, slot, 1, size, h), cols)
+
+    def strip(ref, c, rows):
+        x = jnp.concatenate([ref[first, c, rows, :], ref[1 - first, c, rows, :]], 1)
+        return pltpu.roll(x, across, 1)[:, :frame]
+
     if tall:
         down = lax.rem(2 * hr - corner(offsets, slot, 0, size, h), 2 * hr)
         for c in range(2):
-            both = [jnp.where(core == k, near[c], away[c]) for k in range(2)]
-            moved = pltpu.roll(jnp.concatenate(both, 0), across, 1)[:, :frame]
-            patch[c] = pltpu.roll(moved, down, 0)[:frame]
+            halves = [strip(ref, c, slice(None)) for ref in (near, away)]
+            both = [jnp.where(core == k, halves[0], halves[1]) for k in range(2)]
+            patch[c] = pltpu.roll(jnp.concatenate(both, 0), down, 0)[:frame]
         return
 
     def body(j):
         for ref, half in ((near, core), (away, 1 - core)):
             for c in range(2):
-                x = pltpu.roll(ref[c, at(j * STRIP), :], across, 1)
-                patch[c, at(half * hr + j * STRIP), :] = x[:, :frame]
+                patch[c, at(half * hr + j * STRIP), :] = strip(ref, c, at(j * STRIP))
 
     strips(hr // STRIP, body)
 
@@ -141,10 +155,10 @@
     refs = refs[5:]
     modes = probe.shape[0]
     if n_pieces:
-        pieces = [refs[m * n_pieces : (m + 1) * n_pieces] for m in range(modes)]
-        refs = refs[modes * n_pieces :]
+        streams = grouped(refs, 2 * modes, n_pieces)
+        refs = refs[2 * modes * n_pieces :]
         new_probe = refs.pop(3)
-        update_probe(probe, pieces, coef, new_probe)
+        update_probe(probe, streams, coef, new_probe)
         probe = new_probe
     far, power, patch, tall_parts, wide_parts, product = refs
     frame = probe.shape[-1]
@@ -205,7 +219,8 @@
     fars, powers, others, patches = (refs[i * slots : (i + 1) * slots] for i in range(4))
     refs = refs[4 * slots :]
     before = refs.pop(0) if mode else None
-    probe_grad, grads, tall_parts, wide_parts, product_wide, product_tall = refs[:6]
+    probe_grad, refs = refs[:2], refs[2:]
+    grads, tall_parts, wide_parts, product_wide, product_tall = refs
     frame = probe.shape[-1]
     h = frame // 2
 
@@ -240,9 +255,10 @@
     strips(h // STRIP, columns)
     for p in range(2):
         product_tall[p] = mul_left(tab[1, p], tall_parts[p])
-    key = chunk_key(ORDERS[mode])
+    keys = [chunk_key(o) for o in ORDERS]
     chunk = frame // CHUNKS
     core = lax.axis_index("row")
+    first = left_half()
 
     def results(j):
         x = [[product_tall[p, at(k * h + j * STRIP), :] for k in range(2)] for p in range(2)]
@@ -269,26 +285,29 @@
                     if not last or tall:
                         grads[s, k, rows, :] = g
                         continue
-                    wide = grads.shape[-1]
+                    wide = 2 * grads.shape[-1]
                     g = jnp.concatenate([g, jnp.zeros((STRIP, wide - frame), f32)], 1)
                     g = pltpu.roll(g, corner(offsets, s, 1, wide - 2 * h, h), 1)
                     window[k] = g if s == 0 else window[k] + g
             start = lower * h + j * STRIP
-            rel = (start // chunk) ^ key
             for k in range(2):
-                probe_grad[rel, k, at(start % chunk), :] = step[k]
+                probe_grad[k][(start // chunk) ^ keys[k], at(start % chunk), :] = step[k]
                 if last and not tall:
-                    grads[lower ^ core, k, at(j * STRIP), :] = window[k]
+                    half = window[k].shape[1] // 2
+                    grads[lower ^ core, first, k, at(j * STRIP), :] = window[k][:, :half]
+                    grads[lower ^ core, 1 - first, k, at(j * STRIP), :] = window[k][:, half:]
 
     strips(h // STRIP, results)
 
 
 def place_kernel(offsets, grads, out):
     slots, _, frame, _ = grads.shape
-    _, _, hr, cols = out.shape
+    _, _, _, hr, half = out.shape
+    cols = 2 * half
     h = frame // 2
     size = cols - 2 * h
     core = lax.axis_index("row")
+    first = left_half()
     for c in range(2):
         total = None
         for s in range(slots):
@@ -298,19 +317,23 @@
             g = pltpu.roll(g, corner(offsets, s, 1, size, h), 1)
             total = g if s == 0 else total + g
         for k in range(2):
-            out[k ^ core, c] = total[k * hr : (k + 1) * hr]
+            out[k ^ core, first, c] = total[k * hr : (k + 1) * hr, :half]
+            out[k ^ core, 1 - first, c] = total[k * hr : (k + 1) * hr, half:]
 
 
 def finish_kernel(n_pieces, coef, *refs):
     refs = list(refs)
     near, away, probe = refs[:3]
-    pieces = [refs[3 + m * n_pieces : 3 + (m + 1) * n_pieces] for m in range(probe.shape[0])]
+    streams = grouped(refs[3:], 2 * probe.shape[0], n_pieces)
     tile, new_probe = refs[-2:]
-    update_probe(probe, pieces, coef, new_probe)
-    hr = near.shape[1]
+    update_probe(probe, streams, coef, new_probe)
+    _, _, hr, half = near.shape
     core = lax.axis_index("row")
-    tile[:, pl.ds(pl.multiple_of(core * hr, hr), hr), :] = near[...]
-    tile[:, pl.ds(pl.multiple_of((1 - core) * hr, hr), hr), :] = away[...]
+    first = left_half()
+    for ref, part in ((near, core), (away, 1 - core)):
+        rows = pl.ds(pl.multiple_of(part * hr, hr), hr)
+        tile[:, rows, :half] = ref[first]
+        tile[:, rows, half:] = ref[1 - first]
 
 
 def vmem():
@@ -337,8 +360,12 @@
     return lax.ppermute(x, "row", [(0, 1), (1, 0)])
 
 
-def shift_cols(x, step, tiles):
-    pairs = [(s, s + step) for s in range(tiles) if 0 <= s % GX + step < GX]
+def beside(x, inner, tiles):
+    pairs = []
+    for t in range(tiles):
+        other = t + 1 if (t % 2 == 0) == inner else t - 1
+        if 0 <= other < tiles and other // GX == t // GX:
+            pairs.append((t, other))
     return lax.ppermute(x, "tile", pairs)
 
 
@@ -356,34 +383,47 @@
     return lax.optimization_barrier(groups)
 
 
-def window_sum(grad, size, half, tiles, tall, wide):
+def halves(x, even, inner):
+    half = x.shape[-1] // 2
+    own_first = even == inner
+    a, b = x[..., :half], x[..., half:]
+    return jnp.where(own_first, a, b), jnp.where(own_first, b, a)
+
+
+def joined(own, other, even, inner):
+    own_first = even == inner
+    return jnp.concatenate([jnp.where(own_first, own, other), jnp.where(own_first, other, own)], -1)
+
+
+def window_sum(grad, even, tiles, tall, wide):
     if wide:
-        left, right = grad[:, :, :size], grad[:, :, size:]
-        right_side = shift_cols(left, -1, tiles)
-        left_side = shift_cols(right, 1, tiles)
-        total = jnp.concatenate([left + left_side, right + right_side], 2)
+        got = [beside(grad[1], False, tiles), beside(grad[0], True, tiles)]
+        total = jnp.stack([grad[0] + got[1], grad[1] + got[0]])
         return total + swap_vertical(total, tiles) if tall else total
-    got_left = shift_cols(grad[:, :, half + size :], 1, tiles)
-    got_right = shift_cols(grad[:, :, :half], -1, tiles)
-    return grad[:, :, half : half + size] + jnp.concatenate([got_left, got_right], 2)
+    own, other = zip(*(halves(grad[k], even, k == 0) for k in range(2)))
+    got = [beside(other[1], False, tiles), beside(other[0], True, tiles)]
+    return jnp.stack([own[0] + got[1], own[1] + got[0]])
 
 
 def reduce_all(parts, grad, tiles, window):
     bits = int(math.log2(tiles))
     held = list(parts)
+    orders = [ORDERS[i % 2] for i in range(len(parts))]
+    near = None
     for i in range(HALVINGS):
         n = held[0].shape[0] // 2
-        got = [exchange(h[n:], o[i], tiles) for h, o in zip(held, ORDERS)]
+        got = [exchange(h[n:], o[i], tiles) for h, o in zip(held, orders)]
         held = [h[:n] + g for h, g in zip(held, got)]
-    held, grad = together(held, grad)
-    got = [exchange(h, o[-1], tiles) for h, o in zip(held, ORDERS)]
-    near = window(grad)
+        if i == 0:
+            held[-1], grad = together(held[-1], grad)
+            near = window(grad)
+    got = [exchange(h, o[-1], tiles) for h, o in zip(held, orders)]
     held = [h + g for h, g in zip(held, got)]
     for bit in range(len(ORDERS[0]), bits):
         held = [h + exchange(h, bit, tiles) for h in held]
     pieces = [[h] for h in held]
     for i in reversed(range(HALVINGS)):
-        for p, o in zip(pieces, ORDERS):
+        for p, o in zip(pieces, orders):
             p.append(exchange(p[0] if len(p) == 1 else jnp.concatenate(p, 0), o[i], tiles))
     return pieces, near
 
@@ -398,18 +438,19 @@
     slots = offsets.shape[0]
     modes = probe_modes.shape[0]
     core = lax.axis_index("row")
+    even = lax.axis_index("tile") % 2 == 0
     hr = size // 2
     tab = jnp.asarray(tables(frame))
     perm = jnp.asarray(deinterleave(frame))
     coef = 4.0 / (slots * tiles)
 
     mine = lax.dynamic_slice(own_tile, (0, core * hr, 0), (2, hr, size))
-    from_left = shift_cols(mine[:, :, size - half :], 1, tiles)
-    from_right = shift_cols(mine[:, :, :half], -1, tiles)
-    near = jnp.concatenate([from_left, mine, from_right], 2)
+    own = [jnp.where(even == inner, mine[:, :, half:], mine[:, :, :half]) for inner in (True, False)]
+    got = [beside(own[1], False, tiles), beside(own[0], True, tiles)]
+    near = jnp.stack([joined(own[0], got[1], even, True), joined(own[1], got[0], even, False)])
     if tall:
         other = swap_vertical(near, tiles)
-        near = jnp.where(core == 0, jnp.concatenate([other, near], 1), jnp.concatenate([near, other], 1))
+        near = jnp.where(core == 0, jnp.concatenate([other, near], 2), jnp.concatenate([near, other], 2))
     (amp,) = call(amplitude_kernel, [amplitude.shape], [amplitude, perm])
     away = swap_rows(near)
     near, away, amp = together(near, away, amp)
@@ -422,7 +463,7 @@
 
     matmul = 4 * 2 * 3 * 4 * frame**3
     probe = probe_modes
-    pieces = None
+    streams = None
     for iteration in range(ITERS):
         final = iteration + 1 == ITERS
         fars, powers, others, patches = [], [], [], []
@@ -430,11 +471,11 @@
             args = [offsets, near, away, probe, tab]
             outs = [(modes, 2, frame, frame), (frame, frame), (2, frame, frame)]
             count = 0
-            if pieces is not None:
-                count = len(pieces[0])
-                args += [p for group in pieces for p in group]
+            if streams is not None:
+                count = len(streams[0])
+                args += [p for group in streams for p in group]
                 outs.append(probe.shape)
-                pieces = None
+                streams = None
             got = call(
                 functools.partial(forward_kernel, s, count, coef, tall),
                 outs,
@@ -456,34 +497,34 @@
             if m:
                 args.append(before)
             grads = (2,) + near.shape if last and not tall else (slots, 2, frame, frame)
+            part = (CHUNKS, frame // CHUNKS, frame)
             got = call(
                 functools.partial(inverse_kernel, m, last, tall),
-                [(CHUNKS, 2, frame // CHUNKS, frame), grads],
+                [part, part, grads],
                 args,
                 scratch(slots)
                 + [pltpu.VMEM((2, slots * frame, frame), f32), pltpu.VMEM((2, frame, slots * frame), f32)],
                 matmul * slots,
             )
-            parts.append(got[0])
-            before = got[1]
+            parts += got[:2]
+            before = got[2]
         if tall:
             (before,) = call(place_kernel, [(2,) + near.shape], [offsets, before])
         grad = before[0] + swap_rows(before[1])
         wide = tall or not final
-        pieces, total = reduce_all(
-            parts, grad, tiles, lambda g: window_sum(g, size, half, tiles, tall, wide)
-        )
+        streams, total = reduce_all(parts, grad, tiles, lambda g: window_sum(g, even, tiles, tall, wide))
         if wide:
             near = near + total / MODES
-        else:
-            near = near[:, :, half : half + size] + total / MODES
-        if tall and final:
-            near = near[:, :, half : half + size]
-            near = jnp.where(core == 0, near[:, half:], near[:, : size - half])
+        if final:
+            near = jnp.stack([halves(near[k], even, k == 0)[0] for k in range(2)])
+            if not wide:
+                near = near + total / MODES
+            if tall:
+                near = jnp.where(core == 0, near[:, :, half:], near[:, :, : size - half])
         away = swap_rows(near)
-    args = [near, away, probe] + [p for group in pieces for p in group]
+    args = [near, away, probe] + [p for group in streams for p in group]
     tile, probe = call(
-        functools.partial(finish_kernel, len(pieces[0]), coef), [own_tile.shape, probe.shape], args
+        functools.partial(finish_kernel, len(streams[0]), coef), [own_tile.shape, probe.shape], args
     )
     return (tile[None], probe)
 

time: 134 us -> 142 us (1.060)
  starting transfers between devices: 43.4 us -> 60.4 us
  waiting for transfers between devices: 65.8 us -> 55.8 us
    ppermute x20 -> x40, starting transfers between devices: 25.1 us -> 50 us  [exchange(): return lax.ppermute(x, 'tile', [(s, s ^ 1 << bit) for s in range(tiles)])]
    ppermute x20 -> x40, waiting for transfers between devices: 58.5 us -> 42.1 us  [exchange(): return lax.ppermute(x, 'tile', [(s, s ^ 1 << bit) for s in range(tiles)])]
    ppermute x6, starting transfers between devices: 16.7 us -> 8.85 us  [beside(): return lax.ppermute(x, 'tile', pairs)]
    ppermute x6, waiting for transfers between devices: 4.35 us -> 11.7 us  [beside(): return lax.ppermute(x, 'tile', pairs)]
  transfers between devices with their start and end apart: 35 -> 55, of which waited for: 26 -> 31; matrix products, arithmetic and copies ran while one was open for 1% -> 1% of each run, Pallas kernels for 6% -> 2%
where the time goes in v5:
time: 142 us
  starting transfers between devices  60.4 us (43%)
  waiting for transfers between devices  55.8 us (39%)
  Pallas kernels  20.1 us (14%)
  local copies, waits for them, and re-layouts  2.4 us (2%)
  between operations  1.99 us (1%)
    ppermute x40, starting transfers between devices, exchange(): return lax.ppermute(x, 'tile', [(s, s ^ 1 << bit) for s in range(tiles)])  50 us
    ppermute x40, waiting for transfers between devices, exchange(): return lax.ppermute(x, 'tile', [(s, s ^ 1 << bit) for s in range(tiles)])  42.1 us
    pallas_call x10, Pallas kernels, call(): pl.pallas_call(kernel, out_shape=[jax.ShapeDtypeStruct(o, f32) for o in o...  20.1 us
    ppermute x6, waiting for transfers between devices, beside(): return lax.ppermute(x, 'tile', pairs)  11.7 us
    ppermute x6, starting transfers between devices, beside(): return lax.ppermute(x, 'tile', pairs)  8.85 us
  transfers between devices with their start and end apart: 55, of which 31 were waited for; matrix products, arithmetic and copies ran while one was open for 1% of the time, Pallas kernels for 2%

profile of v5, /device:TPU:0, one launch (start us, length us, event | category | flops | bytes accessed | tf_op | source)
XLA Modules:
  0.0 141.6 jit_solution(5434529281926272745)
XLA Ops:
  1.7 3.0 %collective-permute-start = (f32[2,128,128]{2,1,0:T(8,128)S(1)}, f32[2,128,128]{2,1,0:T(8,128)S(1)}, u32[]{:S(2)}, u32[]{:S(2)}) collective-permute-start(f32[2,128,128]{2,1,0:T(8,128)S(1)} %get-tuple-element.80), channel_id=1, source_target_pairs={{0,2},{2,0},{4,6},{6,4},{8,10},{10,8},{12,14},{14,12},{1,3},{3,1},... | collective-permute-start | bytes 393224 | tf_op jit(solution)/shard_map/ppermute | solution.py:369
  5.4 2.8 %collective-permute-done = f32[2,128,128]{2,1,0:T(8,128)S(1)} collective-permute-done((f32[2,128,128]{2,1,0:T(8,128)S(1)}, f32[2,128,128]{2,1,0:T(8,128)S(1)}, u32[]{:S(2)}, u32[]{:S(2)}) %collective-permute-start) | collective-permute-done | bytes 131104 | tf_op jit(solution)/shard_map/ppermute | solution.py:369
  10.5 2.1 %shard_map.88 = (f32[2,2,256,256]{3,2,1,0:T(8,128)S(1)}, f32[256,256]{1,0:T(8,128)S(1)}, f32[2,256,256]{2,1,0:T(8,128)S(1)}) custom-call(s32[2,2]{1,0:T(2,128)S(1)} %copy-done.4, f32[2,2,128,256]{3,2,1,0:T(8,128)S(1)} %pad_maximum_fusion.refs_1_, f32[2,2,128,256]{3,2,1,0:T(8,128)S(1)} %collective-permute-done.2.refs_2_, f32[2,2,256,256]{3,2,1,0:T(8,128)S(1)} %copy-done.3, ...), custom_call_target="tpu_custom_call" | custom-call | flops 3221225472 | bytes 4980752 | tf_op jit(solution)/shard_map/pallas_call | solution.py:346
  12.5 2.1 %shard_map.87 = (f32[2,2,256,256]{3,2,1,0:T(8,128)S(1)}, f32[256,256]{1,0:T(8,128)S(1)}, f32[2,256,256]{2,1,0:T(8,128)S(1)}) custom-call(s32[2,2]{1,0:T(2,128)S(1)} %copy-done.4, f32[2,2,128,256]{3,2,1,0:T(8,128)S(1)} %pad_maximum_fusion.refs_1_, f32[2,2,128,256]{3,2,1,0:T(8,128)S(1)} %collective-permute-done.2.refs_2_, f32[2,2,256,256]{3,2,1,0:T(8,128)S(1)} %copy-done.3, ...), custom_call_target="tpu_custom_call" | custom-call | flops 3221225472 | bytes 4980752 | tf_op jit(solution)/shard_map/pallas_call | solution.py:346
  16.6 2.2 %shard_map.89 = (f32[4,64,256]{2,1,0:T(8,128)S(1)}, f32[4,64,256]{2,1,0:T(8,128)S(1)}, f32[2,2,256,256]{3,2,1,0:T(8,128)S(1)}) custom-call(s32[2,2]{1,0:T(2,128)S(1)} %copy-done.4, s32[1]{0:T(128)S(6)} %copy.9.refs_1_, bf16[2,2,2,256,256]{4,3,2,1,0:T(8,128)(2,1)S(1)} %copy-done.5, f32[2,256,256]{2,1,0:T(8,128)S(1)} %shard_map.86.refs_3_, ...), custom_call_target="tpu_custom_call" | custom-call | flops 3221225472 | bytes 8388628 | tf_op jit(solution)/shard_map/pallas_call | solution.py:346
  18.8 2.6 %shard_map.90 = (f32[4,64,256]{2,1,0:T(8,128)S(1)}, f32[4,64,256]{2,1,0:T(8,128)S(1)}, f32[2,2,2,128,256]{4,3,2,1,0:T(8,128)S(1)}) custom-call(s32[2,2]{1,0:T(2,128)S(1)} %copy-done.4, s32[1]{0:T(128)S(6)} %copy.9.refs_1_, bf16[2,2,2,256,256]{4,3,2,1,0:T(8,128)(2,1)S(1)} %copy-done.5, f32[2,256,256]{2,1,0:T(8,128)S(1)} %shard_map.86.refs_3_, ...), custom_call_target="tpu_custom_call" | custom-call | flops 3221225472 | bytes 9437204 | tf_op jit(solution)/shard_map/pallas_call | solution.py:346
  21.5 5.9 %collective-permute-start.15 = (f32[2,64,256]{2,1,0:T(8,128)S(1)}, f32[2,64,256]{2,1,0:T(8,128)S(1)}, u32[]{:S(2)}, u32[]{:S(2)}) collective-permute-start(f32[2,64,256]{2,1,0:T(8,128)S(1)} %slice.179), channel_id=1, source_target_pairs={{0,4},{2,6},{4,0},{6,2},{8,12},{10,14},{12,8},{14,10},{1,5},{3,7},... | collective-permute-start | bytes 393224 | tf_op jit(solution)/shard_map/ppermute | solution.py:379
  31.8 1.9 %collective-permute-done.10 = f32[2,64,256]{2,1,0:T(8,128)S(1)} collective-permute-done((f32[2,64,256]{2,1,0:T(8,128)S(1)}, f32[2,64,256]{2,1,0:T(8,128)S(1)}, u32[]{:S(2)}, u32[]{:S(2)}) %collective-permute-start.10) | collective-permute-done | bytes 131104 | tf_op jit(solution)/shard_map/ppermute | solution.py:379
  36.8 2.7 %collective-permute-start.17 = (f32[1,64,256]{2,1,0:T(8,128)S(1)}, f32[1,64,256]{2,1,0:T(8,128)S(1)}, u32[]{:S(2)}, u32[]{:S(2)}) collective-permute-start(f32[1,64,256]{2,1,0:T(8,128)S(1)} %slice_add_fusion.12), channel_id=1, source_target_pairs={{0,8},{2,10},{4,12},{6,14},{8,0},{10,2},{12,4},{14,6},{1,9},{3,11}... | collective-permute-start | bytes 196616 | tf_op jit(solution)/shard_map/ppermute | solution.py:379
  39.5 2.0 %collective-permute-start.12 = (f32[1,64,256]{2,1,0:T(8,128)S(1)}, f32[1,64,256]{2,1,0:T(8,128)S(1)}, u32[]{:S(2)}, u32[]{:S(2)}) collective-permute-start(f32[1,64,256]{2,1,0:T(8,128)S(1)} %slice_add_fusion.13), channel_id=1, source_target_pairs={{0,8},{2,10},{4,12},{6,14},{8,0},{10,2},{12,4},{14,6},{1,9},{3,11}... | collective-permute-start | bytes 196616 | tf_op jit(solution)/shard_map/ppermute | solution.py:379
  41.5 2.3 %collective-permute-start.22 = (f32[1,64,256]{2,1,0:T(8,128)S(1)}, f32[1,64,256]{2,1,0:T(8,128)S(1)}, u32[]{:S(2)}, u32[]{:S(2)}) collective-permute-start(f32[1,64,256]{2,1,0:T(8,128)S(1)} %slice_add_fusion.11), channel_id=1, source_target_pairs={{0,8},{2,10},{4,12},{6,14},{8,0},{10,2},{12,4},{14,6},{1,9},{3,11}... | collective-permute-start | bytes 196616 | tf_op jit(solution)/shard_map/ppermute | solution.py:379
  44.1 3.5 %collective-permute-done.12 = f32[1,64,256]{2,1,0:T(8,128)S(1)} collective-permute-done((f32[1,64,256]{2,1,0:T(8,128)S(1)}, f32[1,64,256]{2,1,0:T(8,128)S(1)}, u32[]{:S(2)}, u32[]{:S(2)}) %collective-permute-start.12) | collective-permute-done | bytes 65568 | tf_op jit(solution)/shard_map/ppermute | solution.py:379
  52.9 2.0 %collective-permute-done.25 = f32[1,64,256]{2,1,0:T(8,128)S(1)} collective-permute-done((f32[1,64,256]{2,1,0:T(8,128)S(1)}, f32[1,64,256]{2,1,0:T(8,128)S(1)}, u32[]{:S(2)}, u32[]{:S(2)}) %collective-permute-start.25) | collective-permute-done | bytes 65568 | tf_op jit(solution)/shard_map/ppermute | solution.py:379
  55.9 6.1 %collective-permute-done.7 = f32[2,128,256]{2,1,0:T(8,128)S(1)} collective-permute-done((f32[2,128,256]{2,1,0:T(8,128)S(1)}, f32[2,128,256]{2,1,0:T(8,128)S(1)}, u32[]{:S(2)}, u32[]{:S(2)}) %collective-permute-start.7) | collective-permute-done | bytes 262176 | tf_op jit(solution)/shard_map/ppermute | solution.py:369
  62.0 2.2 %collective-permute-start.26 = (f32[1,64,256]{2,1,0:T(8,128)S(1)}, f32[1,64,256]{2,1,0:T(8,128)S(1)}, u32[]{:S(2)}, u32[]{:S(2)}) collective-permute-start(f32[1,64,256]{2,1,0:T(8,128)S(1)} %slice_add_fusion.15), channel_id=1, source_target_pairs={{0,8},{2,10},{4,12},{6,14},{8,0},{10,2},{12,4},{14,6},{1,9},{3,11}... | collective-permute-start | bytes 196616 | tf_op jit(solution)/shard_map/ppermute | solution.py:379
  67.2 2.5 %collective-permute-start.27 = (f32[1,64,256]{2,1,0:T(8,128)S(1)}, f32[1,64,256]{2,1,0:T(8,128)S(1)}, u32[]{:S(2)}, u32[]{:S(2)}) collective-permute-start(f32[1,64,256]{2,1,0:T(8,128)S(1)} %add.120.refs_14_), channel_id=1, source_target_pairs={{0,2},{2,0},{4,6},{6,4},{8,10},{10,8},{12,14},{14,12},{1,3},{3,1},... | collective-permute-start | bytes 196616 | tf_op jit(solution)/shard_map/ppermute | solution.py:379
  69.8 2.9 %collective-permute-done.27.refs_15_ = f32[1,64,256]{2,1,0:T(8,128)S(1)} collective-permute-done((f32[1,64,256]{2,1,0:T(8,128)S(1)}, f32[1,64,256]{2,1,0:T(8,128)S(1)}, u32[]{:S(2)}, u32[]{:S(2)}) %collective-permute-start.27) | collective-permute-done | bytes 65568 | tf_op jit(solution)/shard_map/ppermute | solution.py:379
  72.8 1.9 %collective-permute-start.28 = (f32[2,64,256]{2,1,0:T(8,128)S(1)}, f32[2,64,256]{2,1,0:T(8,128)S(1)}, u32[]{:S(2)}, u32[]{:S(2)}) collective-permute-start(f32[2,64,256]{2,1,0:T(8,128)S(1)} %pad_maximum_fusion.4), channel_id=1, source_target_pairs={{0,4},{2,6},{4,0},{6,2},{8,12},{10,14},{12,8},{14,10},{1,5},{3,7},... | collective-permute-start | bytes 393224 | tf_op jit(solution)/shard_map/ppermute | solution.py:379
  74.8 3.0 %collective-permute-done.28.refs_16_ = f32[2,64,256]{2,1,0:T(8,128)S(1)} collective-permute-done((f32[2,64,256]{2,1,0:T(8,128)S(1)}, f32[2,64,256]{2,1,0:T(8,128)S(1)}, u32[]{:S(2)}, u32[]{:S(2)}) %collective-permute-start.28) | collective-permute-done | bytes 131104 | tf_op jit(solution)/shard_map/ppermute | solution.py:379
  77.8 2.1 %shard_map.91 = (f32[2,2,256,256]{3,2,1,0:T(8,128)S(1)}, f32[256,256]{1,0:T(8,128)S(1)}, f32[2,256,256]{2,1,0:T(8,128)S(1)}, f32[2,2,256,256]{3,2,1,0:T(8,128)S(1)}) custom-call(s32[2,2]{1,0:T(2,128)S(1)} %copy-done.4, f32[2,2,128,256]{3,2,1,0:T(8,128)S(1)} %fusion.refs_1_, f32[2,2,128,256]{3,2,1,0:T(8,128)S(1)} %collective-permute-done.9.refs_2_, ...), custom_call_target="tpu_custom_call" | custom-call | flops 3221225472 | bytes 7077904 | tf_op jit(solution)/shard_map/pallas_call | solution.py:346
  80.0 2.1 %shard_map.92 = (f32[2,2,256,256]{3,2,1,0:T(8,128)S(1)}, f32[256,256]{1,0:T(8,128)S(1)}, f32[2,256,256]{2,1,0:T(8,128)S(1)}) custom-call(s32[2,2]{1,0:T(2,128)S(1)} %copy-done.4, f32[2,2,128,256]{3,2,1,0:T(8,128)S(1)} %fusion.refs_1_, f32[2,2,128,256]{3,2,1,0:T(8,128)S(1)} %collective-permute-done.9.refs_2_, ...), custom_call_target="tpu_custom_call" | custom-call | flops 3221225472 | bytes 4980752 | tf_op jit(solution)/shard_map/pallas_call | solution.py:346
  83.8 2.3 %shard_map.93 = (f32[4,64,256]{2,1,0:T(8,128)S(1)}, f32[4,64,256]{2,1,0:T(8,128)S(1)}, f32[2,2,256,256]{3,2,1,0:T(8,128)S(1)}) custom-call(s32[2,2]{1,0:T(2,128)S(1)} %copy-done.4, s32[1]{0:T(128)S(6)} %copy.9.refs_1_, bf16[2,2,2,256,256]{4,3,2,1,0:T(8,128)(2,1)S(1)} %copy-done.5, f32[2,256,256]{2,1,0:T(8,128)S(1)} %shard_map.86.refs_3_, ...), custom_call_target="tpu_custom_call" | custom-call | flops 3221225472 | bytes 8388628 | tf_op jit(solution)/shard_map/pallas_call | solution.py:346
  86.1 2.6 %shard_map.94 = (f32[4,64,256]{2,1,0:T(8,128)S(1)}, f32[4,64,256]{2,1,0:T(8,128)S(1)}, f32[2,2,2,128,256]{4,3,2,1,0:T(8,128)S(1)}) custom-call(s32[2,2]{1,0:T(2,128)S(1)} %copy-done.4, s32[1]{0:T(128)S(6)} %copy.9.refs_1_, bf16[2,2,2,256,256]{4,3,2,1,0:T(8,128)(2,1)S(1)} %copy-done.5, f32[2,256,256]{2,1,0:T(8,128)S(1)} %shard_map.86.refs_3_, ...), custom_call_target="tpu_custom_call" | custom-call | flops 3221225472 | bytes 9437204 | tf_op jit(solution)/shard_map/pallas_call | solution.py:346
  88.8 1.9 %collective-permute-start.41 = (f32[2,64,256]{2,1,0:T(8,128)S(1)}, f32[2,64,256]{2,1,0:T(8,128)S(1)}, u32[]{:S(2)}, u32[]{:S(2)}) collective-permute-start(f32[2,64,256]{2,1,0:T(8,128)S(1)} %slice.203), channel_id=1, source_target_pairs={{0,4},{2,6},{4,0},{6,2},{8,12},{10,14},{12,8},{14,10},{1,5},{3,7},... | collective-permute-start | bytes 393224 | tf_op jit(solution)/shard_map/ppermute | solution.py:379
  94.7 1.9 %collective-permute-start.42 = (f32[1,64,256]{2,1,0:T(8,128)S(1)}, f32[1,64,256]{2,1,0:T(8,128)S(1)}, u32[]{:S(2)}, u32[]{:S(2)}) collective-permute-start(f32[1,64,256]{2,1,0:T(8,128)S(1)} %slice.233), channel_id=1, source_target_pairs={{0,2},{2,0},{4,6},{6,4},{8,10},{10,8},{12,14},{14,12},{1,3},{3,1},... | collective-permute-start | bytes 196616 | tf_op jit(solution)/shard_map/ppermute | solution.py:379
  104.0 2.2 %collective-permute-start.48 = (f32[1,64,256]{2,1,0:T(8,128)S(1)}, f32[1,64,256]{2,1,0:T(8,128)S(1)}, u32[]{:S(2)}, u32[]{:S(2)}) collective-permute-start(f32[1,64,256]{2,1,0:T(8,128)S(1)} %slice_add_fusion.8), channel_id=1, source_target_pairs={{0,8},{2,10},{4,12},{6,14},{8,0},{10,2},{12,4},{14,6},{1,9},{3,11}... | collective-permute-start | bytes 196616 | tf_op jit(solution)/shard_map/ppermute | solution.py:379
  106.3 2.7 %collective-permute-done.43 = f32[1,64,256]{2,1,0:T(8,128)S(1)} collective-permute-done((f32[1,64,256]{2,1,0:T(8,128)S(1)}, f32[1,64,256]{2,1,0:T(8,128)S(1)}, u32[]{:S(2)}, u32[]{:S(2)}) %collective-permute-start.43) | collective-permute-done | bytes 65568 | tf_op jit(solution)/shard_map/ppermute | solution.py:379
  113.8 2.1 %collective-permute-done.39.refs_4_ = f32[1,64,256]{2,1,0:T(8,128)S(1)} collective-permute-done((f32[1,64,256]{2,1,0:T(8,128)S(1)}, f32[1,64,256]{2,1,0:T(8,128)S(1)}, u32[]{:S(2)}, u32[]{:S(2)}) %collective-permute-start.39) | collective-permute-done | bytes 65568 | tf_op jit(solution)/shard_map/ppermute | solution.py:379
  119.0 2.7 %collective-permute-done.51 = f32[1,64,256]{2,1,0:T(8,128)S(1)} collective-permute-done((f32[1,64,256]{2,1,0:T(8,128)S(1)}, f32[1,64,256]{2,1,0:T(8,128)S(1)}, u32[]{:S(2)}, u32[]{:S(2)}) %collective-permute-start.51) | collective-permute-done | bytes 65568 | tf_op jit(solution)/shard_map/ppermute | solution.py:379
  123.4 4.3 %collective-permute-done.52 = f32[1,64,256]{2,1,0:T(8,128)S(1)} collective-permute-done((f32[1,64,256]{2,1,0:T(8,128)S(1)}, f32[1,64,256]{2,1,0:T(8,128)S(1)}, u32[]{:S(2)}, u32[]{:S(2)}) %collective-permute-start.52) | collective-permute-done | bytes 65568 | tf_op jit(solution)/shard_map/ppermute | solution.py:379
  129.8 2.8 %collective-permute-done.33 = f32[2,128,128]{2,1,0:T(8,128)S(1)} collective-permute-done((f32[2,128,128]{2,1,0:T(8,128)S(1)}, f32[2,128,128]{2,1,0:T(8,128)S(1)}, u32[]{:S(2)}, u32[]{:S(2)}) %collective-permute-start.33) | collective-permute-done | bytes 131104 | tf_op jit(solution)/shard_map/ppermute | solution.py:369
  134.8 4.0 %collective-permute-done.50.refs_11_ = f32[2,64,256]{2,1,0:T(8,128)S(1)} collective-permute-done((f32[2,64,256]{2,1,0:T(8,128)S(1)}, f32[2,64,256]{2,1,0:T(8,128)S(1)}, u32[]{:S(2)}, u32[]{:S(2)}) %collective-permute-start.50) | collective-permute-done | bytes 131104 | tf_op jit(solution)/shard_map/ppermute | solution.py:379
  (170 shorter events, 52.2 us)
Async XLA Ops:
  1.7 6.5 %collective-permute-start = (f32[2,128,128]{2,1,0:T(8,128)S(1)}, f32[2,128,128]{2,1,0:T(8,128)S(1)}, u32[]{:S(2)}, u32[]{:S(2)}) collective-permute-start(f32[2,128,128]{2,1,0:T(8,128)S(1)} %get-tuple-element.80), channel_id=1, source_target_pairs={{0,2},{2,0},{4,6},{6,4},{8,10},{10,8},{12,14},{14,12},{1,3},{3,1},... | collective-permute-start | bytes 393224 | tf_op jit(solution)/shard_map/ppermute | solution.py:369
  21.5 9.7 %collective-permute-start.15 = (f32[2,64,256]{2,1,0:T(8,128)S(1)}, f32[2,64,256]{2,1,0:T(8,128)S(1)}, u32[]{:S(2)}, u32[]{:S(2)}) collective-permute-start(f32[2,64,256]{2,1,0:T(8,128)S(1)} %slice.179), channel_id=1, source_target_pairs={{0,4},{2,6},{4,0},{6,2},{8,12},{10,14},{12,8},{14,10},{1,5},{3,7},... | collective-permute-start | bytes 393224 | tf_op jit(solution)/shard_map/ppermute | solution.py:379
  27.3 6.4 %collective-permute-start.10 = (f32[2,64,256]{2,1,0:T(8,128)S(1)}, f32[2,64,256]{2,1,0:T(8,128)S(1)}, u32[]{:S(2)}, u32[]{:S(2)}) collective-permute-start(f32[2,64,256]{2,1,0:T(8,128)S(1)} %slice.175), channel_id=1, source_target_pairs={{0,2},{2,0},{4,6},{6,4},{8,10},{10,8},{12,14},{14,12},{1,3},{3,1},... | collective-permute-start | bytes 393224 | tf_op jit(solution)/shard_map/ppermute | solution.py:379
  27.9 8.2 %collective-permute-start.20 = (f32[2,64,256]{2,1,0:T(8,128)S(1)}, f32[2,64,256]{2,1,0:T(8,128)S(1)}, u32[]{:S(2)}, u32[]{:S(2)}) collective-permute-start(f32[2,64,256]{2,1,0:T(8,128)S(1)} %slice.183), channel_id=1, source_target_pairs={{0,2},{2,0},{4,6},{6,4},{8,10},{10,8},{12,14},{14,12},{1,3},{3,1},... | collective-permute-start | bytes 393224 | tf_op jit(solution)/shard_map/ppermute | solution.py:379
  29.4 14.4 %collective-permute-start.5 = (f32[2,64,256]{2,1,0:T(8,128)S(1)}, f32[2,64,256]{2,1,0:T(8,128)S(1)}, u32[]{:S(2)}, u32[]{:S(2)}) collective-permute-start(f32[2,64,256]{2,1,0:T(8,128)S(1)} %slice.163), channel_id=1, source_target_pairs={{0,4},{2,6},{4,0},{6,2},{8,12},{10,14},{12,8},{14,10},{1,5},{3,7},... | collective-permute-start | bytes 393224 | tf_op jit(solution)/shard_map/ppermute | solution.py:379
  29.5 20.3 %collective-permute-start.6 = (f32[2,2,128,256]{3,2,1,0:T(8,128)S(1)}, f32[2,2,128,256]{3,2,1,0:T(8,128)S(1)}, u32[]{:S(2)}, u32[]{:S(2)}) collective-permute-start(f32[2,2,128,256]{3,2,1,0:T(8,128)S(1)} %slice_bitcast_fusion.1), channel_id=1, source_target_pairs={{0,1},{1,0},{2,3},{3,2},{4,5},{5,4},{6,7},{7,6},{8,9},{9,8},{10,11... | collective-permute-start | bytes 1572872 | tf_op jit(solution)/shard_map/ppermute | solution.py:360
  36.8 7.0 %collective-permute-start.17 = (f32[1,64,256]{2,1,0:T(8,128)S(1)}, f32[1,64,256]{2,1,0:T(8,128)S(1)}, u32[]{:S(2)}, u32[]{:S(2)}) collective-permute-start(f32[1,64,256]{2,1,0:T(8,128)S(1)} %slice_add_fusion.12), channel_id=1, source_target_pairs={{0,8},{2,10},{4,12},{6,14},{8,0},{10,2},{12,4},{14,6},{1,9},{3,11}... | collective-permute-start | bytes 196616 | tf_op jit(solution)/shard_map/ppermute | solution.py:379
  39.5 8.1 %collective-permute-start.12 = (f32[1,64,256]{2,1,0:T(8,128)S(1)}, f32[1,64,256]{2,1,0:T(8,128)S(1)}, u32[]{:S(2)}, u32[]{:S(2)}) collective-permute-start(f32[1,64,256]{2,1,0:T(8,128)S(1)} %slice_add_fusion.13), channel_id=1, source_target_pairs={{0,8},{2,10},{4,12},{6,14},{8,0},{10,2},{12,4},{14,6},{1,9},{3,11}... | collective-permute-start | bytes 196616 | tf_op jit(solution)/shard_map/ppermute | solution.py:379
  41.5 6.9 %collective-permute-start.22 = (f32[1,64,256]{2,1,0:T(8,128)S(1)}, f32[1,64,256]{2,1,0:T(8,128)S(1)}, u32[]{:S(2)}, u32[]{:S(2)}) collective-permute-start(f32[1,64,256]{2,1,0:T(8,128)S(1)} %slice_add_fusion.11), channel_id=1, source_target_pairs={{0,8},{2,10},{4,12},{6,14},{8,0},{10,2},{12,4},{14,6},{1,9},{3,11}... | collective-permute-start | bytes 196616 | tf_op jit(solution)/shard_map/ppermute | solution.py:379
  43.8 8.2 %collective-permute-start.18 = (f32[1,64,256]{2,1,0:T(8,128)S(1)}, f32[1,64,256]{2,1,0:T(8,128)S(1)}, u32[]{:S(2)}, u32[]{:S(2)}) collective-permute-start(f32[1,64,256]{2,1,0:T(8,128)S(1)} %add.115.refs_8_), channel_id=1, source_target_pairs={{0,2},{2,0},{4,6},{6,4},{8,10},{10,8},{12,14},{14,12},{1,3},{3,1},... | collective-permute-start | bytes 196616 | tf_op jit(solution)/shard_map/ppermute | solution.py:379
  47.6 16.9 %collective-permute-start.13 = (f32[1,64,256]{2,1,0:T(8,128)S(1)}, f32[1,64,256]{2,1,0:T(8,128)S(1)}, u32[]{:S(2)}, u32[]{:S(2)}) collective-permute-start(f32[1,64,256]{2,1,0:T(8,128)S(1)} %add.112.refs_5_), channel_id=1, source_target_pairs={{0,4},{2,6},{4,0},{6,2},{8,12},{10,14},{12,8},{14,10},{1,5},{3,7},... | collective-permute-start | bytes 196616 | tf_op jit(solution)/shard_map/ppermute | solution.py:379
  48.4 21.4 %collective-permute-start.23 = (f32[1,64,256]{2,1,0:T(8,128)S(1)}, f32[1,64,256]{2,1,0:T(8,128)S(1)}, u32[]{:S(2)}, u32[]{:S(2)}) collective-permute-start(f32[1,64,256]{2,1,0:T(8,128)S(1)} %add.118.refs_11_), channel_id=1, source_target_pairs={{0,4},{2,6},{4,0},{6,2},{8,12},{10,14},{12,8},{14,10},{1,5},{3,7},... | collective-permute-start | bytes 196616 | tf_op jit(solution)/shard_map/ppermute | solution.py:379
  50.2 11.8 %collective-permute-start.7 = (f32[2,128,256]{2,1,0:T(8,128)S(1)}, f32[2,128,256]{2,1,0:T(8,128)S(1)}, u32[]{:S(2)}, u32[]{:S(2)}) collective-permute-start(f32[2,128,256]{2,1,0:T(8,128)S(1)} %get-tuple-element.76), channel_id=1, source_target_pairs={{0,2},{2,0},{4,6},{6,4},{8,10},{10,8},{12,14},{14,12},{1,3},{3,1},... | collective-permute-start | bytes 786440 | tf_op jit(solution)/shard_map/ppermute | solution.py:369
  52.1 12.2 %collective-permute-start.8 = (f32[2,128,256]{2,1,0:T(8,128)S(1)}, f32[2,128,256]{2,1,0:T(8,128)S(1)}, u32[]{:S(2)}, u32[]{:S(2)}) collective-permute-start(f32[2,128,256]{2,1,0:T(8,128)S(1)} %get-tuple-element.77), channel_id=1, source_target_pairs={{2,4},{4,2},{6,8},{8,6},{10,12},{12,10},{3,5},{5,3},{7,9},{9,7},{1... | collective-permute-start | bytes 786440 | tf_op jit(solution)/shard_map/ppermute | solution.py:369
  54.9 19.8 %collective-permute-start.19 = (f32[2,64,256]{2,1,0:T(8,128)S(1)}, f32[2,64,256]{2,1,0:T(8,128)S(1)}, u32[]{:S(2)}, u32[]{:S(2)}) collective-permute-start(f32[2,64,256]{2,1,0:T(8,128)S(1)} %pad_maximum_fusion.2), channel_id=1, source_target_pairs={{0,4},{2,6},{4,0},{6,2},{8,12},{10,14},{12,8},{14,10},{1,5},{3,7},... | collective-permute-start | bytes 393224 | tf_op jit(solution)/shard_map/ppermute | solution.py:379
  64.4 13.4 %collective-permute-start.9 = (f32[2,2,128,256]{3,2,1,0:T(8,128)S(1)}, f32[2,2,128,256]{3,2,1,0:T(8,128)S(1)}, u32[]{:S(2)}, u32[]{:S(2)}) collective-permute-start(f32[2,2,128,256]{3,2,1,0:T(8,128)S(1)} %fusion.refs_1_), channel_id=1, source_target_pairs={{0,1},{1,0},{2,3},{3,2},{4,5},{5,4},{6,7},{7,6},{8,9},{9,8},{10,11... | collective-permute-start | bytes 1572872 | tf_op jit(solution)/shard_map/ppermute | solution.py:360
  64.5 10.2 %collective-permute-start.14 = (f32[2,64,256]{2,1,0:T(8,128)S(1)}, f32[2,64,256]{2,1,0:T(8,128)S(1)}, u32[]{:S(2)}, u32[]{:S(2)}) collective-permute-start(f32[2,64,256]{2,1,0:T(8,128)S(1)} %pad_maximum_fusion.1), channel_id=1, source_target_pairs={{0,2},{2,0},{4,6},{6,4},{8,10},{10,8},{12,14},{14,12},{1,3},{3,1},... | collective-permute-start | bytes 393224 | tf_op jit(solution)/shard_map/ppermute | solution.py:379
  88.8 5.9 %collective-permute-start.41 = (f32[2,64,256]{2,1,0:T(8,128)S(1)}, f32[2,64,256]{2,1,0:T(8,128)S(1)}, u32[]{:S(2)}, u32[]{:S(2)}) collective-permute-start(f32[2,64,256]{2,1,0:T(8,128)S(1)} %slice.203), channel_id=1, source_target_pairs={{0,4},{2,6},{4,0},{6,2},{8,12},{10,14},{12,8},{14,10},{1,5},{3,7},... | collective-permute-start | bytes 393224 | tf_op jit(solution)/shard_map/ppermute | solution.py:379
  90.7 6.4 %collective-permute-start.36 = (f32[2,64,256]{2,1,0:T(8,128)S(1)}, f32[2,64,256]{2,1,0:T(8,128)S(1)}, u32[]{:S(2)}, u32[]{:S(2)}) collective-permute-start(f32[2,64,256]{2,1,0:T(8,128)S(1)} %slice.199), channel_id=1, source_target_pairs={{0,2},{2,0},{4,6},{6,4},{8,10},{10,8},{12,14},{14,12},{1,3},{3,1},... | collective-permute-start | bytes 393224 | tf_op jit(solution)/shard_map/ppermute | solution.py:379
  91.8 7.8 %collective-permute-start.46 = (f32[2,64,256]{2,1,0:T(8,128)S(1)}, f32[2,64,256]{2,1,0:T(8,128)S(1)}, u32[]{:S(2)}, u32[]{:S(2)}) collective-permute-start(f32[2,64,256]{2,1,0:T(8,128)S(1)} %slice.207), channel_id=1, source_target_pairs={{0,2},{2,0},{4,6},{6,4},{8,10},{10,8},{12,14},{14,12},{1,3},{3,1},... | collective-permute-start | bytes 393224 | tf_op jit(solution)/shard_map/ppermute | solution.py:379
  92.7 17.6 %collective-permute-start.31 = (f32[2,64,256]{2,1,0:T(8,128)S(1)}, f32[2,64,256]{2,1,0:T(8,128)S(1)}, u32[]{:S(2)}, u32[]{:S(2)}) collective-permute-start(f32[2,64,256]{2,1,0:T(8,128)S(1)} %slice.189), channel_id=1, source_target_pairs={{0,4},{2,6},{4,0},{6,2},{8,12},{10,14},{12,8},{14,10},{1,5},{3,7},... | collective-permute-start | bytes 393224 | tf_op jit(solution)/shard_map/ppermute | solution.py:379
  92.9 24.3 %collective-permute-start.32 = (f32[2,2,128,256]{3,2,1,0:T(8,128)S(1)}, f32[2,2,128,256]{3,2,1,0:T(8,128)S(1)}, u32[]{:S(2)}, u32[]{:S(2)}) collective-permute-start(f32[2,2,128,256]{3,2,1,0:T(8,128)S(1)} %slice_bitcast_fusion), channel_id=1, source_target_pairs={{0,1},{1,0},{2,3},{3,2},{4,5},{5,4},{6,7},{7,6},{8,9},{9,8},{10,11... | collective-permute-start | bytes 1572872 | tf_op jit(solution)/shard_map/ppermute | solution.py:360
  100.4 8.6 %collective-permute-start.43 = (f32[1,64,256]{2,1,0:T(8,128)S(1)}, f32[1,64,256]{2,1,0:T(8,128)S(1)}, u32[]{:S(2)}, u32[]{:S(2)}) collective-permute-start(f32[1,64,256]{2,1,0:T(8,128)S(1)} %slice_add_fusion.9), channel_id=1, source_target_pairs={{0,8},{2,10},{4,12},{6,14},{8,0},{10,2},{12,4},{14,6},{1,9},{3,11}... | collective-permute-start | bytes 196616 | tf_op jit(solution)/shard_map/ppermute | solution.py:379
  102.1 8.8 %collective-permute-start.38 = (f32[1,64,256]{2,1,0:T(8,128)S(1)}, f32[1,64,256]{2,1,0:T(8,128)S(1)}, u32[]{:S(2)}, u32[]{:S(2)}) collective-permute-start(f32[1,64,256]{2,1,0:T(8,128)S(1)} %slice_add_fusion.10), channel_id=1, source_target_pairs={{0,8},{2,10},{4,12},{6,14},{8,0},{10,2},{12,4},{14,6},{1,9},{3,11}... | collective-permute-start | bytes 196616 | tf_op jit(solution)/shard_map/ppermute | solution.py:379
  104.0 7.6 %collective-permute-start.48 = (f32[1,64,256]{2,1,0:T(8,128)S(1)}, f32[1,64,256]{2,1,0:T(8,128)S(1)}, u32[]{:S(2)}, u32[]{:S(2)}) collective-permute-start(f32[1,64,256]{2,1,0:T(8,128)S(1)} %slice_add_fusion.8), channel_id=1, source_target_pairs={{0,8},{2,10},{4,12},{6,14},{8,0},{10,2},{12,4},{14,6},{1,9},{3,11}... | collective-permute-start | bytes 196616 | tf_op jit(solution)/shard_map/ppermute | solution.py:379
  111.7 21.1 %collective-permute-start.49 = (f32[1,64,256]{2,1,0:T(8,128)S(1)}, f32[1,64,256]{2,1,0:T(8,128)S(1)}, u32[]{:S(2)}, u32[]{:S(2)}) collective-permute-start(f32[1,64,256]{2,1,0:T(8,128)S(1)} %add.134.refs_9_), channel_id=1, source_target_pairs={{0,4},{2,6},{4,0},{6,2},{8,12},{10,14},{12,8},{14,10},{1,5},{3,7},... | collective-permute-start | bytes 196616 | tf_op jit(solution)/shard_map/ppermute | solution.py:379
  113.3 21.4 %collective-permute-start.45 = (f32[2,64,256]{2,1,0:T(8,128)S(1)}, f32[2,64,256]{2,1,0:T(8,128)S(1)}, u32[]{:S(2)}, u32[]{:S(2)}) collective-permute-start(f32[2,64,256]{2,1,0:T(8,128)S(1)} %pad_maximum_fusion.6), channel_id=1, source_target_pairs={{0,4},{2,6},{4,0},{6,2},{8,12},{10,14},{12,8},{14,10},{1,5},{3,7},... | collective-permute-start | bytes 393224 | tf_op jit(solution)/shard_map/ppermute | solution.py:379
  116.0 18.8 %collective-permute-start.40 = (f32[2,64,256]{2,1,0:T(8,128)S(1)}, f32[2,64,256]{2,1,0:T(8,128)S(1)}, u32[]{:S(2)}, u32[]{:S(2)}) collective-permute-start(f32[2,64,256]{2,1,0:T(8,128)S(1)} %pad_maximum_fusion.5), channel_id=1, source_target_pairs={{0,2},{2,0},{4,6},{6,4},{8,10},{10,8},{12,14},{14,12},{1,3},{3,1},... | collective-permute-start | bytes 393224 | tf_op jit(solution)/shard_map/ppermute | solution.py:379
  118.3 11.2 %collective-permute-start.34 = (f32[2,128,128]{2,1,0:T(8,128)S(1)}, f32[2,128,128]{2,1,0:T(8,128)S(1)}, u32[]{:S(2)}, u32[]{:S(2)}) collective-permute-start(f32[2,128,128]{2,1,0:T(8,128)S(1)} %slice_select_fusion.2), channel_id=1, source_target_pairs={{2,4},{4,2},{6,8},{8,6},{10,12},{12,10},{3,5},{5,3},{7,9},{9,7},{1... | collective-permute-start | bytes 393224 | tf_op jit(solution)/shard_map/ppermute | solution.py:369
  121.7 5.9 %collective-permute-start.52 = (f32[1,64,256]{2,1,0:T(8,128)S(1)}, f32[1,64,256]{2,1,0:T(8,128)S(1)}, u32[]{:S(2)}, u32[]{:S(2)}) collective-permute-start(f32[1,64,256]{2,1,0:T(8,128)S(1)} %slice_add_fusion.14), channel_id=1, source_target_pairs={{0,8},{2,10},{4,12},{6,14},{8,0},{10,2},{12,4},{14,6},{1,9},{3,11}... | collective-permute-start | bytes 196616 | tf_op jit(solution)/shard_map/ppermute | solution.py:379
  132.7 7.6 %collective-permute-start.35 = (f32[2,2,128,128]{3,2,1,0:T(8,128)S(1)}, f32[2,2,128,128]{3,2,1,0:T(8,128)S(1)}, u32[]{:S(2)}, u32[]{:S(2)}) collective-permute-start(f32[2,2,128,128]{3,2,1,0:T(8,128)S(1)} %maximum_add_fusion.refs_0_), channel_id=1, source_target_pairs={{0,1},{1,0},{2,3},{3,2},{4,5},{5,4},{6,7},{7,6},{8,9},{9,8},{10,11... | collective-permute-start | bytes 786440 | tf_op jit(solution)/shard_map/ppermute | solution.py:360
  132.8 6.0 %collective-permute-start.50 = (f32[2,64,256]{2,1,0:T(8,128)S(1)}, f32[2,64,256]{2,1,0:T(8,128)S(1)}, u32[]{:S(2)}, u32[]{:S(2)}) collective-permute-start(f32[2,64,256]{2,1,0:T(8,128)S(1)} %pad_maximum_fusion.7), channel_id=1, source_target_pairs={{0,2},{2,0},{4,6},{6,4},{8,10},{10,8},{12,14},{14,12},{1,3},{3,1},... | collective-permute-start | bytes 393224 | tf_op jit(solution)/shard_map/ppermute | solution.py:379
  (29 other events, 110.0 us)

commit v6 on v5

--- a/solution.py
+++ b/solution.py
@@ -105,14 +105,13 @@
 
 def update_probe(old, streams, coef, out):
     rows = old.shape[2] // CHUNKS
-    for i, pieces in enumerate(streams):
-        mode, part = divmod(i, 2)
-        key = chunk_key(ORDERS[part])
+    for mode, pieces in enumerate(streams):
+        key = chunk_key(ORDERS[mode])
         rel = 0
         for piece in pieces:
             for k in range(piece.shape[0]):
                 here = pl.ds(pl.multiple_of((rel ^ key) * rows, rows), rows)
-                out[mode, part, here, :] = old[mode, part, here, :] + coef * piece[k]
+                out[mode, :, here, :] = old[mode, :, here, :] + coef * piece[k]
                 rel += 1
 
 
@@ -155,8 +154,8 @@
     refs = refs[5:]
     modes = probe.shape[0]
     if n_pieces:
-        streams = grouped(refs, 2 * modes, n_pieces)
-        refs = refs[2 * modes * n_pieces :]
+        streams = grouped(refs, modes, n_pieces)
+        refs = refs[modes * n_pieces :]
         new_probe = refs.pop(3)
         update_probe(probe, streams, coef, new_probe)
         probe = new_probe
@@ -219,8 +218,7 @@
     fars, powers, others, patches = (refs[i * slots : (i + 1) * slots] for i in range(4))
     refs = refs[4 * slots :]
     before = refs.pop(0) if mode else None
-    probe_grad, refs = refs[:2], refs[2:]
-    grads, tall_parts, wide_parts, product_wide, product_tall = refs
+    probe_grad, grads, tall_parts, wide_parts, product_wide, product_tall = refs
     frame = probe.shape[-1]
     h = frame // 2
 
@@ -255,7 +253,7 @@
     strips(h // STRIP, columns)
     for p in range(2):
         product_tall[p] = mul_left(tab[1, p], tall_parts[p])
-    keys = [chunk_key(o) for o in ORDERS]
+    key = chunk_key(ORDERS[mode])
     chunk = frame // CHUNKS
     core = lax.axis_index("row")
     first = left_half()
@@ -291,7 +289,7 @@
                     window[k] = g if s == 0 else window[k] + g
             start = lower * h + j * STRIP
             for k in range(2):
-                probe_grad[k][(start // chunk) ^ keys[k], at(start % chunk), :] = step[k]
+                probe_grad[(start // chunk) ^ key, k, at(start % chunk), :] = step[k]
                 if last and not tall:
                     half = window[k].shape[1] // 2
                     grads[lower ^ core, first, k, at(j * STRIP), :] = window[k][:, :half]
@@ -324,7 +322,7 @@
 def finish_kernel(n_pieces, coef, *refs):
     refs = list(refs)
     near, away, probe = refs[:3]
-    streams = grouped(refs[3:], 2 * probe.shape[0], n_pieces)
+    streams = grouped(refs[3:], probe.shape[0], n_pieces)
     tile, new_probe = refs[-2:]
     update_probe(probe, streams, coef, new_probe)
     _, _, hr, half = near.shape
@@ -395,37 +393,32 @@
     return jnp.concatenate([jnp.where(own_first, own, other), jnp.where(own_first, other, own)], -1)
 
 
-def window_sum(grad, even, tiles, tall, wide):
+def window_parts(grad, even, wide):
     if wide:
-        got = [beside(grad[1], False, tiles), beside(grad[0], True, tiles)]
-        total = jnp.stack([grad[0] + got[1], grad[1] + got[0]])
-        return total + swap_vertical(total, tiles) if tall else total
-    own, other = zip(*(halves(grad[k], even, k == 0) for k in range(2)))
-    got = [beside(other[1], False, tiles), beside(other[0], True, tiles)]
-    return jnp.stack([own[0] + got[1], own[1] + got[0]])
-
-
-def reduce_all(parts, grad, tiles, window):
+        return [grad[0], grad[1]], [grad[0], grad[1]]
+    return zip(*(halves(grad[k], even, k == 0) for k in range(2)))
+
+
+def reduce_all(parts, grad, even, tiles, wide):
     bits = int(math.log2(tiles))
     held = list(parts)
-    orders = [ORDERS[i % 2] for i in range(len(parts))]
-    near = None
+    stay, go = window_parts(grad, even, wide)
+    go = list(go)
+    got = [None, None]
     for i in range(HALVINGS):
         n = held[0].shape[0] // 2
-        got = [exchange(h[n:], o[i], tiles) for h, o in zip(held, orders)]
-        held = [h[:n] + g for h, g in zip(held, got)]
-        if i == 0:
-            held[-1], grad = together(held[-1], grad)
-            near = window(grad)
-    got = [exchange(h, o[-1], tiles) for h, o in zip(held, orders)]
-    held = [h + g for h, g in zip(held, got)]
+        held = [h[:n] + exchange(h[n:], o[i], tiles) for h, o in zip(held, ORDERS)]
+        held[-1], go[1 - i] = together(held[-1], go[1 - i])
+        got[1 - i] = beside(go[1 - i], i == 1, tiles)
+    total = jnp.stack([stay[0] + got[0], stay[1] + got[1]])
+    held = [h + exchange(h, o[-1], tiles) for h, o in zip(held, ORDERS)]
     for bit in range(len(ORDERS[0]), bits):
         held = [h + exchange(h, bit, tiles) for h in held]
     pieces = [[h] for h in held]
     for i in reversed(range(HALVINGS)):
-        for p, o in zip(pieces, orders):
+        for p, o in zip(pieces, ORDERS):
             p.append(exchange(p[0] if len(p) == 1 else jnp.concatenate(p, 0), o[i], tiles))
-    return pieces, near
+    return pieces, total
 
 
 def per_device(object_tiles, probe_modes, amplitude, offsets, counts):
@@ -497,22 +490,24 @@
             if m:
                 args.append(before)
             grads = (2,) + near.shape if last and not tall else (slots, 2, frame, frame)
-            part = (CHUNKS, frame // CHUNKS, frame)
+            part = (CHUNKS, 2, frame // CHUNKS, frame)
             got = call(
                 functools.partial(inverse_kernel, m, last, tall),
-                [part, part, grads],
+                [part, grads],
                 args,
                 scratch(slots)
                 + [pltpu.VMEM((2, slots * frame, frame), f32), pltpu.VMEM((2, frame, slots * frame), f32)],
                 matmul * slots,
             )
-            parts += got[:2]
-            before = got[2]
+            parts.append(got[0])
+            before = got[1]
         if tall:
             (before,) = call(place_kernel, [(2,) + near.shape], [offsets, before])
         grad = before[0] + swap_rows(before[1])
         wide = tall or not final
-        streams, total = reduce_all(parts, grad, tiles, lambda g: window_sum(g, even, tiles, tall, wide))
+        streams, total = reduce_all(parts, grad, even, tiles, wide)
+        if tall:
+            total = total + swap_vertical(total, tiles)
         if wide:
             near = near + total / MODES
         if final:

time: 142 us -> 133 us (0.937)
  starting transfers between devices: 60.4 us -> 36.4 us
  waiting for transfers between devices: 55.8 us -> 71.4 us
    ppermute x40 -> x20, waiting for transfers between devices: 42.1 us -> 66.7 us  [exchange(): return lax.ppermute(x, 'tile', [(s, s ^ 1 << bit) for s in range(tiles)])]
    ppermute x40 -> x20, starting transfers between devices: 50 us -> 27 us  [exchange(): return lax.ppermute(x, 'tile', [(s, s ^ 1 << bit) for s in range(tiles)])]
    ppermute x6, waiting for transfers between devices: 11.7 us -> 2.84 us  [beside(): return lax.ppermute(x, 'tile', pairs)]
  transfers between devices with their start and end apart: 55 -> 35, of which waited for: 31 -> 19; matrix products, arithmetic and copies ran while one was open for 1% -> 1% of each run, Pallas kernels for 2% -> 4%
where the time goes in v6:
time: 133 us
  waiting for transfers between devices  71.4 us (54%)
  starting transfers between devices  36.4 us (27%)
  Pallas kernels  20.2 us (15%)
  local copies, waits for them, and re-layouts  2.38 us (2%)
  between operations  1.81 us (1%)
    ppermute x20, waiting for transfers between devices, exchange(): return lax.ppermute(x, 'tile', [(s, s ^ 1 << bit) for s in range(tiles)])  66.7 us
    ppermute x20, starting transfers between devices, exchange(): return lax.ppermute(x, 'tile', [(s, s ^ 1 << bit) for s in range(tiles)])  27 us
    pallas_call x10, Pallas kernels, call(): pl.pallas_call(kernel, out_shape=[jax.ShapeDtypeStruct(o, f32) for o in o...  20.2 us
    ppermute x6, starting transfers between devices, beside(): return lax.ppermute(x, 'tile', pairs)  7.67 us
    ppermute x6, waiting for transfers between devices, beside(): return lax.ppermute(x, 'tile', pairs)  2.84 us
  transfers between devices with their start and end apart: 35, of which 19 were waited for; matrix products, arithmetic and copies ran while one was open for 1% of the time, Pallas kernels for 4%

profile of v6, /device:TPU:0, one launch (start us, length us, event | category | flops | bytes accessed | tf_op | source)
XLA Modules:
  0.0 133.2 jit_solution(5571371139301435698)
XLA Ops:
  1.7 3.0 %collective-permute-start = (f32[2,128,128]{2,1,0:T(8,128)S(1)}, f32[2,128,128]{2,1,0:T(8,128)S(1)}, u32[]{:S(2)}, u32[]{:S(2)}) collective-permute-start(f32[2,128,128]{2,1,0:T(8,128)S(1)} %get-tuple-element.80), channel_id=1, source_target_pairs={{0,2},{2,0},{4,6},{6,4},{8,10},{10,8},{12,14},{14,12},{1,3},{3,1},... | collective-permute-start | bytes 393224 | tf_op jit(solution)/shard_map/ppermute | solution.py:367
  5.4 2.8 %collective-permute-done = f32[2,128,128]{2,1,0:T(8,128)S(1)} collective-permute-done((f32[2,128,128]{2,1,0:T(8,128)S(1)}, f32[2,128,128]{2,1,0:T(8,128)S(1)}, u32[]{:S(2)}, u32[]{:S(2)}) %collective-permute-start) | collective-permute-done | bytes 131104 | tf_op jit(solution)/shard_map/ppermute | solution.py:367
  10.5 2.1 %shard_map.88 = (f32[2,2,256,256]{3,2,1,0:T(8,128)S(1)}, f32[256,256]{1,0:T(8,128)S(1)}, f32[2,256,256]{2,1,0:T(8,128)S(1)}) custom-call(s32[2,2]{1,0:T(2,128)S(1)} %copy-done.4, f32[2,2,128,256]{3,2,1,0:T(8,128)S(1)} %pad_maximum_fusion.refs_1_, f32[2,2,128,256]{3,2,1,0:T(8,128)S(1)} %collective-permute-done.2.refs_2_, f32[2,2,256,256]{3,2,1,0:T(8,128)S(1)} %copy-done.3, ...), custom_call_target="tpu_custom_call" | custom-call | flops 3221225472 | bytes 4980752 | tf_op jit(solution)/shard_map/pallas_call | solution.py:344
  12.5 2.1 %shard_map.87 = (f32[2,2,256,256]{3,2,1,0:T(8,128)S(1)}, f32[256,256]{1,0:T(8,128)S(1)}, f32[2,256,256]{2,1,0:T(8,128)S(1)}) custom-call(s32[2,2]{1,0:T(2,128)S(1)} %copy-done.4, f32[2,2,128,256]{3,2,1,0:T(8,128)S(1)} %pad_maximum_fusion.refs_1_, f32[2,2,128,256]{3,2,1,0:T(8,128)S(1)} %collective-permute-done.2.refs_2_, f32[2,2,256,256]{3,2,1,0:T(8,128)S(1)} %copy-done.3, ...), custom_call_target="tpu_custom_call" | custom-call | flops 3221225472 | bytes 4980752 | tf_op jit(solution)/shard_map/pallas_call | solution.py:344
  16.6 2.3 %shard_map.89 = (f32[4,2,64,256]{3,2,1,0:T(8,128)S(1)}, f32[2,2,256,256]{3,2,1,0:T(8,128)S(1)}) custom-call(s32[2,2]{1,0:T(2,128)S(1)} %copy-done.4, s32[1]{0:T(128)S(6)} %copy.9.refs_1_, bf16[2,2,2,256,256]{4,3,2,1,0:T(8,128)(2,1)S(1)} %copy-done.5, f32[2,256,256]{2,1,0:T(8,128)S(1)} %shard_map.86.refs_3_, f32[2,2,256,256]{3,2,1,0:T(8,128)S(1)} %copy-done.3, ...), custom_call_target="tpu_custom_call" | custom-call | flops 3221225472 | bytes 8388628 | tf_op jit(solution)/shard_map/pallas_call | solution.py:344
  18.9 2.6 %shard_map.90 = (f32[4,2,64,256]{3,2,1,0:T(8,128)S(1)}, f32[2,2,2,128,256]{4,3,2,1,0:T(8,128)S(1)}) custom-call(s32[2,2]{1,0:T(2,128)S(1)} %copy-done.4, s32[1]{0:T(128)S(6)} %copy.9.refs_1_, bf16[2,2,2,256,256]{4,3,2,1,0:T(8,128)(2,1)S(1)} %copy-done.5, f32[2,256,256]{2,1,0:T(8,128)S(1)} %shard_map.86.refs_3_, f32[2,2,256,256]{3,2,1,0:T(8,128)S(1)} %copy-done.3, ...), custom_call_target="tpu_custom_call" | custom-call | flops 3221225472 | bytes 9437204 | tf_op jit(solution)/shard_map/pallas_call | solution.py:344
  21.8 5.9 %collective-permute-start.6 = (f32[2,2,64,256]{3,2,1,0:T(8,128)S(1)}, f32[2,2,64,256]{3,2,1,0:T(8,128)S(1)}, u32[]{:S(2)}, u32[]{:S(2)}) collective-permute-start(f32[2,2,64,256]{3,2,1,0:T(8,128)S(1)} %slice.118), channel_id=1, source_target_pairs={{0,4},{2,6},{4,0},{6,2},{8,12},{10,14},{12,8},{14,10},{1,5},{3,7},... | collective-permute-start | bytes 786440 | tf_op jit(solution)/shard_map/ppermute | solution.py:377
  28.3 6.2 %collective-permute-done.6 = f32[2,2,64,256]{3,2,1,0:T(8,128)S(1)} collective-permute-done((f32[2,2,64,256]{3,2,1,0:T(8,128)S(1)}, f32[2,2,64,256]{3,2,1,0:T(8,128)S(1)}, u32[]{:S(2)}, u32[]{:S(2)}) %collective-permute-start.6) | collective-permute-done | bytes 262176 | tf_op jit(solution)/shard_map/ppermute | solution.py:377
  38.0 2.0 %collective-permute-done.7 = f32[1,2,64,256]{3,2,1,0:T(8,128)S(1)} collective-permute-done((f32[1,2,64,256]{3,2,1,0:T(8,128)S(1)}, f32[1,2,64,256]{3,2,1,0:T(8,128)S(1)}, u32[]{:S(2)}, u32[]{:S(2)}) %collective-permute-start.7) | collective-permute-done | bytes 131104 | tf_op jit(solution)/shard_map/ppermute | solution.py:377
  40.0 1.9 %collective-permute-start.8 = (f32[2,128,256]{2,1,0:T(8,128)S(1)}, f32[2,128,256]{2,1,0:T(8,128)S(1)}, u32[]{:S(2)}, u32[]{:S(2)}) collective-permute-start(f32[2,128,256]{2,1,0:T(8,128)S(1)} %get-tuple-element.49), channel_id=1, source_target_pairs={{0,2},{2,0},{4,6},{6,4},{8,10},{10,8},{12,14},{14,12},{1,3},{3,1},... | collective-permute-start | bytes 786440 | tf_op jit(solution)/shard_map/ppermute | solution.py:367
  41.9 2.7 %collective-permute-start.13 = (f32[1,2,64,256]{3,2,1,0:T(8,128)S(1)}, f32[1,2,64,256]{3,2,1,0:T(8,128)S(1)}, u32[]{:S(2)}, u32[]{:S(2)}) collective-permute-start(f32[1,2,64,256]{3,2,1,0:T(8,128)S(1)} %slice_add_fusion.5), channel_id=1, source_target_pairs={{0,8},{2,10},{4,12},{6,14},{8,0},{10,2},{12,4},{14,6},{1,9},{3,11}... | collective-permute-start | bytes 393224 | tf_op jit(solution)/shard_map/ppermute | solution.py:377
  44.5 8.0 %collective-permute-done.13 = f32[1,2,64,256]{3,2,1,0:T(8,128)S(1)} collective-permute-done((f32[1,2,64,256]{3,2,1,0:T(8,128)S(1)}, f32[1,2,64,256]{3,2,1,0:T(8,128)S(1)}, u32[]{:S(2)}, u32[]{:S(2)}) %collective-permute-start.13) | collective-permute-done | bytes 131104 | tf_op jit(solution)/shard_map/ppermute | solution.py:377
  53.9 7.0 %collective-permute-done.16 = f32[1,2,64,256]{3,2,1,0:T(8,128)S(1)} collective-permute-done((f32[1,2,64,256]{3,2,1,0:T(8,128)S(1)}, f32[1,2,64,256]{3,2,1,0:T(8,128)S(1)}, u32[]{:S(2)}, u32[]{:S(2)}) %collective-permute-start.16) | collective-permute-done | bytes 131104 | tf_op jit(solution)/shard_map/ppermute | solution.py:377
  61.7 1.4 %collective-permute-start.15 = (f32[2,2,64,256]{3,2,1,0:T(8,128)S(1)}, f32[2,2,64,256]{3,2,1,0:T(8,128)S(1)}, u32[]{:S(2)}, u32[]{:S(2)}) collective-permute-start(f32[2,2,64,256]{3,2,1,0:T(8,128)S(1)} %pad_maximum_fusion.1), channel_id=1, source_target_pairs={{0,2},{2,0},{4,6},{6,4},{8,10},{10,8},{12,14},{14,12},{1,3},{3,1},... | collective-permute-start | bytes 786440 | tf_op jit(solution)/shard_map/ppermute | solution.py:377
  63.1 2.9 %collective-permute-done.17.refs_9_ = f32[1,2,64,256]{3,2,1,0:T(8,128)S(1)} collective-permute-done((f32[1,2,64,256]{3,2,1,0:T(8,128)S(1)}, f32[1,2,64,256]{3,2,1,0:T(8,128)S(1)}, u32[]{:S(2)}, u32[]{:S(2)}) %collective-permute-start.17) | collective-permute-done | bytes 131104 | tf_op jit(solution)/shard_map/ppermute | solution.py:377
  66.1 2.7 %collective-permute-done.15.refs_7_ = f32[2,2,64,256]{3,2,1,0:T(8,128)S(1)} collective-permute-done((f32[2,2,64,256]{3,2,1,0:T(8,128)S(1)}, f32[2,2,64,256]{3,2,1,0:T(8,128)S(1)}, u32[]{:S(2)}, u32[]{:S(2)}) %collective-permute-start.15) | collective-permute-done | bytes 262176 | tf_op jit(solution)/shard_map/ppermute | solution.py:377
  68.8 3.6 %collective-permute-done.18.refs_10_ = f32[2,2,64,256]{3,2,1,0:T(8,128)S(1)} collective-permute-done((f32[2,2,64,256]{3,2,1,0:T(8,128)S(1)}, f32[2,2,64,256]{3,2,1,0:T(8,128)S(1)}, u32[]{:S(2)}, u32[]{:S(2)}) %collective-permute-start.18) | collective-permute-done | bytes 262176 | tf_op jit(solution)/shard_map/ppermute | solution.py:377
  72.5 2.1 %shard_map.91 = (f32[2,2,256,256]{3,2,1,0:T(8,128)S(1)}, f32[256,256]{1,0:T(8,128)S(1)}, f32[2,256,256]{2,1,0:T(8,128)S(1)}, f32[2,2,256,256]{3,2,1,0:T(8,128)S(1)}) custom-call(s32[2,2]{1,0:T(2,128)S(1)} %copy-done.4, f32[2,2,128,256]{3,2,1,0:T(8,128)S(1)} %fusion.refs_1_, f32[2,2,128,256]{3,2,1,0:T(8,128)S(1)} %collective-permute-done.10.refs_2_, ...), custom_call_target="tpu_custom_call" | custom-call | flops 3221225472 | bytes 7077904 | tf_op jit(solution)/shard_map/pallas_call | solution.py:344
  74.7 2.1 %shard_map.92 = (f32[2,2,256,256]{3,2,1,0:T(8,128)S(1)}, f32[256,256]{1,0:T(8,128)S(1)}, f32[2,256,256]{2,1,0:T(8,128)S(1)}) custom-call(s32[2,2]{1,0:T(2,128)S(1)} %copy-done.4, f32[2,2,128,256]{3,2,1,0:T(8,128)S(1)} %fusion.refs_1_, f32[2,2,128,256]{3,2,1,0:T(8,128)S(1)} %collective-permute-done.10.refs_2_, ...), custom_call_target="tpu_custom_call" | custom-call | flops 3221225472 | bytes 4980752 | tf_op jit(solution)/shard_map/pallas_call | solution.py:344
  78.5 2.3 %shard_map.93 = (f32[4,2,64,256]{3,2,1,0:T(8,128)S(1)}, f32[2,2,256,256]{3,2,1,0:T(8,128)S(1)}) custom-call(s32[2,2]{1,0:T(2,128)S(1)} %copy-done.4, s32[1]{0:T(128)S(6)} %copy.9.refs_1_, bf16[2,2,2,256,256]{4,3,2,1,0:T(8,128)(2,1)S(1)} %copy-done.5, f32[2,256,256]{2,1,0:T(8,128)S(1)} %shard_map.86.refs_3_, ...), custom_call_target="tpu_custom_call" | custom-call | flops 3221225472 | bytes 8388628 | tf_op jit(solution)/shard_map/pallas_call | solution.py:344
  81.8 2.6 %shard_map.94 = (f32[4,2,64,256]{3,2,1,0:T(8,128)S(1)}, f32[2,2,2,128,256]{4,3,2,1,0:T(8,128)S(1)}) custom-call(s32[2,2]{1,0:T(2,128)S(1)} %copy-done.4, s32[1]{0:T(128)S(6)} %copy.9.refs_1_, bf16[2,2,2,256,256]{4,3,2,1,0:T(8,128)(2,1)S(1)} %copy-done.5, f32[2,256,256]{2,1,0:T(8,128)S(1)} %shard_map.86.refs_3_, ...), custom_call_target="tpu_custom_call" | custom-call | flops 3221225472 | bytes 9437204 | tf_op jit(solution)/shard_map/pallas_call | solution.py:344
  85.0 4.4 %collective-permute-done.27 = f32[2,2,64,256]{3,2,1,0:T(8,128)S(1)} collective-permute-done((f32[2,2,64,256]{3,2,1,0:T(8,128)S(1)}, f32[2,2,64,256]{3,2,1,0:T(8,128)S(1)}, u32[]{:S(2)}, u32[]{:S(2)}) %collective-permute-start.27) | collective-permute-done | bytes 262176 | tf_op jit(solution)/shard_map/ppermute | solution.py:377
  89.6 6.0 %collective-permute-done.28 = f32[1,2,64,256]{3,2,1,0:T(8,128)S(1)} collective-permute-done((f32[1,2,64,256]{3,2,1,0:T(8,128)S(1)}, f32[1,2,64,256]{3,2,1,0:T(8,128)S(1)}, u32[]{:S(2)}, u32[]{:S(2)}) %collective-permute-start.28) | collective-permute-done | bytes 131104 | tf_op jit(solution)/shard_map/ppermute | solution.py:377
  95.6 2.6 %collective-permute-start.29 = (f32[1,2,64,256]{3,2,1,0:T(8,128)S(1)}, f32[1,2,64,256]{3,2,1,0:T(8,128)S(1)}, u32[]{:S(2)}, u32[]{:S(2)}) collective-permute-start(f32[1,2,64,256]{3,2,1,0:T(8,128)S(1)} %slice_add_fusion.4), channel_id=1, source_target_pairs={{0,8},{2,10},{4,12},{6,14},{8,0},{10,2},{12,4},{14,6},{1,9},{3,11}... | collective-permute-start | bytes 393224 | tf_op jit(solution)/shard_map/ppermute | solution.py:377
  98.2 5.8 %collective-permute-done.29 = f32[1,2,64,256]{3,2,1,0:T(8,128)S(1)} collective-permute-done((f32[1,2,64,256]{3,2,1,0:T(8,128)S(1)}, f32[1,2,64,256]{3,2,1,0:T(8,128)S(1)}, u32[]{:S(2)}, u32[]{:S(2)}) %collective-permute-start.29) | collective-permute-done | bytes 131104 | tf_op jit(solution)/shard_map/ppermute | solution.py:377
  106.2 3.2 %collective-permute-done.30.refs_4_ = f32[1,2,64,256]{3,2,1,0:T(8,128)S(1)} collective-permute-done((f32[1,2,64,256]{3,2,1,0:T(8,128)S(1)}, f32[1,2,64,256]{3,2,1,0:T(8,128)S(1)}, u32[]{:S(2)}, u32[]{:S(2)}) %collective-permute-start.30) | collective-permute-done | bytes 131104 | tf_op jit(solution)/shard_map/ppermute | solution.py:377
  109.4 1.6 %collective-permute-start.31 = (f32[2,2,64,256]{3,2,1,0:T(8,128)S(1)}, f32[2,2,64,256]{3,2,1,0:T(8,128)S(1)}, u32[]{:S(2)}, u32[]{:S(2)}) collective-permute-start(f32[2,2,64,256]{3,2,1,0:T(8,128)S(1)} %pad_maximum_fusion.3), channel_id=1, source_target_pairs={{0,2},{2,0},{4,6},{6,4},{8,10},{10,8},{12,14},{14,12},{1,3},{3,1},... | collective-permute-start | bytes 786440 | tf_op jit(solution)/shard_map/ppermute | solution.py:377
  111.6 3.9 %collective-permute-start.32 = (f32[1,2,64,256]{3,2,1,0:T(8,128)S(1)}, f32[1,2,64,256]{3,2,1,0:T(8,128)S(1)}, u32[]{:S(2)}, u32[]{:S(2)}) collective-permute-start(f32[1,2,64,256]{3,2,1,0:T(8,128)S(1)} %slice_add_fusion.6), channel_id=1, source_target_pairs={{0,8},{2,10},{4,12},{6,14},{8,0},{10,2},{12,4},{14,6},{1,9},{3,11}... | collective-permute-start | bytes 393224 | tf_op jit(solution)/shard_map/ppermute | solution.py:377
  115.5 4.2 %collective-permute-done.32 = f32[1,2,64,256]{3,2,1,0:T(8,128)S(1)} collective-permute-done((f32[1,2,64,256]{3,2,1,0:T(8,128)S(1)}, f32[1,2,64,256]{3,2,1,0:T(8,128)S(1)}, u32[]{:S(2)}, u32[]{:S(2)}) %collective-permute-start.32) | collective-permute-done | bytes 131104 | tf_op jit(solution)/shard_map/ppermute | solution.py:377
  120.9 3.9 %collective-permute-done.33.refs_7_ = f32[1,2,64,256]{3,2,1,0:T(8,128)S(1)} collective-permute-done((f32[1,2,64,256]{3,2,1,0:T(8,128)S(1)}, f32[1,2,64,256]{3,2,1,0:T(8,128)S(1)}, u32[]{:S(2)}, u32[]{:S(2)}) %collective-permute-start.33) | collective-permute-done | bytes 131104 | tf_op jit(solution)/shard_map/ppermute | solution.py:377
  125.9 5.9 %collective-permute-done.34.refs_8_ = f32[2,2,64,256]{3,2,1,0:T(8,128)S(1)} collective-permute-done((f32[2,2,64,256]{3,2,1,0:T(8,128)S(1)}, f32[2,2,64,256]{3,2,1,0:T(8,128)S(1)}, u32[]{:S(2)}, u32[]{:S(2)}) %collective-permute-start.34) | collective-permute-done | bytes 262176 | tf_op jit(solution)/shard_map/ppermute | solution.py:377
  131.9 1.3 shard_map.95
  (106 shorter events, 20.3 us)
Async XLA Ops:
  1.7 6.5 %collective-permute-start = (f32[2,128,128]{2,1,0:T(8,128)S(1)}, f32[2,128,128]{2,1,0:T(8,128)S(1)}, u32[]{:S(2)}, u32[]{:S(2)}) collective-permute-start(f32[2,128,128]{2,1,0:T(8,128)S(1)} %get-tuple-element.80), channel_id=1, source_target_pairs={{0,2},{2,0},{4,6},{6,4},{8,10},{10,8},{12,14},{14,12},{1,3},{3,1},... | collective-permute-start | bytes 393224 | tf_op jit(solution)/shard_map/ppermute | solution.py:367
  4.8 3.5 %collective-permute-start.1 = (f32[2,128,128]{2,1,0:T(8,128)S(1)}, f32[2,128,128]{2,1,0:T(8,128)S(1)}, u32[]{:S(2)}, u32[]{:S(2)}) collective-permute-start(f32[2,128,128]{2,1,0:T(8,128)S(1)} %get-tuple-element.81), channel_id=1, source_target_pairs={{2,4},{4,2},{6,8},{8,6},{10,12},{12,10},{3,5},{5,3},{7,9},{9,7},{1... | collective-permute-start | bytes 393224 | tf_op jit(solution)/shard_map/ppermute | solution.py:367
  8.5 2.0 %collective-permute-start.2 = (f32[2,2,128,256]{3,2,1,0:T(8,128)S(1)}, f32[2,2,128,256]{3,2,1,0:T(8,128)S(1)}, u32[]{:S(2)}, u32[]{:S(2)}) collective-permute-start(f32[2,2,128,256]{3,2,1,0:T(8,128)S(1)} %pad_maximum_fusion.refs_1_), channel_id=1, source_target_pairs={{0,1},{1,0},{2,3},{3,2},{4,5},{5,4},{6,7},{7,6},{8,9},{9,8},{10,11... | collective-permute-start | bytes 1572872 | tf_op jit(solution)/shard_map/ppermute | solution.py:358
  21.6 13.0 %collective-permute-start.5 = (f32[2,2,128,256]{3,2,1,0:T(8,128)S(1)}, f32[2,2,128,256]{3,2,1,0:T(8,128)S(1)}, u32[]{:S(2)}, u32[]{:S(2)}) collective-permute-start(f32[2,2,128,256]{3,2,1,0:T(8,128)S(1)} %slice_bitcast_fusion.1), channel_id=1, source_target_pairs={{0,1},{1,0},{2,3},{3,2},{4,5},{5,4},{6,7},{7,6},{8,9},{9,8},{10,11... | collective-permute-start | bytes 1572872 | tf_op jit(solution)/shard_map/ppermute | solution.py:358
  21.8 12.7 %collective-permute-start.6 = (f32[2,2,64,256]{3,2,1,0:T(8,128)S(1)}, f32[2,2,64,256]{3,2,1,0:T(8,128)S(1)}, u32[]{:S(2)}, u32[]{:S(2)}) collective-permute-start(f32[2,2,64,256]{3,2,1,0:T(8,128)S(1)} %slice.118), channel_id=1, source_target_pairs={{0,4},{2,6},{4,0},{6,2},{8,12},{10,14},{12,8},{14,10},{1,5},{3,7},... | collective-permute-start | bytes 786440 | tf_op jit(solution)/shard_map/ppermute | solution.py:377
  27.7 8.4 %collective-permute-start.11 = (f32[2,2,64,256]{3,2,1,0:T(8,128)S(1)}, f32[2,2,64,256]{3,2,1,0:T(8,128)S(1)}, u32[]{:S(2)}, u32[]{:S(2)}) collective-permute-start(f32[2,2,64,256]{3,2,1,0:T(8,128)S(1)} %slice.129), channel_id=1, source_target_pairs={{0,2},{2,0},{4,6},{6,4},{8,10},{10,8},{12,14},{14,12},{1,3},{3,1},... | collective-permute-start | bytes 786440 | tf_op jit(solution)/shard_map/ppermute | solution.py:377
  34.7 5.3 %collective-permute-start.7 = (f32[1,2,64,256]{3,2,1,0:T(8,128)S(1)}, f32[1,2,64,256]{3,2,1,0:T(8,128)S(1)}, u32[]{:S(2)}, u32[]{:S(2)}) collective-permute-start(f32[1,2,64,256]{3,2,1,0:T(8,128)S(1)} %slice.121), channel_id=1, source_target_pairs={{0,2},{2,0},{4,6},{6,4},{8,10},{10,8},{12,14},{14,12},{1,3},{3,1},... | collective-permute-start | bytes 393224 | tf_op jit(solution)/shard_map/ppermute | solution.py:377
  36.1 5.7 %collective-permute-start.12 = (f32[1,2,64,256]{3,2,1,0:T(8,128)S(1)}, f32[1,2,64,256]{3,2,1,0:T(8,128)S(1)}, u32[]{:S(2)}, u32[]{:S(2)}) collective-permute-start(f32[1,2,64,256]{3,2,1,0:T(8,128)S(1)} %slice.159), channel_id=1, source_target_pairs={{0,4},{2,6},{4,0},{6,2},{8,12},{10,14},{12,8},{14,10},{1,5},{3,7},... | collective-permute-start | bytes 393224 | tf_op jit(solution)/shard_map/ppermute | solution.py:377
  37.1 16.5 %collective-permute-start.9 = (f32[2,128,256]{2,1,0:T(8,128)S(1)}, f32[2,128,256]{2,1,0:T(8,128)S(1)}, u32[]{:S(2)}, u32[]{:S(2)}) collective-permute-start(f32[2,128,256]{2,1,0:T(8,128)S(1)} %get-tuple-element.50), channel_id=1, source_target_pairs={{2,4},{4,2},{6,8},{8,6},{10,12},{12,10},{3,5},{5,3},{7,9},{9,7},{1... | collective-permute-start | bytes 786440 | tf_op jit(solution)/shard_map/ppermute | solution.py:367
  40.0 13.7 %collective-permute-start.8 = (f32[2,128,256]{2,1,0:T(8,128)S(1)}, f32[2,128,256]{2,1,0:T(8,128)S(1)}, u32[]{:S(2)}, u32[]{:S(2)}) collective-permute-start(f32[2,128,256]{2,1,0:T(8,128)S(1)} %get-tuple-element.49), channel_id=1, source_target_pairs={{0,2},{2,0},{4,6},{6,4},{8,10},{10,8},{12,14},{14,12},{1,3},{3,1},... | collective-permute-start | bytes 786440 | tf_op jit(solution)/shard_map/ppermute | solution.py:367
  41.9 10.7 %collective-permute-start.13 = (f32[1,2,64,256]{3,2,1,0:T(8,128)S(1)}, f32[1,2,64,256]{3,2,1,0:T(8,128)S(1)}, u32[]{:S(2)}, u32[]{:S(2)}) collective-permute-start(f32[1,2,64,256]{3,2,1,0:T(8,128)S(1)} %slice_add_fusion.5), channel_id=1, source_target_pairs={{0,8},{2,10},{4,12},{6,14},{8,0},{10,2},{12,4},{14,6},{1,9},{3,11}... | collective-permute-start | bytes 393224 | tf_op jit(solution)/shard_map/ppermute | solution.py:377
  52.6 9.1 %collective-permute-start.14 = (f32[1,2,64,256]{3,2,1,0:T(8,128)S(1)}, f32[1,2,64,256]{3,2,1,0:T(8,128)S(1)}, u32[]{:S(2)}, u32[]{:S(2)}) collective-permute-start(f32[1,2,64,256]{3,2,1,0:T(8,128)S(1)} %add.77.refs_5_), channel_id=1, source_target_pairs={{0,4},{2,6},{4,0},{6,2},{8,12},{10,14},{12,8},{14,10},{1,5},{3,7},... | collective-permute-start | bytes 393224 | tf_op jit(solution)/shard_map/ppermute | solution.py:377
  53.7 7.3 %collective-permute-start.16 = (f32[1,2,64,256]{3,2,1,0:T(8,128)S(1)}, f32[1,2,64,256]{3,2,1,0:T(8,128)S(1)}, u32[]{:S(2)}, u32[]{:S(2)}) collective-permute-start(f32[1,2,64,256]{3,2,1,0:T(8,128)S(1)} %slice_add_fusion.7), channel_id=1, source_target_pairs={{0,8},{2,10},{4,12},{6,14},{8,0},{10,2},{12,4},{14,6},{1,9},{3,11}... | collective-permute-start | bytes 393224 | tf_op jit(solution)/shard_map/ppermute | solution.py:377
  53.8 18.6 %collective-permute-start.10 = (f32[2,2,128,256]{3,2,1,0:T(8,128)S(1)}, f32[2,2,128,256]{3,2,1,0:T(8,128)S(1)}, u32[]{:S(2)}, u32[]{:S(2)}) collective-permute-start(f32[2,2,128,256]{3,2,1,0:T(8,128)S(1)} %fusion.refs_1_), channel_id=1, source_target_pairs={{0,1},{1,0},{2,3},{3,2},{4,5},{5,4},{6,7},{7,6},{8,9},{9,8},{10,11... | collective-permute-start | bytes 1572872 | tf_op jit(solution)/shard_map/ppermute | solution.py:358
  61.0 5.0 %collective-permute-start.17 = (f32[1,2,64,256]{3,2,1,0:T(8,128)S(1)}, f32[1,2,64,256]{3,2,1,0:T(8,128)S(1)}, u32[]{:S(2)}, u32[]{:S(2)}) collective-permute-start(f32[1,2,64,256]{3,2,1,0:T(8,128)S(1)} %add.78.refs_8_), channel_id=1, source_target_pairs={{0,2},{2,0},{4,6},{6,4},{8,10},{10,8},{12,14},{14,12},{1,3},{3,1},... | collective-permute-start | bytes 393224 | tf_op jit(solution)/shard_map/ppermute | solution.py:377
  61.7 7.1 %collective-permute-start.15 = (f32[2,2,64,256]{3,2,1,0:T(8,128)S(1)}, f32[2,2,64,256]{3,2,1,0:T(8,128)S(1)}, u32[]{:S(2)}, u32[]{:S(2)}) collective-permute-start(f32[2,2,64,256]{3,2,1,0:T(8,128)S(1)} %pad_maximum_fusion.1), channel_id=1, source_target_pairs={{0,2},{2,0},{4,6},{6,4},{8,10},{10,8},{12,14},{14,12},{1,3},{3,1},... | collective-permute-start | bytes 786440 | tf_op jit(solution)/shard_map/ppermute | solution.py:377
  66.0 6.4 %collective-permute-start.18 = (f32[2,2,64,256]{3,2,1,0:T(8,128)S(1)}, f32[2,2,64,256]{3,2,1,0:T(8,128)S(1)}, u32[]{:S(2)}, u32[]{:S(2)}) collective-permute-start(f32[2,2,64,256]{3,2,1,0:T(8,128)S(1)} %pad_maximum_fusion.2), channel_id=1, source_target_pairs={{0,4},{2,6},{4,0},{6,2},{8,12},{10,14},{12,8},{14,10},{1,5},{3,7},... | collective-permute-start | bytes 786440 | tf_op jit(solution)/shard_map/ppermute | solution.py:377
  74.6 2.8 %collective-permute-start.19 = (f32[256,256]{1,0:T(8,128)S(1)}, f32[256,256]{1,0:T(8,128)S(1)}, u32[]{:S(2)}, u32[]{:S(2)}) collective-permute-start(f32[256,256]{1,0:T(8,128)S(1)} %get-tuple-element.56.refs_7_), channel_id=1, source_target_pairs={{0,1},{1,0},{2,3},{3,2},{4,5},{5,4},{6,7},{7,6},{8,9},{9,8},{10,11... | collective-permute-start | bytes 786440 | tf_op jit(solution)/shard_map/ppermute | solution.py:358
  80.8 8.7 %collective-permute-start.27 = (f32[2,2,64,256]{3,2,1,0:T(8,128)S(1)}, f32[2,2,64,256]{3,2,1,0:T(8,128)S(1)}, u32[]{:S(2)}, u32[]{:S(2)}) collective-permute-start(f32[2,2,64,256]{3,2,1,0:T(8,128)S(1)} %slice.145), channel_id=1, source_target_pairs={{0,2},{2,0},{4,6},{6,4},{8,10},{10,8},{12,14},{14,12},{1,3},{3,1},... | collective-permute-start | bytes 786440 | tf_op jit(solution)/shard_map/ppermute | solution.py:377
  84.4 13.7 %collective-permute-start.22 = (f32[2,2,64,256]{3,2,1,0:T(8,128)S(1)}, f32[2,2,64,256]{3,2,1,0:T(8,128)S(1)}, u32[]{:S(2)}, u32[]{:S(2)}) collective-permute-start(f32[2,2,64,256]{3,2,1,0:T(8,128)S(1)} %slice.138), channel_id=1, source_target_pairs={{0,4},{2,6},{4,0},{6,2},{8,12},{10,14},{12,8},{14,10},{1,5},{3,7},... | collective-permute-start | bytes 786440 | tf_op jit(solution)/shard_map/ppermute | solution.py:377
  85.0 19.2 %collective-permute-start.21 = (f32[2,2,128,256]{3,2,1,0:T(8,128)S(1)}, f32[2,2,128,256]{3,2,1,0:T(8,128)S(1)}, u32[]{:S(2)}, u32[]{:S(2)}) collective-permute-start(f32[2,2,128,256]{3,2,1,0:T(8,128)S(1)} %slice_bitcast_fusion), channel_id=1, source_target_pairs={{0,1},{1,0},{2,3},{3,2},{4,5},{5,4},{6,7},{7,6},{8,9},{9,8},{10,11... | collective-permute-start | bytes 1572872 | tf_op jit(solution)/shard_map/ppermute | solution.py:358
  89.5 6.1 %collective-permute-start.28 = (f32[1,2,64,256]{3,2,1,0:T(8,128)S(1)}, f32[1,2,64,256]{3,2,1,0:T(8,128)S(1)}, u32[]{:S(2)}, u32[]{:S(2)}) collective-permute-start(f32[1,2,64,256]{3,2,1,0:T(8,128)S(1)} %slice.167), channel_id=1, source_target_pairs={{0,4},{2,6},{4,0},{6,2},{8,12},{10,14},{12,8},{14,10},{1,5},{3,7},... | collective-permute-start | bytes 393224 | tf_op jit(solution)/shard_map/ppermute | solution.py:377
  95.6 8.4 %collective-permute-start.29 = (f32[1,2,64,256]{3,2,1,0:T(8,128)S(1)}, f32[1,2,64,256]{3,2,1,0:T(8,128)S(1)}, u32[]{:S(2)}, u32[]{:S(2)}) collective-permute-start(f32[1,2,64,256]{3,2,1,0:T(8,128)S(1)} %slice_add_fusion.4), channel_id=1, source_target_pairs={{0,8},{2,10},{4,12},{6,14},{8,0},{10,2},{12,4},{14,6},{1,9},{3,11}... | collective-permute-start | bytes 393224 | tf_op jit(solution)/shard_map/ppermute | solution.py:377
  104.0 5.4 %collective-permute-start.30 = (f32[1,2,64,256]{3,2,1,0:T(8,128)S(1)}, f32[1,2,64,256]{3,2,1,0:T(8,128)S(1)}, u32[]{:S(2)}, u32[]{:S(2)}) collective-permute-start(f32[1,2,64,256]{3,2,1,0:T(8,128)S(1)} %add.87.refs_3_), channel_id=1, source_target_pairs={{0,4},{2,6},{4,0},{6,2},{8,12},{10,14},{12,8},{14,10},{1,5},{3,7},... | collective-permute-start | bytes 393224 | tf_op jit(solution)/shard_map/ppermute | solution.py:377
  104.3 6.7 %collective-permute-start.23 = (f32[1,2,64,256]{3,2,1,0:T(8,128)S(1)}, f32[1,2,64,256]{3,2,1,0:T(8,128)S(1)}, u32[]{:S(2)}, u32[]{:S(2)}) collective-permute-start(f32[1,2,64,256]{3,2,1,0:T(8,128)S(1)} %slice.143), channel_id=1, source_target_pairs={{0,2},{2,0},{4,6},{6,4},{8,10},{10,8},{12,14},{14,12},{1,3},{3,1},... | collective-permute-start | bytes 393224 | tf_op jit(solution)/shard_map/ppermute | solution.py:377
  105.5 10.0 %collective-permute-start.25 = (f32[2,128,128]{2,1,0:T(8,128)S(1)}, f32[2,128,128]{2,1,0:T(8,128)S(1)}, u32[]{:S(2)}, u32[]{:S(2)}) collective-permute-start(f32[2,128,128]{2,1,0:T(8,128)S(1)} %slice_select_fusion.2), channel_id=1, source_target_pairs={{2,4},{4,2},{6,8},{8,6},{10,12},{12,10},{3,5},{5,3},{7,9},{9,7},{1... | collective-permute-start | bytes 393224 | tf_op jit(solution)/shard_map/ppermute | solution.py:367
  109.4 16.5 %collective-permute-start.31 = (f32[2,2,64,256]{3,2,1,0:T(8,128)S(1)}, f32[2,2,64,256]{3,2,1,0:T(8,128)S(1)}, u32[]{:S(2)}, u32[]{:S(2)}) collective-permute-start(f32[2,2,64,256]{3,2,1,0:T(8,128)S(1)} %pad_maximum_fusion.3), channel_id=1, source_target_pairs={{0,2},{2,0},{4,6},{6,4},{8,10},{10,8},{12,14},{14,12},{1,3},{3,1},... | collective-permute-start | bytes 786440 | tf_op jit(solution)/shard_map/ppermute | solution.py:377
  111.0 9.8 %collective-permute-start.24 = (f32[2,128,128]{2,1,0:T(8,128)S(1)}, f32[2,128,128]{2,1,0:T(8,128)S(1)}, u32[]{:S(2)}, u32[]{:S(2)}) collective-permute-start(f32[2,128,128]{2,1,0:T(8,128)S(1)} %slice_select_fusion.3), channel_id=1, source_target_pairs={{0,2},{2,0},{4,6},{6,4},{8,10},{10,8},{12,14},{14,12},{1,3},{3,1},... | collective-permute-start | bytes 393224 | tf_op jit(solution)/shard_map/ppermute | solution.py:367
  111.6 8.1 %collective-permute-start.32 = (f32[1,2,64,256]{3,2,1,0:T(8,128)S(1)}, f32[1,2,64,256]{3,2,1,0:T(8,128)S(1)}, u32[]{:S(2)}, u32[]{:S(2)}) collective-permute-start(f32[1,2,64,256]{3,2,1,0:T(8,128)S(1)} %slice_add_fusion.6), channel_id=1, source_target_pairs={{0,8},{2,10},{4,12},{6,14},{8,0},{10,2},{12,4},{14,6},{1,9},{3,11}... | collective-permute-start | bytes 393224 | tf_op jit(solution)/shard_map/ppermute | solution.py:377
  119.8 5.0 %collective-permute-start.33 = (f32[1,2,64,256]{3,2,1,0:T(8,128)S(1)}, f32[1,2,64,256]{3,2,1,0:T(8,128)S(1)}, u32[]{:S(2)}, u32[]{:S(2)}) collective-permute-start(f32[1,2,64,256]{3,2,1,0:T(8,128)S(1)} %add.88.refs_6_), channel_id=1, source_target_pairs={{0,2},{2,0},{4,6},{6,4},{8,10},{10,8},{12,14},{14,12},{1,3},{3,1},... | collective-permute-start | bytes 393224 | tf_op jit(solution)/shard_map/ppermute | solution.py:377
  120.8 5.1 %collective-permute-start.26 = (f32[2,2,128,128]{3,2,1,0:T(8,128)S(1)}, f32[2,2,128,128]{3,2,1,0:T(8,128)S(1)}, u32[]{:S(2)}, u32[]{:S(2)}) collective-permute-start(f32[2,2,128,128]{3,2,1,0:T(8,128)S(1)} %maximum_add_fusion.refs_0_), channel_id=1, source_target_pairs={{0,1},{1,0},{2,3},{3,2},{4,5},{5,4},{6,7},{7,6},{8,9},{9,8},{10,11... | collective-permute-start | bytes 786440 | tf_op jit(solution)/shard_map/ppermute | solution.py:358
  124.8 7.1 %collective-permute-start.34 = (f32[2,2,64,256]{3,2,1,0:T(8,128)S(1)}, f32[2,2,64,256]{3,2,1,0:T(8,128)S(1)}, u32[]{:S(2)}, u32[]{:S(2)}) collective-permute-start(f32[2,2,64,256]{3,2,1,0:T(8,128)S(1)} %pad_maximum_fusion.4), channel_id=1, source_target_pairs={{0,4},{2,6},{4,0},{6,2},{8,12},{10,14},{12,8},{14,10},{1,5},{3,7},... | collective-permute-start | bytes 786440 | tf_op jit(solution)/shard_map/ppermute | solution.py:377
  (9 other events, 14.6 us)

commit v7 on v6

--- a/solution.py
+++ b/solution.py
@@ -12,8 +12,8 @@
 MODES = 4
 GX = 8
 ITERS = 2
-HALVINGS = 2
-CHUNKS = 1 << HALVINGS
+BLOCK_BITS = 2
+CHUNKS = 1 << BLOCK_BITS
 STRIP = 16
 ORDERS = ((0, 1, 2), (1, 0, 2))
 
@@ -88,9 +88,8 @@
         out[s] = dot(high, perm[0]) + (dot(mid, perm[0]) + dot(low, perm[0]))
 
 
-def chunk_key(order):
-    t = lax.axis_index("tile")
-    return sum(((t >> order[i]) & 1) << (HALVINGS - 1 - i) for i in range(HALVINGS))
+def chunk_key():
+    return lax.rem(lax.axis_index("tile"), CHUNKS)
 
 
 def corner(offsets, slot, dim, size, margin):
@@ -105,8 +104,8 @@
 
 def update_probe(old, streams, coef, out):
     rows = old.shape[2] // CHUNKS
+    key = chunk_key()
     for mode, pieces in enumerate(streams):
-        key = chunk_key(ORDERS[mode])
         rel = 0
         for piece in pieces:
             for k in range(piece.shape[0]):
@@ -253,7 +252,7 @@
     strips(h // STRIP, columns)
     for p in range(2):
         product_tall[p] = mul_left(tab[1, p], tall_parts[p])
-    key = chunk_key(ORDERS[mode])
+    key = chunk_key()
     chunk = frame // CHUNKS
     core = lax.axis_index("row")
     first = left_half()
@@ -373,8 +372,8 @@
     return lax.ppermute(x, ("tile", "row"), pairs)
 
 
-def exchange(x, bit, tiles):
-    return lax.ppermute(x, "tile", [(s, s ^ (1 << bit)) for s in range(tiles)])
+def exchange(x, mask, tiles):
+    return lax.ppermute(x, "tile", [(s, s ^ mask) for s in range(tiles)])
 
 
 def together(*groups):
@@ -400,25 +399,23 @@
 
 
 def reduce_all(parts, grad, even, tiles, wide):
-    bits = int(math.log2(tiles))
-    held = list(parts)
     stay, go = window_parts(grad, even, wide)
-    go = list(go)
-    got = [None, None]
-    for i in range(HALVINGS):
-        n = held[0].shape[0] // 2
-        held = [h[:n] + exchange(h[n:], o[i], tiles) for h, o in zip(held, ORDERS)]
-        held[-1], go[1 - i] = together(held[-1], go[1 - i])
-        got[1 - i] = beside(go[1 - i], i == 1, tiles)
-    total = jnp.stack([stay[0] + got[0], stay[1] + got[1]])
-    held = [h + exchange(h, o[-1], tiles) for h, o in zip(held, ORDERS)]
-    for bit in range(len(ORDERS[0]), bits):
-        held = [h + exchange(h, bit, tiles) for h in held]
-    pieces = [[h] for h in held]
-    for i in reversed(range(HALVINGS)):
-        for p, o in zip(pieces, ORDERS):
-            p.append(exchange(p[0] if len(p) == 1 else jnp.concatenate(p, 0), o[i], tiles))
-    return pieces, total
+    got = [[p[:1]] + [exchange(p[k : k + 1], k, tiles) for k in range(1, CHUNKS)] for p in parts]
+    streams = []
+    for m in range(len(parts)):
+        held = sum(got[m][1:], got[m][0])
+        if m == 0:
+            held, go = together(held, tuple(go))
+            outer = beside(go[1], False, tiles)
+            inner = beside(go[0], True, tiles)
+        mask = CHUNKS
+        while mask < tiles:
+            held = held + exchange(held, mask, tiles)
+            mask *= 2
+        if m + 1 < len(parts):
+            held, got[m + 1] = together(held, got[m + 1])
+        streams.append([held] + [exchange(held, k, tiles) for k in range(1, CHUNKS)])
+    return streams, jnp.stack([stay[0] + inner, stay[1] + outer])
 
 
 def per_device(object_tiles, probe_modes, amplitude, offsets, counts):

time: 133 us -> 132 us (level)
  waiting for transfers between devices: 71.4 us -> 46.8 us
  starting transfers between devices: 36.4 us -> 60.2 us
    ppermute x20 -> x28, waiting for transfers between devices: 66.7 us -> 31.1 us  [exchange(): return lax.ppermute(x, 'tile', [(s, s ^ mask) for s in range(tiles)])]
    ppermute x20 -> x28, starting transfers between devices: 27 us -> 51.4 us  [exchange(): return lax.ppermute(x, 'tile', [(s, s ^ mask) for s in range(tiles)])]
    ppermute x6, waiting for transfers between devices: 2.84 us -> 13.7 us  [beside(): return lax.ppermute(x, 'tile', pairs)]
  transfers between devices with their start and end apart: 35 -> 43, of which waited for: 19 -> 21; matrix products, arithmetic and copies ran while one was open for 1% -> 1% of each run, Pallas kernels for 4% -> 2%
where the time goes in v7:
time: 132 us
  starting transfers between devices  60.2 us (46%)
  waiting for transfers between devices  46.8 us (35%)
  Pallas kernels  20.1 us (15%)
  local copies, waits for them, and re-layouts  2.39 us (2%)
  between operations  1.78 us (1%)
    ppermute x28, starting transfers between devices, exchange(): return lax.ppermute(x, 'tile', [(s, s ^ mask) for s in range(tiles)])  51.4 us
    ppermute x28, waiting for transfers between devices, exchange(): return lax.ppermute(x, 'tile', [(s, s ^ mask) for s in range(tiles)])  31.1 us
    pallas_call x10, Pallas kernels, call(): pl.pallas_call(kernel, out_shape=[jax.ShapeDtypeStruct(o, f32) for o in o...  20.1 us
    ppermute x6, waiting for transfers between devices, beside(): return lax.ppermute(x, 'tile', pairs)  13.7 us
    ppermute x6, starting transfers between devices, beside(): return lax.ppermute(x, 'tile', pairs)  6.73 us
  transfers between devices with their start and end apart: 43, of which 21 were waited for; matrix products, arithmetic and copies ran while one was open for 1% of the time, Pallas kernels for 2%

profile of v7, /device:TPU:0, one launch (start us, length us, event | category | flops | bytes accessed | tf_op | source)
XLA Modules:
  0.0 132.0 jit_solution(10777188786706671272)
XLA Ops:
  1.7 3.0 %collective-permute-start = (f32[2,128,128]{2,1,0:T(8,128)S(1)}, f32[2,128,128]{2,1,0:T(8,128)S(1)}, u32[]{:S(2)}, u32[]{:S(2)}) collective-permute-start(f32[2,128,128]{2,1,0:T(8,128)S(1)} %get-tuple-element.110), channel_id=1, source_target_pairs={{0,2},{2,0},{4,6},{6,4},{8,10},{10,8},{12,14},{14,12},{1,3},{3,1},... | collective-permute-start | bytes 393224 | tf_op jit(solution)/shard_map/ppermute | solution.py:366
  5.4 2.8 %collective-permute-done = f32[2,128,128]{2,1,0:T(8,128)S(1)} collective-permute-done((f32[2,128,128]{2,1,0:T(8,128)S(1)}, f32[2,128,128]{2,1,0:T(8,128)S(1)}, u32[]{:S(2)}, u32[]{:S(2)}) %collective-permute-start) | collective-permute-done | bytes 131104 | tf_op jit(solution)/shard_map/ppermute | solution.py:366
  10.5 2.1 %shard_map.87 = (f32[2,2,256,256]{3,2,1,0:T(8,128)S(1)}, f32[256,256]{1,0:T(8,128)S(1)}, f32[2,256,256]{2,1,0:T(8,128)S(1)}) custom-call(s32[2,2]{1,0:T(2,128)S(1)} %copy-done.4, f32[2,2,128,256]{3,2,1,0:T(8,128)S(1)} %pad_maximum_fusion.refs_1_, f32[2,2,128,256]{3,2,1,0:T(8,128)S(1)} %collective-permute-done.2.refs_2_, f32[2,2,256,256]{3,2,1,0:T(8,128)S(1)} %copy-done.3, ...), custom_call_target="tpu_custom_call" | custom-call | flops 3221225472 | bytes 4980752 | tf_op jit(solution)/shard_map/pallas_call | solution.py:343
  12.5 2.1 %shard_map.88 = (f32[2,2,256,256]{3,2,1,0:T(8,128)S(1)}, f32[256,256]{1,0:T(8,128)S(1)}, f32[2,256,256]{2,1,0:T(8,128)S(1)}) custom-call(s32[2,2]{1,0:T(2,128)S(1)} %copy-done.4, f32[2,2,128,256]{3,2,1,0:T(8,128)S(1)} %pad_maximum_fusion.refs_1_, f32[2,2,128,256]{3,2,1,0:T(8,128)S(1)} %collective-permute-done.2.refs_2_, f32[2,2,256,256]{3,2,1,0:T(8,128)S(1)} %copy-done.3, ...), custom_call_target="tpu_custom_call" | custom-call | flops 3221225472 | bytes 4980752 | tf_op jit(solution)/shard_map/pallas_call | solution.py:343
  16.6 2.3 %shard_map.89 = (f32[4,2,64,256]{3,2,1,0:T(8,128)S(1)}, f32[2,2,256,256]{3,2,1,0:T(8,128)S(1)}) custom-call(s32[2,2]{1,0:T(2,128)S(1)} %copy-done.4, s32[1]{0:T(128)S(6)} %copy.9.refs_1_, bf16[2,2,2,256,256]{4,3,2,1,0:T(8,128)(2,1)S(1)} %copy-done.5, f32[2,256,256]{2,1,0:T(8,128)S(1)} %shard_map.86.refs_3_, f32[2,2,256,256]{3,2,1,0:T(8,128)S(1)} %copy-done.3, ...), custom_call_target="tpu_custom_call" | custom-call | flops 3221225472 | bytes 8388628 | tf_op jit(solution)/shard_map/pallas_call | solution.py:343
  18.9 2.6 %shard_map.90 = (f32[4,2,64,256]{3,2,1,0:T(8,128)S(1)}, f32[2,2,2,128,256]{4,3,2,1,0:T(8,128)S(1)}) custom-call(s32[2,2]{1,0:T(2,128)S(1)} %copy-done.4, s32[1]{0:T(128)S(6)} %copy.9.refs_1_, bf16[2,2,2,256,256]{4,3,2,1,0:T(8,128)(2,1)S(1)} %copy-done.5, f32[2,256,256]{2,1,0:T(8,128)S(1)} %shard_map.86.refs_3_, f32[2,2,256,256]{3,2,1,0:T(8,128)S(1)} %copy-done.3, ...), custom_call_target="tpu_custom_call" | custom-call | flops 3221225472 | bytes 9437204 | tf_op jit(solution)/shard_map/pallas_call | solution.py:343
  21.8 5.8 %collective-permute-start.8 = (f32[1,2,64,256]{3,2,1,0:T(8,128)S(1)}, f32[1,2,64,256]{3,2,1,0:T(8,128)S(1)}, u32[]{:S(2)}, u32[]{:S(2)}) collective-permute-start(f32[1,2,64,256]{3,2,1,0:T(8,128)S(1)} %get-tuple-element.106), channel_id=1, source_target_pairs={{0,6},{2,4},{4,2},{6,0},{8,14},{10,12},{12,10},{14,8},{1,7},{3,5},... | collective-permute-start | bytes 393224 | tf_op jit(solution)/shard_map/ppermute | solution.py:376
  29.1 2.8 %collective-permute-done.8 = f32[1,2,64,256]{3,2,1,0:T(8,128)S(1)} collective-permute-done((f32[1,2,64,256]{3,2,1,0:T(8,128)S(1)}, f32[1,2,64,256]{3,2,1,0:T(8,128)S(1)}, u32[]{:S(2)}, u32[]{:S(2)}) %collective-permute-start.8) | collective-permute-done | bytes 131104 | tf_op jit(solution)/shard_map/ppermute | solution.py:376
  31.9 2.5 %collective-permute-done.7 = f32[1,2,64,256]{3,2,1,0:T(8,128)S(1)} collective-permute-done((f32[1,2,64,256]{3,2,1,0:T(8,128)S(1)}, f32[1,2,64,256]{3,2,1,0:T(8,128)S(1)}, u32[]{:S(2)}, u32[]{:S(2)}) %collective-permute-start.7) | collective-permute-done | bytes 131104 | tf_op jit(solution)/shard_map/ppermute | solution.py:376
  37.1 4.5 %collective-permute-start.13 = (f32[1,2,64,256]{3,2,1,0:T(8,128)S(1)}, f32[1,2,64,256]{3,2,1,0:T(8,128)S(1)}, u32[]{:S(2)}, u32[]{:S(2)}) collective-permute-start(f32[1,2,64,256]{3,2,1,0:T(8,128)S(1)} %get-tuple-element.97), channel_id=1, source_target_pairs={{0,2},{2,0},{4,6},{6,4},{8,10},{10,8},{12,14},{14,12},{1,3},{3,1},... | collective-permute-start | bytes 393224 | tf_op jit(solution)/shard_map/ppermute | solution.py:376
  43.2 8.0 %collective-permute-done.9 = f32[2,128,256]{2,1,0:T(8,128)S(1)} collective-permute-done((f32[2,128,256]{2,1,0:T(8,128)S(1)}, f32[2,128,256]{2,1,0:T(8,128)S(1)}, u32[]{:S(2)}, u32[]{:S(2)}) %collective-permute-start.9) | collective-permute-done | bytes 262176 | tf_op jit(solution)/shard_map/ppermute | solution.py:366
  51.1 4.8 %collective-permute-start.12 = (f32[1,2,64,256]{3,2,1,0:T(8,128)S(1)}, f32[1,2,64,256]{3,2,1,0:T(8,128)S(1)}, u32[]{:S(2)}, u32[]{:S(2)}) collective-permute-start(f32[1,2,64,256]{3,2,1,0:T(8,128)S(1)} %add_add_fusion.3), channel_id=1, source_target_pairs={{0,8},{2,10},{4,12},{6,14},{8,0},{10,2},{12,4},{14,6},{1,9},{3,11}... | collective-permute-start | bytes 393224 | tf_op jit(solution)/shard_map/ppermute | solution.py:376
  56.2 2.7 %collective-permute-done.12 = f32[1,2,64,256]{3,2,1,0:T(8,128)S(1)} collective-permute-done((f32[1,2,64,256]{3,2,1,0:T(8,128)S(1)}, f32[1,2,64,256]{3,2,1,0:T(8,128)S(1)}, u32[]{:S(2)}, u32[]{:S(2)}) %collective-permute-start.12) | collective-permute-done | bytes 131104 | tf_op jit(solution)/shard_map/ppermute | solution.py:376
  59.0 3.1 %collective-permute-start.19 = (f32[1,2,64,256]{3,2,1,0:T(8,128)S(1)}, f32[1,2,64,256]{3,2,1,0:T(8,128)S(1)}, u32[]{:S(2)}, u32[]{:S(2)}) collective-permute-start(f32[1,2,64,256]{3,2,1,0:T(8,128)S(1)} %add_add_fusion.2), channel_id=1, source_target_pairs={{0,8},{2,10},{4,12},{6,14},{8,0},{10,2},{12,4},{14,6},{1,9},{3,11}... | collective-permute-start | bytes 393224 | tf_op jit(solution)/shard_map/ppermute | solution.py:376
  62.1 5.6 %collective-permute-start.17 = (f32[1,2,64,256]{3,2,1,0:T(8,128)S(1)}, f32[1,2,64,256]{3,2,1,0:T(8,128)S(1)}, u32[]{:S(2)}, u32[]{:S(2)}) collective-permute-start(f32[1,2,64,256]{3,2,1,0:T(8,128)S(1)} %add.88.refs_5_), channel_id=1, source_target_pairs={{0,4},{2,6},{4,0},{6,2},{8,12},{10,14},{12,8},{14,10},{1,5},{3,7},... | collective-permute-start | bytes 393224 | tf_op jit(solution)/shard_map/ppermute | solution.py:376
  69.8 2.8 %collective-permute-start.21 = (f32[1,2,64,256]{3,2,1,0:T(8,128)S(1)}, f32[1,2,64,256]{3,2,1,0:T(8,128)S(1)}, u32[]{:S(2)}, u32[]{:S(2)}) collective-permute-start(f32[1,2,64,256]{3,2,1,0:T(8,128)S(1)} %add.92.refs_9_), channel_id=1, source_target_pairs={{0,4},{2,6},{4,0},{6,2},{8,12},{10,14},{12,8},{14,10},{1,5},{3,7},... | collective-permute-start | bytes 393224 | tf_op jit(solution)/shard_map/ppermute | solution.py:376
  75.6 2.9 %collective-permute-done.22.refs_12_ = f32[1,2,64,256]{3,2,1,0:T(8,128)S(1)} collective-permute-done((f32[1,2,64,256]{3,2,1,0:T(8,128)S(1)}, f32[1,2,64,256]{3,2,1,0:T(8,128)S(1)}, u32[]{:S(2)}, u32[]{:S(2)}) %collective-permute-start.22) | collective-permute-done | bytes 131104 | tf_op jit(solution)/shard_map/ppermute | solution.py:376
  78.6 2.1 %shard_map.91 = (f32[2,2,256,256]{3,2,1,0:T(8,128)S(1)}, f32[256,256]{1,0:T(8,128)S(1)}, f32[2,256,256]{2,1,0:T(8,128)S(1)}, f32[2,2,256,256]{3,2,1,0:T(8,128)S(1)}) custom-call(s32[2,2]{1,0:T(2,128)S(1)} %copy-done.4, f32[2,2,128,256]{3,2,1,0:T(8,128)S(1)} %fusion.refs_1_, f32[2,2,128,256]{3,2,1,0:T(8,128)S(1)} %collective-permute-done.11.refs_2_, ...), custom_call_target="tpu_custom_call" | custom-call | flops 3221225472 | bytes 7077904 | tf_op jit(solution)/shard_map/pallas_call | solution.py:343
  80.8 2.1 %shard_map.92 = (f32[2,2,256,256]{3,2,1,0:T(8,128)S(1)}, f32[256,256]{1,0:T(8,128)S(1)}, f32[2,256,256]{2,1,0:T(8,128)S(1)}) custom-call(s32[2,2]{1,0:T(2,128)S(1)} %copy-done.4, f32[2,2,128,256]{3,2,1,0:T(8,128)S(1)} %fusion.refs_1_, f32[2,2,128,256]{3,2,1,0:T(8,128)S(1)} %collective-permute-done.11.refs_2_, ...), custom_call_target="tpu_custom_call" | custom-call | flops 3221225472 | bytes 4980752 | tf_op jit(solution)/shard_map/pallas_call | solution.py:343
  84.6 2.2 %shard_map.93 = (f32[4,2,64,256]{3,2,1,0:T(8,128)S(1)}, f32[2,2,256,256]{3,2,1,0:T(8,128)S(1)}) custom-call(s32[2,2]{1,0:T(2,128)S(1)} %copy-done.4, s32[1]{0:T(128)S(6)} %copy.9.refs_1_, bf16[2,2,2,256,256]{4,3,2,1,0:T(8,128)(2,1)S(1)} %copy-done.5, f32[2,256,256]{2,1,0:T(8,128)S(1)} %shard_map.86.refs_3_, ...), custom_call_target="tpu_custom_call" | custom-call | flops 3221225472 | bytes 8388628 | tf_op jit(solution)/shard_map/pallas_call | solution.py:343
  86.8 2.6 %shard_map.94 = (f32[4,2,64,256]{3,2,1,0:T(8,128)S(1)}, f32[2,2,2,128,256]{4,3,2,1,0:T(8,128)S(1)}) custom-call(s32[2,2]{1,0:T(2,128)S(1)} %copy-done.4, s32[1]{0:T(128)S(6)} %copy.9.refs_1_, bf16[2,2,2,256,256]{4,3,2,1,0:T(8,128)(2,1)S(1)} %copy-done.5, f32[2,256,256]{2,1,0:T(8,128)S(1)} %shard_map.86.refs_3_, ...), custom_call_target="tpu_custom_call" | custom-call | flops 3221225472 | bytes 9437204 | tf_op jit(solution)/shard_map/pallas_call | solution.py:343
  94.7 2.6 %collective-permute-done.28 = f32[1,2,64,256]{3,2,1,0:T(8,128)S(1)} collective-permute-done((f32[1,2,64,256]{3,2,1,0:T(8,128)S(1)}, f32[1,2,64,256]{3,2,1,0:T(8,128)S(1)}, u32[]{:S(2)}, u32[]{:S(2)}) %collective-permute-start.28) | collective-permute-done | bytes 131104 | tf_op jit(solution)/shard_map/ppermute | solution.py:376
  100.8 2.5 %collective-permute-start.32 = (f32[1,2,64,256]{3,2,1,0:T(8,128)S(1)}, f32[1,2,64,256]{3,2,1,0:T(8,128)S(1)}, u32[]{:S(2)}, u32[]{:S(2)}) collective-permute-start(f32[1,2,64,256]{3,2,1,0:T(8,128)S(1)} %add_add_fusion.1), channel_id=1, source_target_pairs={{0,8},{2,10},{4,12},{6,14},{8,0},{10,2},{12,4},{14,6},{1,9},{3,11}... | collective-permute-start | bytes 393224 | tf_op jit(solution)/shard_map/ppermute | solution.py:376
  104.1 6.0 %collective-permute-done.32 = f32[1,2,64,256]{3,2,1,0:T(8,128)S(1)} collective-permute-done((f32[1,2,64,256]{3,2,1,0:T(8,128)S(1)}, f32[1,2,64,256]{3,2,1,0:T(8,128)S(1)}, u32[]{:S(2)}, u32[]{:S(2)}) %collective-permute-start.32) | collective-permute-done | bytes 131104 | tf_op jit(solution)/shard_map/ppermute | solution.py:376
  110.1 1.9 %collective-permute-start.39 = (f32[1,2,64,256]{3,2,1,0:T(8,128)S(1)}, f32[1,2,64,256]{3,2,1,0:T(8,128)S(1)}, u32[]{:S(2)}, u32[]{:S(2)}) collective-permute-start(f32[1,2,64,256]{3,2,1,0:T(8,128)S(1)} %add_add_fusion), channel_id=1, source_target_pairs={{0,8},{2,10},{4,12},{6,14},{8,0},{10,2},{12,4},{14,6},{1,9},{3,11}... | collective-permute-start | bytes 393224 | tf_op jit(solution)/shard_map/ppermute | solution.py:376
  112.0 3.0 %collective-permute-done.29 = f32[2,128,128]{2,1,0:T(8,128)S(1)} collective-permute-done((f32[2,128,128]{2,1,0:T(8,128)S(1)}, f32[2,128,128]{2,1,0:T(8,128)S(1)}, u32[]{:S(2)}, u32[]{:S(2)}) %collective-permute-start.29) | collective-permute-done | bytes 131104 | tf_op jit(solution)/shard_map/ppermute | solution.py:366
  115.2 1.9 %collective-permute-start.37 = (f32[1,2,64,256]{3,2,1,0:T(8,128)S(1)}, f32[1,2,64,256]{3,2,1,0:T(8,128)S(1)}, u32[]{:S(2)}, u32[]{:S(2)}) collective-permute-start(f32[1,2,64,256]{3,2,1,0:T(8,128)S(1)} %add.100.refs_3_), channel_id=1, source_target_pairs={{0,4},{2,6},{4,0},{6,2},{8,12},{10,14},{12,8},{14,10},{1,5},{3,7},... | collective-permute-start | bytes 393224 | tf_op jit(solution)/shard_map/ppermute | solution.py:376
  117.1 1.6 %collective-permute-start.38 = (f32[1,2,64,256]{3,2,1,0:T(8,128)S(1)}, f32[1,2,64,256]{3,2,1,0:T(8,128)S(1)}, u32[]{:S(2)}, u32[]{:S(2)}) collective-permute-start(f32[1,2,64,256]{3,2,1,0:T(8,128)S(1)} %add.100.refs_3_), channel_id=1, source_target_pairs={{0,6},{2,4},{4,2},{6,0},{8,14},{10,12},{12,10},{14,8},{1,7},{3,5},... | collective-permute-start | bytes 393224 | tf_op jit(solution)/shard_map/ppermute | solution.py:376
  119.4 1.6 %collective-permute-done.36.refs_4_ = f32[1,2,64,256]{3,2,1,0:T(8,128)S(1)} collective-permute-done((f32[1,2,64,256]{3,2,1,0:T(8,128)S(1)}, f32[1,2,64,256]{3,2,1,0:T(8,128)S(1)}, u32[]{:S(2)}, u32[]{:S(2)}) %collective-permute-start.36) | collective-permute-done | bytes 131104 | tf_op jit(solution)/shard_map/ppermute | solution.py:376
  121.6 1.8 %collective-permute-start.42 = (f32[1,2,64,256]{3,2,1,0:T(8,128)S(1)}, f32[1,2,64,256]{3,2,1,0:T(8,128)S(1)}, u32[]{:S(2)}, u32[]{:S(2)}) collective-permute-start(f32[1,2,64,256]{3,2,1,0:T(8,128)S(1)} %add.104.refs_7_), channel_id=1, source_target_pairs={{0,6},{2,4},{4,2},{6,0},{8,14},{10,12},{12,10},{14,8},{1,7},{3,5},... | collective-permute-start | bytes 393224 | tf_op jit(solution)/shard_map/ppermute | solution.py:376
  123.4 2.4 %collective-permute-done.38.refs_6_ = f32[1,2,64,256]{3,2,1,0:T(8,128)S(1)} collective-permute-done((f32[1,2,64,256]{3,2,1,0:T(8,128)S(1)}, f32[1,2,64,256]{3,2,1,0:T(8,128)S(1)}, u32[]{:S(2)}, u32[]{:S(2)}) %collective-permute-start.38) | collective-permute-done | bytes 131104 | tf_op jit(solution)/shard_map/ppermute | solution.py:376
  127.5 3.2 %collective-permute-done.42.refs_10_ = f32[1,2,64,256]{3,2,1,0:T(8,128)S(1)} collective-permute-done((f32[1,2,64,256]{3,2,1,0:T(8,128)S(1)}, f32[1,2,64,256]{3,2,1,0:T(8,128)S(1)}, u32[]{:S(2)}, u32[]{:S(2)}) %collective-permute-start.42) | collective-permute-done | bytes 131104 | tf_op jit(solution)/shard_map/ppermute | solution.py:376
  (110 shorter events, 32.2 us)
Async XLA Ops:
  1.7 6.5 %collective-permute-start = (f32[2,128,128]{2,1,0:T(8,128)S(1)}, f32[2,128,128]{2,1,0:T(8,128)S(1)}, u32[]{:S(2)}, u32[]{:S(2)}) collective-permute-start(f32[2,128,128]{2,1,0:T(8,128)S(1)} %get-tuple-element.110), channel_id=1, source_target_pairs={{0,2},{2,0},{4,6},{6,4},{8,10},{10,8},{12,14},{14,12},{1,3},{3,1},... | collective-permute-start | bytes 393224 | tf_op jit(solution)/shard_map/ppermute | solution.py:366
  21.5 13.0 %collective-permute-start.5 = (f32[2,2,128,256]{3,2,1,0:T(8,128)S(1)}, f32[2,2,128,256]{3,2,1,0:T(8,128)S(1)}, u32[]{:S(2)}, u32[]{:S(2)}) collective-permute-start(f32[2,2,128,256]{3,2,1,0:T(8,128)S(1)} %slice_bitcast_fusion.1), channel_id=1, source_target_pairs={{0,1},{1,0},{2,3},{3,2},{4,5},{5,4},{6,7},{7,6},{8,9},{9,8},{10,11... | collective-permute-start | bytes 1572872 | tf_op jit(solution)/shard_map/ppermute | solution.py:357
  21.8 10.1 %collective-permute-start.8 = (f32[1,2,64,256]{3,2,1,0:T(8,128)S(1)}, f32[1,2,64,256]{3,2,1,0:T(8,128)S(1)}, u32[]{:S(2)}, u32[]{:S(2)}) collective-permute-start(f32[1,2,64,256]{3,2,1,0:T(8,128)S(1)} %get-tuple-element.106), channel_id=1, source_target_pairs={{0,6},{2,4},{4,2},{6,0},{8,14},{10,12},{12,10},{14,8},{1,7},{3,5},... | collective-permute-start | bytes 393224 | tf_op jit(solution)/shard_map/ppermute | solution.py:376
  27.6 6.9 %collective-permute-start.7 = (f32[1,2,64,256]{3,2,1,0:T(8,128)S(1)}, f32[1,2,64,256]{3,2,1,0:T(8,128)S(1)}, u32[]{:S(2)}, u32[]{:S(2)}) collective-permute-start(f32[1,2,64,256]{3,2,1,0:T(8,128)S(1)} %get-tuple-element.107), channel_id=1, source_target_pairs={{0,4},{2,6},{4,0},{6,2},{8,12},{10,14},{12,8},{14,10},{1,5},{3,7},... | collective-permute-start | bytes 393224 | tf_op jit(solution)/shard_map/ppermute | solution.py:376
  27.9 6.6 %collective-permute-start.6 = (f32[1,2,64,256]{3,2,1,0:T(8,128)S(1)}, f32[1,2,64,256]{3,2,1,0:T(8,128)S(1)}, u32[]{:S(2)}, u32[]{:S(2)}) collective-permute-start(f32[1,2,64,256]{3,2,1,0:T(8,128)S(1)} %get-tuple-element.105), channel_id=1, source_target_pairs={{0,2},{2,0},{4,6},{6,4},{8,10},{10,8},{12,14},{14,12},{1,3},{3,1},... | collective-permute-start | bytes 393224 | tf_op jit(solution)/shard_map/ppermute | solution.py:376
  34.6 16.5 %collective-permute-start.9 = (f32[2,128,256]{2,1,0:T(8,128)S(1)}, f32[2,128,256]{2,1,0:T(8,128)S(1)}, u32[]{:S(2)}, u32[]{:S(2)}) collective-permute-start(f32[2,128,256]{2,1,0:T(8,128)S(1)} %get-tuple-element.56), channel_id=1, source_target_pairs={{0,2},{2,0},{4,6},{6,4},{8,10},{10,8},{12,14},{14,12},{1,3},{3,1},... | collective-permute-start | bytes 786440 | tf_op jit(solution)/shard_map/ppermute | solution.py:366
  36.2 19.8 %collective-permute-start.10 = (f32[2,128,256]{2,1,0:T(8,128)S(1)}, f32[2,128,256]{2,1,0:T(8,128)S(1)}, u32[]{:S(2)}, u32[]{:S(2)}) collective-permute-start(f32[2,128,256]{2,1,0:T(8,128)S(1)} %get-tuple-element.57), channel_id=1, source_target_pairs={{2,4},{4,2},{6,8},{8,6},{10,12},{12,10},{3,5},{5,3},{7,9},{9,7},{1... | collective-permute-start | bytes 786440 | tf_op jit(solution)/shard_map/ppermute | solution.py:366
  37.1 21.9 %collective-permute-start.13 = (f32[1,2,64,256]{3,2,1,0:T(8,128)S(1)}, f32[1,2,64,256]{3,2,1,0:T(8,128)S(1)}, u32[]{:S(2)}, u32[]{:S(2)}) collective-permute-start(f32[1,2,64,256]{3,2,1,0:T(8,128)S(1)} %get-tuple-element.97), channel_id=1, source_target_pairs={{0,2},{2,0},{4,6},{6,4},{8,10},{10,8},{12,14},{14,12},{1,3},{3,1},... | collective-permute-start | bytes 393224 | tf_op jit(solution)/shard_map/ppermute | solution.py:376
  41.6 17.3 %collective-permute-start.14 = (f32[1,2,64,256]{3,2,1,0:T(8,128)S(1)}, f32[1,2,64,256]{3,2,1,0:T(8,128)S(1)}, u32[]{:S(2)}, u32[]{:S(2)}) collective-permute-start(f32[1,2,64,256]{3,2,1,0:T(8,128)S(1)} %get-tuple-element.96), channel_id=1, source_target_pairs={{0,4},{2,6},{4,0},{6,2},{8,12},{10,14},{12,8},{14,10},{1,5},{3,7},... | collective-permute-start | bytes 393224 | tf_op jit(solution)/shard_map/ppermute | solution.py:376
  43.2 15.8 %collective-permute-start.15 = (f32[1,2,64,256]{3,2,1,0:T(8,128)S(1)}, f32[1,2,64,256]{3,2,1,0:T(8,128)S(1)}, u32[]{:S(2)}, u32[]{:S(2)}) collective-permute-start(f32[1,2,64,256]{3,2,1,0:T(8,128)S(1)} %get-tuple-element.95), channel_id=1, source_target_pairs={{0,6},{2,4},{4,2},{6,0},{8,14},{10,12},{12,10},{14,8},{1,7},{3,5},... | collective-permute-start | bytes 393224 | tf_op jit(solution)/shard_map/ppermute | solution.py:376
  51.1 7.8 %collective-permute-start.12 = (f32[1,2,64,256]{3,2,1,0:T(8,128)S(1)}, f32[1,2,64,256]{3,2,1,0:T(8,128)S(1)}, u32[]{:S(2)}, u32[]{:S(2)}) collective-permute-start(f32[1,2,64,256]{3,2,1,0:T(8,128)S(1)} %add_add_fusion.3), channel_id=1, source_target_pairs={{0,8},{2,10},{4,12},{6,14},{8,0},{10,2},{12,4},{14,6},{1,9},{3,11}... | collective-permute-start | bytes 393224 | tf_op jit(solution)/shard_map/ppermute | solution.py:376
  56.1 22.5 %collective-permute-start.11 = (f32[2,2,128,256]{3,2,1,0:T(8,128)S(1)}, f32[2,2,128,256]{3,2,1,0:T(8,128)S(1)}, u32[]{:S(2)}, u32[]{:S(2)}) collective-permute-start(f32[2,2,128,256]{3,2,1,0:T(8,128)S(1)} %fusion.refs_1_), channel_id=1, source_target_pairs={{0,1},{1,0},{2,3},{3,2},{4,5},{5,4},{6,7},{7,6},{8,9},{9,8},{10,11... | collective-permute-start | bytes 1572872 | tf_op jit(solution)/shard_map/ppermute | solution.py:357
  59.0 10.2 %collective-permute-start.19 = (f32[1,2,64,256]{3,2,1,0:T(8,128)S(1)}, f32[1,2,64,256]{3,2,1,0:T(8,128)S(1)}, u32[]{:S(2)}, u32[]{:S(2)}) collective-permute-start(f32[1,2,64,256]{3,2,1,0:T(8,128)S(1)} %add_add_fusion.2), channel_id=1, source_target_pairs={{0,8},{2,10},{4,12},{6,14},{8,0},{10,2},{12,4},{14,6},{1,9},{3,11}... | collective-permute-start | bytes 393224 | tf_op jit(solution)/shard_map/ppermute | solution.py:376
  62.1 7.8 %collective-permute-start.16 = (f32[1,2,64,256]{3,2,1,0:T(8,128)S(1)}, f32[1,2,64,256]{3,2,1,0:T(8,128)S(1)}, u32[]{:S(2)}, u32[]{:S(2)}) collective-permute-start(f32[1,2,64,256]{3,2,1,0:T(8,128)S(1)} %add.88.refs_5_), channel_id=1, source_target_pairs={{0,2},{2,0},{4,6},{6,4},{8,10},{10,8},{12,14},{14,12},{1,3},{3,1},... | collective-permute-start | bytes 393224 | tf_op jit(solution)/shard_map/ppermute | solution.py:376
  62.1 10.6 %collective-permute-start.17 = (f32[1,2,64,256]{3,2,1,0:T(8,128)S(1)}, f32[1,2,64,256]{3,2,1,0:T(8,128)S(1)}, u32[]{:S(2)}, u32[]{:S(2)}) collective-permute-start(f32[1,2,64,256]{3,2,1,0:T(8,128)S(1)} %add.88.refs_5_), channel_id=1, source_target_pairs={{0,4},{2,6},{4,0},{6,2},{8,12},{10,14},{12,8},{14,10},{1,5},{3,7},... | collective-permute-start | bytes 393224 | tf_op jit(solution)/shard_map/ppermute | solution.py:376
  67.7 6.4 %collective-permute-start.18 = (f32[1,2,64,256]{3,2,1,0:T(8,128)S(1)}, f32[1,2,64,256]{3,2,1,0:T(8,128)S(1)}, u32[]{:S(2)}, u32[]{:S(2)}) collective-permute-start(f32[1,2,64,256]{3,2,1,0:T(8,128)S(1)} %add.88.refs_5_), channel_id=1, source_target_pairs={{0,6},{2,4},{4,2},{6,0},{8,14},{10,12},{12,10},{14,8},{1,7},{3,5},... | collective-permute-start | bytes 393224 | tf_op jit(solution)/shard_map/ppermute | solution.py:376
  89.4 11.2 %collective-permute-start.25 = (f32[2,2,128,256]{3,2,1,0:T(8,128)S(1)}, f32[2,2,128,256]{3,2,1,0:T(8,128)S(1)}, u32[]{:S(2)}, u32[]{:S(2)}) collective-permute-start(f32[2,2,128,256]{3,2,1,0:T(8,128)S(1)} %slice_bitcast_fusion), channel_id=1, source_target_pairs={{0,1},{1,0},{2,3},{3,2},{4,5},{5,4},{6,7},{7,6},{8,9},{9,8},{10,11... | collective-permute-start | bytes 1572872 | tf_op jit(solution)/shard_map/ppermute | solution.py:357
  89.9 7.3 %collective-permute-start.28 = (f32[1,2,64,256]{3,2,1,0:T(8,128)S(1)}, f32[1,2,64,256]{3,2,1,0:T(8,128)S(1)}, u32[]{:S(2)}, u32[]{:S(2)}) collective-permute-start(f32[1,2,64,256]{3,2,1,0:T(8,128)S(1)} %get-tuple-element.93), channel_id=1, source_target_pairs={{0,6},{2,4},{4,2},{6,0},{8,14},{10,12},{12,10},{14,8},{1,7},{3,5},... | collective-permute-start | bytes 393224 | tf_op jit(solution)/shard_map/ppermute | solution.py:376
  91.4 7.9 %collective-permute-start.27 = (f32[1,2,64,256]{3,2,1,0:T(8,128)S(1)}, f32[1,2,64,256]{3,2,1,0:T(8,128)S(1)}, u32[]{:S(2)}, u32[]{:S(2)}) collective-permute-start(f32[1,2,64,256]{3,2,1,0:T(8,128)S(1)} %get-tuple-element.94), channel_id=1, source_target_pairs={{0,4},{2,6},{4,0},{6,2},{8,12},{10,14},{12,8},{14,10},{1,5},{3,7},... | collective-permute-start | bytes 393224 | tf_op jit(solution)/shard_map/ppermute | solution.py:376
  92.5 8.1 %collective-permute-start.26 = (f32[1,2,64,256]{3,2,1,0:T(8,128)S(1)}, f32[1,2,64,256]{3,2,1,0:T(8,128)S(1)}, u32[]{:S(2)}, u32[]{:S(2)}) collective-permute-start(f32[1,2,64,256]{3,2,1,0:T(8,128)S(1)} %get-tuple-element.92), channel_id=1, source_target_pairs={{0,2},{2,0},{4,6},{6,4},{8,10},{10,8},{12,14},{14,12},{1,3},{3,1},... | collective-permute-start | bytes 393224 | tf_op jit(solution)/shard_map/ppermute | solution.py:376
  93.5 16.5 %collective-permute-start.33 = (f32[1,2,64,256]{3,2,1,0:T(8,128)S(1)}, f32[1,2,64,256]{3,2,1,0:T(8,128)S(1)}, u32[]{:S(2)}, u32[]{:S(2)}) collective-permute-start(f32[1,2,64,256]{3,2,1,0:T(8,128)S(1)} %get-tuple-element.88), channel_id=1, source_target_pairs={{0,2},{2,0},{4,6},{6,4},{8,10},{10,8},{12,14},{14,12},{1,3},{3,1},... | collective-permute-start | bytes 393224 | tf_op jit(solution)/shard_map/ppermute | solution.py:376
  97.2 12.8 %collective-permute-start.34 = (f32[1,2,64,256]{3,2,1,0:T(8,128)S(1)}, f32[1,2,64,256]{3,2,1,0:T(8,128)S(1)}, u32[]{:S(2)}, u32[]{:S(2)}) collective-permute-start(f32[1,2,64,256]{3,2,1,0:T(8,128)S(1)} %get-tuple-element.87), channel_id=1, source_target_pairs={{0,4},{2,6},{4,0},{6,2},{8,12},{10,14},{12,8},{14,10},{1,5},{3,7},... | collective-permute-start | bytes 393224 | tf_op jit(solution)/shard_map/ppermute | solution.py:376
  99.3 10.8 %collective-permute-start.35 = (f32[1,2,64,256]{3,2,1,0:T(8,128)S(1)}, f32[1,2,64,256]{3,2,1,0:T(8,128)S(1)}, u32[]{:S(2)}, u32[]{:S(2)}) collective-permute-start(f32[1,2,64,256]{3,2,1,0:T(8,128)S(1)} %get-tuple-element.86), channel_id=1, source_target_pairs={{0,6},{2,4},{4,2},{6,0},{8,14},{10,12},{12,10},{14,8},{1,7},{3,5},... | collective-permute-start | bytes 393224 | tf_op jit(solution)/shard_map/ppermute | solution.py:376
  100.8 9.2 %collective-permute-start.32 = (f32[1,2,64,256]{3,2,1,0:T(8,128)S(1)}, f32[1,2,64,256]{3,2,1,0:T(8,128)S(1)}, u32[]{:S(2)}, u32[]{:S(2)}) collective-permute-start(f32[1,2,64,256]{3,2,1,0:T(8,128)S(1)} %add_add_fusion.1), channel_id=1, source_target_pairs={{0,8},{2,10},{4,12},{6,14},{8,0},{10,2},{12,4},{14,6},{1,9},{3,11}... | collective-permute-start | bytes 393224 | tf_op jit(solution)/shard_map/ppermute | solution.py:376
  103.4 8.6 %collective-permute-start.30 = (f32[2,128,128]{2,1,0:T(8,128)S(1)}, f32[2,128,128]{2,1,0:T(8,128)S(1)}, u32[]{:S(2)}, u32[]{:S(2)}) collective-permute-start(f32[2,128,128]{2,1,0:T(8,128)S(1)} %slice_select_fusion.2), channel_id=1, source_target_pairs={{2,4},{4,2},{6,8},{8,6},{10,12},{12,10},{3,5},{5,3},{7,9},{9,7},{1... | collective-permute-start | bytes 393224 | tf_op jit(solution)/shard_map/ppermute | solution.py:366
  110.1 8.6 %collective-permute-start.39 = (f32[1,2,64,256]{3,2,1,0:T(8,128)S(1)}, f32[1,2,64,256]{3,2,1,0:T(8,128)S(1)}, u32[]{:S(2)}, u32[]{:S(2)}) collective-permute-start(f32[1,2,64,256]{3,2,1,0:T(8,128)S(1)} %add_add_fusion), channel_id=1, source_target_pairs={{0,8},{2,10},{4,12},{6,14},{8,0},{10,2},{12,4},{14,6},{1,9},{3,11}... | collective-permute-start | bytes 393224 | tf_op jit(solution)/shard_map/ppermute | solution.py:376
  115.1 10.8 %collective-permute-start.31 = (f32[2,2,128,128]{3,2,1,0:T(8,128)S(1)}, f32[2,2,128,128]{3,2,1,0:T(8,128)S(1)}, u32[]{:S(2)}, u32[]{:S(2)}) collective-permute-start(f32[2,2,128,128]{3,2,1,0:T(8,128)S(1)} %maximum_add_fusion.refs_0_), channel_id=1, source_target_pairs={{0,1},{1,0},{2,3},{3,2},{4,5},{5,4},{6,7},{7,6},{8,9},{9,8},{10,11... | collective-permute-start | bytes 786440 | tf_op jit(solution)/shard_map/ppermute | solution.py:357
  115.2 6.4 %collective-permute-start.37 = (f32[1,2,64,256]{3,2,1,0:T(8,128)S(1)}, f32[1,2,64,256]{3,2,1,0:T(8,128)S(1)}, u32[]{:S(2)}, u32[]{:S(2)}) collective-permute-start(f32[1,2,64,256]{3,2,1,0:T(8,128)S(1)} %add.100.refs_3_), channel_id=1, source_target_pairs={{0,4},{2,6},{4,0},{6,2},{8,12},{10,14},{12,8},{14,10},{1,5},{3,7},... | collective-permute-start | bytes 393224 | tf_op jit(solution)/shard_map/ppermute | solution.py:376
  117.1 8.8 %collective-permute-start.38 = (f32[1,2,64,256]{3,2,1,0:T(8,128)S(1)}, f32[1,2,64,256]{3,2,1,0:T(8,128)S(1)}, u32[]{:S(2)}, u32[]{:S(2)}) collective-permute-start(f32[1,2,64,256]{3,2,1,0:T(8,128)S(1)} %add.100.refs_3_), channel_id=1, source_target_pairs={{0,6},{2,4},{4,2},{6,0},{8,14},{10,12},{12,10},{14,8},{1,7},{3,5},... | collective-permute-start | bytes 393224 | tf_op jit(solution)/shard_map/ppermute | solution.py:376
  118.7 8.0 %collective-permute-start.40 = (f32[1,2,64,256]{3,2,1,0:T(8,128)S(1)}, f32[1,2,64,256]{3,2,1,0:T(8,128)S(1)}, u32[]{:S(2)}, u32[]{:S(2)}) collective-permute-start(f32[1,2,64,256]{3,2,1,0:T(8,128)S(1)} %add.104.refs_7_), channel_id=1, source_target_pairs={{0,2},{2,0},{4,6},{6,4},{8,10},{10,8},{12,14},{14,12},{1,3},{3,1},... | collective-permute-start | bytes 393224 | tf_op jit(solution)/shard_map/ppermute | solution.py:376
  121.1 6.4 %collective-permute-start.41 = (f32[1,2,64,256]{3,2,1,0:T(8,128)S(1)}, f32[1,2,64,256]{3,2,1,0:T(8,128)S(1)}, u32[]{:S(2)}, u32[]{:S(2)}) collective-permute-start(f32[1,2,64,256]{3,2,1,0:T(8,128)S(1)} %add.104.refs_7_), channel_id=1, source_target_pairs={{0,4},{2,6},{4,0},{6,2},{8,12},{10,14},{12,8},{14,10},{1,5},{3,7},... | collective-permute-start | bytes 393224 | tf_op jit(solution)/shard_map/ppermute | solution.py:376
  121.6 9.1 %collective-permute-start.42 = (f32[1,2,64,256]{3,2,1,0:T(8,128)S(1)}, f32[1,2,64,256]{3,2,1,0:T(8,128)S(1)}, u32[]{:S(2)}, u32[]{:S(2)}) collective-permute-start(f32[1,2,64,256]{3,2,1,0:T(8,128)S(1)} %add.104.refs_7_), channel_id=1, source_target_pairs={{0,6},{2,4},{4,2},{6,0},{8,14},{10,12},{12,10},{14,8},{1,7},{3,5},... | collective-permute-start | bytes 393224 | tf_op jit(solution)/shard_map/ppermute | solution.py:376
  (17 other events, 51.3 us)

commit v8 on v7

--- a/solution.py
+++ b/solution.py
@@ -59,9 +59,9 @@
     return dot(jnp.concatenate([x[0], x[1], x[0]], 1), jnp.concatenate([table[0], table[0], table[1]], 0))
 
 
-def put(ref, where, rows, cols, x):
+def put(ref, item, where, rows, x):
     for k, part in enumerate(split(x)):
-        ref[where, k, rows, cols] = part
+        ref[item, where, k, rows, :] = part
 
 
 def strips(count, body):
@@ -163,37 +163,32 @@
     h = frame // 2
     shift_in(offsets, slot, near, away, patch, tall)
 
-    def exits(j):
-        for m in range(modes):
-            pair = []
-            for start in (j * STRIP, h + j * STRIP):
-                rows = at(start)
-                pr, pi = probe[m, 0, rows, :], probe[m, 1, rows, :]
-                ar, ai = patch[0, rows, :], patch[1, rows, :]
-                pair.append((pr * ar - pi * ai, pr * ai + pi * ar))
-            cols = slice(m * frame, (m + 1) * frame)
-            for k in range(2):
-                put(tall_parts, 0, at(k * h + j * STRIP), cols, pair[0][k] + pair[1][k])
-                put(tall_parts, 1, at(k * h + j * STRIP), cols, pair[0][k] - pair[1][k])
-
-    strips(h // STRIP, exits)
-    for p in range(2):
-        product[p] = mul_left(tab[0, p], tall_parts[p])
-
-    def columns(j):
+    def exits(m, j):
+        pair = []
+        for start in (j * STRIP, h + j * STRIP):
+            rows = at(start)
+            pr, pi = probe[m, 0, rows, :], probe[m, 1, rows, :]
+            ar, ai = patch[0, rows, :], patch[1, rows, :]
+            pair.append((pr * ar - pi * ai, pr * ai + pi * ar))
+        for k in range(2):
+            put(tall_parts, m, 0, at(k * h + j * STRIP), pair[0][k] + pair[1][k])
+            put(tall_parts, m, 1, at(k * h + j * STRIP), pair[0][k] - pair[1][k])
+
+    def columns(m, j):
         for p in range(2):
-            for m in range(modes):
-                cols = slice(m * frame, (m + 1) * frame)
-                y = [product[p, at(k * h + j * STRIP), cols] for k in range(2)]
-                rows = at(m * frame + p * h + j * STRIP)
-                put(wide_parts, 0, rows, slice(None), jnp.concatenate([v[:, :h] + v[:, h:] for v in y], 1))
-                put(wide_parts, 1, rows, slice(None), jnp.concatenate([v[:, :h] - v[:, h:] for v in y], 1))
-
-    strips(h // STRIP, columns)
-    for q in range(2):
-        out = mul_right(wide_parts[q], tab[1, q])
-        for m in range(modes):
-            far[m, q] = out[m * frame : (m + 1) * frame]
+            y = [product[m, p, at(k * h + j * STRIP), :] for k in range(2)]
+            rows = at(p * h + j * STRIP)
+            put(wide_parts, m, 0, rows, jnp.concatenate([v[:, :h] + v[:, h:] for v in y], 1))
+            put(wide_parts, m, 1, rows, jnp.concatenate([v[:, :h] - v[:, h:] for v in y], 1))
+
+    for m in range(modes):
+        strips(h // STRIP, functools.partial(exits, m))
+        for p in range(2):
+            product[m, p] = mul_left(tab[0, p], tall_parts[m, p])
+    for m in range(modes):
+        strips(h // STRIP, functools.partial(columns, m))
+        for q in range(2):
+            far[m, q] = mul_right(wide_parts[m, q], tab[1, q])
 
     def powers(j):
         rows = at(j * STRIP)
@@ -221,55 +216,46 @@
     frame = probe.shape[-1]
     h = frame // 2
 
-    def factors(j):
+    def factors(s, j):
         rows = at(j * STRIP)
-        for s in range(slots):
-            factor = amp[s, rows, :] / (jnp.sqrt(powers[s][rows, :] + others[s][rows, :]) + 0.5)
-            for q in range(2):
-                f = factor[:, q * h : (q + 1) * h]
-                put(
-                    wide_parts,
-                    q,
-                    at(s * frame + j * STRIP),
-                    slice(None),
-                    fars[s][mode, q, rows, :] * jnp.concatenate([f, f], 1),
-                )
-
-    strips(frame // STRIP, factors)
-    for q in range(2):
-        product_wide[q] = mul_right(wide_parts[q], tab[0, q])
-
-    def columns(j):
+        factor = amp[s, rows, :] / (jnp.sqrt(powers[s][rows, :] + others[s][rows, :]) + 0.5)
+        for q in range(2):
+            f = factor[:, q * h : (q + 1) * h]
+            put(wide_parts, s, q, rows, fars[s][mode, q, rows, :] * jnp.concatenate([f, f], 1))
+
+    def columns(s, j):
         for p in range(2):
-            for s in range(slots):
-                rows = at(s * frame + p * h + j * STRIP)
-                he, ho = product_wide[0, rows, :], product_wide[1, rows, :]
-                cols = slice(s * frame, (s + 1) * frame)
-                for k in range(2):
-                    a, b = he[:, k * h : (k + 1) * h], ho[:, k * h : (k + 1) * h]
-                    put(tall_parts, p, at(k * h + j * STRIP), cols, jnp.concatenate([a + b, a - b], 1))
-
-    strips(h // STRIP, columns)
-    for p in range(2):
-        product_tall[p] = mul_left(tab[1, p], tall_parts[p])
+            he, ho = (product_wide[s, q, at(p * h + j * STRIP), :] for q in range(2))
+            for k in range(2):
+                a, b = he[:, k * h : (k + 1) * h], ho[:, k * h : (k + 1) * h]
+                put(tall_parts, s, p, at(k * h + j * STRIP), jnp.concatenate([a + b, a - b], 1))
+
+    for s in range(slots):
+        strips(frame // STRIP, functools.partial(factors, s))
+        for q in range(2):
+            product_wide[s, q] = mul_right(wide_parts[s, q], tab[0, q])
+    for s in range(slots):
+        strips(h // STRIP, functools.partial(columns, s))
+        for p in range(2):
+            product_tall[s, p] = mul_left(tab[1, p], tall_parts[s, p])
     key = chunk_key()
     chunk = frame // CHUNKS
     core = lax.axis_index("row")
     first = left_half()
 
     def results(j):
-        x = [[product_tall[p, at(k * h + j * STRIP), :] for k in range(2)] for p in range(2)]
+        x = [
+            [[product_tall[s, p, at(k * h + j * STRIP), :] for k in range(2)] for p in range(2)]
+            for s in range(slots)
+        ]
         for lower in range(2):
             rows = at(lower * h + j * STRIP)
             pr, pi = probe[mode, 0, rows, :], probe[mode, 1, rows, :]
             step = [None, None]
             window = [None, None]
             for s in range(slots):
-                cols = slice(s * frame, (s + 1) * frame)
-                xr, xi = (
-                    x[0][k][:, cols] - x[1][k][:, cols] if lower else x[0][k][:, cols] + x[1][k][:, cols]
-                    for k in range(2)
-                )
+                even, odd = x[s]
+                xr, xi = (even[k] - odd[k] if lower else even[k] + odd[k] for k in range(2))
                 live = (s < counts[0]).astype(f32)
                 ar, ai = patches[s][0, rows, :], patches[s][1, rows, :]
                 ur = (xr - (pr * ar - pi * ai)) * live
@@ -414,6 +400,8 @@
             mask *= 2
         if m + 1 < len(parts):
             held, got[m + 1] = together(held, got[m + 1])
+        else:
+            held, inner, outer, *streams = together(held, inner, outer, *streams)
         streams.append([held] + [exchange(held, k, tiles) for k in range(1, CHUNKS)])
     return streams, jnp.stack([stay[0] + inner, stay[1] + outer])
 
@@ -446,10 +434,7 @@
     near, away, amp = together(near, away, amp)
 
     def scratch(count):
-        return [
-            pltpu.VMEM((2, 2, frame, count * frame), bf16),
-            pltpu.VMEM((2, 2, count * frame, frame), bf16),
-        ]
+        return [pltpu.VMEM((count, 2, 2, frame, frame), bf16) for _ in range(2)]
 
     matmul = 4 * 2 * 3 * 4 * frame**3
     probe = probe_modes
@@ -470,7 +455,7 @@
                 functools.partial(forward_kernel, s, count, coef, tall),
                 outs,
                 args,
-                scratch(modes) + [pltpu.VMEM((2, frame, modes * frame), f32)],
+                scratch(modes) + [pltpu.VMEM((modes, 2, frame, frame), f32)],
                 matmul * modes,
             )
             if count:
@@ -492,8 +477,7 @@
                 functools.partial(inverse_kernel, m, last, tall),
                 [part, grads],
                 args,
-                scratch(slots)
-                + [pltpu.VMEM((2, slots * frame, frame), f32), pltpu.VMEM((2, frame, slots * frame), f32)],
+                scratch(slots) + [pltpu.VMEM((slots, 2, frame, frame), f32) for _ in range(2)],
                 matmul * slots,
             )
             parts.append(got[0])

time: 132 us -> 132 us (level)
  starting transfers between devices: 60.2 us -> 49.4 us
  waiting for transfers between devices: 46.8 us -> 57.5 us
    ppermute x28, waiting for transfers between devices: 31.1 us -> 52.7 us  [exchange(): return lax.ppermute(x, 'tile', [(s, s ^ mask) for s in range(tiles)])]
    ppermute x6, waiting for transfers between devices: 13.7 us -> 2.84 us  [beside(): return lax.ppermute(x, 'tile', pairs)]
    ppermute x28, starting transfers between devices: 51.4 us -> 41.1 us  [exchange(): return lax.ppermute(x, 'tile', [(s, s ^ mask) for s in range(tiles)])]
  transfers between devices with their start and end apart: 43 -> 43, of which waited for: 21 -> 24; matrix products, arithmetic and copies ran while one was open for 1% -> 0% of each run, Pallas kernels for 2% -> 2%
where the time goes in v8:
time: 132 us; the launch traced here: 131 us
  waiting for transfers between devices  57.5 us (44%)
  starting transfers between devices  49.4 us (37%)
  Pallas kernels  19.4 us (15%)
  local copies, waits for them, and re-layouts  2.39 us (2%)
  between operations  1.82 us (1%)
    ppermute x28, waiting for transfers between devices, exchange(): return lax.ppermute(x, 'tile', [(s, s ^ mask) for s in range(tiles)])  52.7 us
    ppermute x28, starting transfers between devices, exchange(): return lax.ppermute(x, 'tile', [(s, s ^ mask) for s in range(tiles)])  41.1 us
    pallas_call x10, Pallas kernels, call(): pl.pallas_call(kernel, out_shape=[jax.ShapeDtypeStruct(o, f32) for o in o...  19.4 us
    ppermute x6, starting transfers between devices, beside(): return lax.ppermute(x, 'tile', pairs)  6.29 us
    ppermute x6, waiting for transfers between devices, beside(): return lax.ppermute(x, 'tile', pairs)  2.84 us
  transfers between devices with their start and end apart: 43, of which 24 were waited for; matrix products, arithmetic and copies ran while one was open for 0% of the time, Pallas kernels for 2%

profile of v8, /device:TPU:0, one launch (start us, length us, event | category | flops | bytes accessed | tf_op | source)
XLA Modules:
  0.0 131.3 jit_solution(18208445613737926958)
XLA Ops:
  1.7 3.0 %collective-permute-start = (f32[2,128,128]{2,1,0:T(8,128)S(1)}, f32[2,128,128]{2,1,0:T(8,128)S(1)}, u32[]{:S(2)}, u32[]{:S(2)}) collective-permute-start(f32[2,128,128]{2,1,0:T(8,128)S(1)} %get-tuple-element.138), channel_id=1, source_target_pairs={{0,2},{2,0},{4,6},{6,4},{8,10},{10,8},{12,14},{14,12},{1,3},{3,1},... | collective-permute-start | bytes 393224 | tf_op jit(solution)/shard_map/ppermute | solution.py:352
  5.4 2.8 %collective-permute-done = f32[2,128,128]{2,1,0:T(8,128)S(1)} collective-permute-done((f32[2,128,128]{2,1,0:T(8,128)S(1)}, f32[2,128,128]{2,1,0:T(8,128)S(1)}, u32[]{:S(2)}, u32[]{:S(2)}) %collective-permute-start) | collective-permute-done | bytes 131104 | tf_op jit(solution)/shard_map/ppermute | solution.py:352
  10.5 2.0 %shard_map.87 = (f32[2,2,256,256]{3,2,1,0:T(8,128)S(1)}, f32[256,256]{1,0:T(8,128)S(1)}, f32[2,256,256]{2,1,0:T(8,128)S(1)}) custom-call(s32[2,2]{1,0:T(2,128)S(1)} %copy-done.4, f32[2,2,128,256]{3,2,1,0:T(8,128)S(1)} %pad_maximum_fusion.refs_1_, f32[2,2,128,256]{3,2,1,0:T(8,128)S(1)} %collective-permute-done.2.refs_2_, f32[2,2,256,256]{3,2,1,0:T(8,128)S(1)} %copy-done.3, ...), custom_call_target="tpu_custom_call" | custom-call | flops 3221225472 | bytes 4980752 | tf_op jit(solution)/shard_map/pallas_call | solution.py:329
  12.5 2.0 %shard_map.88 = (f32[2,2,256,256]{3,2,1,0:T(8,128)S(1)}, f32[256,256]{1,0:T(8,128)S(1)}, f32[2,256,256]{2,1,0:T(8,128)S(1)}) custom-call(s32[2,2]{1,0:T(2,128)S(1)} %copy-done.4, f32[2,2,128,256]{3,2,1,0:T(8,128)S(1)} %pad_maximum_fusion.refs_1_, f32[2,2,128,256]{3,2,1,0:T(8,128)S(1)} %collective-permute-done.2.refs_2_, f32[2,2,256,256]{3,2,1,0:T(8,128)S(1)} %copy-done.3, ...), custom_call_target="tpu_custom_call" | custom-call | flops 3221225472 | bytes 4980752 | tf_op jit(solution)/shard_map/pallas_call | solution.py:329
  16.5 2.1 %shard_map.89 = (f32[4,2,64,256]{3,2,1,0:T(8,128)S(1)}, f32[2,2,256,256]{3,2,1,0:T(8,128)S(1)}) custom-call(s32[2,2]{1,0:T(2,128)S(1)} %copy-done.4, s32[1]{0:T(128)S(6)} %copy.9.refs_1_, bf16[2,2,2,256,256]{4,3,2,1,0:T(8,128)(2,1)S(1)} %copy-done.5, f32[2,256,256]{2,1,0:T(8,128)S(1)} %shard_map.86.refs_3_, f32[2,2,256,256]{3,2,1,0:T(8,128)S(1)} %copy-done.3, ...), custom_call_target="tpu_custom_call" | custom-call | flops 3221225472 | bytes 8388628 | tf_op jit(solution)/shard_map/pallas_call | solution.py:329
  18.7 2.4 %shard_map.90 = (f32[4,2,64,256]{3,2,1,0:T(8,128)S(1)}, f32[2,2,2,128,256]{4,3,2,1,0:T(8,128)S(1)}) custom-call(s32[2,2]{1,0:T(2,128)S(1)} %copy-done.4, s32[1]{0:T(128)S(6)} %copy.9.refs_1_, bf16[2,2,2,256,256]{4,3,2,1,0:T(8,128)(2,1)S(1)} %copy-done.5, f32[2,256,256]{2,1,0:T(8,128)S(1)} %shard_map.86.refs_3_, f32[2,2,256,256]{3,2,1,0:T(8,128)S(1)} %copy-done.3, ...), custom_call_target="tpu_custom_call" | custom-call | flops 3221225472 | bytes 9437204 | tf_op jit(solution)/shard_map/pallas_call | solution.py:329
  21.3 5.8 %collective-permute-start.8 = (f32[1,2,64,256]{3,2,1,0:T(8,128)S(1)}, f32[1,2,64,256]{3,2,1,0:T(8,128)S(1)}, u32[]{:S(2)}, u32[]{:S(2)}) collective-permute-start(f32[1,2,64,256]{3,2,1,0:T(8,128)S(1)} %get-tuple-element.134), channel_id=1, source_target_pairs={{0,6},{2,4},{4,2},{6,0},{8,14},{10,12},{12,10},{14,8},{1,7},{3,5},... | collective-permute-start | bytes 393224 | tf_op jit(solution)/shard_map/ppermute | solution.py:362
  28.7 2.8 %collective-permute-done.8 = f32[1,2,64,256]{3,2,1,0:T(8,128)S(1)} collective-permute-done((f32[1,2,64,256]{3,2,1,0:T(8,128)S(1)}, f32[1,2,64,256]{3,2,1,0:T(8,128)S(1)}, u32[]{:S(2)}, u32[]{:S(2)}) %collective-permute-start.8) | collective-permute-done | bytes 131104 | tf_op jit(solution)/shard_map/ppermute | solution.py:362
  31.5 2.5 %collective-permute-done.7 = f32[1,2,64,256]{3,2,1,0:T(8,128)S(1)} collective-permute-done((f32[1,2,64,256]{3,2,1,0:T(8,128)S(1)}, f32[1,2,64,256]{3,2,1,0:T(8,128)S(1)}, u32[]{:S(2)}, u32[]{:S(2)}) %collective-permute-start.7) | collective-permute-done | bytes 131104 | tf_op jit(solution)/shard_map/ppermute | solution.py:362
  34.2 3.7 %collective-permute-start.9 = (f32[1,2,64,256]{3,2,1,0:T(8,128)S(1)}, f32[1,2,64,256]{3,2,1,0:T(8,128)S(1)}, u32[]{:S(2)}, u32[]{:S(2)}) collective-permute-start(f32[1,2,64,256]{3,2,1,0:T(8,128)S(1)} %add_add_fusion.3), channel_id=1, source_target_pairs={{0,8},{2,10},{4,12},{6,14},{8,0},{10,2},{12,4},{14,6},{1,9},{3,11}... | collective-permute-start | bytes 393224 | tf_op jit(solution)/shard_map/ppermute | solution.py:362
  42.0 2.5 %collective-permute-done.9 = f32[1,2,64,256]{3,2,1,0:T(8,128)S(1)} collective-permute-done((f32[1,2,64,256]{3,2,1,0:T(8,128)S(1)}, f32[1,2,64,256]{3,2,1,0:T(8,128)S(1)}, u32[]{:S(2)}, u32[]{:S(2)}) %collective-permute-start.9) | collective-permute-done | bytes 131104 | tf_op jit(solution)/shard_map/ppermute | solution.py:362
  46.1 2.8 %collective-permute-done.12 = f32[1,2,64,256]{3,2,1,0:T(8,128)S(1)} collective-permute-done((f32[1,2,64,256]{3,2,1,0:T(8,128)S(1)}, f32[1,2,64,256]{3,2,1,0:T(8,128)S(1)}, u32[]{:S(2)}, u32[]{:S(2)}) %collective-permute-start.12) | collective-permute-done | bytes 131104 | tf_op jit(solution)/shard_map/ppermute | solution.py:362
  49.0 3.3 %collective-permute-start.16 = (f32[1,2,64,256]{3,2,1,0:T(8,128)S(1)}, f32[1,2,64,256]{3,2,1,0:T(8,128)S(1)}, u32[]{:S(2)}, u32[]{:S(2)}) collective-permute-start(f32[1,2,64,256]{3,2,1,0:T(8,128)S(1)} %add.85.refs_5_), channel_id=1, source_target_pairs={{0,2},{2,0},{4,6},{6,4},{8,10},{10,8},{12,14},{14,12},{1,3},{3,1},... | collective-permute-start | bytes 393224 | tf_op jit(solution)/shard_map/ppermute | solution.py:362
  52.4 7.4 %collective-permute-done.13 = f32[1,2,64,256]{3,2,1,0:T(8,128)S(1)} collective-permute-done((f32[1,2,64,256]{3,2,1,0:T(8,128)S(1)}, f32[1,2,64,256]{3,2,1,0:T(8,128)S(1)}, u32[]{:S(2)}, u32[]{:S(2)}) %collective-permute-start.13) | collective-permute-done | bytes 131104 | tf_op jit(solution)/shard_map/ppermute | solution.py:362
  59.9 5.8 %collective-permute-done.18.refs_8_ = f32[1,2,64,256]{3,2,1,0:T(8,128)S(1)} collective-permute-done((f32[1,2,64,256]{3,2,1,0:T(8,128)S(1)}, f32[1,2,64,256]{3,2,1,0:T(8,128)S(1)}, u32[]{:S(2)}, u32[]{:S(2)}) %collective-permute-start.18) | collective-permute-done | bytes 131104 | tf_op jit(solution)/shard_map/ppermute | solution.py:362
  66.8 2.7 %collective-permute-start.22 = (f32[1,2,64,256]{3,2,1,0:T(8,128)S(1)}, f32[1,2,64,256]{3,2,1,0:T(8,128)S(1)}, u32[]{:S(2)}, u32[]{:S(2)}) collective-permute-start(f32[1,2,64,256]{3,2,1,0:T(8,128)S(1)} %add.89.refs_9_), channel_id=1, source_target_pairs={{0,6},{2,4},{4,2},{6,0},{8,14},{10,12},{12,10},{14,8},{1,7},{3,5},... | collective-permute-start | bytes 393224 | tf_op jit(solution)/shard_map/ppermute | solution.py:362
  69.5 2.4 %collective-permute-done.20.refs_10_ = f32[1,2,64,256]{3,2,1,0:T(8,128)S(1)} collective-permute-done((f32[1,2,64,256]{3,2,1,0:T(8,128)S(1)}, f32[1,2,64,256]{3,2,1,0:T(8,128)S(1)}, u32[]{:S(2)}, u32[]{:S(2)}) %collective-permute-start.20) | collective-permute-done | bytes 131104 | tf_op jit(solution)/shard_map/ppermute | solution.py:362
  72.4 3.4 %collective-permute-done.22.refs_12_ = f32[1,2,64,256]{3,2,1,0:T(8,128)S(1)} collective-permute-done((f32[1,2,64,256]{3,2,1,0:T(8,128)S(1)}, f32[1,2,64,256]{3,2,1,0:T(8,128)S(1)}, u32[]{:S(2)}, u32[]{:S(2)}) %collective-permute-start.22) | collective-permute-done | bytes 131104 | tf_op jit(solution)/shard_map/ppermute | solution.py:362
  75.8 2.1 %shard_map.91 = (f32[2,2,256,256]{3,2,1,0:T(8,128)S(1)}, f32[256,256]{1,0:T(8,128)S(1)}, f32[2,256,256]{2,1,0:T(8,128)S(1)}, f32[2,2,256,256]{3,2,1,0:T(8,128)S(1)}) custom-call(s32[2,2]{1,0:T(2,128)S(1)} %copy-done.4, f32[2,2,128,256]{3,2,1,0:T(8,128)S(1)} %fusion.refs_1_, f32[2,2,128,256]{3,2,1,0:T(8,128)S(1)} %collective-permute-done.19.refs_2_, ...), custom_call_target="tpu_custom_call" | custom-call | flops 3221225472 | bytes 7077904 | tf_op jit(solution)/shard_map/pallas_call | solution.py:329
  78.0 2.0 %shard_map.92 = (f32[2,2,256,256]{3,2,1,0:T(8,128)S(1)}, f32[256,256]{1,0:T(8,128)S(1)}, f32[2,256,256]{2,1,0:T(8,128)S(1)}) custom-call(s32[2,2]{1,0:T(2,128)S(1)} %copy-done.4, f32[2,2,128,256]{3,2,1,0:T(8,128)S(1)} %fusion.refs_1_, f32[2,2,128,256]{3,2,1,0:T(8,128)S(1)} %collective-permute-done.19.refs_2_, ...), custom_call_target="tpu_custom_call" | custom-call | flops 3221225472 | bytes 4980752 | tf_op jit(solution)/shard_map/pallas_call | solution.py:329
  81.8 2.2 %shard_map.93 = (f32[4,2,64,256]{3,2,1,0:T(8,128)S(1)}, f32[2,2,256,256]{3,2,1,0:T(8,128)S(1)}) custom-call(s32[2,2]{1,0:T(2,128)S(1)} %copy-done.4, s32[1]{0:T(128)S(6)} %copy.9.refs_1_, bf16[2,2,2,256,256]{4,3,2,1,0:T(8,128)(2,1)S(1)} %copy-done.5, f32[2,256,256]{2,1,0:T(8,128)S(1)} %shard_map.86.refs_3_, ...), custom_call_target="tpu_custom_call" | custom-call | flops 3221225472 | bytes 8388628 | tf_op jit(solution)/shard_map/pallas_call | solution.py:329
  83.9 2.4 %shard_map.94 = (f32[4,2,64,256]{3,2,1,0:T(8,128)S(1)}, f32[2,2,2,128,256]{4,3,2,1,0:T(8,128)S(1)}) custom-call(s32[2,2]{1,0:T(2,128)S(1)} %copy-done.4, s32[1]{0:T(128)S(6)} %copy.9.refs_1_, bf16[2,2,2,256,256]{4,3,2,1,0:T(8,128)(2,1)S(1)} %copy-done.5, f32[2,256,256]{2,1,0:T(8,128)S(1)} %shard_map.86.refs_3_, ...), custom_call_target="tpu_custom_call" | custom-call | flops 3221225472 | bytes 9437204 | tf_op jit(solution)/shard_map/pallas_call | solution.py:329
  88.7 1.8 %collective-permute-start.26 = (f32[1,2,64,256]{3,2,1,0:T(8,128)S(1)}, f32[1,2,64,256]{3,2,1,0:T(8,128)S(1)}, u32[]{:S(2)}, u32[]{:S(2)}) collective-permute-start(f32[1,2,64,256]{3,2,1,0:T(8,128)S(1)} %get-tuple-element.120), channel_id=1, source_target_pairs={{0,2},{2,0},{4,6},{6,4},{8,10},{10,8},{12,14},{14,12},{1,3},{3,1},... | collective-permute-start | bytes 393224 | tf_op jit(solution)/shard_map/ppermute | solution.py:362
  90.8 3.4 %collective-permute-done.28 = f32[1,2,64,256]{3,2,1,0:T(8,128)S(1)} collective-permute-done((f32[1,2,64,256]{3,2,1,0:T(8,128)S(1)}, f32[1,2,64,256]{3,2,1,0:T(8,128)S(1)}, u32[]{:S(2)}, u32[]{:S(2)}) %collective-permute-start.28) | collective-permute-done | bytes 131104 | tf_op jit(solution)/shard_map/ppermute | solution.py:362
  95.0 2.7 %collective-permute-start.32 = (f32[1,2,64,256]{3,2,1,0:T(8,128)S(1)}, f32[1,2,64,256]{3,2,1,0:T(8,128)S(1)}, u32[]{:S(2)}, u32[]{:S(2)}) collective-permute-start(f32[1,2,64,256]{3,2,1,0:T(8,128)S(1)} %get-tuple-element.114), channel_id=1, source_target_pairs={{0,6},{2,4},{4,2},{6,0},{8,14},{10,12},{12,10},{14,8},{1,7},{3,5},... | collective-permute-start | bytes 393224 | tf_op jit(solution)/shard_map/ppermute | solution.py:362
  99.4 6.4 %collective-permute-done.29 = f32[1,2,64,256]{3,2,1,0:T(8,128)S(1)} collective-permute-done((f32[1,2,64,256]{3,2,1,0:T(8,128)S(1)}, f32[1,2,64,256]{3,2,1,0:T(8,128)S(1)}, u32[]{:S(2)}, u32[]{:S(2)}) %collective-permute-start.29) | collective-permute-done | bytes 131104 | tf_op jit(solution)/shard_map/ppermute | solution.py:362
  107.8 4.8 %collective-permute-start.36 = (f32[1,2,64,256]{3,2,1,0:T(8,128)S(1)}, f32[1,2,64,256]{3,2,1,0:T(8,128)S(1)}, u32[]{:S(2)}, u32[]{:S(2)}) collective-permute-start(f32[1,2,64,256]{3,2,1,0:T(8,128)S(1)} %add.97.refs_3_), channel_id=1, source_target_pairs={{0,2},{2,0},{4,6},{6,4},{8,10},{10,8},{12,14},{14,12},{1,3},{3,1},... | collective-permute-start | bytes 393224 | tf_op jit(solution)/shard_map/ppermute | solution.py:362
  114.3 3.1 %collective-permute-done.36.refs_4_ = f32[1,2,64,256]{3,2,1,0:T(8,128)S(1)} collective-permute-done((f32[1,2,64,256]{3,2,1,0:T(8,128)S(1)}, f32[1,2,64,256]{3,2,1,0:T(8,128)S(1)}, u32[]{:S(2)}, u32[]{:S(2)}) %collective-permute-start.36) | collective-permute-done | bytes 131104 | tf_op jit(solution)/shard_map/ppermute | solution.py:362
  119.6 2.3 %collective-permute-start.40 = (f32[1,2,64,256]{3,2,1,0:T(8,128)S(1)}, f32[1,2,64,256]{3,2,1,0:T(8,128)S(1)}, u32[]{:S(2)}, u32[]{:S(2)}) collective-permute-start(f32[1,2,64,256]{3,2,1,0:T(8,128)S(1)} %add.101.refs_7_), channel_id=1, source_target_pairs={{0,2},{2,0},{4,6},{6,4},{8,10},{10,8},{12,14},{14,12},{1,3},{3,1},... | collective-permute-start | bytes 393224 | tf_op jit(solution)/shard_map/ppermute | solution.py:362
  123.5 2.5 %collective-permute-done.40.refs_8_ = f32[1,2,64,256]{3,2,1,0:T(8,128)S(1)} collective-permute-done((f32[1,2,64,256]{3,2,1,0:T(8,128)S(1)}, f32[1,2,64,256]{3,2,1,0:T(8,128)S(1)}, u32[]{:S(2)}, u32[]{:S(2)}) %collective-permute-start.40) | collective-permute-done | bytes 131104 | tf_op jit(solution)/shard_map/ppermute | solution.py:362
  126.0 2.3 %collective-permute-done.41.refs_9_ = f32[1,2,64,256]{3,2,1,0:T(8,128)S(1)} collective-permute-done((f32[1,2,64,256]{3,2,1,0:T(8,128)S(1)}, f32[1,2,64,256]{3,2,1,0:T(8,128)S(1)}, u32[]{:S(2)}, u32[]{:S(2)}) %collective-permute-start.41) | collective-permute-done | bytes 131104 | tf_op jit(solution)/shard_map/ppermute | solution.py:362
  128.3 1.7 %collective-permute-done.42.refs_10_ = f32[1,2,64,256]{3,2,1,0:T(8,128)S(1)} collective-permute-done((f32[1,2,64,256]{3,2,1,0:T(8,128)S(1)}, f32[1,2,64,256]{3,2,1,0:T(8,128)S(1)}, u32[]{:S(2)}, u32[]{:S(2)}) %collective-permute-start.42) | collective-permute-done | bytes 131104 | tf_op jit(solution)/shard_map/ppermute | solution.py:362
  (110 shorter events, 30.1 us)
Async XLA Ops:
  1.7 6.5 %collective-permute-start = (f32[2,128,128]{2,1,0:T(8,128)S(1)}, f32[2,128,128]{2,1,0:T(8,128)S(1)}, u32[]{:S(2)}, u32[]{:S(2)}) collective-permute-start(f32[2,128,128]{2,1,0:T(8,128)S(1)} %get-tuple-element.138), channel_id=1, source_target_pairs={{0,2},{2,0},{4,6},{6,4},{8,10},{10,8},{12,14},{14,12},{1,3},{3,1},... | collective-permute-start | bytes 393224 | tf_op jit(solution)/shard_map/ppermute | solution.py:352
  21.1 13.0 %collective-permute-start.5 = (f32[2,2,128,256]{3,2,1,0:T(8,128)S(1)}, f32[2,2,128,256]{3,2,1,0:T(8,128)S(1)}, u32[]{:S(2)}, u32[]{:S(2)}) collective-permute-start(f32[2,2,128,256]{3,2,1,0:T(8,128)S(1)} %slice_bitcast_fusion.1), channel_id=1, source_target_pairs={{0,1},{1,0},{2,3},{3,2},{4,5},{5,4},{6,7},{7,6},{8,9},{9,8},{10,11... | collective-permute-start | bytes 1572872 | tf_op jit(solution)/shard_map/ppermute | solution.py:343
  21.3 10.1 %collective-permute-start.8 = (f32[1,2,64,256]{3,2,1,0:T(8,128)S(1)}, f32[1,2,64,256]{3,2,1,0:T(8,128)S(1)}, u32[]{:S(2)}, u32[]{:S(2)}) collective-permute-start(f32[1,2,64,256]{3,2,1,0:T(8,128)S(1)} %get-tuple-element.134), channel_id=1, source_target_pairs={{0,6},{2,4},{4,2},{6,0},{8,14},{10,12},{12,10},{14,8},{1,7},{3,5},... | collective-permute-start | bytes 393224 | tf_op jit(solution)/shard_map/ppermute | solution.py:362
  27.2 6.9 %collective-permute-start.7 = (f32[1,2,64,256]{3,2,1,0:T(8,128)S(1)}, f32[1,2,64,256]{3,2,1,0:T(8,128)S(1)}, u32[]{:S(2)}, u32[]{:S(2)}) collective-permute-start(f32[1,2,64,256]{3,2,1,0:T(8,128)S(1)} %get-tuple-element.135), channel_id=1, source_target_pairs={{0,4},{2,6},{4,0},{6,2},{8,12},{10,14},{12,8},{14,10},{1,5},{3,7},... | collective-permute-start | bytes 393224 | tf_op jit(solution)/shard_map/ppermute | solution.py:362
  27.5 6.5 %collective-permute-start.6 = (f32[1,2,64,256]{3,2,1,0:T(8,128)S(1)}, f32[1,2,64,256]{3,2,1,0:T(8,128)S(1)}, u32[]{:S(2)}, u32[]{:S(2)}) collective-permute-start(f32[1,2,64,256]{3,2,1,0:T(8,128)S(1)} %get-tuple-element.133), channel_id=1, source_target_pairs={{0,2},{2,0},{4,6},{6,4},{8,10},{10,8},{12,14},{14,12},{1,3},{3,1},... | collective-permute-start | bytes 393224 | tf_op jit(solution)/shard_map/ppermute | solution.py:362
  34.2 10.3 %collective-permute-start.9 = (f32[1,2,64,256]{3,2,1,0:T(8,128)S(1)}, f32[1,2,64,256]{3,2,1,0:T(8,128)S(1)}, u32[]{:S(2)}, u32[]{:S(2)}) collective-permute-start(f32[1,2,64,256]{3,2,1,0:T(8,128)S(1)} %add_add_fusion.3), channel_id=1, source_target_pairs={{0,8},{2,10},{4,12},{6,14},{8,0},{10,2},{12,4},{14,6},{1,9},{3,11}... | collective-permute-start | bytes 393224 | tf_op jit(solution)/shard_map/ppermute | solution.py:362
  37.9 7.5 %collective-permute-start.10 = (f32[1,2,64,256]{3,2,1,0:T(8,128)S(1)}, f32[1,2,64,256]{3,2,1,0:T(8,128)S(1)}, u32[]{:S(2)}, u32[]{:S(2)}) collective-permute-start(f32[1,2,64,256]{3,2,1,0:T(8,128)S(1)} %get-tuple-element.129), channel_id=1, source_target_pairs={{0,2},{2,0},{4,6},{6,4},{8,10},{10,8},{12,14},{14,12},{1,3},{3,1},... | collective-permute-start | bytes 393224 | tf_op jit(solution)/shard_map/ppermute | solution.py:362
  38.5 7.6 %collective-permute-start.11 = (f32[1,2,64,256]{3,2,1,0:T(8,128)S(1)}, f32[1,2,64,256]{3,2,1,0:T(8,128)S(1)}, u32[]{:S(2)}, u32[]{:S(2)}) collective-permute-start(f32[1,2,64,256]{3,2,1,0:T(8,128)S(1)} %get-tuple-element.128), channel_id=1, source_target_pairs={{0,4},{2,6},{4,0},{6,2},{8,12},{10,14},{12,8},{14,10},{1,5},{3,7},... | collective-permute-start | bytes 393224 | tf_op jit(solution)/shard_map/ppermute | solution.py:362
  40.1 8.8 %collective-permute-start.12 = (f32[1,2,64,256]{3,2,1,0:T(8,128)S(1)}, f32[1,2,64,256]{3,2,1,0:T(8,128)S(1)}, u32[]{:S(2)}, u32[]{:S(2)}) collective-permute-start(f32[1,2,64,256]{3,2,1,0:T(8,128)S(1)} %get-tuple-element.127), channel_id=1, source_target_pairs={{0,6},{2,4},{4,2},{6,0},{8,14},{10,12},{12,10},{14,8},{1,7},{3,5},... | collective-permute-start | bytes 393224 | tf_op jit(solution)/shard_map/ppermute | solution.py:362
  41.4 18.4 %collective-permute-start.14 = (f32[2,128,256]{2,1,0:T(8,128)S(1)}, f32[2,128,256]{2,1,0:T(8,128)S(1)}, u32[]{:S(2)}, u32[]{:S(2)}) collective-permute-start(f32[2,128,256]{2,1,0:T(8,128)S(1)} %get-tuple-element.76), channel_id=1, source_target_pairs={{0,2},{2,0},{4,6},{6,4},{8,10},{10,8},{12,14},{14,12},{1,3},{3,1},... | collective-permute-start | bytes 786440 | tf_op jit(solution)/shard_map/ppermute | solution.py:352
  44.5 15.3 %collective-permute-start.15 = (f32[2,128,256]{2,1,0:T(8,128)S(1)}, f32[2,128,256]{2,1,0:T(8,128)S(1)}, u32[]{:S(2)}, u32[]{:S(2)}) collective-permute-start(f32[2,128,256]{2,1,0:T(8,128)S(1)} %get-tuple-element.77), channel_id=1, source_target_pairs={{2,4},{4,2},{6,8},{8,6},{10,12},{12,10},{3,5},{5,3},{7,9},{9,7},{1... | collective-permute-start | bytes 786440 | tf_op jit(solution)/shard_map/ppermute | solution.py:352
  48.9 10.9 %collective-permute-start.13 = (f32[1,2,64,256]{3,2,1,0:T(8,128)S(1)}, f32[1,2,64,256]{3,2,1,0:T(8,128)S(1)}, u32[]{:S(2)}, u32[]{:S(2)}) collective-permute-start(f32[1,2,64,256]{3,2,1,0:T(8,128)S(1)} %add_add_fusion.2), channel_id=1, source_target_pairs={{0,8},{2,10},{4,12},{6,14},{8,0},{10,2},{12,4},{14,6},{1,9},{3,11}... | collective-permute-start | bytes 393224 | tf_op jit(solution)/shard_map/ppermute | solution.py:362
  49.0 10.9 %collective-permute-start.16 = (f32[1,2,64,256]{3,2,1,0:T(8,128)S(1)}, f32[1,2,64,256]{3,2,1,0:T(8,128)S(1)}, u32[]{:S(2)}, u32[]{:S(2)}) collective-permute-start(f32[1,2,64,256]{3,2,1,0:T(8,128)S(1)} %add.85.refs_5_), channel_id=1, source_target_pairs={{0,2},{2,0},{4,6},{6,4},{8,10},{10,8},{12,14},{14,12},{1,3},{3,1},... | collective-permute-start | bytes 393224 | tf_op jit(solution)/shard_map/ppermute | solution.py:362
  52.3 7.5 %collective-permute-start.17 = (f32[1,2,64,256]{3,2,1,0:T(8,128)S(1)}, f32[1,2,64,256]{3,2,1,0:T(8,128)S(1)}, u32[]{:S(2)}, u32[]{:S(2)}) collective-permute-start(f32[1,2,64,256]{3,2,1,0:T(8,128)S(1)} %add.85.refs_5_), channel_id=1, source_target_pairs={{0,4},{2,6},{4,0},{6,2},{8,12},{10,14},{12,8},{14,10},{1,5},{3,7},... | collective-permute-start | bytes 393224 | tf_op jit(solution)/shard_map/ppermute | solution.py:362
  65.8 10.0 %collective-permute-start.19 = (f32[2,2,128,256]{3,2,1,0:T(8,128)S(1)}, f32[2,2,128,256]{3,2,1,0:T(8,128)S(1)}, u32[]{:S(2)}, u32[]{:S(2)}) collective-permute-start(f32[2,2,128,256]{3,2,1,0:T(8,128)S(1)} %fusion.refs_1_), channel_id=1, source_target_pairs={{0,1},{1,0},{2,3},{3,2},{4,5},{5,4},{6,7},{7,6},{8,9},{9,8},{10,11... | collective-permute-start | bytes 1572872 | tf_op jit(solution)/shard_map/ppermute | solution.py:343
  66.0 6.4 %collective-permute-start.21 = (f32[1,2,64,256]{3,2,1,0:T(8,128)S(1)}, f32[1,2,64,256]{3,2,1,0:T(8,128)S(1)}, u32[]{:S(2)}, u32[]{:S(2)}) collective-permute-start(f32[1,2,64,256]{3,2,1,0:T(8,128)S(1)} %add.89.refs_9_), channel_id=1, source_target_pairs={{0,4},{2,6},{4,0},{6,2},{8,12},{10,14},{12,8},{14,10},{1,5},{3,7},... | collective-permute-start | bytes 393224 | tf_op jit(solution)/shard_map/ppermute | solution.py:362
  66.8 9.1 %collective-permute-start.22 = (f32[1,2,64,256]{3,2,1,0:T(8,128)S(1)}, f32[1,2,64,256]{3,2,1,0:T(8,128)S(1)}, u32[]{:S(2)}, u32[]{:S(2)}) collective-permute-start(f32[1,2,64,256]{3,2,1,0:T(8,128)S(1)} %add.89.refs_9_), channel_id=1, source_target_pairs={{0,6},{2,4},{4,2},{6,0},{8,14},{10,12},{12,10},{14,8},{1,7},{3,5},... | collective-permute-start | bytes 393224 | tf_op jit(solution)/shard_map/ppermute | solution.py:362
  86.4 11.4 %collective-permute-start.25 = (f32[2,2,128,256]{3,2,1,0:T(8,128)S(1)}, f32[2,2,128,256]{3,2,1,0:T(8,128)S(1)}, u32[]{:S(2)}, u32[]{:S(2)}) collective-permute-start(f32[2,2,128,256]{3,2,1,0:T(8,128)S(1)} %slice_bitcast_fusion), channel_id=1, source_target_pairs={{0,1},{1,0},{2,3},{3,2},{4,5},{5,4},{6,7},{7,6},{8,9},{9,8},{10,11... | collective-permute-start | bytes 1572872 | tf_op jit(solution)/shard_map/ppermute | solution.py:343
  86.9 7.3 %collective-permute-start.28 = (f32[1,2,64,256]{3,2,1,0:T(8,128)S(1)}, f32[1,2,64,256]{3,2,1,0:T(8,128)S(1)}, u32[]{:S(2)}, u32[]{:S(2)}) collective-permute-start(f32[1,2,64,256]{3,2,1,0:T(8,128)S(1)} %get-tuple-element.121), channel_id=1, source_target_pairs={{0,6},{2,4},{4,2},{6,0},{8,14},{10,12},{12,10},{14,8},{1,7},{3,5},... | collective-permute-start | bytes 393224 | tf_op jit(solution)/shard_map/ppermute | solution.py:362
  87.4 7.7 %collective-permute-start.27 = (f32[1,2,64,256]{3,2,1,0:T(8,128)S(1)}, f32[1,2,64,256]{3,2,1,0:T(8,128)S(1)}, u32[]{:S(2)}, u32[]{:S(2)}) collective-permute-start(f32[1,2,64,256]{3,2,1,0:T(8,128)S(1)} %get-tuple-element.122), channel_id=1, source_target_pairs={{0,4},{2,6},{4,0},{6,2},{8,12},{10,14},{12,8},{14,10},{1,5},{3,7},... | collective-permute-start | bytes 393224 | tf_op jit(solution)/shard_map/ppermute | solution.py:362
  88.7 9.0 %collective-permute-start.26 = (f32[1,2,64,256]{3,2,1,0:T(8,128)S(1)}, f32[1,2,64,256]{3,2,1,0:T(8,128)S(1)}, u32[]{:S(2)}, u32[]{:S(2)}) collective-permute-start(f32[1,2,64,256]{3,2,1,0:T(8,128)S(1)} %get-tuple-element.120), channel_id=1, source_target_pairs={{0,2},{2,0},{4,6},{6,4},{8,10},{10,8},{12,14},{14,12},{1,3},{3,1},... | collective-permute-start | bytes 393224 | tf_op jit(solution)/shard_map/ppermute | solution.py:362
  90.5 15.3 %collective-permute-start.30 = (f32[1,2,64,256]{3,2,1,0:T(8,128)S(1)}, f32[1,2,64,256]{3,2,1,0:T(8,128)S(1)}, u32[]{:S(2)}, u32[]{:S(2)}) collective-permute-start(f32[1,2,64,256]{3,2,1,0:T(8,128)S(1)} %get-tuple-element.116), channel_id=1, source_target_pairs={{0,2},{2,0},{4,6},{6,4},{8,10},{10,8},{12,14},{14,12},{1,3},{3,1},... | collective-permute-start | bytes 393224 | tf_op jit(solution)/shard_map/ppermute | solution.py:362
  94.2 11.6 %collective-permute-start.31 = (f32[1,2,64,256]{3,2,1,0:T(8,128)S(1)}, f32[1,2,64,256]{3,2,1,0:T(8,128)S(1)}, u32[]{:S(2)}, u32[]{:S(2)}) collective-permute-start(f32[1,2,64,256]{3,2,1,0:T(8,128)S(1)} %get-tuple-element.115), channel_id=1, source_target_pairs={{0,4},{2,6},{4,0},{6,2},{8,12},{10,14},{12,8},{14,10},{1,5},{3,7},... | collective-permute-start | bytes 393224 | tf_op jit(solution)/shard_map/ppermute | solution.py:362
  95.0 10.8 %collective-permute-start.32 = (f32[1,2,64,256]{3,2,1,0:T(8,128)S(1)}, f32[1,2,64,256]{3,2,1,0:T(8,128)S(1)}, u32[]{:S(2)}, u32[]{:S(2)}) collective-permute-start(f32[1,2,64,256]{3,2,1,0:T(8,128)S(1)} %get-tuple-element.114), channel_id=1, source_target_pairs={{0,6},{2,4},{4,2},{6,0},{8,14},{10,12},{12,10},{14,8},{1,7},{3,5},... | collective-permute-start | bytes 393224 | tf_op jit(solution)/shard_map/ppermute | solution.py:362
  98.0 7.8 %collective-permute-start.29 = (f32[1,2,64,256]{3,2,1,0:T(8,128)S(1)}, f32[1,2,64,256]{3,2,1,0:T(8,128)S(1)}, u32[]{:S(2)}, u32[]{:S(2)}) collective-permute-start(f32[1,2,64,256]{3,2,1,0:T(8,128)S(1)} %add_add_fusion.1), channel_id=1, source_target_pairs={{0,8},{2,10},{4,12},{6,14},{8,0},{10,2},{12,4},{14,6},{1,9},{3,11}... | collective-permute-start | bytes 393224 | tf_op jit(solution)/shard_map/ppermute | solution.py:362
  105.9 7.7 %collective-permute-start.33 = (f32[1,2,64,256]{3,2,1,0:T(8,128)S(1)}, f32[1,2,64,256]{3,2,1,0:T(8,128)S(1)}, u32[]{:S(2)}, u32[]{:S(2)}) collective-permute-start(f32[1,2,64,256]{3,2,1,0:T(8,128)S(1)} %add_add_fusion), channel_id=1, source_target_pairs={{0,8},{2,10},{4,12},{6,14},{8,0},{10,2},{12,4},{14,6},{1,9},{3,11}... | collective-permute-start | bytes 393224 | tf_op jit(solution)/shard_map/ppermute | solution.py:362
  106.7 7.6 %collective-permute-start.34 = (f32[2,128,128]{2,1,0:T(8,128)S(1)}, f32[2,128,128]{2,1,0:T(8,128)S(1)}, u32[]{:S(2)}, u32[]{:S(2)}) collective-permute-start(f32[2,128,128]{2,1,0:T(8,128)S(1)} %slice_select_fusion.3), channel_id=1, source_target_pairs={{0,2},{2,0},{4,6},{6,4},{8,10},{10,8},{12,14},{14,12},{1,3},{3,1},... | collective-permute-start | bytes 393224 | tf_op jit(solution)/shard_map/ppermute | solution.py:352
  107.2 7.1 %collective-permute-start.35 = (f32[2,128,128]{2,1,0:T(8,128)S(1)}, f32[2,128,128]{2,1,0:T(8,128)S(1)}, u32[]{:S(2)}, u32[]{:S(2)}) collective-permute-start(f32[2,128,128]{2,1,0:T(8,128)S(1)} %slice_select_fusion.2), channel_id=1, source_target_pairs={{2,4},{4,2},{6,8},{8,6},{10,12},{12,10},{3,5},{5,3},{7,9},{9,7},{1... | collective-permute-start | bytes 393224 | tf_op jit(solution)/shard_map/ppermute | solution.py:352
  107.8 9.5 %collective-permute-start.36 = (f32[1,2,64,256]{3,2,1,0:T(8,128)S(1)}, f32[1,2,64,256]{3,2,1,0:T(8,128)S(1)}, u32[]{:S(2)}, u32[]{:S(2)}) collective-permute-start(f32[1,2,64,256]{3,2,1,0:T(8,128)S(1)} %add.97.refs_3_), channel_id=1, source_target_pairs={{0,2},{2,0},{4,6},{6,4},{8,10},{10,8},{12,14},{14,12},{1,3},{3,1},... | collective-permute-start | bytes 393224 | tf_op jit(solution)/shard_map/ppermute | solution.py:362
  119.6 10.5 %collective-permute-start.39 = (f32[2,2,128,128]{3,2,1,0:T(8,128)S(1)}, f32[2,2,128,128]{3,2,1,0:T(8,128)S(1)}, u32[]{:S(2)}, u32[]{:S(2)}) collective-permute-start(f32[2,2,128,128]{3,2,1,0:T(8,128)S(1)} %maximum_add_fusion.refs_0_), channel_id=1, source_target_pairs={{0,1},{1,0},{2,3},{3,2},{4,5},{5,4},{6,7},{7,6},{8,9},{9,8},{10,11... | collective-permute-start | bytes 786440 | tf_op jit(solution)/shard_map/ppermute | solution.py:343
  119.6 6.4 %collective-permute-start.40 = (f32[1,2,64,256]{3,2,1,0:T(8,128)S(1)}, f32[1,2,64,256]{3,2,1,0:T(8,128)S(1)}, u32[]{:S(2)}, u32[]{:S(2)}) collective-permute-start(f32[1,2,64,256]{3,2,1,0:T(8,128)S(1)} %add.101.refs_7_), channel_id=1, source_target_pairs={{0,2},{2,0},{4,6},{6,4},{8,10},{10,8},{12,14},{14,12},{1,3},{3,1},... | collective-permute-start | bytes 393224 | tf_op jit(solution)/shard_map/ppermute | solution.py:362
  122.7 7.3 %collective-permute-start.42 = (f32[1,2,64,256]{3,2,1,0:T(8,128)S(1)}, f32[1,2,64,256]{3,2,1,0:T(8,128)S(1)}, u32[]{:S(2)}, u32[]{:S(2)}) collective-permute-start(f32[1,2,64,256]{3,2,1,0:T(8,128)S(1)} %add.101.refs_7_), channel_id=1, source_target_pairs={{0,6},{2,4},{4,2},{6,0},{8,14},{10,12},{12,10},{14,8},{1,7},{3,5},... | collective-permute-start | bytes 393224 | tf_op jit(solution)/shard_map/ppermute | solution.py:362
  (17 other events, 53.0 us)

commit v9 on v8

--- a/solution.py
+++ b/solution.py
@@ -12,8 +12,9 @@
 MODES = 4
 GX = 8
 ITERS = 2
-BLOCK_BITS = 2
-CHUNKS = 1 << BLOCK_BITS
+HALVINGS = 2
+CHUNKS = 1 << HALVINGS
+ORDERS = ((0, 1, 2), (1, 0, 2))
 STRIP = 16
 ORDERS = ((0, 1, 2), (1, 0, 2))
 
@@ -88,8 +89,9 @@
         out[s] = dot(high, perm[0]) + (dot(mid, perm[0]) + dot(low, perm[0]))
 
 
-def chunk_key():
-    return lax.rem(lax.axis_index("tile"), CHUNKS)
+def chunk_key(order):
+    t = lax.axis_index("tile")
+    return sum(((t >> order[i]) & 1) << (HALVINGS - 1 - i) for i in range(HALVINGS))
 
 
 def corner(offsets, slot, dim, size, margin):
@@ -104,8 +106,8 @@
 
 def update_probe(old, streams, coef, out):
     rows = old.shape[2] // CHUNKS
-    key = chunk_key()
     for mode, pieces in enumerate(streams):
+        key = chunk_key(ORDERS[mode])
         rel = 0
         for piece in pieces:
             for k in range(piece.shape[0]):
@@ -238,7 +240,7 @@
         strips(h // STRIP, functools.partial(columns, s))
         for p in range(2):
             product_tall[s, p] = mul_left(tab[1, p], tall_parts[s, p])
-    key = chunk_key()
+    key = chunk_key(ORDERS[mode])
     chunk = frame // CHUNKS
     core = lax.axis_index("row")
     first = left_half()
@@ -358,8 +360,8 @@
     return lax.ppermute(x, ("tile", "row"), pairs)
 
 
-def exchange(x, mask, tiles):
-    return lax.ppermute(x, "tile", [(s, s ^ mask) for s in range(tiles)])
+def exchange(x, bit, tiles):
+    return lax.ppermute(x, "tile", [(s, s ^ (1 << bit)) for s in range(tiles)])
 
 
 def together(*groups):
@@ -385,25 +387,26 @@
 
 
 def reduce_all(parts, grad, even, tiles, wide):
+    bits = int(math.log2(tiles))
     stay, go = window_parts(grad, even, wide)
-    got = [[p[:1]] + [exchange(p[k : k + 1], k, tiles) for k in range(1, CHUNKS)] for p in parts]
-    streams = []
-    for m in range(len(parts)):
-        held = sum(got[m][1:], got[m][0])
-        if m == 0:
-            held, go = together(held, tuple(go))
-            outer = beside(go[1], False, tiles)
-            inner = beside(go[0], True, tiles)
-        mask = CHUNKS
-        while mask < tiles:
-            held = held + exchange(held, mask, tiles)
-            mask *= 2
-        if m + 1 < len(parts):
-            held, got[m + 1] = together(held, got[m + 1])
-        else:
-            held, inner, outer, *streams = together(held, inner, outer, *streams)
-        streams.append([held] + [exchange(held, k, tiles) for k in range(1, CHUNKS)])
-    return streams, jnp.stack([stay[0] + inner, stay[1] + outer])
+    held = list(parts)
+    go, got = list(go), [None, None]
+    for i in range(HALVINGS):
+        n = held[0].shape[0] // 2
+        held = [h[:n] + exchange(h[n:], o[i], tiles) for h, o in zip(held, ORDERS)]
+        held, go[1 - i] = together(held, go[1 - i])
+        got[1 - i] = beside(go[1 - i], i == 1, tiles)
+    held = [h + exchange(h, o[-1], tiles) for h, o in zip(held, ORDERS)]
+    held, got = together(held, got)
+    for bit in range(len(ORDERS[0]), bits):
+        held = [h + exchange(h, bit, tiles) for h in held]
+    pieces = [[h] for h in held]
+    for i in reversed(range(HALVINGS)):
+        for p, o in zip(pieces, ORDERS):
+            p.append(exchange(p[0] if len(p) == 1 else jnp.concatenate(p, 0), o[i], tiles))
+        if i:
+            (pieces,) = together(pieces)
+    return pieces, jnp.stack([a + b for a, b in zip(stay, got)])
 
 
 def per_device(object_tiles, probe_modes, amplitude, offsets, counts):

time: 132 us -> 129 us (0.977)
  starting transfers between devices: 49.4 us -> 40.3 us
  waiting for transfers between devices: 57.5 us -> 63.5 us
    ppermute x28 -> x20, starting transfers between devices: 41.1 us -> 31.5 us  [exchange(): return lax.ppermute(x, 'tile', [(s, s ^ 1 << bit) for s in range(tiles)])]
    ppermute x28 -> x20, waiting for transfers between devices: 52.7 us -> 58.7 us  [exchange(): return lax.ppermute(x, 'tile', [(s, s ^ 1 << bit) for s in range(tiles)])]
  transfers between devices with their start and end apart: 43 -> 35, of which waited for: 24 -> 24; matrix products, arithmetic and copies ran while one was open for 0% -> 1% of each run, Pallas kernels for 2% -> 6%
where the time goes in v9:
time: 129 us; the launch traced here: 128 us
  waiting for transfers between devices  63.5 us (49%)
  starting transfers between devices  40.3 us (31%)
  Pallas kernels  19.5 us (15%)
  local copies, waits for them, and re-layouts  2.38 us (2%)
  between operations  1.84 us (1%)
    ppermute x20, waiting for transfers between devices, exchange(): return lax.ppermute(x, 'tile', [(s, s ^ 1 << bit) for s in range(tiles)])  58.7 us
    ppermute x20, starting transfers between devices, exchange(): return lax.ppermute(x, 'tile', [(s, s ^ 1 << bit) for s in range(tiles)])  31.5 us
    pallas_call x10, Pallas kernels, call(): pl.pallas_call(kernel, out_shape=[jax.ShapeDtypeStruct(o, f32) for o in o...  19.5 us
    ppermute x6, starting transfers between devices, beside(): return lax.ppermute(x, 'tile', pairs)  7.24 us
    ppermute x6, waiting for transfers between devices, beside(): return lax.ppermute(x, 'tile', pairs)  2.84 us
  transfers between devices with their start and end apart: 35, of which 24 were waited for; matrix products, arithmetic and copies ran while one was open for 1% of the time, Pallas kernels for 6%

profile of v9, /device:TPU:0, one launch (start us, length us, event | category | flops | bytes accessed | tf_op | source)
XLA Modules:
  0.0 128.4 jit_solution(15488285044361336566)
XLA Ops:
  1.7 3.0 %collective-permute-start = (f32[2,128,128]{2,1,0:T(8,128)S(1)}, f32[2,128,128]{2,1,0:T(8,128)S(1)}, u32[]{:S(2)}, u32[]{:S(2)}) collective-permute-start(f32[2,128,128]{2,1,0:T(8,128)S(1)} %get-tuple-element.120), channel_id=1, source_target_pairs={{0,2},{2,0},{4,6},{6,4},{8,10},{10,8},{12,14},{14,12},{1,3},{3,1},... | collective-permute-start | bytes 393224 | tf_op jit(solution)/shard_map/ppermute | solution.py:354
  5.4 2.8 %collective-permute-done = f32[2,128,128]{2,1,0:T(8,128)S(1)} collective-permute-done((f32[2,128,128]{2,1,0:T(8,128)S(1)}, f32[2,128,128]{2,1,0:T(8,128)S(1)}, u32[]{:S(2)}, u32[]{:S(2)}) %collective-permute-start) | collective-permute-done | bytes 131104 | tf_op jit(solution)/shard_map/ppermute | solution.py:354
  10.5 2.0 %shard_map.87 = (f32[2,2,256,256]{3,2,1,0:T(8,128)S(1)}, f32[256,256]{1,0:T(8,128)S(1)}, f32[2,256,256]{2,1,0:T(8,128)S(1)}) custom-call(s32[2,2]{1,0:T(2,128)S(1)} %copy-done.4, f32[2,2,128,256]{3,2,1,0:T(8,128)S(1)} %pad_maximum_fusion.refs_1_, f32[2,2,128,256]{3,2,1,0:T(8,128)S(1)} %collective-permute-done.2.refs_2_, f32[2,2,256,256]{3,2,1,0:T(8,128)S(1)} %copy-done.3, ...), custom_call_target="tpu_custom_call" | custom-call | flops 3221225472 | bytes 4980752 | tf_op jit(solution)/shard_map/pallas_call | solution.py:331
  12.5 2.0 %shard_map.88 = (f32[2,2,256,256]{3,2,1,0:T(8,128)S(1)}, f32[256,256]{1,0:T(8,128)S(1)}, f32[2,256,256]{2,1,0:T(8,128)S(1)}) custom-call(s32[2,2]{1,0:T(2,128)S(1)} %copy-done.4, f32[2,2,128,256]{3,2,1,0:T(8,128)S(1)} %pad_maximum_fusion.refs_1_, f32[2,2,128,256]{3,2,1,0:T(8,128)S(1)} %collective-permute-done.2.refs_2_, f32[2,2,256,256]{3,2,1,0:T(8,128)S(1)} %copy-done.3, ...), custom_call_target="tpu_custom_call" | custom-call | flops 3221225472 | bytes 4980752 | tf_op jit(solution)/shard_map/pallas_call | solution.py:331
  16.5 2.2 %shard_map.89 = (f32[4,2,64,256]{3,2,1,0:T(8,128)S(1)}, f32[2,2,256,256]{3,2,1,0:T(8,128)S(1)}) custom-call(s32[2,2]{1,0:T(2,128)S(1)} %copy-done.4, s32[1]{0:T(128)S(6)} %copy.9.refs_1_, bf16[2,2,2,256,256]{4,3,2,1,0:T(8,128)(2,1)S(1)} %copy-done.5, f32[2,256,256]{2,1,0:T(8,128)S(1)} %shard_map.86.refs_3_, f32[2,2,256,256]{3,2,1,0:T(8,128)S(1)} %copy-done.3, ...), custom_call_target="tpu_custom_call" | custom-call | flops 3221225472 | bytes 8388628 | tf_op jit(solution)/shard_map/pallas_call | solution.py:331
  18.7 4.7 %collective-permute-start.6 = (f32[2,2,64,256]{3,2,1,0:T(8,128)S(1)}, f32[2,2,64,256]{3,2,1,0:T(8,128)S(1)}, u32[]{:S(2)}, u32[]{:S(2)}) collective-permute-start(f32[2,2,64,256]{3,2,1,0:T(8,128)S(1)} %slice.118), channel_id=1, source_target_pairs={{0,2},{2,0},{4,6},{6,4},{8,10},{10,8},{12,14},{14,12},{1,3},{3,1},... | collective-permute-start | bytes 786440 | tf_op jit(solution)/shard_map/ppermute | solution.py:364
  23.4 2.4 %shard_map.90 = (f32[4,2,64,256]{3,2,1,0:T(8,128)S(1)}, f32[2,2,2,128,256]{4,3,2,1,0:T(8,128)S(1)}) custom-call(s32[2,2]{1,0:T(2,128)S(1)} %copy-done.4, s32[1]{0:T(128)S(6)} %copy.9.refs_1_, bf16[2,2,2,256,256]{4,3,2,1,0:T(8,128)(2,1)S(1)} %copy-done.5, f32[2,256,256]{2,1,0:T(8,128)S(1)} %shard_map.86.refs_3_, f32[2,2,256,256]{3,2,1,0:T(8,128)S(1)} %copy-done.3, ...), custom_call_target="tpu_custom_call" | custom-call | flops 3221225472 | bytes 9437204 | tf_op jit(solution)/shard_map/pallas_call | solution.py:331
  26.0 1.8 %collective-permute-start.7 = (f32[2,2,64,256]{3,2,1,0:T(8,128)S(1)}, f32[2,2,64,256]{3,2,1,0:T(8,128)S(1)}, u32[]{:S(2)}, u32[]{:S(2)}) collective-permute-start(f32[2,2,64,256]{3,2,1,0:T(8,128)S(1)} %slice.120), channel_id=1, source_target_pairs={{0,4},{2,6},{4,0},{6,2},{8,12},{10,14},{12,8},{14,10},{1,5},{3,7},... | collective-permute-start | bytes 786440 | tf_op jit(solution)/shard_map/ppermute | solution.py:364
  27.8 2.3 %collective-permute-done.6 = f32[2,2,64,256]{3,2,1,0:T(8,128)S(1)} collective-permute-done((f32[2,2,64,256]{3,2,1,0:T(8,128)S(1)}, f32[2,2,64,256]{3,2,1,0:T(8,128)S(1)}, u32[]{:S(2)}, u32[]{:S(2)}) %collective-permute-start.6) | collective-permute-done | bytes 262176 | tf_op jit(solution)/shard_map/ppermute | solution.py:364
  30.1 4.7 %collective-permute-done.7 = f32[2,2,64,256]{3,2,1,0:T(8,128)S(1)} collective-permute-done((f32[2,2,64,256]{3,2,1,0:T(8,128)S(1)}, f32[2,2,64,256]{3,2,1,0:T(8,128)S(1)}, u32[]{:S(2)}, u32[]{:S(2)}) %collective-permute-start.7) | collective-permute-done | bytes 262176 | tf_op jit(solution)/shard_map/ppermute | solution.py:364
  35.0 1.8 %collective-permute-start.8 = (f32[1,2,64,256]{3,2,1,0:T(8,128)S(1)}, f32[1,2,64,256]{3,2,1,0:T(8,128)S(1)}, u32[]{:S(2)}, u32[]{:S(2)}) collective-permute-start(f32[1,2,64,256]{3,2,1,0:T(8,128)S(1)} %slice.123), channel_id=1, source_target_pairs={{0,4},{2,6},{4,0},{6,2},{8,12},{10,14},{12,8},{14,10},{1,5},{3,7},... | collective-permute-start | bytes 393224 | tf_op jit(solution)/shard_map/ppermute | solution.py:364
  36.7 1.6 %collective-permute-start.9 = (f32[1,2,64,256]{3,2,1,0:T(8,128)S(1)}, f32[1,2,64,256]{3,2,1,0:T(8,128)S(1)}, u32[]{:S(2)}, u32[]{:S(2)}) collective-permute-start(f32[1,2,64,256]{3,2,1,0:T(8,128)S(1)} %slice.125), channel_id=1, source_target_pairs={{0,2},{2,0},{4,6},{6,4},{8,10},{10,8},{12,14},{14,12},{1,3},{3,1},... | collective-permute-start | bytes 393224 | tf_op jit(solution)/shard_map/ppermute | solution.py:364
  40.2 1.6 %collective-permute-done.9 = f32[1,2,64,256]{3,2,1,0:T(8,128)S(1)} collective-permute-done((f32[1,2,64,256]{3,2,1,0:T(8,128)S(1)}, f32[1,2,64,256]{3,2,1,0:T(8,128)S(1)}, u32[]{:S(2)}, u32[]{:S(2)}) %collective-permute-start.9) | collective-permute-done | bytes 131104 | tf_op jit(solution)/shard_map/ppermute | solution.py:364
  41.8 1.6 %collective-permute-start.12 = (f32[2,128,256]{2,1,0:T(8,128)S(1)}, f32[2,128,256]{2,1,0:T(8,128)S(1)}, u32[]{:S(2)}, u32[]{:S(2)}) collective-permute-start(f32[2,128,256]{2,1,0:T(8,128)S(1)} %get-tuple-element.73), channel_id=1, source_target_pairs={{0,2},{2,0},{4,6},{6,4},{8,10},{10,8},{12,14},{14,12},{1,3},{3,1},... | collective-permute-start | bytes 786440 | tf_op jit(solution)/shard_map/ppermute | solution.py:354
  43.4 6.7 %collective-permute-start.10 = (f32[1,2,64,256]{3,2,1,0:T(8,128)S(1)}, f32[1,2,64,256]{3,2,1,0:T(8,128)S(1)}, u32[]{:S(2)}, u32[]{:S(2)}) collective-permute-start(f32[1,2,64,256]{3,2,1,0:T(8,128)S(1)} %slice_add_fusion.7), channel_id=1, source_target_pairs={{0,8},{2,10},{4,12},{6,14},{8,0},{10,2},{12,4},{14,6},{1,9},{3,11}... | collective-permute-start | bytes 393224 | tf_op jit(solution)/shard_map/ppermute | solution.py:364
  50.1 8.1 %collective-permute-done.10 = f32[1,2,64,256]{3,2,1,0:T(8,128)S(1)} collective-permute-done((f32[1,2,64,256]{3,2,1,0:T(8,128)S(1)}, f32[1,2,64,256]{3,2,1,0:T(8,128)S(1)}, u32[]{:S(2)}, u32[]{:S(2)}) %collective-permute-start.10) | collective-permute-done | bytes 131104 | tf_op jit(solution)/shard_map/ppermute | solution.py:364
  61.3 3.5 %collective-permute-done.15.refs_6_ = f32[1,2,64,256]{3,2,1,0:T(8,128)S(1)} collective-permute-done((f32[1,2,64,256]{3,2,1,0:T(8,128)S(1)}, f32[1,2,64,256]{3,2,1,0:T(8,128)S(1)}, u32[]{:S(2)}, u32[]{:S(2)}) %collective-permute-start.15) | collective-permute-done | bytes 131104 | tf_op jit(solution)/shard_map/ppermute | solution.py:364
  67.0 4.3 %collective-permute-done.17.refs_7_ = f32[2,2,64,256]{3,2,1,0:T(8,128)S(1)} collective-permute-done((f32[2,2,64,256]{3,2,1,0:T(8,128)S(1)}, f32[2,2,64,256]{3,2,1,0:T(8,128)S(1)}, u32[]{:S(2)}, u32[]{:S(2)}) %collective-permute-start.17) | collective-permute-done | bytes 262176 | tf_op jit(solution)/shard_map/ppermute | solution.py:364
  72.8 2.1 %shard_map.91 = (f32[2,2,256,256]{3,2,1,0:T(8,128)S(1)}, f32[256,256]{1,0:T(8,128)S(1)}, f32[2,256,256]{2,1,0:T(8,128)S(1)}, f32[2,2,256,256]{3,2,1,0:T(8,128)S(1)}) custom-call(s32[2,2]{1,0:T(2,128)S(1)} %copy-done.4, f32[2,2,128,256]{3,2,1,0:T(8,128)S(1)} %fusion.refs_1_, f32[2,2,128,256]{3,2,1,0:T(8,128)S(1)} %collective-permute-done.14.refs_2_, ...), custom_call_target="tpu_custom_call" | custom-call | flops 3221225472 | bytes 7077904 | tf_op jit(solution)/shard_map/pallas_call | solution.py:331
  74.9 2.0 %shard_map.92 = (f32[2,2,256,256]{3,2,1,0:T(8,128)S(1)}, f32[256,256]{1,0:T(8,128)S(1)}, f32[2,256,256]{2,1,0:T(8,128)S(1)}) custom-call(s32[2,2]{1,0:T(2,128)S(1)} %copy-done.4, f32[2,2,128,256]{3,2,1,0:T(8,128)S(1)} %fusion.refs_1_, f32[2,2,128,256]{3,2,1,0:T(8,128)S(1)} %collective-permute-done.14.refs_2_, ...), custom_call_target="tpu_custom_call" | custom-call | flops 3221225472 | bytes 4980752 | tf_op jit(solution)/shard_map/pallas_call | solution.py:331
  78.7 2.2 %shard_map.93 = (f32[4,2,64,256]{3,2,1,0:T(8,128)S(1)}, f32[2,2,256,256]{3,2,1,0:T(8,128)S(1)}) custom-call(s32[2,2]{1,0:T(2,128)S(1)} %copy-done.4, s32[1]{0:T(128)S(6)} %copy.9.refs_1_, bf16[2,2,2,256,256]{4,3,2,1,0:T(8,128)(2,1)S(1)} %copy-done.5, f32[2,256,256]{2,1,0:T(8,128)S(1)} %shard_map.86.refs_3_, ...), custom_call_target="tpu_custom_call" | custom-call | flops 3221225472 | bytes 8388628 | tf_op jit(solution)/shard_map/pallas_call | solution.py:331
  81.6 2.4 %shard_map.94 = (f32[4,2,64,256]{3,2,1,0:T(8,128)S(1)}, f32[2,2,2,128,256]{4,3,2,1,0:T(8,128)S(1)}) custom-call(s32[2,2]{1,0:T(2,128)S(1)} %copy-done.4, s32[1]{0:T(128)S(6)} %copy.9.refs_1_, bf16[2,2,2,256,256]{4,3,2,1,0:T(8,128)(2,1)S(1)} %copy-done.5, f32[2,256,256]{2,1,0:T(8,128)S(1)} %shard_map.86.refs_3_, ...), custom_call_target="tpu_custom_call" | custom-call | flops 3221225472 | bytes 9437204 | tf_op jit(solution)/shard_map/pallas_call | solution.py:331
  84.1 2.0 %collective-permute-start.23 = (f32[2,2,64,256]{3,2,1,0:T(8,128)S(1)}, f32[2,2,64,256]{3,2,1,0:T(8,128)S(1)}, u32[]{:S(2)}, u32[]{:S(2)}) collective-permute-start(f32[2,2,64,256]{3,2,1,0:T(8,128)S(1)} %slice.140), channel_id=1, source_target_pairs={{0,4},{2,6},{4,0},{6,2},{8,12},{10,14},{12,8},{14,10},{1,5},{3,7},... | collective-permute-start | bytes 786440 | tf_op jit(solution)/shard_map/ppermute | solution.py:364
  86.2 3.3 %collective-permute-done.22 = f32[2,2,64,256]{3,2,1,0:T(8,128)S(1)} collective-permute-done((f32[2,2,64,256]{3,2,1,0:T(8,128)S(1)}, f32[2,2,64,256]{3,2,1,0:T(8,128)S(1)}, u32[]{:S(2)}, u32[]{:S(2)}) %collective-permute-start.22) | collective-permute-done | bytes 262176 | tf_op jit(solution)/shard_map/ppermute | solution.py:364
  89.6 3.1 %collective-permute-done.23 = f32[2,2,64,256]{3,2,1,0:T(8,128)S(1)} collective-permute-done((f32[2,2,64,256]{3,2,1,0:T(8,128)S(1)}, f32[2,2,64,256]{3,2,1,0:T(8,128)S(1)}, u32[]{:S(2)}, u32[]{:S(2)}) %collective-permute-start.23) | collective-permute-done | bytes 262176 | tf_op jit(solution)/shard_map/ppermute | solution.py:364
  92.9 1.8 %collective-permute-start.24 = (f32[1,2,64,256]{3,2,1,0:T(8,128)S(1)}, f32[1,2,64,256]{3,2,1,0:T(8,128)S(1)}, u32[]{:S(2)}, u32[]{:S(2)}) collective-permute-start(f32[1,2,64,256]{3,2,1,0:T(8,128)S(1)} %slice.145), channel_id=1, source_target_pairs={{0,4},{2,6},{4,0},{6,2},{8,12},{10,14},{12,8},{14,10},{1,5},{3,7},... | collective-permute-start | bytes 393224 | tf_op jit(solution)/shard_map/ppermute | solution.py:364
  95.7 2.2 %collective-permute-done.24 = f32[1,2,64,256]{3,2,1,0:T(8,128)S(1)} collective-permute-done((f32[1,2,64,256]{3,2,1,0:T(8,128)S(1)}, f32[1,2,64,256]{3,2,1,0:T(8,128)S(1)}, u32[]{:S(2)}, u32[]{:S(2)}) %collective-permute-start.24) | collective-permute-done | bytes 131104 | tf_op jit(solution)/shard_map/ppermute | solution.py:364
  97.9 1.8 %collective-permute-done.25 = f32[1,2,64,256]{3,2,1,0:T(8,128)S(1)} collective-permute-done((f32[1,2,64,256]{3,2,1,0:T(8,128)S(1)}, f32[1,2,64,256]{3,2,1,0:T(8,128)S(1)}, u32[]{:S(2)}, u32[]{:S(2)}) %collective-permute-start.25) | collective-permute-done | bytes 131104 | tf_op jit(solution)/shard_map/ppermute | solution.py:364
  101.2 1.6 %collective-permute-start.27 = (f32[1,2,64,256]{3,2,1,0:T(8,128)S(1)}, f32[1,2,64,256]{3,2,1,0:T(8,128)S(1)}, u32[]{:S(2)}, u32[]{:S(2)}) collective-permute-start(f32[1,2,64,256]{3,2,1,0:T(8,128)S(1)} %slice_add_fusion.4), channel_id=1, source_target_pairs={{0,8},{2,10},{4,12},{6,14},{8,0},{10,2},{12,4},{14,6},{1,9},{3,11}... | collective-permute-start | bytes 393224 | tf_op jit(solution)/shard_map/ppermute | solution.py:364
  103.2 9.4 %collective-permute-done.26 = f32[1,2,64,256]{3,2,1,0:T(8,128)S(1)} collective-permute-done((f32[1,2,64,256]{3,2,1,0:T(8,128)S(1)}, f32[1,2,64,256]{3,2,1,0:T(8,128)S(1)}, u32[]{:S(2)}, u32[]{:S(2)}) %collective-permute-start.26) | collective-permute-done | bytes 131104 | tf_op jit(solution)/shard_map/ppermute | solution.py:364
  115.7 3.4 %collective-permute-done.31.refs_4_ = f32[1,2,64,256]{3,2,1,0:T(8,128)S(1)} collective-permute-done((f32[1,2,64,256]{3,2,1,0:T(8,128)S(1)}, f32[1,2,64,256]{3,2,1,0:T(8,128)S(1)}, u32[]{:S(2)}, u32[]{:S(2)}) %collective-permute-start.31) | collective-permute-done | bytes 131104 | tf_op jit(solution)/shard_map/ppermute | solution.py:364
  121.3 4.3 %collective-permute-done.33.refs_5_ = f32[2,2,64,256]{3,2,1,0:T(8,128)S(1)} collective-permute-done((f32[2,2,64,256]{3,2,1,0:T(8,128)S(1)}, f32[2,2,64,256]{3,2,1,0:T(8,128)S(1)}, u32[]{:S(2)}, u32[]{:S(2)}) %collective-permute-start.33) | collective-permute-done | bytes 262176 | tf_op jit(solution)/shard_map/ppermute | solution.py:364
  (106 shorter events, 28.0 us)
Async XLA Ops:
  1.7 6.5 %collective-permute-start = (f32[2,128,128]{2,1,0:T(8,128)S(1)}, f32[2,128,128]{2,1,0:T(8,128)S(1)}, u32[]{:S(2)}, u32[]{:S(2)}) collective-permute-start(f32[2,128,128]{2,1,0:T(8,128)S(1)} %get-tuple-element.120), channel_id=1, source_target_pairs={{0,2},{2,0},{4,6},{6,4},{8,10},{10,8},{12,14},{14,12},{1,3},{3,1},... | collective-permute-start | bytes 393224 | tf_op jit(solution)/shard_map/ppermute | solution.py:354
  4.8 3.5 %collective-permute-start.1 = (f32[2,128,128]{2,1,0:T(8,128)S(1)}, f32[2,128,128]{2,1,0:T(8,128)S(1)}, u32[]{:S(2)}, u32[]{:S(2)}) collective-permute-start(f32[2,128,128]{2,1,0:T(8,128)S(1)} %get-tuple-element.121), channel_id=1, source_target_pairs={{2,4},{4,2},{6,8},{8,6},{10,12},{12,10},{3,5},{5,3},{7,9},{9,7},{1... | collective-permute-start | bytes 393224 | tf_op jit(solution)/shard_map/ppermute | solution.py:354
  8.5 2.0 %collective-permute-start.2 = (f32[2,2,128,256]{3,2,1,0:T(8,128)S(1)}, f32[2,2,128,256]{3,2,1,0:T(8,128)S(1)}, u32[]{:S(2)}, u32[]{:S(2)}) collective-permute-start(f32[2,2,128,256]{3,2,1,0:T(8,128)S(1)} %pad_maximum_fusion.refs_1_), channel_id=1, source_target_pairs={{0,1},{1,0},{2,3},{3,2},{4,5},{5,4},{6,7},{7,6},{8,9},{9,8},{10,11... | collective-permute-start | bytes 1572872 | tf_op jit(solution)/shard_map/ppermute | solution.py:345
  18.7 11.3 %collective-permute-start.6 = (f32[2,2,64,256]{3,2,1,0:T(8,128)S(1)}, f32[2,2,64,256]{3,2,1,0:T(8,128)S(1)}, u32[]{:S(2)}, u32[]{:S(2)}) collective-permute-start(f32[2,2,64,256]{3,2,1,0:T(8,128)S(1)} %slice.118), channel_id=1, source_target_pairs={{0,2},{2,0},{4,6},{6,4},{8,10},{10,8},{12,14},{14,12},{1,3},{3,1},... | collective-permute-start | bytes 786440 | tf_op jit(solution)/shard_map/ppermute | solution.py:364
  25.9 8.9 %collective-permute-start.5 = (f32[2,2,128,256]{3,2,1,0:T(8,128)S(1)}, f32[2,2,128,256]{3,2,1,0:T(8,128)S(1)}, u32[]{:S(2)}, u32[]{:S(2)}) collective-permute-start(f32[2,2,128,256]{3,2,1,0:T(8,128)S(1)} %slice_bitcast_fusion.1), channel_id=1, source_target_pairs={{0,1},{1,0},{2,3},{3,2},{4,5},{5,4},{6,7},{7,6},{8,9},{9,8},{10,11... | collective-permute-start | bytes 1572872 | tf_op jit(solution)/shard_map/ppermute | solution.py:345
  26.0 8.8 %collective-permute-start.7 = (f32[2,2,64,256]{3,2,1,0:T(8,128)S(1)}, f32[2,2,64,256]{3,2,1,0:T(8,128)S(1)}, u32[]{:S(2)}, u32[]{:S(2)}) collective-permute-start(f32[2,2,64,256]{3,2,1,0:T(8,128)S(1)} %slice.120), channel_id=1, source_target_pairs={{0,4},{2,6},{4,0},{6,2},{8,12},{10,14},{12,8},{14,10},{1,5},{3,7},... | collective-permute-start | bytes 786440 | tf_op jit(solution)/shard_map/ppermute | solution.py:364
  35.0 5.2 %collective-permute-start.8 = (f32[1,2,64,256]{3,2,1,0:T(8,128)S(1)}, f32[1,2,64,256]{3,2,1,0:T(8,128)S(1)}, u32[]{:S(2)}, u32[]{:S(2)}) collective-permute-start(f32[1,2,64,256]{3,2,1,0:T(8,128)S(1)} %slice.123), channel_id=1, source_target_pairs={{0,4},{2,6},{4,0},{6,2},{8,12},{10,14},{12,8},{14,10},{1,5},{3,7},... | collective-permute-start | bytes 393224 | tf_op jit(solution)/shard_map/ppermute | solution.py:364
  36.7 5.0 %collective-permute-start.9 = (f32[1,2,64,256]{3,2,1,0:T(8,128)S(1)}, f32[1,2,64,256]{3,2,1,0:T(8,128)S(1)}, u32[]{:S(2)}, u32[]{:S(2)}) collective-permute-start(f32[1,2,64,256]{3,2,1,0:T(8,128)S(1)} %slice.125), channel_id=1, source_target_pairs={{0,2},{2,0},{4,6},{6,4},{8,10},{10,8},{12,14},{14,12},{1,3},{3,1},... | collective-permute-start | bytes 393224 | tf_op jit(solution)/shard_map/ppermute | solution.py:364
  38.3 21.4 %collective-permute-start.13 = (f32[2,128,256]{2,1,0:T(8,128)S(1)}, f32[2,128,256]{2,1,0:T(8,128)S(1)}, u32[]{:S(2)}, u32[]{:S(2)}) collective-permute-start(f32[2,128,256]{2,1,0:T(8,128)S(1)} %get-tuple-element.74), channel_id=1, source_target_pairs={{2,4},{4,2},{6,8},{8,6},{10,12},{12,10},{3,5},{5,3},{7,9},{9,7},{1... | collective-permute-start | bytes 786440 | tf_op jit(solution)/shard_map/ppermute | solution.py:354
  41.8 17.9 %collective-permute-start.12 = (f32[2,128,256]{2,1,0:T(8,128)S(1)}, f32[2,128,256]{2,1,0:T(8,128)S(1)}, u32[]{:S(2)}, u32[]{:S(2)}) collective-permute-start(f32[2,128,256]{2,1,0:T(8,128)S(1)} %get-tuple-element.73), channel_id=1, source_target_pairs={{0,2},{2,0},{4,6},{6,4},{8,10},{10,8},{12,14},{14,12},{1,3},{3,1},... | collective-permute-start | bytes 786440 | tf_op jit(solution)/shard_map/ppermute | solution.py:354
  43.4 14.9 %collective-permute-start.10 = (f32[1,2,64,256]{3,2,1,0:T(8,128)S(1)}, f32[1,2,64,256]{3,2,1,0:T(8,128)S(1)}, u32[]{:S(2)}, u32[]{:S(2)}) collective-permute-start(f32[1,2,64,256]{3,2,1,0:T(8,128)S(1)} %slice_add_fusion.7), channel_id=1, source_target_pairs={{0,8},{2,10},{4,12},{6,14},{8,0},{10,2},{12,4},{14,6},{1,9},{3,11}... | collective-permute-start | bytes 393224 | tf_op jit(solution)/shard_map/ppermute | solution.py:364
  50.1 9.6 %collective-permute-start.11 = (f32[1,2,64,256]{3,2,1,0:T(8,128)S(1)}, f32[1,2,64,256]{3,2,1,0:T(8,128)S(1)}, u32[]{:S(2)}, u32[]{:S(2)}) collective-permute-start(f32[1,2,64,256]{3,2,1,0:T(8,128)S(1)} %slice_add_fusion.6), channel_id=1, source_target_pairs={{0,8},{2,10},{4,12},{6,14},{8,0},{10,2},{12,4},{14,6},{1,9},{3,11}... | collective-permute-start | bytes 393224 | tf_op jit(solution)/shard_map/ppermute | solution.py:364
  59.7 5.0 %collective-permute-start.15 = (f32[1,2,64,256]{3,2,1,0:T(8,128)S(1)}, f32[1,2,64,256]{3,2,1,0:T(8,128)S(1)}, u32[]{:S(2)}, u32[]{:S(2)}) collective-permute-start(f32[1,2,64,256]{3,2,1,0:T(8,128)S(1)} %add.74.refs_5_), channel_id=1, source_target_pairs={{0,4},{2,6},{4,0},{6,2},{8,12},{10,14},{12,8},{14,10},{1,5},{3,7},... | collective-permute-start | bytes 393224 | tf_op jit(solution)/shard_map/ppermute | solution.py:364
  59.8 5.0 %collective-permute-start.16 = (f32[1,2,64,256]{3,2,1,0:T(8,128)S(1)}, f32[1,2,64,256]{3,2,1,0:T(8,128)S(1)}, u32[]{:S(2)}, u32[]{:S(2)}) collective-permute-start(f32[1,2,64,256]{3,2,1,0:T(8,128)S(1)} %add.75.refs_8_), channel_id=1, source_target_pairs={{0,2},{2,0},{4,6},{6,4},{8,10},{10,8},{12,14},{14,12},{1,3},{3,1},... | collective-permute-start | bytes 393224 | tf_op jit(solution)/shard_map/ppermute | solution.py:364
  61.2 11.5 %collective-permute-start.14 = (f32[2,2,128,256]{3,2,1,0:T(8,128)S(1)}, f32[2,2,128,256]{3,2,1,0:T(8,128)S(1)}, u32[]{:S(2)}, u32[]{:S(2)}) collective-permute-start(f32[2,2,128,256]{3,2,1,0:T(8,128)S(1)} %fusion.refs_1_), channel_id=1, source_target_pairs={{0,1},{1,0},{2,3},{3,2},{4,5},{5,4},{6,7},{7,6},{8,9},{9,8},{10,11... | collective-permute-start | bytes 1572872 | tf_op jit(solution)/shard_map/ppermute | solution.py:345
  64.9 6.4 %collective-permute-start.17 = (f32[2,2,64,256]{3,2,1,0:T(8,128)S(1)}, f32[2,2,64,256]{3,2,1,0:T(8,128)S(1)}, u32[]{:S(2)}, u32[]{:S(2)}) collective-permute-start(f32[2,2,64,256]{3,2,1,0:T(8,128)S(1)} %pad_maximum_fusion.1), channel_id=1, source_target_pairs={{0,2},{2,0},{4,6},{6,4},{8,10},{10,8},{12,14},{14,12},{1,3},{3,1},... | collective-permute-start | bytes 786440 | tf_op jit(solution)/shard_map/ppermute | solution.py:364
  66.3 6.4 %collective-permute-start.18 = (f32[2,2,64,256]{3,2,1,0:T(8,128)S(1)}, f32[2,2,64,256]{3,2,1,0:T(8,128)S(1)}, u32[]{:S(2)}, u32[]{:S(2)}) collective-permute-start(f32[2,2,64,256]{3,2,1,0:T(8,128)S(1)} %pad_maximum_fusion.2), channel_id=1, source_target_pairs={{0,4},{2,6},{4,0},{6,2},{8,12},{10,14},{12,8},{14,10},{1,5},{3,7},... | collective-permute-start | bytes 786440 | tf_op jit(solution)/shard_map/ppermute | solution.py:364
  74.9 2.7 %collective-permute-start.19 = (f32[256,256]{1,0:T(8,128)S(1)}, f32[256,256]{1,0:T(8,128)S(1)}, u32[]{:S(2)}, u32[]{:S(2)}) collective-permute-start(f32[256,256]{1,0:T(8,128)S(1)} %get-tuple-element.86.refs_7_), channel_id=1, source_target_pairs={{0,1},{1,0},{2,3},{3,2},{4,5},{5,4},{6,7},{7,6},{8,9},{9,8},{10,11... | collective-permute-start | bytes 786440 | tf_op jit(solution)/shard_map/ppermute | solution.py:345
  80.9 8.7 %collective-permute-start.22 = (f32[2,2,64,256]{3,2,1,0:T(8,128)S(1)}, f32[2,2,64,256]{3,2,1,0:T(8,128)S(1)}, u32[]{:S(2)}, u32[]{:S(2)}) collective-permute-start(f32[2,2,64,256]{3,2,1,0:T(8,128)S(1)} %slice.138), channel_id=1, source_target_pairs={{0,2},{2,0},{4,6},{6,4},{8,10},{10,8},{12,14},{14,12},{1,3},{3,1},... | collective-permute-start | bytes 786440 | tf_op jit(solution)/shard_map/ppermute | solution.py:364
  84.1 8.6 %collective-permute-start.23 = (f32[2,2,64,256]{3,2,1,0:T(8,128)S(1)}, f32[2,2,64,256]{3,2,1,0:T(8,128)S(1)}, u32[]{:S(2)}, u32[]{:S(2)}) collective-permute-start(f32[2,2,64,256]{3,2,1,0:T(8,128)S(1)} %slice.140), channel_id=1, source_target_pairs={{0,4},{2,6},{4,0},{6,2},{8,12},{10,14},{12,8},{14,10},{1,5},{3,7},... | collective-permute-start | bytes 786440 | tf_op jit(solution)/shard_map/ppermute | solution.py:364
  86.1 6.6 %collective-permute-start.21 = (f32[2,2,128,256]{3,2,1,0:T(8,128)S(1)}, f32[2,2,128,256]{3,2,1,0:T(8,128)S(1)}, u32[]{:S(2)}, u32[]{:S(2)}) collective-permute-start(f32[2,2,128,256]{3,2,1,0:T(8,128)S(1)} %slice_bitcast_fusion), channel_id=1, source_target_pairs={{0,1},{1,0},{2,3},{3,2},{4,5},{5,4},{6,7},{7,6},{8,9},{9,8},{10,11... | collective-permute-start | bytes 1572872 | tf_op jit(solution)/shard_map/ppermute | solution.py:345
  92.9 5.0 %collective-permute-start.24 = (f32[1,2,64,256]{3,2,1,0:T(8,128)S(1)}, f32[1,2,64,256]{3,2,1,0:T(8,128)S(1)}, u32[]{:S(2)}, u32[]{:S(2)}) collective-permute-start(f32[1,2,64,256]{3,2,1,0:T(8,128)S(1)} %slice.145), channel_id=1, source_target_pairs={{0,4},{2,6},{4,0},{6,2},{8,12},{10,14},{12,8},{14,10},{1,5},{3,7},... | collective-permute-start | bytes 393224 | tf_op jit(solution)/shard_map/ppermute | solution.py:364
  94.7 5.0 %collective-permute-start.25 = (f32[1,2,64,256]{3,2,1,0:T(8,128)S(1)}, f32[1,2,64,256]{3,2,1,0:T(8,128)S(1)}, u32[]{:S(2)}, u32[]{:S(2)}) collective-permute-start(f32[1,2,64,256]{3,2,1,0:T(8,128)S(1)} %slice.147), channel_id=1, source_target_pairs={{0,2},{2,0},{4,6},{6,4},{8,10},{10,8},{12,14},{14,12},{1,3},{3,1},... | collective-permute-start | bytes 393224 | tf_op jit(solution)/shard_map/ppermute | solution.py:364
  95.0 19.0 %collective-permute-start.29 = (f32[2,128,128]{2,1,0:T(8,128)S(1)}, f32[2,128,128]{2,1,0:T(8,128)S(1)}, u32[]{:S(2)}, u32[]{:S(2)}) collective-permute-start(f32[2,128,128]{2,1,0:T(8,128)S(1)} %slice_select_fusion.2), channel_id=1, source_target_pairs={{2,4},{4,2},{6,8},{8,6},{10,12},{12,10},{3,5},{5,3},{7,9},{9,7},{1... | collective-permute-start | bytes 393224 | tf_op jit(solution)/shard_map/ppermute | solution.py:354
  99.7 12.9 %collective-permute-start.26 = (f32[1,2,64,256]{3,2,1,0:T(8,128)S(1)}, f32[1,2,64,256]{3,2,1,0:T(8,128)S(1)}, u32[]{:S(2)}, u32[]{:S(2)}) collective-permute-start(f32[1,2,64,256]{3,2,1,0:T(8,128)S(1)} %slice_add_fusion.5), channel_id=1, source_target_pairs={{0,8},{2,10},{4,12},{6,14},{8,0},{10,2},{12,4},{14,6},{1,9},{3,11}... | collective-permute-start | bytes 393224 | tf_op jit(solution)/shard_map/ppermute | solution.py:364
  101.2 12.9 %collective-permute-start.27 = (f32[1,2,64,256]{3,2,1,0:T(8,128)S(1)}, f32[1,2,64,256]{3,2,1,0:T(8,128)S(1)}, u32[]{:S(2)}, u32[]{:S(2)}) collective-permute-start(f32[1,2,64,256]{3,2,1,0:T(8,128)S(1)} %slice_add_fusion.4), channel_id=1, source_target_pairs={{0,8},{2,10},{4,12},{6,14},{8,0},{10,2},{12,4},{14,6},{1,9},{3,11}... | collective-permute-start | bytes 393224 | tf_op jit(solution)/shard_map/ppermute | solution.py:364
  102.7 11.3 %collective-permute-start.28 = (f32[2,128,128]{2,1,0:T(8,128)S(1)}, f32[2,128,128]{2,1,0:T(8,128)S(1)}, u32[]{:S(2)}, u32[]{:S(2)}) collective-permute-start(f32[2,128,128]{2,1,0:T(8,128)S(1)} %slice_select_fusion.3), channel_id=1, source_target_pairs={{0,2},{2,0},{4,6},{6,4},{8,10},{10,8},{12,14},{14,12},{1,3},{3,1},... | collective-permute-start | bytes 393224 | tf_op jit(solution)/shard_map/ppermute | solution.py:354
  114.1 5.0 %collective-permute-start.31 = (f32[1,2,64,256]{3,2,1,0:T(8,128)S(1)}, f32[1,2,64,256]{3,2,1,0:T(8,128)S(1)}, u32[]{:S(2)}, u32[]{:S(2)}) collective-permute-start(f32[1,2,64,256]{3,2,1,0:T(8,128)S(1)} %add.84.refs_3_), channel_id=1, source_target_pairs={{0,4},{2,6},{4,0},{6,2},{8,12},{10,14},{12,8},{14,10},{1,5},{3,7},... | collective-permute-start | bytes 393224 | tf_op jit(solution)/shard_map/ppermute | solution.py:364
  114.2 5.0 %collective-permute-start.32 = (f32[1,2,64,256]{3,2,1,0:T(8,128)S(1)}, f32[1,2,64,256]{3,2,1,0:T(8,128)S(1)}, u32[]{:S(2)}, u32[]{:S(2)}) collective-permute-start(f32[1,2,64,256]{3,2,1,0:T(8,128)S(1)} %add.85.refs_6_), channel_id=1, source_target_pairs={{0,2},{2,0},{4,6},{6,4},{8,10},{10,8},{12,14},{14,12},{1,3},{3,1},... | collective-permute-start | bytes 393224 | tf_op jit(solution)/shard_map/ppermute | solution.py:364
  115.7 5.7 %collective-permute-start.30 = (f32[2,2,128,128]{3,2,1,0:T(8,128)S(1)}, f32[2,2,128,128]{3,2,1,0:T(8,128)S(1)}, u32[]{:S(2)}, u32[]{:S(2)}) collective-permute-start(f32[2,2,128,128]{3,2,1,0:T(8,128)S(1)} %maximum_add_fusion.refs_0_), channel_id=1, source_target_pairs={{0,1},{1,0},{2,3},{3,2},{4,5},{5,4},{6,7},{7,6},{8,9},{9,8},{10,11... | collective-permute-start | bytes 786440 | tf_op jit(solution)/shard_map/ppermute | solution.py:345
  119.2 6.4 %collective-permute-start.33 = (f32[2,2,64,256]{3,2,1,0:T(8,128)S(1)}, f32[2,2,64,256]{3,2,1,0:T(8,128)S(1)}, u32[]{:S(2)}, u32[]{:S(2)}) collective-permute-start(f32[2,2,64,256]{3,2,1,0:T(8,128)S(1)} %pad_maximum_fusion.3), channel_id=1, source_target_pairs={{0,2},{2,0},{4,6},{6,4},{8,10},{10,8},{12,14},{14,12},{1,3},{3,1},... | collective-permute-start | bytes 786440 | tf_op jit(solution)/shard_map/ppermute | solution.py:364
  120.7 6.4 %collective-permute-start.34 = (f32[2,2,64,256]{3,2,1,0:T(8,128)S(1)}, f32[2,2,64,256]{3,2,1,0:T(8,128)S(1)}, u32[]{:S(2)}, u32[]{:S(2)}) collective-permute-start(f32[2,2,64,256]{3,2,1,0:T(8,128)S(1)} %pad_maximum_fusion.4), channel_id=1, source_target_pairs={{0,4},{2,6},{4,0},{6,2},{8,12},{10,14},{12,8},{14,10},{1,5},{3,7},... | collective-permute-start | bytes 786440 | tf_op jit(solution)/shard_map/ppermute | solution.py:364
  (9 other events, 14.6 us)

commit v10 on v9

--- a/solution.py
+++ b/solution.py
@@ -211,16 +211,26 @@
     offsets, counts, tab, amp, probe = refs[:5]
     refs = refs[5:]
     slots = amp.shape[0]
-    fars, powers, others, patches = (refs[i * slots : (i + 1) * slots] for i in range(4))
-    refs = refs[4 * slots :]
-    before = refs.pop(0) if mode else None
+    fars, patches = refs[:slots], refs[slots : 2 * slots]
+    refs = refs[2 * slots :]
+    if mode:
+        factors_in, before = refs[:2]
+        refs = refs[2:]
+    else:
+        powers, others = refs[:slots], refs[slots : 2 * slots]
+        refs = refs[2 * slots :]
+        factors_out = refs.pop(2)
     probe_grad, grads, tall_parts, wide_parts, product_wide, product_tall = refs
     frame = probe.shape[-1]
     h = frame // 2
 
     def factors(s, j):
         rows = at(j * STRIP)
-        factor = amp[s, rows, :] / (jnp.sqrt(powers[s][rows, :] + others[s][rows, :]) + 0.5)
+        if mode:
+            factor = factors_in[s, rows, :]
+        else:
+            factor = amp[s, rows, :] / (jnp.sqrt(powers[s][rows, :] + others[s][rows, :]) + 0.5)
+            factors_out[s, rows, :] = factor
         for q in range(2):
             f = factor[:, q * h : (q + 1) * h]
             put(wide_parts, s, q, rows, fars[s][mode, q, rows, :] * jnp.concatenate([f, f], 1))
@@ -394,8 +404,12 @@
     for i in range(HALVINGS):
         n = held[0].shape[0] // 2
         held = [h[:n] + exchange(h[n:], o[i], tiles) for h, o in zip(held, ORDERS)]
-        held, go[1 - i] = together(held, go[1 - i])
-        got[1 - i] = beside(go[1 - i], i == 1, tiles)
+        if i == 0:
+            held, go[1] = together(held, go[1])
+            got[1] = beside(go[1], False, tiles)
+        else:
+            held, go[0], got[1] = together(held, go[0], got[1])
+            got[0] = beside(go[0], True, tiles)
     held = [h + exchange(h, o[-1], tiles) for h, o in zip(held, ORDERS)]
     held, got = together(held, got)
     for bit in range(len(ORDERS[0]), bits):
@@ -428,13 +442,13 @@
     mine = lax.dynamic_slice(own_tile, (0, core * hr, 0), (2, hr, size))
     own = [jnp.where(even == inner, mine[:, :, half:], mine[:, :, :half]) for inner in (True, False)]
     got = [beside(own[1], False, tiles), beside(own[0], True, tiles)]
+    (amp,) = call(amplitude_kernel, [amplitude.shape], [amplitude, perm])
+    got, amp = together(got, amp)
     near = jnp.stack([joined(own[0], got[1], even, True), joined(own[1], got[0], even, False)])
     if tall:
         other = swap_vertical(near, tiles)
         near = jnp.where(core == 0, jnp.concatenate([other, near], 2), jnp.concatenate([near, other], 2))
-    (amp,) = call(amplitude_kernel, [amplitude.shape], [amplitude, perm])
     away = swap_rows(near)
-    near, away, amp = together(near, away, amp)
 
     def scratch(count):
         return [pltpu.VMEM((count, 2, 2, frame, frame), bf16) for _ in range(2)]
@@ -467,24 +481,24 @@
             powers.append(got[1])
             patches.append(got[2])
             others.append(swap_rows(got[1]))
-        before = None
+        before = factors = None
         parts = []
         for m in range(modes):
             last = m == modes - 1
-            args = [offsets, counts, tab, amp, probe] + fars + powers + others + patches
-            if m:
-                args.append(before)
+            args = [offsets, counts, tab, amp, probe] + fars + patches
+            args += [factors, before] if m else powers + others
             grads = (2,) + near.shape if last and not tall else (slots, 2, frame, frame)
             part = (CHUNKS, 2, frame // CHUNKS, frame)
             got = call(
                 functools.partial(inverse_kernel, m, last, tall),
-                [part, grads],
+                [part, grads] if m else [part, grads, amp.shape],
                 args,
                 scratch(slots) + [pltpu.VMEM((slots, 2, frame, frame), f32) for _ in range(2)],
                 matmul * slots,
             )
             parts.append(got[0])
             before = got[1]
+            factors = got[2] if m == 0 else None
         if tall:
             (before,) = call(place_kernel, [(2,) + near.shape], [offsets, before])
         grad = before[0] + swap_rows(before[1])

time: 129 us -> 135 us (1.047)
  starting transfers between devices: 40.3 us -> 48.7 us
  waiting for transfers between devices: 63.5 us -> 62 us
    ppermute x6, starting transfers between devices: 7.24 us -> 18.8 us  [beside(): return lax.ppermute(x, 'tile', pairs)]
    ppermute x20, waiting for transfers between devices: 58.7 us -> 54.4 us  [exchange(): return lax.ppermute(x, 'tile', [(s, s ^ 1 << bit) for s in range(tiles)])]
    ppermute x20, starting transfers between devices: 31.5 us -> 28.2 us  [exchange(): return lax.ppermute(x, 'tile', [(s, s ^ 1 << bit) for s in range(tiles)])]
    ppermute x9, waiting for transfers between devices: 1.92 us -> 3.52 us  [swap_rows(): return lax.ppermute(x, 'row', [(0, 1), (1, 0)])]
  transfers between devices with their start and end apart: 35 -> 35, of which waited for: 24 -> 24; matrix products, arithmetic and copies ran while one was open for 1% -> 1% of each run, Pallas kernels for 6% -> 7%
where the time goes in v10:
time: 135 us
  waiting for transfers between devices  62 us (46%)
  starting transfers between devices  48.7 us (36%)
  Pallas kernels  19.8 us (15%)
  between operations  1.82 us (1%)
  local copies, waits for them, and re-layouts  1.37 us (1%)
    ppermute x20, waiting for transfers between devices, exchange(): return lax.ppermute(x, 'tile', [(s, s ^ 1 << bit) for s in range(tiles)])  54.4 us
    ppermute x20, starting transfers between devices, exchange(): return lax.ppermute(x, 'tile', [(s, s ^ 1 << bit) for s in range(tiles)])  28.2 us
    pallas_call x10, Pallas kernels, call(): pl.pallas_call(kernel, out_shape=[jax.ShapeDtypeStruct(o, f32) for o in o...  19.8 us
    ppermute x6, starting transfers between devices, beside(): return lax.ppermute(x, 'tile', pairs)  18.8 us
    ppermute x6, waiting for transfers between devices, beside(): return lax.ppermute(x, 'tile', pairs)  4.02 us
    ppermute x9, waiting for transfers between devices, swap_rows(): return lax.ppermute(x, 'row', [(0, 1), (1, 0)])  3.52 us
  transfers between devices with their start and end apart: 35, of which 24 were waited for; matrix products, arithmetic and copies ran while one was open for 1% of the time, Pallas kernels for 7%

profile of v10, /device:TPU:0, one launch (start us, length us, event | category | flops | bytes accessed | tf_op | source)
XLA Modules:
  0.0 134.6 jit_solution(10051674544980922674)
XLA Ops:
  2.6 5.8 %collective-permute-start.1 = (f32[2,128,128]{2,1,0:T(8,128)S(1)}, f32[2,128,128]{2,1,0:T(8,128)S(1)}, u32[]{:S(2)}, u32[]{:S(2)}) collective-permute-start(f32[2,128,128]{2,1,0:T(8,128)S(1)} %get-tuple-element.130), channel_id=1, source_target_pairs={{0,2},{2,0},{4,6},{6,4},{8,10},{10,8},{12,14},{14,12},{1,3},{3,1},... | collective-permute-start | bytes 393224 | tf_op jit(solution)/shard_map/ppermute | solution.py:364
  9.2 4.0 %collective-permute-done.1 = f32[2,128,128]{2,1,0:T(8,128)S(1)} collective-permute-done((f32[2,128,128]{2,1,0:T(8,128)S(1)}, f32[2,128,128]{2,1,0:T(8,128)S(1)}, u32[]{:S(2)}, u32[]{:S(2)}) %collective-permute-start.1) | collective-permute-done | bytes 131104 | tf_op jit(solution)/shard_map/ppermute | solution.py:364
  13.5 1.9 %collective-permute-done.2.refs_2_ = f32[2,2,128,256]{3,2,1,0:T(8,128)S(1)} collective-permute-done((f32[2,2,128,256]{3,2,1,0:T(8,128)S(1)}, f32[2,2,128,256]{3,2,1,0:T(8,128)S(1)}, u32[]{:S(2)}, u32[]{:S(2)}) %collective-permute-start.2) | collective-permute-done | bytes 524320 | tf_op jit(solution)/shard_map/ppermute | solution.py:355
  15.4 2.1 %shard_map.87 = (f32[2,2,256,256]{3,2,1,0:T(8,128)S(1)}, f32[256,256]{1,0:T(8,128)S(1)}, f32[2,256,256]{2,1,0:T(8,128)S(1)}) custom-call(s32[2,2]{1,0:T(2,128)S(1)} %copy-done.4, f32[2,2,128,256]{3,2,1,0:T(8,128)S(1)} %pad_maximum_fusion.refs_1_, f32[2,2,128,256]{3,2,1,0:T(8,128)S(1)} %collective-permute-done.2.refs_2_, f32[2,2,256,256]{3,2,1,0:T(8,128)S(1)} %copy-done.3, ...), custom_call_target="tpu_custom_call" | custom-call | flops 3221225472 | bytes 4980752 | tf_op jit(solution)/shard_map/pallas_call | solution.py:341
  17.6 2.1 %shard_map.88 = (f32[2,2,256,256]{3,2,1,0:T(8,128)S(1)}, f32[256,256]{1,0:T(8,128)S(1)}, f32[2,256,256]{2,1,0:T(8,128)S(1)}) custom-call(s32[2,2]{1,0:T(2,128)S(1)} %copy-done.4, f32[2,2,128,256]{3,2,1,0:T(8,128)S(1)} %pad_maximum_fusion.refs_1_, f32[2,2,128,256]{3,2,1,0:T(8,128)S(1)} %collective-permute-done.2.refs_2_, f32[2,2,256,256]{3,2,1,0:T(8,128)S(1)} %copy-done.3, ...), custom_call_target="tpu_custom_call" | custom-call | flops 3221225472 | bytes 4980752 | tf_op jit(solution)/shard_map/pallas_call | solution.py:341
  21.3 2.2 %shard_map.89 = (f32[4,2,64,256]{3,2,1,0:T(8,128)S(1)}, f32[2,2,256,256]{3,2,1,0:T(8,128)S(1)}, f32[2,256,256]{2,1,0:T(8,128)S(1)}) custom-call(s32[2,2]{1,0:T(2,128)S(1)} %copy-done.4, s32[1]{0:T(128)S(6)} %copy.9.refs_1_, bf16[2,2,2,256,256]{4,3,2,1,0:T(8,128)(2,1)S(1)} %copy-done.5, f32[2,256,256]{2,1,0:T(8,128)S(1)} %shard_map.86.refs_3_, ...), custom_call_target="tpu_custom_call" | custom-call | flops 3221225472 | bytes 8912916 | tf_op jit(solution)/shard_map/pallas_call | solution.py:341
  23.6 2.6 %collective-permute-start.6 = (f32[2,2,64,256]{3,2,1,0:T(8,128)S(1)}, f32[2,2,64,256]{3,2,1,0:T(8,128)S(1)}, u32[]{:S(2)}, u32[]{:S(2)}) collective-permute-start(f32[2,2,64,256]{3,2,1,0:T(8,128)S(1)} %slice.118), channel_id=1, source_target_pairs={{0,2},{2,0},{4,6},{6,4},{8,10},{10,8},{12,14},{14,12},{1,3},{3,1},... | collective-permute-start | bytes 786440 | tf_op jit(solution)/shard_map/ppermute | solution.py:374
  26.1 2.4 %shard_map.90 = (f32[4,2,64,256]{3,2,1,0:T(8,128)S(1)}, f32[2,2,2,128,256]{4,3,2,1,0:T(8,128)S(1)}) custom-call(s32[2,2]{1,0:T(2,128)S(1)} %copy-done.4, s32[1]{0:T(128)S(6)} %copy.9.refs_1_, bf16[2,2,2,256,256]{4,3,2,1,0:T(8,128)(2,1)S(1)} %copy-done.5, f32[2,256,256]{2,1,0:T(8,128)S(1)} %shard_map.86.refs_3_, f32[2,2,256,256]{3,2,1,0:T(8,128)S(1)} %copy-done.3, ...), custom_call_target="tpu_custom_call" | custom-call | flops 3221225472 | bytes 8912916 | tf_op jit(solution)/shard_map/pallas_call | solution.py:341
  30.4 2.5 %collective-permute-done.6 = f32[2,2,64,256]{3,2,1,0:T(8,128)S(1)} collective-permute-done((f32[2,2,64,256]{3,2,1,0:T(8,128)S(1)}, f32[2,2,64,256]{3,2,1,0:T(8,128)S(1)}, u32[]{:S(2)}, u32[]{:S(2)}) %collective-permute-start.6) | collective-permute-done | bytes 262176 | tf_op jit(solution)/shard_map/ppermute | solution.py:374
  33.0 4.5 %collective-permute-done.7 = f32[2,2,64,256]{3,2,1,0:T(8,128)S(1)} collective-permute-done((f32[2,2,64,256]{3,2,1,0:T(8,128)S(1)}, f32[2,2,64,256]{3,2,1,0:T(8,128)S(1)}, u32[]{:S(2)}, u32[]{:S(2)}) %collective-permute-start.7) | collective-permute-done | bytes 262176 | tf_op jit(solution)/shard_map/ppermute | solution.py:374
  40.8 2.0 %collective-permute-done.8 = f32[1,2,64,256]{3,2,1,0:T(8,128)S(1)} collective-permute-done((f32[1,2,64,256]{3,2,1,0:T(8,128)S(1)}, f32[1,2,64,256]{3,2,1,0:T(8,128)S(1)}, u32[]{:S(2)}, u32[]{:S(2)}) %collective-permute-start.8) | collective-permute-done | bytes 131104 | tf_op jit(solution)/shard_map/ppermute | solution.py:374
  44.4 7.1 %collective-permute-start.13 = (f32[2,128,256]{2,1,0:T(8,128)S(1)}, f32[2,128,256]{2,1,0:T(8,128)S(1)}, u32[]{:S(2)}, u32[]{:S(2)}) collective-permute-start(f32[2,128,256]{2,1,0:T(8,128)S(1)} %get-tuple-element.79), channel_id=1, source_target_pairs={{0,2},{2,0},{4,6},{6,4},{8,10},{10,8},{12,14},{14,12},{1,3},{3,1},... | collective-permute-start | bytes 786440 | tf_op jit(solution)/shard_map/ppermute | solution.py:364
  54.5 7.1 %collective-permute-done.11 = f32[1,2,64,256]{3,2,1,0:T(8,128)S(1)} collective-permute-done((f32[1,2,64,256]{3,2,1,0:T(8,128)S(1)}, f32[1,2,64,256]{3,2,1,0:T(8,128)S(1)}, u32[]{:S(2)}, u32[]{:S(2)}) %collective-permute-start.11) | collective-permute-done | bytes 131104 | tf_op jit(solution)/shard_map/ppermute | solution.py:374
  61.5 2.5 %collective-permute-done.12 = f32[1,2,64,256]{3,2,1,0:T(8,128)S(1)} collective-permute-done((f32[1,2,64,256]{3,2,1,0:T(8,128)S(1)}, f32[1,2,64,256]{3,2,1,0:T(8,128)S(1)}, u32[]{:S(2)}, u32[]{:S(2)}) %collective-permute-start.12) | collective-permute-done | bytes 131104 | tf_op jit(solution)/shard_map/ppermute | solution.py:374
  65.0 4.5 %collective-permute-done.15.refs_6_ = f32[1,2,64,256]{3,2,1,0:T(8,128)S(1)} collective-permute-done((f32[1,2,64,256]{3,2,1,0:T(8,128)S(1)}, f32[1,2,64,256]{3,2,1,0:T(8,128)S(1)}, u32[]{:S(2)}, u32[]{:S(2)}) %collective-permute-start.15) | collective-permute-done | bytes 131104 | tf_op jit(solution)/shard_map/ppermute | solution.py:374
  69.9 1.9 %collective-permute-start.18 = (f32[2,2,64,256]{3,2,1,0:T(8,128)S(1)}, f32[2,2,64,256]{3,2,1,0:T(8,128)S(1)}, u32[]{:S(2)}, u32[]{:S(2)}) collective-permute-start(f32[2,2,64,256]{3,2,1,0:T(8,128)S(1)} %pad_maximum_fusion.2), channel_id=1, source_target_pairs={{0,4},{2,6},{4,0},{6,2},{8,12},{10,14},{12,8},{14,10},{1,5},{3,7},... | collective-permute-start | bytes 786440 | tf_op jit(solution)/shard_map/ppermute | solution.py:374
  71.9 5.0 %collective-permute-done.17.refs_7_ = f32[2,2,64,256]{3,2,1,0:T(8,128)S(1)} collective-permute-done((f32[2,2,64,256]{3,2,1,0:T(8,128)S(1)}, f32[2,2,64,256]{3,2,1,0:T(8,128)S(1)}, u32[]{:S(2)}, u32[]{:S(2)}) %collective-permute-start.17) | collective-permute-done | bytes 262176 | tf_op jit(solution)/shard_map/ppermute | solution.py:374
  76.9 2.1 %shard_map.91 = (f32[2,2,256,256]{3,2,1,0:T(8,128)S(1)}, f32[256,256]{1,0:T(8,128)S(1)}, f32[2,256,256]{2,1,0:T(8,128)S(1)}, f32[2,2,256,256]{3,2,1,0:T(8,128)S(1)}) custom-call(s32[2,2]{1,0:T(2,128)S(1)} %copy-done.4, f32[2,2,128,256]{3,2,1,0:T(8,128)S(1)} %fusion.refs_1_, f32[2,2,128,256]{3,2,1,0:T(8,128)S(1)} %collective-permute-done.14.refs_2_, ...), custom_call_target="tpu_custom_call" | custom-call | flops 3221225472 | bytes 7077904 | tf_op jit(solution)/shard_map/pallas_call | solution.py:341
  79.2 2.1 %shard_map.92 = (f32[2,2,256,256]{3,2,1,0:T(8,128)S(1)}, f32[256,256]{1,0:T(8,128)S(1)}, f32[2,256,256]{2,1,0:T(8,128)S(1)}) custom-call(s32[2,2]{1,0:T(2,128)S(1)} %copy-done.4, f32[2,2,128,256]{3,2,1,0:T(8,128)S(1)} %fusion.refs_1_, f32[2,2,128,256]{3,2,1,0:T(8,128)S(1)} %collective-permute-done.14.refs_2_, ...), custom_call_target="tpu_custom_call" | custom-call | flops 3221225472 | bytes 4980752 | tf_op jit(solution)/shard_map/pallas_call | solution.py:341
  83.0 2.2 %shard_map.93 = (f32[4,2,64,256]{3,2,1,0:T(8,128)S(1)}, f32[2,2,256,256]{3,2,1,0:T(8,128)S(1)}, f32[2,256,256]{2,1,0:T(8,128)S(1)}) custom-call(s32[2,2]{1,0:T(2,128)S(1)} %copy-done.4, s32[1]{0:T(128)S(6)} %copy.9.refs_1_, bf16[2,2,2,256,256]{4,3,2,1,0:T(8,128)(2,1)S(1)} %copy-done.5, f32[2,256,256]{2,1,0:T(8,128)S(1)} %shard_map.86.refs_3_, ...), custom_call_target="tpu_custom_call" | custom-call | flops 3221225472 | bytes 8912916 | tf_op jit(solution)/shard_map/pallas_call | solution.py:341
  87.0 2.4 %shard_map.94 = (f32[4,2,64,256]{3,2,1,0:T(8,128)S(1)}, f32[2,2,2,128,256]{4,3,2,1,0:T(8,128)S(1)}) custom-call(s32[2,2]{1,0:T(2,128)S(1)} %copy-done.4, s32[1]{0:T(128)S(6)} %copy.9.refs_1_, bf16[2,2,2,256,256]{4,3,2,1,0:T(8,128)(2,1)S(1)} %copy-done.5, f32[2,256,256]{2,1,0:T(8,128)S(1)} %shard_map.86.refs_3_, ...), custom_call_target="tpu_custom_call" | custom-call | flops 3221225472 | bytes 8912916 | tf_op jit(solution)/shard_map/pallas_call | solution.py:341
  91.0 2.8 %collective-permute-done.22 = f32[2,2,64,256]{3,2,1,0:T(8,128)S(1)} collective-permute-done((f32[2,2,64,256]{3,2,1,0:T(8,128)S(1)}, f32[2,2,64,256]{3,2,1,0:T(8,128)S(1)}, u32[]{:S(2)}, u32[]{:S(2)}) %collective-permute-start.22) | collective-permute-done | bytes 262176 | tf_op jit(solution)/shard_map/ppermute | solution.py:374
  93.9 3.9 %collective-permute-done.23 = f32[2,2,64,256]{3,2,1,0:T(8,128)S(1)} collective-permute-done((f32[2,2,64,256]{3,2,1,0:T(8,128)S(1)}, f32[2,2,64,256]{3,2,1,0:T(8,128)S(1)}, u32[]{:S(2)}, u32[]{:S(2)}) %collective-permute-start.23) | collective-permute-done | bytes 262176 | tf_op jit(solution)/shard_map/ppermute | solution.py:374
  100.5 2.6 %collective-permute-done.24 = f32[1,2,64,256]{3,2,1,0:T(8,128)S(1)} collective-permute-done((f32[1,2,64,256]{3,2,1,0:T(8,128)S(1)}, f32[1,2,64,256]{3,2,1,0:T(8,128)S(1)}, u32[]{:S(2)}, u32[]{:S(2)}) %collective-permute-start.24) | collective-permute-done | bytes 131104 | tf_op jit(solution)/shard_map/ppermute | solution.py:374
  104.5 4.4 %collective-permute-start.27 = (f32[1,2,64,256]{3,2,1,0:T(8,128)S(1)}, f32[1,2,64,256]{3,2,1,0:T(8,128)S(1)}, u32[]{:S(2)}, u32[]{:S(2)}) collective-permute-start(f32[1,2,64,256]{3,2,1,0:T(8,128)S(1)} %slice_add_fusion.5), channel_id=1, source_target_pairs={{0,8},{2,10},{4,12},{6,14},{8,0},{10,2},{12,4},{14,6},{1,9},{3,11}... | collective-permute-start | bytes 393224 | tf_op jit(solution)/shard_map/ppermute | solution.py:374
  109.0 3.6 %collective-permute-start.29 = (f32[2,128,128]{2,1,0:T(8,128)S(1)}, f32[2,128,128]{2,1,0:T(8,128)S(1)}, u32[]{:S(2)}, u32[]{:S(2)}) collective-permute-start(f32[2,128,128]{2,1,0:T(8,128)S(1)} %slice_select_fusion.3), channel_id=1, source_target_pairs={{0,2},{2,0},{4,6},{6,4},{8,10},{10,8},{12,14},{14,12},{1,3},{3,1},... | collective-permute-start | bytes 393224 | tf_op jit(solution)/shard_map/ppermute | solution.py:364
  112.6 5.0 %collective-permute-done.27 = f32[1,2,64,256]{3,2,1,0:T(8,128)S(1)} collective-permute-done((f32[1,2,64,256]{3,2,1,0:T(8,128)S(1)}, f32[1,2,64,256]{3,2,1,0:T(8,128)S(1)}, u32[]{:S(2)}, u32[]{:S(2)}) %collective-permute-start.27) | collective-permute-done | bytes 131104 | tf_op jit(solution)/shard_map/ppermute | solution.py:374
  119.6 2.1 %collective-permute-start.32 = (f32[1,2,64,256]{3,2,1,0:T(8,128)S(1)}, f32[1,2,64,256]{3,2,1,0:T(8,128)S(1)}, u32[]{:S(2)}, u32[]{:S(2)}) collective-permute-start(f32[1,2,64,256]{3,2,1,0:T(8,128)S(1)} %add.85.refs_6_), channel_id=1, source_target_pairs={{0,2},{2,0},{4,6},{6,4},{8,10},{10,8},{12,14},{14,12},{1,3},{3,1},... | collective-permute-start | bytes 393224 | tf_op jit(solution)/shard_map/ppermute | solution.py:374
  121.9 2.4 %collective-permute-done.31.refs_4_ = f32[1,2,64,256]{3,2,1,0:T(8,128)S(1)} collective-permute-done((f32[1,2,64,256]{3,2,1,0:T(8,128)S(1)}, f32[1,2,64,256]{3,2,1,0:T(8,128)S(1)}, u32[]{:S(2)}, u32[]{:S(2)}) %collective-permute-start.31) | collective-permute-done | bytes 131104 | tf_op jit(solution)/shard_map/ppermute | solution.py:374
  124.7 2.1 %collective-permute-start.33 = (f32[2,2,64,256]{3,2,1,0:T(8,128)S(1)}, f32[2,2,64,256]{3,2,1,0:T(8,128)S(1)}, u32[]{:S(2)}, u32[]{:S(2)}) collective-permute-start(f32[2,2,64,256]{3,2,1,0:T(8,128)S(1)} %pad_maximum_fusion.3), channel_id=1, source_target_pairs={{0,2},{2,0},{4,6},{6,4},{8,10},{10,8},{12,14},{14,12},{1,3},{3,1},... | collective-permute-start | bytes 786440 | tf_op jit(solution)/shard_map/ppermute | solution.py:374
  126.9 2.0 %collective-permute-start.34 = (f32[2,2,64,256]{3,2,1,0:T(8,128)S(1)}, f32[2,2,64,256]{3,2,1,0:T(8,128)S(1)}, u32[]{:S(2)}, u32[]{:S(2)}) collective-permute-start(f32[2,2,64,256]{3,2,1,0:T(8,128)S(1)} %pad_maximum_fusion.4), channel_id=1, source_target_pairs={{0,4},{2,6},{4,0},{6,2},{8,12},{10,14},{12,8},{14,10},{1,5},{3,7},... | collective-permute-start | bytes 786440 | tf_op jit(solution)/shard_map/ppermute | solution.py:374
  128.9 2.7 %collective-permute-done.33.refs_5_ = f32[2,2,64,256]{3,2,1,0:T(8,128)S(1)} collective-permute-done((f32[2,2,64,256]{3,2,1,0:T(8,128)S(1)}, f32[2,2,64,256]{3,2,1,0:T(8,128)S(1)}, u32[]{:S(2)}, u32[]{:S(2)}) %collective-permute-start.33) | collective-permute-done | bytes 262176 | tf_op jit(solution)/shard_map/ppermute | solution.py:374
  (106 shorter events, 30.0 us)
Async XLA Ops:
  1.7 7.4 %collective-permute-start = (f32[2,128,128]{2,1,0:T(8,128)S(1)}, f32[2,128,128]{2,1,0:T(8,128)S(1)}, u32[]{:S(2)}, u32[]{:S(2)}) collective-permute-start(f32[2,128,128]{2,1,0:T(8,128)S(1)} %get-tuple-element.131), channel_id=1, source_target_pairs={{2,4},{4,2},{6,8},{8,6},{10,12},{12,10},{3,5},{5,3},{7,9},{9,7},{1... | collective-permute-start | bytes 393224 | tf_op jit(solution)/shard_map/ppermute | solution.py:364
  2.6 10.6 %collective-permute-start.1 = (f32[2,128,128]{2,1,0:T(8,128)S(1)}, f32[2,128,128]{2,1,0:T(8,128)S(1)}, u32[]{:S(2)}, u32[]{:S(2)}) collective-permute-start(f32[2,128,128]{2,1,0:T(8,128)S(1)} %get-tuple-element.130), channel_id=1, source_target_pairs={{0,2},{2,0},{4,6},{6,4},{8,10},{10,8},{12,14},{14,12},{1,3},{3,1},... | collective-permute-start | bytes 393224 | tf_op jit(solution)/shard_map/ppermute | solution.py:364
  17.4 3.4 %collective-permute-start.3 = (f32[256,256]{1,0:T(8,128)S(1)}, f32[256,256]{1,0:T(8,128)S(1)}, u32[]{:S(2)}, u32[]{:S(2)}) collective-permute-start(f32[256,256]{1,0:T(8,128)S(1)} %get-tuple-element.67.refs_9_), channel_id=1, source_target_pairs={{0,1},{1,0},{2,3},{3,2},{4,5},{5,4},{6,7},{7,6},{8,9},{9,8},{10,11... | collective-permute-start | bytes 786440 | tf_op jit(solution)/shard_map/ppermute | solution.py:355
  23.6 9.4 %collective-permute-start.6 = (f32[2,2,64,256]{3,2,1,0:T(8,128)S(1)}, f32[2,2,64,256]{3,2,1,0:T(8,128)S(1)}, u32[]{:S(2)}, u32[]{:S(2)}) collective-permute-start(f32[2,2,64,256]{3,2,1,0:T(8,128)S(1)} %slice.118), channel_id=1, source_target_pairs={{0,2},{2,0},{4,6},{6,4},{8,10},{10,8},{12,14},{14,12},{1,3},{3,1},... | collective-permute-start | bytes 786440 | tf_op jit(solution)/shard_map/ppermute | solution.py:374
  28.6 8.9 %collective-permute-start.5 = (f32[2,2,128,256]{3,2,1,0:T(8,128)S(1)}, f32[2,2,128,256]{3,2,1,0:T(8,128)S(1)}, u32[]{:S(2)}, u32[]{:S(2)}) collective-permute-start(f32[2,2,128,256]{3,2,1,0:T(8,128)S(1)} %slice_bitcast_fusion.1), channel_id=1, source_target_pairs={{0,1},{1,0},{2,3},{3,2},{4,5},{5,4},{6,7},{7,6},{8,9},{9,8},{10,11... | collective-permute-start | bytes 1572872 | tf_op jit(solution)/shard_map/ppermute | solution.py:355
  28.8 8.7 %collective-permute-start.7 = (f32[2,2,64,256]{3,2,1,0:T(8,128)S(1)}, f32[2,2,64,256]{3,2,1,0:T(8,128)S(1)}, u32[]{:S(2)}, u32[]{:S(2)}) collective-permute-start(f32[2,2,64,256]{3,2,1,0:T(8,128)S(1)} %slice.120), channel_id=1, source_target_pairs={{0,4},{2,6},{4,0},{6,2},{8,12},{10,14},{12,8},{14,10},{1,5},{3,7},... | collective-permute-start | bytes 786440 | tf_op jit(solution)/shard_map/ppermute | solution.py:374
  37.7 5.1 %collective-permute-start.8 = (f32[1,2,64,256]{3,2,1,0:T(8,128)S(1)}, f32[1,2,64,256]{3,2,1,0:T(8,128)S(1)}, u32[]{:S(2)}, u32[]{:S(2)}) collective-permute-start(f32[1,2,64,256]{3,2,1,0:T(8,128)S(1)} %slice.123), channel_id=1, source_target_pairs={{0,4},{2,6},{4,0},{6,2},{8,12},{10,14},{12,8},{14,10},{1,5},{3,7},... | collective-permute-start | bytes 393224 | tf_op jit(solution)/shard_map/ppermute | solution.py:374
  39.3 5.0 %collective-permute-start.9 = (f32[1,2,64,256]{3,2,1,0:T(8,128)S(1)}, f32[1,2,64,256]{3,2,1,0:T(8,128)S(1)}, u32[]{:S(2)}, u32[]{:S(2)}) collective-permute-start(f32[1,2,64,256]{3,2,1,0:T(8,128)S(1)} %slice.125), channel_id=1, source_target_pairs={{0,2},{2,0},{4,6},{6,4},{8,10},{10,8},{12,14},{14,12},{1,3},{3,1},... | collective-permute-start | bytes 393224 | tf_op jit(solution)/shard_map/ppermute | solution.py:374
  39.9 4.5 %collective-permute-start.10 = (f32[2,128,256]{2,1,0:T(8,128)S(1)}, f32[2,128,256]{2,1,0:T(8,128)S(1)}, u32[]{:S(2)}, u32[]{:S(2)}) collective-permute-start(f32[2,128,256]{2,1,0:T(8,128)S(1)} %get-tuple-element.76), channel_id=1, source_target_pairs={{2,4},{4,2},{6,8},{8,6},{10,12},{12,10},{3,5},{5,3},{7,9},{9,7},{1... | collective-permute-start | bytes 786440 | tf_op jit(solution)/shard_map/ppermute | solution.py:364
  44.4 19.7 %collective-permute-start.13 = (f32[2,128,256]{2,1,0:T(8,128)S(1)}, f32[2,128,256]{2,1,0:T(8,128)S(1)}, u32[]{:S(2)}, u32[]{:S(2)}) collective-permute-start(f32[2,128,256]{2,1,0:T(8,128)S(1)} %get-tuple-element.79), channel_id=1, source_target_pairs={{0,2},{2,0},{4,6},{6,4},{8,10},{10,8},{12,14},{14,12},{1,3},{3,1},... | collective-permute-start | bytes 786440 | tf_op jit(solution)/shard_map/ppermute | solution.py:364
  51.5 10.0 %collective-permute-start.11 = (f32[1,2,64,256]{3,2,1,0:T(8,128)S(1)}, f32[1,2,64,256]{3,2,1,0:T(8,128)S(1)}, u32[]{:S(2)}, u32[]{:S(2)}) collective-permute-start(f32[1,2,64,256]{3,2,1,0:T(8,128)S(1)} %slice_add_fusion.7), channel_id=1, source_target_pairs={{0,8},{2,10},{4,12},{6,14},{8,0},{10,2},{12,4},{14,6},{1,9},{3,11}... | collective-permute-start | bytes 393224 | tf_op jit(solution)/shard_map/ppermute | solution.py:374
  53.2 10.9 %collective-permute-start.12 = (f32[1,2,64,256]{3,2,1,0:T(8,128)S(1)}, f32[1,2,64,256]{3,2,1,0:T(8,128)S(1)}, u32[]{:S(2)}, u32[]{:S(2)}) collective-permute-start(f32[1,2,64,256]{3,2,1,0:T(8,128)S(1)} %slice_add_fusion.6), channel_id=1, source_target_pairs={{0,8},{2,10},{4,12},{6,14},{8,0},{10,2},{12,4},{14,6},{1,9},{3,11}... | collective-permute-start | bytes 393224 | tf_op jit(solution)/shard_map/ppermute | solution.py:374
  64.1 5.3 %collective-permute-start.15 = (f32[1,2,64,256]{3,2,1,0:T(8,128)S(1)}, f32[1,2,64,256]{3,2,1,0:T(8,128)S(1)}, u32[]{:S(2)}, u32[]{:S(2)}) collective-permute-start(f32[1,2,64,256]{3,2,1,0:T(8,128)S(1)} %add.74.refs_5_), channel_id=1, source_target_pairs={{0,4},{2,6},{4,0},{6,2},{8,12},{10,14},{12,8},{14,10},{1,5},{3,7},... | collective-permute-start | bytes 393224 | tf_op jit(solution)/shard_map/ppermute | solution.py:374
  64.2 5.3 %collective-permute-start.16 = (f32[1,2,64,256]{3,2,1,0:T(8,128)S(1)}, f32[1,2,64,256]{3,2,1,0:T(8,128)S(1)}, u32[]{:S(2)}, u32[]{:S(2)}) collective-permute-start(f32[1,2,64,256]{3,2,1,0:T(8,128)S(1)} %add.75.refs_8_), channel_id=1, source_target_pairs={{0,2},{2,0},{4,6},{6,4},{8,10},{10,8},{12,14},{14,12},{1,3},{3,1},... | collective-permute-start | bytes 393224 | tf_op jit(solution)/shard_map/ppermute | solution.py:374
  64.9 12.0 %collective-permute-start.14 = (f32[2,2,128,256]{3,2,1,0:T(8,128)S(1)}, f32[2,2,128,256]{3,2,1,0:T(8,128)S(1)}, u32[]{:S(2)}, u32[]{:S(2)}) collective-permute-start(f32[2,2,128,256]{3,2,1,0:T(8,128)S(1)} %fusion.refs_1_), channel_id=1, source_target_pairs={{0,1},{1,0},{2,3},{3,2},{4,5},{5,4},{6,7},{7,6},{8,9},{9,8},{10,11... | collective-permute-start | bytes 1572872 | tf_op jit(solution)/shard_map/ppermute | solution.py:355
  69.6 7.3 %collective-permute-start.17 = (f32[2,2,64,256]{3,2,1,0:T(8,128)S(1)}, f32[2,2,64,256]{3,2,1,0:T(8,128)S(1)}, u32[]{:S(2)}, u32[]{:S(2)}) collective-permute-start(f32[2,2,64,256]{3,2,1,0:T(8,128)S(1)} %pad_maximum_fusion.1), channel_id=1, source_target_pairs={{0,2},{2,0},{4,6},{6,4},{8,10},{10,8},{12,14},{14,12},{1,3},{3,1},... | collective-permute-start | bytes 786440 | tf_op jit(solution)/shard_map/ppermute | solution.py:374
  69.9 7.0 %collective-permute-start.18 = (f32[2,2,64,256]{3,2,1,0:T(8,128)S(1)}, f32[2,2,64,256]{3,2,1,0:T(8,128)S(1)}, u32[]{:S(2)}, u32[]{:S(2)}) collective-permute-start(f32[2,2,64,256]{3,2,1,0:T(8,128)S(1)} %pad_maximum_fusion.2), channel_id=1, source_target_pairs={{0,4},{2,6},{4,0},{6,2},{8,12},{10,14},{12,8},{14,10},{1,5},{3,7},... | collective-permute-start | bytes 786440 | tf_op jit(solution)/shard_map/ppermute | solution.py:374
  79.1 2.8 %collective-permute-start.19 = (f32[256,256]{1,0:T(8,128)S(1)}, f32[256,256]{1,0:T(8,128)S(1)}, u32[]{:S(2)}, u32[]{:S(2)}) collective-permute-start(f32[256,256]{1,0:T(8,128)S(1)} %get-tuple-element.94.refs_9_), channel_id=1, source_target_pairs={{0,1},{1,0},{2,3},{3,2},{4,5},{5,4},{6,7},{7,6},{8,9},{9,8},{10,11... | collective-permute-start | bytes 786440 | tf_op jit(solution)/shard_map/ppermute | solution.py:355
  85.2 8.7 %collective-permute-start.22 = (f32[2,2,64,256]{3,2,1,0:T(8,128)S(1)}, f32[2,2,64,256]{3,2,1,0:T(8,128)S(1)}, u32[]{:S(2)}, u32[]{:S(2)}) collective-permute-start(f32[2,2,64,256]{3,2,1,0:T(8,128)S(1)} %slice.138), channel_id=1, source_target_pairs={{0,2},{2,0},{4,6},{6,4},{8,10},{10,8},{12,14},{14,12},{1,3},{3,1},... | collective-permute-start | bytes 786440 | tf_op jit(solution)/shard_map/ppermute | solution.py:374
  89.5 8.3 %collective-permute-start.23 = (f32[2,2,64,256]{3,2,1,0:T(8,128)S(1)}, f32[2,2,64,256]{3,2,1,0:T(8,128)S(1)}, u32[]{:S(2)}, u32[]{:S(2)}) collective-permute-start(f32[2,2,64,256]{3,2,1,0:T(8,128)S(1)} %slice.140), channel_id=1, source_target_pairs={{0,4},{2,6},{4,0},{6,2},{8,12},{10,14},{12,8},{14,10},{1,5},{3,7},... | collective-permute-start | bytes 786440 | tf_op jit(solution)/shard_map/ppermute | solution.py:374
  90.9 7.0 %collective-permute-start.21 = (f32[2,2,128,256]{3,2,1,0:T(8,128)S(1)}, f32[2,2,128,256]{3,2,1,0:T(8,128)S(1)}, u32[]{:S(2)}, u32[]{:S(2)}) collective-permute-start(f32[2,2,128,256]{3,2,1,0:T(8,128)S(1)} %slice_bitcast_fusion), channel_id=1, source_target_pairs={{0,1},{1,0},{2,3},{3,2},{4,5},{5,4},{6,7},{7,6},{8,9},{9,8},{10,11... | collective-permute-start | bytes 1572872 | tf_op jit(solution)/shard_map/ppermute | solution.py:355
  98.1 5.0 %collective-permute-start.24 = (f32[1,2,64,256]{3,2,1,0:T(8,128)S(1)}, f32[1,2,64,256]{3,2,1,0:T(8,128)S(1)}, u32[]{:S(2)}, u32[]{:S(2)}) collective-permute-start(f32[1,2,64,256]{3,2,1,0:T(8,128)S(1)} %slice.145), channel_id=1, source_target_pairs={{0,4},{2,6},{4,0},{6,2},{8,12},{10,14},{12,8},{14,10},{1,5},{3,7},... | collective-permute-start | bytes 393224 | tf_op jit(solution)/shard_map/ppermute | solution.py:374
  99.5 5.0 %collective-permute-start.25 = (f32[1,2,64,256]{3,2,1,0:T(8,128)S(1)}, f32[1,2,64,256]{3,2,1,0:T(8,128)S(1)}, u32[]{:S(2)}, u32[]{:S(2)}) collective-permute-start(f32[1,2,64,256]{3,2,1,0:T(8,128)S(1)} %slice.147), channel_id=1, source_target_pairs={{0,2},{2,0},{4,6},{6,4},{8,10},{10,8},{12,14},{14,12},{1,3},{3,1},... | collective-permute-start | bytes 393224 | tf_op jit(solution)/shard_map/ppermute | solution.py:374
  99.9 4.7 %collective-permute-start.26 = (f32[2,128,128]{2,1,0:T(8,128)S(1)}, f32[2,128,128]{2,1,0:T(8,128)S(1)}, u32[]{:S(2)}, u32[]{:S(2)}) collective-permute-start(f32[2,128,128]{2,1,0:T(8,128)S(1)} %slice_select_fusion.2), channel_id=1, source_target_pairs={{2,4},{4,2},{6,8},{8,6},{10,12},{12,10},{3,5},{5,3},{7,9},{9,7},{1... | collective-permute-start | bytes 393224 | tf_op jit(solution)/shard_map/ppermute | solution.py:364
  104.5 13.0 %collective-permute-start.27 = (f32[1,2,64,256]{3,2,1,0:T(8,128)S(1)}, f32[1,2,64,256]{3,2,1,0:T(8,128)S(1)}, u32[]{:S(2)}, u32[]{:S(2)}) collective-permute-start(f32[1,2,64,256]{3,2,1,0:T(8,128)S(1)} %slice_add_fusion.5), channel_id=1, source_target_pairs={{0,8},{2,10},{4,12},{6,14},{8,0},{10,2},{12,4},{14,6},{1,9},{3,11}... | collective-permute-start | bytes 393224 | tf_op jit(solution)/shard_map/ppermute | solution.py:374
  108.9 10.3 %collective-permute-start.28 = (f32[1,2,64,256]{3,2,1,0:T(8,128)S(1)}, f32[1,2,64,256]{3,2,1,0:T(8,128)S(1)}, u32[]{:S(2)}, u32[]{:S(2)}) collective-permute-start(f32[1,2,64,256]{3,2,1,0:T(8,128)S(1)} %slice_add_fusion.4), channel_id=1, source_target_pairs={{0,8},{2,10},{4,12},{6,14},{8,0},{10,2},{12,4},{14,6},{1,9},{3,11}... | collective-permute-start | bytes 393224 | tf_op jit(solution)/shard_map/ppermute | solution.py:374
  109.0 10.3 %collective-permute-start.29 = (f32[2,128,128]{2,1,0:T(8,128)S(1)}, f32[2,128,128]{2,1,0:T(8,128)S(1)}, u32[]{:S(2)}, u32[]{:S(2)}) collective-permute-start(f32[2,128,128]{2,1,0:T(8,128)S(1)} %slice_select_fusion.3), channel_id=1, source_target_pairs={{0,2},{2,0},{4,6},{6,4},{8,10},{10,8},{12,14},{14,12},{1,3},{3,1},... | collective-permute-start | bytes 393224 | tf_op jit(solution)/shard_map/ppermute | solution.py:364
  119.3 5.0 %collective-permute-start.31 = (f32[1,2,64,256]{3,2,1,0:T(8,128)S(1)}, f32[1,2,64,256]{3,2,1,0:T(8,128)S(1)}, u32[]{:S(2)}, u32[]{:S(2)}) collective-permute-start(f32[1,2,64,256]{3,2,1,0:T(8,128)S(1)} %add.84.refs_3_), channel_id=1, source_target_pairs={{0,4},{2,6},{4,0},{6,2},{8,12},{10,14},{12,8},{14,10},{1,5},{3,7},... | collective-permute-start | bytes 393224 | tf_op jit(solution)/shard_map/ppermute | solution.py:374
  119.6 5.1 %collective-permute-start.32 = (f32[1,2,64,256]{3,2,1,0:T(8,128)S(1)}, f32[1,2,64,256]{3,2,1,0:T(8,128)S(1)}, u32[]{:S(2)}, u32[]{:S(2)}) collective-permute-start(f32[1,2,64,256]{3,2,1,0:T(8,128)S(1)} %add.85.refs_6_), channel_id=1, source_target_pairs={{0,2},{2,0},{4,6},{6,4},{8,10},{10,8},{12,14},{14,12},{1,3},{3,1},... | collective-permute-start | bytes 393224 | tf_op jit(solution)/shard_map/ppermute | solution.py:374
  121.8 7.0 %collective-permute-start.30 = (f32[2,2,128,128]{3,2,1,0:T(8,128)S(1)}, f32[2,2,128,128]{3,2,1,0:T(8,128)S(1)}, u32[]{:S(2)}, u32[]{:S(2)}) collective-permute-start(f32[2,2,128,128]{3,2,1,0:T(8,128)S(1)} %maximum_add_fusion.refs_0_), channel_id=1, source_target_pairs={{0,1},{1,0},{2,3},{3,2},{4,5},{5,4},{6,7},{7,6},{8,9},{9,8},{10,11... | collective-permute-start | bytes 786440 | tf_op jit(solution)/shard_map/ppermute | solution.py:355
  124.7 6.8 %collective-permute-start.33 = (f32[2,2,64,256]{3,2,1,0:T(8,128)S(1)}, f32[2,2,64,256]{3,2,1,0:T(8,128)S(1)}, u32[]{:S(2)}, u32[]{:S(2)}) collective-permute-start(f32[2,2,64,256]{3,2,1,0:T(8,128)S(1)} %pad_maximum_fusion.3), channel_id=1, source_target_pairs={{0,2},{2,0},{4,6},{6,4},{8,10},{10,8},{12,14},{14,12},{1,3},{3,1},... | collective-permute-start | bytes 786440 | tf_op jit(solution)/shard_map/ppermute | solution.py:374
  126.9 6.4 %collective-permute-start.34 = (f32[2,2,64,256]{3,2,1,0:T(8,128)S(1)}, f32[2,2,64,256]{3,2,1,0:T(8,128)S(1)}, u32[]{:S(2)}, u32[]{:S(2)}) collective-permute-start(f32[2,2,64,256]{3,2,1,0:T(8,128)S(1)} %pad_maximum_fusion.4), channel_id=1, source_target_pairs={{0,4},{2,6},{4,0},{6,2},{8,12},{10,14},{12,8},{14,10},{1,5},{3,7},... | collective-permute-start | bytes 786440 | tf_op jit(solution)/shard_map/ppermute | solution.py:374
  (9 other events, 25.9 us)

commit v11 on v9

--- a/solution.py
+++ b/solution.py
@@ -394,10 +394,14 @@
     for i in range(HALVINGS):
         n = held[0].shape[0] // 2
         held = [h[:n] + exchange(h[n:], o[i], tiles) for h, o in zip(held, ORDERS)]
-        held, go[1 - i] = together(held, go[1 - i])
-        got[1 - i] = beside(go[1 - i], i == 1, tiles)
+        if i == 0:
+            held, go[1] = together(held, go[1])
+            got[1] = beside(go[1], False, tiles)
+        else:
+            (held,) = together(held)
     held = [h + exchange(h, o[-1], tiles) for h, o in zip(held, ORDERS)]
-    held, got = together(held, got)
+    held, go[0], got[1] = together(held, go[0], got[1])
+    got[0] = beside(go[0], True, tiles)
     for bit in range(len(ORDERS[0]), bits):
         held = [h + exchange(h, bit, tiles) for h in held]
     pieces = [[h] for h in held]
@@ -405,7 +409,7 @@
         for p, o in zip(pieces, ORDERS):
             p.append(exchange(p[0] if len(p) == 1 else jnp.concatenate(p, 0), o[i], tiles))
         if i:
-            (pieces,) = together(pieces)
+            pieces, got = together(pieces, got)
     return pieces, jnp.stack([a + b for a, b in zip(stay, got)])
 
 

time: 129 us -> 137 us (1.062)
  waiting for transfers between devices: 63.5 us -> 78.5 us
  starting transfers between devices: 40.3 us -> 34 us
    ppermute x20, waiting for transfers between devices: 58.7 us -> 72.3 us  [exchange(): return lax.ppermute(x, 'tile', [(s, s ^ 1 << bit) for s in range(tiles)])]
    ppermute x20, starting transfers between devices: 31.5 us -> 26.1 us  [exchange(): return lax.ppermute(x, 'tile', [(s, s ^ 1 << bit) for s in range(tiles)])]
    ppermute x6, waiting for transfers between devices: 2.84 us -> 4.25 us  [beside(): return lax.ppermute(x, 'tile', pairs)]
  transfers between devices with their start and end apart: 35 -> 35, of which waited for: 24 -> 25; matrix products, arithmetic and copies ran while one was open for 1% -> 0% of each run, Pallas kernels for 6% -> 6%
where the time goes in v11:
time: 137 us
  waiting for transfers between devices  78.5 us (57%)
  starting transfers between devices  34 us (25%)
  Pallas kernels  19.4 us (14%)
  local copies, waits for them, and re-layouts  2.39 us (2%)
  between operations  1.82 us (1%)
    ppermute x20, waiting for transfers between devices, exchange(): return lax.ppermute(x, 'tile', [(s, s ^ 1 << bit) for s in range(tiles)])  72.3 us
    ppermute x20, starting transfers between devices, exchange(): return lax.ppermute(x, 'tile', [(s, s ^ 1 << bit) for s in range(tiles)])  26.1 us
    pallas_call x10, Pallas kernels, call(): pl.pallas_call(kernel, out_shape=[jax.ShapeDtypeStruct(o, f32) for o in o...  19.4 us
    ppermute x6, starting transfers between devices, beside(): return lax.ppermute(x, 'tile', pairs)  6.37 us
    ppermute x6, waiting for transfers between devices, beside(): return lax.ppermute(x, 'tile', pairs)  4.25 us
  transfers between devices with their start and end apart: 35, of which 25 were waited for; matrix products, arithmetic and copies ran while one was open for 0% of the time, Pallas kernels for 6%

profile of v11, /device:TPU:0, one launch (start us, length us, event | category | flops | bytes accessed | tf_op | source)
XLA Modules:
  0.0 137.1 jit_solution(3152651222525816029)
XLA Ops:
  1.7 3.0 %collective-permute-start = (f32[2,128,128]{2,1,0:T(8,128)S(1)}, f32[2,128,128]{2,1,0:T(8,128)S(1)}, u32[]{:S(2)}, u32[]{:S(2)}) collective-permute-start(f32[2,128,128]{2,1,0:T(8,128)S(1)} %get-tuple-element.124), channel_id=1, source_target_pairs={{0,2},{2,0},{4,6},{6,4},{8,10},{10,8},{12,14},{14,12},{1,3},{3,1},... | collective-permute-start | bytes 393224 | tf_op jit(solution)/shard_map/ppermute | solution.py:354
  5.4 2.8 %collective-permute-done = f32[2,128,128]{2,1,0:T(8,128)S(1)} collective-permute-done((f32[2,128,128]{2,1,0:T(8,128)S(1)}, f32[2,128,128]{2,1,0:T(8,128)S(1)}, u32[]{:S(2)}, u32[]{:S(2)}) %collective-permute-start) | collective-permute-done | bytes 131104 | tf_op jit(solution)/shard_map/ppermute | solution.py:354
  10.5 2.0 %shard_map.87 = (f32[2,2,256,256]{3,2,1,0:T(8,128)S(1)}, f32[256,256]{1,0:T(8,128)S(1)}, f32[2,256,256]{2,1,0:T(8,128)S(1)}) custom-call(s32[2,2]{1,0:T(2,128)S(1)} %copy-done.4, f32[2,2,128,256]{3,2,1,0:T(8,128)S(1)} %pad_maximum_fusion.refs_1_, f32[2,2,128,256]{3,2,1,0:T(8,128)S(1)} %collective-permute-done.2.refs_2_, f32[2,2,256,256]{3,2,1,0:T(8,128)S(1)} %copy-done.3, ...), custom_call_target="tpu_custom_call" | custom-call | flops 3221225472 | bytes 4980752 | tf_op jit(solution)/shard_map/pallas_call | solution.py:331
  12.5 2.0 %shard_map.88 = (f32[2,2,256,256]{3,2,1,0:T(8,128)S(1)}, f32[256,256]{1,0:T(8,128)S(1)}, f32[2,256,256]{2,1,0:T(8,128)S(1)}) custom-call(s32[2,2]{1,0:T(2,128)S(1)} %copy-done.4, f32[2,2,128,256]{3,2,1,0:T(8,128)S(1)} %pad_maximum_fusion.refs_1_, f32[2,2,128,256]{3,2,1,0:T(8,128)S(1)} %collective-permute-done.2.refs_2_, f32[2,2,256,256]{3,2,1,0:T(8,128)S(1)} %copy-done.3, ...), custom_call_target="tpu_custom_call" | custom-call | flops 3221225472 | bytes 4980752 | tf_op jit(solution)/shard_map/pallas_call | solution.py:331
  16.5 2.1 %shard_map.89 = (f32[4,2,64,256]{3,2,1,0:T(8,128)S(1)}, f32[2,2,256,256]{3,2,1,0:T(8,128)S(1)}) custom-call(s32[2,2]{1,0:T(2,128)S(1)} %copy-done.4, s32[1]{0:T(128)S(6)} %copy.9.refs_1_, bf16[2,2,2,256,256]{4,3,2,1,0:T(8,128)(2,1)S(1)} %copy-done.5, f32[2,256,256]{2,1,0:T(8,128)S(1)} %shard_map.86.refs_3_, f32[2,2,256,256]{3,2,1,0:T(8,128)S(1)} %copy-done.3, ...), custom_call_target="tpu_custom_call" | custom-call | flops 3221225472 | bytes 8388628 | tf_op jit(solution)/shard_map/pallas_call | solution.py:331
  18.7 4.7 %collective-permute-start.6 = (f32[2,2,64,256]{3,2,1,0:T(8,128)S(1)}, f32[2,2,64,256]{3,2,1,0:T(8,128)S(1)}, u32[]{:S(2)}, u32[]{:S(2)}) collective-permute-start(f32[2,2,64,256]{3,2,1,0:T(8,128)S(1)} %slice.118), channel_id=1, source_target_pairs={{0,2},{2,0},{4,6},{6,4},{8,10},{10,8},{12,14},{14,12},{1,3},{3,1},... | collective-permute-start | bytes 786440 | tf_op jit(solution)/shard_map/ppermute | solution.py:364
  23.4 2.4 %shard_map.90 = (f32[4,2,64,256]{3,2,1,0:T(8,128)S(1)}, f32[2,2,2,128,256]{4,3,2,1,0:T(8,128)S(1)}) custom-call(s32[2,2]{1,0:T(2,128)S(1)} %copy-done.4, s32[1]{0:T(128)S(6)} %copy.9.refs_1_, bf16[2,2,2,256,256]{4,3,2,1,0:T(8,128)(2,1)S(1)} %copy-done.5, f32[2,256,256]{2,1,0:T(8,128)S(1)} %shard_map.86.refs_3_, f32[2,2,256,256]{3,2,1,0:T(8,128)S(1)} %copy-done.3, ...), custom_call_target="tpu_custom_call" | custom-call | flops 3221225472 | bytes 9437204 | tf_op jit(solution)/shard_map/pallas_call | solution.py:331
  25.9 1.8 %collective-permute-start.7 = (f32[2,2,64,256]{3,2,1,0:T(8,128)S(1)}, f32[2,2,64,256]{3,2,1,0:T(8,128)S(1)}, u32[]{:S(2)}, u32[]{:S(2)}) collective-permute-start(f32[2,2,64,256]{3,2,1,0:T(8,128)S(1)} %slice.120), channel_id=1, source_target_pairs={{0,4},{2,6},{4,0},{6,2},{8,12},{10,14},{12,8},{14,10},{1,5},{3,7},... | collective-permute-start | bytes 786440 | tf_op jit(solution)/shard_map/ppermute | solution.py:364
  27.7 2.3 %collective-permute-done.6 = f32[2,2,64,256]{3,2,1,0:T(8,128)S(1)} collective-permute-done((f32[2,2,64,256]{3,2,1,0:T(8,128)S(1)}, f32[2,2,64,256]{3,2,1,0:T(8,128)S(1)}, u32[]{:S(2)}, u32[]{:S(2)}) %collective-permute-start.6) | collective-permute-done | bytes 262176 | tf_op jit(solution)/shard_map/ppermute | solution.py:364
  30.0 4.7 %collective-permute-done.7 = f32[2,2,64,256]{3,2,1,0:T(8,128)S(1)} collective-permute-done((f32[2,2,64,256]{3,2,1,0:T(8,128)S(1)}, f32[2,2,64,256]{3,2,1,0:T(8,128)S(1)}, u32[]{:S(2)}, u32[]{:S(2)}) %collective-permute-start.7) | collective-permute-done | bytes 262176 | tf_op jit(solution)/shard_map/ppermute | solution.py:364
  34.9 1.8 %collective-permute-start.8 = (f32[1,2,64,256]{3,2,1,0:T(8,128)S(1)}, f32[1,2,64,256]{3,2,1,0:T(8,128)S(1)}, u32[]{:S(2)}, u32[]{:S(2)}) collective-permute-start(f32[1,2,64,256]{3,2,1,0:T(8,128)S(1)} %slice.123), channel_id=1, source_target_pairs={{0,4},{2,6},{4,0},{6,2},{8,12},{10,14},{12,8},{14,10},{1,5},{3,7},... | collective-permute-start | bytes 393224 | tf_op jit(solution)/shard_map/ppermute | solution.py:364
  36.6 1.6 %collective-permute-start.9 = (f32[1,2,64,256]{3,2,1,0:T(8,128)S(1)}, f32[1,2,64,256]{3,2,1,0:T(8,128)S(1)}, u32[]{:S(2)}, u32[]{:S(2)}) collective-permute-start(f32[1,2,64,256]{3,2,1,0:T(8,128)S(1)} %slice.125), channel_id=1, source_target_pairs={{0,2},{2,0},{4,6},{6,4},{8,10},{10,8},{12,14},{14,12},{1,3},{3,1},... | collective-permute-start | bytes 393224 | tf_op jit(solution)/shard_map/ppermute | solution.py:364
  40.1 1.6 %collective-permute-done.9 = f32[1,2,64,256]{3,2,1,0:T(8,128)S(1)} collective-permute-done((f32[1,2,64,256]{3,2,1,0:T(8,128)S(1)}, f32[1,2,64,256]{3,2,1,0:T(8,128)S(1)}, u32[]{:S(2)}, u32[]{:S(2)}) %collective-permute-start.9) | collective-permute-done | bytes 131104 | tf_op jit(solution)/shard_map/ppermute | solution.py:364
  41.7 2.3 %collective-permute-start.10 = (f32[1,2,64,256]{3,2,1,0:T(8,128)S(1)}, f32[1,2,64,256]{3,2,1,0:T(8,128)S(1)}, u32[]{:S(2)}, u32[]{:S(2)}) collective-permute-start(f32[1,2,64,256]{3,2,1,0:T(8,128)S(1)} %slice_add_fusion.7), channel_id=1, source_target_pairs={{0,8},{2,10},{4,12},{6,14},{8,0},{10,2},{12,4},{14,6},{1,9},{3,11}... | collective-permute-start | bytes 393224 | tf_op jit(solution)/shard_map/ppermute | solution.py:364
  44.7 13.5 %collective-permute-done.10 = f32[1,2,64,256]{3,2,1,0:T(8,128)S(1)} collective-permute-done((f32[1,2,64,256]{3,2,1,0:T(8,128)S(1)}, f32[1,2,64,256]{3,2,1,0:T(8,128)S(1)}, u32[]{:S(2)}, u32[]{:S(2)}) %collective-permute-start.10) | collective-permute-done | bytes 131104 | tf_op jit(solution)/shard_map/ppermute | solution.py:364
  61.7 3.0 %collective-permute-done.13.refs_6_ = f32[1,2,64,256]{3,2,1,0:T(8,128)S(1)} collective-permute-done((f32[1,2,64,256]{3,2,1,0:T(8,128)S(1)}, f32[1,2,64,256]{3,2,1,0:T(8,128)S(1)}, u32[]{:S(2)}, u32[]{:S(2)}) %collective-permute-start.13) | collective-permute-done | bytes 131104 | tf_op jit(solution)/shard_map/ppermute | solution.py:364
  64.7 4.5 %collective-permute-done.14.refs_9_ = f32[1,2,64,256]{3,2,1,0:T(8,128)S(1)} collective-permute-done((f32[1,2,64,256]{3,2,1,0:T(8,128)S(1)}, f32[1,2,64,256]{3,2,1,0:T(8,128)S(1)}, u32[]{:S(2)}, u32[]{:S(2)}) %collective-permute-start.14) | collective-permute-done | bytes 131104 | tf_op jit(solution)/shard_map/ppermute | solution.py:364
  70.6 7.6 %collective-permute-done.17.refs_7_ = f32[2,2,64,256]{3,2,1,0:T(8,128)S(1)} collective-permute-done((f32[2,2,64,256]{3,2,1,0:T(8,128)S(1)}, f32[2,2,64,256]{3,2,1,0:T(8,128)S(1)}, u32[]{:S(2)}, u32[]{:S(2)}) %collective-permute-start.17) | collective-permute-done | bytes 262176 | tf_op jit(solution)/shard_map/ppermute | solution.py:364
  78.3 2.1 %shard_map.91 = (f32[2,2,256,256]{3,2,1,0:T(8,128)S(1)}, f32[256,256]{1,0:T(8,128)S(1)}, f32[2,256,256]{2,1,0:T(8,128)S(1)}, f32[2,2,256,256]{3,2,1,0:T(8,128)S(1)}) custom-call(s32[2,2]{1,0:T(2,128)S(1)} %copy-done.4, f32[2,2,128,256]{3,2,1,0:T(8,128)S(1)} %fusion.refs_1_, f32[2,2,128,256]{3,2,1,0:T(8,128)S(1)} %collective-permute-done.16.refs_2_, ...), custom_call_target="tpu_custom_call" | custom-call | flops 3221225472 | bytes 7077904 | tf_op jit(solution)/shard_map/pallas_call | solution.py:331
  80.5 2.0 %shard_map.92 = (f32[2,2,256,256]{3,2,1,0:T(8,128)S(1)}, f32[256,256]{1,0:T(8,128)S(1)}, f32[2,256,256]{2,1,0:T(8,128)S(1)}) custom-call(s32[2,2]{1,0:T(2,128)S(1)} %copy-done.4, f32[2,2,128,256]{3,2,1,0:T(8,128)S(1)} %fusion.refs_1_, f32[2,2,128,256]{3,2,1,0:T(8,128)S(1)} %collective-permute-done.16.refs_2_, ...), custom_call_target="tpu_custom_call" | custom-call | flops 3221225472 | bytes 4980752 | tf_op jit(solution)/shard_map/pallas_call | solution.py:331
  84.3 2.1 %shard_map.93 = (f32[4,2,64,256]{3,2,1,0:T(8,128)S(1)}, f32[2,2,256,256]{3,2,1,0:T(8,128)S(1)}) custom-call(s32[2,2]{1,0:T(2,128)S(1)} %copy-done.4, s32[1]{0:T(128)S(6)} %copy.9.refs_1_, bf16[2,2,2,256,256]{4,3,2,1,0:T(8,128)(2,1)S(1)} %copy-done.5, f32[2,256,256]{2,1,0:T(8,128)S(1)} %shard_map.86.refs_3_, ...), custom_call_target="tpu_custom_call" | custom-call | flops 3221225472 | bytes 8388628 | tf_op jit(solution)/shard_map/pallas_call | solution.py:331
  86.4 1.8 %collective-permute-start.22 = (f32[2,2,64,256]{3,2,1,0:T(8,128)S(1)}, f32[2,2,64,256]{3,2,1,0:T(8,128)S(1)}, u32[]{:S(2)}, u32[]{:S(2)}) collective-permute-start(f32[2,2,64,256]{3,2,1,0:T(8,128)S(1)} %slice.138), channel_id=1, source_target_pairs={{0,2},{2,0},{4,6},{6,4},{8,10},{10,8},{12,14},{14,12},{1,3},{3,1},... | collective-permute-start | bytes 786440 | tf_op jit(solution)/shard_map/ppermute | solution.py:364
  88.3 2.4 %shard_map.94 = (f32[4,2,64,256]{3,2,1,0:T(8,128)S(1)}, f32[2,2,2,128,256]{4,3,2,1,0:T(8,128)S(1)}) custom-call(s32[2,2]{1,0:T(2,128)S(1)} %copy-done.4, s32[1]{0:T(128)S(6)} %copy.9.refs_1_, bf16[2,2,2,256,256]{4,3,2,1,0:T(8,128)(2,1)S(1)} %copy-done.5, f32[2,256,256]{2,1,0:T(8,128)S(1)} %shard_map.86.refs_3_, ...), custom_call_target="tpu_custom_call" | custom-call | flops 3221225472 | bytes 9437204 | tf_op jit(solution)/shard_map/pallas_call | solution.py:331
  91.2 3.9 %collective-permute-done.22 = f32[2,2,64,256]{3,2,1,0:T(8,128)S(1)} collective-permute-done((f32[2,2,64,256]{3,2,1,0:T(8,128)S(1)}, f32[2,2,64,256]{3,2,1,0:T(8,128)S(1)}, u32[]{:S(2)}, u32[]{:S(2)}) %collective-permute-start.22) | collective-permute-done | bytes 262176 | tf_op jit(solution)/shard_map/ppermute | solution.py:364
  95.1 3.9 %collective-permute-done.23 = f32[2,2,64,256]{3,2,1,0:T(8,128)S(1)} collective-permute-done((f32[2,2,64,256]{3,2,1,0:T(8,128)S(1)}, f32[2,2,64,256]{3,2,1,0:T(8,128)S(1)}, u32[]{:S(2)}, u32[]{:S(2)}) %collective-permute-start.23) | collective-permute-done | bytes 262176 | tf_op jit(solution)/shard_map/ppermute | solution.py:364
  101.1 3.2 %collective-permute-done.24 = f32[1,2,64,256]{3,2,1,0:T(8,128)S(1)} collective-permute-done((f32[1,2,64,256]{3,2,1,0:T(8,128)S(1)}, f32[1,2,64,256]{3,2,1,0:T(8,128)S(1)}, u32[]{:S(2)}, u32[]{:S(2)}) %collective-permute-start.24) | collective-permute-done | bytes 131104 | tf_op jit(solution)/shard_map/ppermute | solution.py:364
  104.7 3.1 %collective-permute-start.26 = (f32[1,2,64,256]{3,2,1,0:T(8,128)S(1)}, f32[1,2,64,256]{3,2,1,0:T(8,128)S(1)}, u32[]{:S(2)}, u32[]{:S(2)}) collective-permute-start(f32[1,2,64,256]{3,2,1,0:T(8,128)S(1)} %slice_add_fusion.5), channel_id=1, source_target_pairs={{0,8},{2,10},{4,12},{6,14},{8,0},{10,2},{12,4},{14,6},{1,9},{3,11}... | collective-permute-start | bytes 393224 | tf_op jit(solution)/shard_map/ppermute | solution.py:364
  107.9 10.2 %collective-permute-done.26 = f32[1,2,64,256]{3,2,1,0:T(8,128)S(1)} collective-permute-done((f32[1,2,64,256]{3,2,1,0:T(8,128)S(1)}, f32[1,2,64,256]{3,2,1,0:T(8,128)S(1)}, u32[]{:S(2)}, u32[]{:S(2)}) %collective-permute-start.26) | collective-permute-done | bytes 131104 | tf_op jit(solution)/shard_map/ppermute | solution.py:364
  121.8 2.8 %collective-permute-done.29.refs_4_ = f32[1,2,64,256]{3,2,1,0:T(8,128)S(1)} collective-permute-done((f32[1,2,64,256]{3,2,1,0:T(8,128)S(1)}, f32[1,2,64,256]{3,2,1,0:T(8,128)S(1)}, u32[]{:S(2)}, u32[]{:S(2)}) %collective-permute-start.29) | collective-permute-done | bytes 131104 | tf_op jit(solution)/shard_map/ppermute | solution.py:364
  124.7 1.4 %collective-permute-done.31 = f32[2,128,128]{2,1,0:T(8,128)S(1)} collective-permute-done((f32[2,128,128]{2,1,0:T(8,128)S(1)}, f32[2,128,128]{2,1,0:T(8,128)S(1)}, u32[]{:S(2)}, u32[]{:S(2)}) %collective-permute-start.31) | collective-permute-done | bytes 131104 | tf_op jit(solution)/shard_map/ppermute | solution.py:354
  127.3 1.7 %collective-permute-start.34 = (f32[2,2,64,256]{3,2,1,0:T(8,128)S(1)}, f32[2,2,64,256]{3,2,1,0:T(8,128)S(1)}, u32[]{:S(2)}, u32[]{:S(2)}) collective-permute-start(f32[2,2,64,256]{3,2,1,0:T(8,128)S(1)} %pad_maximum_fusion.4), channel_id=1, source_target_pairs={{0,4},{2,6},{4,0},{6,2},{8,12},{10,14},{12,8},{14,10},{1,5},{3,7},... | collective-permute-start | bytes 786440 | tf_op jit(solution)/shard_map/ppermute | solution.py:364
  129.1 6.0 %collective-permute-done.33.refs_5_ = f32[2,2,64,256]{3,2,1,0:T(8,128)S(1)} collective-permute-done((f32[2,2,64,256]{3,2,1,0:T(8,128)S(1)}, f32[2,2,64,256]{3,2,1,0:T(8,128)S(1)}, u32[]{:S(2)}, u32[]{:S(2)}) %collective-permute-start.33) | collective-permute-done | bytes 262176 | tf_op jit(solution)/shard_map/ppermute | solution.py:364
  (106 shorter events, 24.7 us)
Async XLA Ops:
  1.7 6.5 %collective-permute-start = (f32[2,128,128]{2,1,0:T(8,128)S(1)}, f32[2,128,128]{2,1,0:T(8,128)S(1)}, u32[]{:S(2)}, u32[]{:S(2)}) collective-permute-start(f32[2,128,128]{2,1,0:T(8,128)S(1)} %get-tuple-element.124), channel_id=1, source_target_pairs={{0,2},{2,0},{4,6},{6,4},{8,10},{10,8},{12,14},{14,12},{1,3},{3,1},... | collective-permute-start | bytes 393224 | tf_op jit(solution)/shard_map/ppermute | solution.py:354
  4.8 3.5 %collective-permute-start.1 = (f32[2,128,128]{2,1,0:T(8,128)S(1)}, f32[2,128,128]{2,1,0:T(8,128)S(1)}, u32[]{:S(2)}, u32[]{:S(2)}) collective-permute-start(f32[2,128,128]{2,1,0:T(8,128)S(1)} %get-tuple-element.125), channel_id=1, source_target_pairs={{2,4},{4,2},{6,8},{8,6},{10,12},{12,10},{3,5},{5,3},{7,9},{9,7},{1... | collective-permute-start | bytes 393224 | tf_op jit(solution)/shard_map/ppermute | solution.py:354
  8.5 2.0 %collective-permute-start.2 = (f32[2,2,128,256]{3,2,1,0:T(8,128)S(1)}, f32[2,2,128,256]{3,2,1,0:T(8,128)S(1)}, u32[]{:S(2)}, u32[]{:S(2)}) collective-permute-start(f32[2,2,128,256]{3,2,1,0:T(8,128)S(1)} %pad_maximum_fusion.refs_1_), channel_id=1, source_target_pairs={{0,1},{1,0},{2,3},{3,2},{4,5},{5,4},{6,7},{7,6},{8,9},{9,8},{10,11... | collective-permute-start | bytes 1572872 | tf_op jit(solution)/shard_map/ppermute | solution.py:345
  18.7 11.3 %collective-permute-start.6 = (f32[2,2,64,256]{3,2,1,0:T(8,128)S(1)}, f32[2,2,64,256]{3,2,1,0:T(8,128)S(1)}, u32[]{:S(2)}, u32[]{:S(2)}) collective-permute-start(f32[2,2,64,256]{3,2,1,0:T(8,128)S(1)} %slice.118), channel_id=1, source_target_pairs={{0,2},{2,0},{4,6},{6,4},{8,10},{10,8},{12,14},{14,12},{1,3},{3,1},... | collective-permute-start | bytes 786440 | tf_op jit(solution)/shard_map/ppermute | solution.py:364
  25.8 8.9 %collective-permute-start.5 = (f32[2,2,128,256]{3,2,1,0:T(8,128)S(1)}, f32[2,2,128,256]{3,2,1,0:T(8,128)S(1)}, u32[]{:S(2)}, u32[]{:S(2)}) collective-permute-start(f32[2,2,128,256]{3,2,1,0:T(8,128)S(1)} %slice_bitcast_fusion.1), channel_id=1, source_target_pairs={{0,1},{1,0},{2,3},{3,2},{4,5},{5,4},{6,7},{7,6},{8,9},{9,8},{10,11... | collective-permute-start | bytes 1572872 | tf_op jit(solution)/shard_map/ppermute | solution.py:345
  25.9 8.8 %collective-permute-start.7 = (f32[2,2,64,256]{3,2,1,0:T(8,128)S(1)}, f32[2,2,64,256]{3,2,1,0:T(8,128)S(1)}, u32[]{:S(2)}, u32[]{:S(2)}) collective-permute-start(f32[2,2,64,256]{3,2,1,0:T(8,128)S(1)} %slice.120), channel_id=1, source_target_pairs={{0,4},{2,6},{4,0},{6,2},{8,12},{10,14},{12,8},{14,10},{1,5},{3,7},... | collective-permute-start | bytes 786440 | tf_op jit(solution)/shard_map/ppermute | solution.py:364
  34.9 5.2 %collective-permute-start.8 = (f32[1,2,64,256]{3,2,1,0:T(8,128)S(1)}, f32[1,2,64,256]{3,2,1,0:T(8,128)S(1)}, u32[]{:S(2)}, u32[]{:S(2)}) collective-permute-start(f32[1,2,64,256]{3,2,1,0:T(8,128)S(1)} %slice.123), channel_id=1, source_target_pairs={{0,4},{2,6},{4,0},{6,2},{8,12},{10,14},{12,8},{14,10},{1,5},{3,7},... | collective-permute-start | bytes 393224 | tf_op jit(solution)/shard_map/ppermute | solution.py:364
  36.6 5.0 %collective-permute-start.9 = (f32[1,2,64,256]{3,2,1,0:T(8,128)S(1)}, f32[1,2,64,256]{3,2,1,0:T(8,128)S(1)}, u32[]{:S(2)}, u32[]{:S(2)}) collective-permute-start(f32[1,2,64,256]{3,2,1,0:T(8,128)S(1)} %slice.125), channel_id=1, source_target_pairs={{0,2},{2,0},{4,6},{6,4},{8,10},{10,8},{12,14},{14,12},{1,3},{3,1},... | collective-permute-start | bytes 393224 | tf_op jit(solution)/shard_map/ppermute | solution.py:364
  38.2 21.3 %collective-permute-start.12 = (f32[2,128,256]{2,1,0:T(8,128)S(1)}, f32[2,128,256]{2,1,0:T(8,128)S(1)}, u32[]{:S(2)}, u32[]{:S(2)}) collective-permute-start(f32[2,128,256]{2,1,0:T(8,128)S(1)} %get-tuple-element.75), channel_id=1, source_target_pairs={{2,4},{4,2},{6,8},{8,6},{10,12},{12,10},{3,5},{5,3},{7,9},{9,7},{1... | collective-permute-start | bytes 786440 | tf_op jit(solution)/shard_map/ppermute | solution.py:354
  41.7 16.5 %collective-permute-start.10 = (f32[1,2,64,256]{3,2,1,0:T(8,128)S(1)}, f32[1,2,64,256]{3,2,1,0:T(8,128)S(1)}, u32[]{:S(2)}, u32[]{:S(2)}) collective-permute-start(f32[1,2,64,256]{3,2,1,0:T(8,128)S(1)} %slice_add_fusion.7), channel_id=1, source_target_pairs={{0,8},{2,10},{4,12},{6,14},{8,0},{10,2},{12,4},{14,6},{1,9},{3,11}... | collective-permute-start | bytes 393224 | tf_op jit(solution)/shard_map/ppermute | solution.py:364
  44.0 15.6 %collective-permute-start.11 = (f32[1,2,64,256]{3,2,1,0:T(8,128)S(1)}, f32[1,2,64,256]{3,2,1,0:T(8,128)S(1)}, u32[]{:S(2)}, u32[]{:S(2)}) collective-permute-start(f32[1,2,64,256]{3,2,1,0:T(8,128)S(1)} %slice_add_fusion.6), channel_id=1, source_target_pairs={{0,8},{2,10},{4,12},{6,14},{8,0},{10,2},{12,4},{14,6},{1,9},{3,11}... | collective-permute-start | bytes 393224 | tf_op jit(solution)/shard_map/ppermute | solution.py:364
  59.6 9.6 %collective-permute-start.15 = (f32[2,128,256]{2,1,0:T(8,128)S(1)}, f32[2,128,256]{2,1,0:T(8,128)S(1)}, u32[]{:S(2)}, u32[]{:S(2)}) collective-permute-start(f32[2,128,256]{2,1,0:T(8,128)S(1)} %get-tuple-element.78), channel_id=1, source_target_pairs={{0,2},{2,0},{4,6},{6,4},{8,10},{10,8},{12,14},{14,12},{1,3},{3,1},... | collective-permute-start | bytes 786440 | tf_op jit(solution)/shard_map/ppermute | solution.py:354
  59.7 5.0 %collective-permute-start.13 = (f32[1,2,64,256]{3,2,1,0:T(8,128)S(1)}, f32[1,2,64,256]{3,2,1,0:T(8,128)S(1)}, u32[]{:S(2)}, u32[]{:S(2)}) collective-permute-start(f32[1,2,64,256]{3,2,1,0:T(8,128)S(1)} %add.74.refs_5_), channel_id=1, source_target_pairs={{0,4},{2,6},{4,0},{6,2},{8,12},{10,14},{12,8},{14,10},{1,5},{3,7},... | collective-permute-start | bytes 393224 | tf_op jit(solution)/shard_map/ppermute | solution.py:364
  60.9 8.2 %collective-permute-start.14 = (f32[1,2,64,256]{3,2,1,0:T(8,128)S(1)}, f32[1,2,64,256]{3,2,1,0:T(8,128)S(1)}, u32[]{:S(2)}, u32[]{:S(2)}) collective-permute-start(f32[1,2,64,256]{3,2,1,0:T(8,128)S(1)} %add.75.refs_8_), channel_id=1, source_target_pairs={{0,2},{2,0},{4,6},{6,4},{8,10},{10,8},{12,14},{14,12},{1,3},{3,1},... | collective-permute-start | bytes 393224 | tf_op jit(solution)/shard_map/ppermute | solution.py:364
  69.3 9.0 %collective-permute-start.16 = (f32[2,2,128,256]{3,2,1,0:T(8,128)S(1)}, f32[2,2,128,256]{3,2,1,0:T(8,128)S(1)}, u32[]{:S(2)}, u32[]{:S(2)}) collective-permute-start(f32[2,2,128,256]{3,2,1,0:T(8,128)S(1)} %fusion.refs_1_), channel_id=1, source_target_pairs={{0,1},{1,0},{2,3},{3,2},{4,5},{5,4},{6,7},{7,6},{8,9},{9,8},{10,11... | collective-permute-start | bytes 1572872 | tf_op jit(solution)/shard_map/ppermute | solution.py:345
  69.4 8.8 %collective-permute-start.17 = (f32[2,2,64,256]{3,2,1,0:T(8,128)S(1)}, f32[2,2,64,256]{3,2,1,0:T(8,128)S(1)}, u32[]{:S(2)}, u32[]{:S(2)}) collective-permute-start(f32[2,2,64,256]{3,2,1,0:T(8,128)S(1)} %pad_maximum_fusion.1), channel_id=1, source_target_pairs={{0,2},{2,0},{4,6},{6,4},{8,10},{10,8},{12,14},{14,12},{1,3},{3,1},... | collective-permute-start | bytes 786440 | tf_op jit(solution)/shard_map/ppermute | solution.py:364
  69.8 8.5 %collective-permute-start.18 = (f32[2,2,64,256]{3,2,1,0:T(8,128)S(1)}, f32[2,2,64,256]{3,2,1,0:T(8,128)S(1)}, u32[]{:S(2)}, u32[]{:S(2)}) collective-permute-start(f32[2,2,64,256]{3,2,1,0:T(8,128)S(1)} %pad_maximum_fusion.2), channel_id=1, source_target_pairs={{0,4},{2,6},{4,0},{6,2},{8,12},{10,14},{12,8},{14,10},{1,5},{3,7},... | collective-permute-start | bytes 786440 | tf_op jit(solution)/shard_map/ppermute | solution.py:364
  80.4 2.7 %collective-permute-start.19 = (f32[256,256]{1,0:T(8,128)S(1)}, f32[256,256]{1,0:T(8,128)S(1)}, u32[]{:S(2)}, u32[]{:S(2)}) collective-permute-start(f32[256,256]{1,0:T(8,128)S(1)} %get-tuple-element.89.refs_7_), channel_id=1, source_target_pairs={{0,1},{1,0},{2,3},{3,2},{4,5},{5,4},{6,7},{7,6},{8,9},{9,8},{10,11... | collective-permute-start | bytes 786440 | tf_op jit(solution)/shard_map/ppermute | solution.py:345
  86.4 8.6 %collective-permute-start.22 = (f32[2,2,64,256]{3,2,1,0:T(8,128)S(1)}, f32[2,2,64,256]{3,2,1,0:T(8,128)S(1)}, u32[]{:S(2)}, u32[]{:S(2)}) collective-permute-start(f32[2,2,64,256]{3,2,1,0:T(8,128)S(1)} %slice.138), channel_id=1, source_target_pairs={{0,2},{2,0},{4,6},{6,4},{8,10},{10,8},{12,14},{14,12},{1,3},{3,1},... | collective-permute-start | bytes 786440 | tf_op jit(solution)/shard_map/ppermute | solution.py:364
  90.7 8.4 %collective-permute-start.23 = (f32[2,2,64,256]{3,2,1,0:T(8,128)S(1)}, f32[2,2,64,256]{3,2,1,0:T(8,128)S(1)}, u32[]{:S(2)}, u32[]{:S(2)}) collective-permute-start(f32[2,2,64,256]{3,2,1,0:T(8,128)S(1)} %slice.140), channel_id=1, source_target_pairs={{0,4},{2,6},{4,0},{6,2},{8,12},{10,14},{12,8},{14,10},{1,5},{3,7},... | collective-permute-start | bytes 786440 | tf_op jit(solution)/shard_map/ppermute | solution.py:364
  91.1 8.0 %collective-permute-start.21 = (f32[2,2,128,256]{3,2,1,0:T(8,128)S(1)}, f32[2,2,128,256]{3,2,1,0:T(8,128)S(1)}, u32[]{:S(2)}, u32[]{:S(2)}) collective-permute-start(f32[2,2,128,256]{3,2,1,0:T(8,128)S(1)} %slice_bitcast_fusion), channel_id=1, source_target_pairs={{0,1},{1,0},{2,3},{3,2},{4,5},{5,4},{6,7},{7,6},{8,9},{9,8},{10,11... | collective-permute-start | bytes 1572872 | tf_op jit(solution)/shard_map/ppermute | solution.py:345
  99.3 5.0 %collective-permute-start.24 = (f32[1,2,64,256]{3,2,1,0:T(8,128)S(1)}, f32[1,2,64,256]{3,2,1,0:T(8,128)S(1)}, u32[]{:S(2)}, u32[]{:S(2)}) collective-permute-start(f32[1,2,64,256]{3,2,1,0:T(8,128)S(1)} %slice.145), channel_id=1, source_target_pairs={{0,4},{2,6},{4,0},{6,2},{8,12},{10,14},{12,8},{14,10},{1,5},{3,7},... | collective-permute-start | bytes 393224 | tf_op jit(solution)/shard_map/ppermute | solution.py:364
  99.7 5.0 %collective-permute-start.25 = (f32[1,2,64,256]{3,2,1,0:T(8,128)S(1)}, f32[1,2,64,256]{3,2,1,0:T(8,128)S(1)}, u32[]{:S(2)}, u32[]{:S(2)}) collective-permute-start(f32[1,2,64,256]{3,2,1,0:T(8,128)S(1)} %slice.147), channel_id=1, source_target_pairs={{0,2},{2,0},{4,6},{6,4},{8,10},{10,8},{12,14},{14,12},{1,3},{3,1},... | collective-permute-start | bytes 393224 | tf_op jit(solution)/shard_map/ppermute | solution.py:364
  100.4 19.2 %collective-permute-start.28 = (f32[2,128,128]{2,1,0:T(8,128)S(1)}, f32[2,128,128]{2,1,0:T(8,128)S(1)}, u32[]{:S(2)}, u32[]{:S(2)}) collective-permute-start(f32[2,128,128]{2,1,0:T(8,128)S(1)} %slice_select_fusion.2), channel_id=1, source_target_pairs={{2,4},{4,2},{6,8},{8,6},{10,12},{12,10},{3,5},{5,3},{7,9},{9,7},{1... | collective-permute-start | bytes 393224 | tf_op jit(solution)/shard_map/ppermute | solution.py:354
  104.7 13.4 %collective-permute-start.26 = (f32[1,2,64,256]{3,2,1,0:T(8,128)S(1)}, f32[1,2,64,256]{3,2,1,0:T(8,128)S(1)}, u32[]{:S(2)}, u32[]{:S(2)}) collective-permute-start(f32[1,2,64,256]{3,2,1,0:T(8,128)S(1)} %slice_add_fusion.5), channel_id=1, source_target_pairs={{0,8},{2,10},{4,12},{6,14},{8,0},{10,2},{12,4},{14,6},{1,9},{3,11}... | collective-permute-start | bytes 393224 | tf_op jit(solution)/shard_map/ppermute | solution.py:364
  107.8 11.7 %collective-permute-start.27 = (f32[1,2,64,256]{3,2,1,0:T(8,128)S(1)}, f32[1,2,64,256]{3,2,1,0:T(8,128)S(1)}, u32[]{:S(2)}, u32[]{:S(2)}) collective-permute-start(f32[1,2,64,256]{3,2,1,0:T(8,128)S(1)} %slice_add_fusion.4), channel_id=1, source_target_pairs={{0,8},{2,10},{4,12},{6,14},{8,0},{10,2},{12,4},{14,6},{1,9},{3,11}... | collective-permute-start | bytes 393224 | tf_op jit(solution)/shard_map/ppermute | solution.py:364
  119.6 5.0 %collective-permute-start.29 = (f32[1,2,64,256]{3,2,1,0:T(8,128)S(1)}, f32[1,2,64,256]{3,2,1,0:T(8,128)S(1)}, u32[]{:S(2)}, u32[]{:S(2)}) collective-permute-start(f32[1,2,64,256]{3,2,1,0:T(8,128)S(1)} %add.84.refs_3_), channel_id=1, source_target_pairs={{0,4},{2,6},{4,0},{6,2},{8,12},{10,14},{12,8},{14,10},{1,5},{3,7},... | collective-permute-start | bytes 393224 | tf_op jit(solution)/shard_map/ppermute | solution.py:364
  119.7 5.0 %collective-permute-start.30 = (f32[1,2,64,256]{3,2,1,0:T(8,128)S(1)}, f32[1,2,64,256]{3,2,1,0:T(8,128)S(1)}, u32[]{:S(2)}, u32[]{:S(2)}) collective-permute-start(f32[1,2,64,256]{3,2,1,0:T(8,128)S(1)} %add.85.refs_6_), channel_id=1, source_target_pairs={{0,2},{2,0},{4,6},{6,4},{8,10},{10,8},{12,14},{14,12},{1,3},{3,1},... | collective-permute-start | bytes 393224 | tf_op jit(solution)/shard_map/ppermute | solution.py:364
  120.7 5.5 %collective-permute-start.31 = (f32[2,128,128]{2,1,0:T(8,128)S(1)}, f32[2,128,128]{2,1,0:T(8,128)S(1)}, u32[]{:S(2)}, u32[]{:S(2)}) collective-permute-start(f32[2,128,128]{2,1,0:T(8,128)S(1)} %slice_select_fusion.3), channel_id=1, source_target_pairs={{0,2},{2,0},{4,6},{6,4},{8,10},{10,8},{12,14},{14,12},{1,3},{3,1},... | collective-permute-start | bytes 393224 | tf_op jit(solution)/shard_map/ppermute | solution.py:354
  126.2 2.8 %collective-permute-start.32 = (f32[2,2,128,128]{3,2,1,0:T(8,128)S(1)}, f32[2,2,128,128]{3,2,1,0:T(8,128)S(1)}, u32[]{:S(2)}, u32[]{:S(2)}) collective-permute-start(f32[2,2,128,128]{3,2,1,0:T(8,128)S(1)} %maximum_add_fusion.refs_0_), channel_id=1, source_target_pairs={{0,1},{1,0},{2,3},{3,2},{4,5},{5,4},{6,7},{7,6},{8,9},{9,8},{10,11... | collective-permute-start | bytes 786440 | tf_op jit(solution)/shard_map/ppermute | solution.py:345
  126.3 8.8 %collective-permute-start.33 = (f32[2,2,64,256]{3,2,1,0:T(8,128)S(1)}, f32[2,2,64,256]{3,2,1,0:T(8,128)S(1)}, u32[]{:S(2)}, u32[]{:S(2)}) collective-permute-start(f32[2,2,64,256]{3,2,1,0:T(8,128)S(1)} %pad_maximum_fusion.3), channel_id=1, source_target_pairs={{0,2},{2,0},{4,6},{6,4},{8,10},{10,8},{12,14},{14,12},{1,3},{3,1},... | collective-permute-start | bytes 786440 | tf_op jit(solution)/shard_map/ppermute | solution.py:364
  127.3 8.5 %collective-permute-start.34 = (f32[2,2,64,256]{3,2,1,0:T(8,128)S(1)}, f32[2,2,64,256]{3,2,1,0:T(8,128)S(1)}, u32[]{:S(2)}, u32[]{:S(2)}) collective-permute-start(f32[2,2,64,256]{3,2,1,0:T(8,128)S(1)} %pad_maximum_fusion.4), channel_id=1, source_target_pairs={{0,4},{2,6},{4,0},{6,2},{8,12},{10,14},{12,8},{14,10},{1,5},{3,7},... | collective-permute-start | bytes 786440 | tf_op jit(solution)/shard_map/ppermute | solution.py:364
  (9 other events, 14.6 us)

commit v12 on v9

--- a/solution.py
+++ b/solution.py
@@ -14,9 +14,9 @@
 ITERS = 2
 HALVINGS = 2
 CHUNKS = 1 << HALVINGS
-ORDERS = ((0, 1, 2), (1, 0, 2))
+ORDERS = ((0, 1, 2), (1, 2, 0))
 STRIP = 16
-ORDERS = ((0, 1, 2), (1, 0, 2))
+ORDERS = ((0, 1, 2), (1, 2, 0))
 
 f32 = jnp.float32
 bf16 = jnp.bfloat16

time: 129 us -> 133 us (1.031)
  waiting for transfers between devices: 63.5 us -> 71.2 us
  starting transfers between devices: 40.3 us -> 36.9 us
    ppermute x20, waiting for transfers between devices: 58.7 us -> 66.5 us  [exchange(): return lax.ppermute(x, 'tile', [(s, s ^ 1 << bit) for s in range(tiles)])]
    ppermute x20, starting transfers between devices: 31.5 us -> 27.3 us  [exchange(): return lax.ppermute(x, 'tile', [(s, s ^ 1 << bit) for s in range(tiles)])]
  transfers between devices with their start and end apart: 35 -> 35, of which waited for: 24 -> 23; matrix products, arithmetic and copies ran while one was open for 1% -> 1% of each run, Pallas kernels for 6% -> 6%
where the time goes in v12:
time: 133 us
  waiting for transfers between devices  71.2 us (54%)
  starting transfers between devices  36.9 us (28%)
  Pallas kernels  19.5 us (15%)
  local copies, waits for them, and re-layouts  2.38 us (2%)
  between operations  1.86 us (1%)
    ppermute x20, waiting for transfers between devices, exchange(): return lax.ppermute(x, 'tile', [(s, s ^ 1 << bit) for s in range(tiles)])  66.5 us
    ppermute x20, starting transfers between devices, exchange(): return lax.ppermute(x, 'tile', [(s, s ^ 1 << bit) for s in range(tiles)])  27.3 us
    pallas_call x10, Pallas kernels, call(): pl.pallas_call(kernel, out_shape=[jax.ShapeDtypeStruct(o, f32) for o in o...  19.5 us
    ppermute x6, starting transfers between devices, beside(): return lax.ppermute(x, 'tile', pairs)  8.09 us
    ppermute x6, waiting for transfers between devices, beside(): return lax.ppermute(x, 'tile', pairs)  2.84 us
  transfers between devices with their start and end apart: 35, of which 23 were waited for; matrix products, arithmetic and copies ran while one was open for 1% of the time, Pallas kernels for 6%

profile of v12, /device:TPU:0, one launch (start us, length us, event | category | flops | bytes accessed | tf_op | source)
XLA Modules:
  0.0 132.8 jit_solution(51616960930359740)
XLA Ops:
  1.7 3.0 %collective-permute-start = (f32[2,128,128]{2,1,0:T(8,128)S(1)}, f32[2,128,128]{2,1,0:T(8,128)S(1)}, u32[]{:S(2)}, u32[]{:S(2)}) collective-permute-start(f32[2,128,128]{2,1,0:T(8,128)S(1)} %get-tuple-element.120), channel_id=1, source_target_pairs={{0,2},{2,0},{4,6},{6,4},{8,10},{10,8},{12,14},{14,12},{1,3},{3,1},... | collective-permute-start | bytes 393224 | tf_op jit(solution)/shard_map/ppermute | solution.py:354
  5.4 2.8 %collective-permute-done = f32[2,128,128]{2,1,0:T(8,128)S(1)} collective-permute-done((f32[2,128,128]{2,1,0:T(8,128)S(1)}, f32[2,128,128]{2,1,0:T(8,128)S(1)}, u32[]{:S(2)}, u32[]{:S(2)}) %collective-permute-start) | collective-permute-done | bytes 131104 | tf_op jit(solution)/shard_map/ppermute | solution.py:354
  10.5 2.0 %shard_map.87 = (f32[2,2,256,256]{3,2,1,0:T(8,128)S(1)}, f32[256,256]{1,0:T(8,128)S(1)}, f32[2,256,256]{2,1,0:T(8,128)S(1)}) custom-call(s32[2,2]{1,0:T(2,128)S(1)} %copy-done.4, f32[2,2,128,256]{3,2,1,0:T(8,128)S(1)} %pad_maximum_fusion.refs_1_, f32[2,2,128,256]{3,2,1,0:T(8,128)S(1)} %collective-permute-done.2.refs_2_, f32[2,2,256,256]{3,2,1,0:T(8,128)S(1)} %copy-done.3, ...), custom_call_target="tpu_custom_call" | custom-call | flops 3221225472 | bytes 4980752 | tf_op jit(solution)/shard_map/pallas_call | solution.py:331
  12.5 2.0 %shard_map.88 = (f32[2,2,256,256]{3,2,1,0:T(8,128)S(1)}, f32[256,256]{1,0:T(8,128)S(1)}, f32[2,256,256]{2,1,0:T(8,128)S(1)}) custom-call(s32[2,2]{1,0:T(2,128)S(1)} %copy-done.4, f32[2,2,128,256]{3,2,1,0:T(8,128)S(1)} %pad_maximum_fusion.refs_1_, f32[2,2,128,256]{3,2,1,0:T(8,128)S(1)} %collective-permute-done.2.refs_2_, f32[2,2,256,256]{3,2,1,0:T(8,128)S(1)} %copy-done.3, ...), custom_call_target="tpu_custom_call" | custom-call | flops 3221225472 | bytes 4980752 | tf_op jit(solution)/shard_map/pallas_call | solution.py:331
  16.5 2.2 %shard_map.89 = (f32[4,2,64,256]{3,2,1,0:T(8,128)S(1)}, f32[2,2,256,256]{3,2,1,0:T(8,128)S(1)}) custom-call(s32[2,2]{1,0:T(2,128)S(1)} %copy-done.4, s32[1]{0:T(128)S(6)} %copy.9.refs_1_, bf16[2,2,2,256,256]{4,3,2,1,0:T(8,128)(2,1)S(1)} %copy-done.5, f32[2,256,256]{2,1,0:T(8,128)S(1)} %shard_map.86.refs_3_, f32[2,2,256,256]{3,2,1,0:T(8,128)S(1)} %copy-done.3, ...), custom_call_target="tpu_custom_call" | custom-call | flops 3221225472 | bytes 8388628 | tf_op jit(solution)/shard_map/pallas_call | solution.py:331
  18.7 4.7 %collective-permute-start.6 = (f32[2,2,64,256]{3,2,1,0:T(8,128)S(1)}, f32[2,2,64,256]{3,2,1,0:T(8,128)S(1)}, u32[]{:S(2)}, u32[]{:S(2)}) collective-permute-start(f32[2,2,64,256]{3,2,1,0:T(8,128)S(1)} %slice.118), channel_id=1, source_target_pairs={{0,2},{2,0},{4,6},{6,4},{8,10},{10,8},{12,14},{14,12},{1,3},{3,1},... | collective-permute-start | bytes 786440 | tf_op jit(solution)/shard_map/ppermute | solution.py:364
  23.4 2.4 %shard_map.90 = (f32[4,2,64,256]{3,2,1,0:T(8,128)S(1)}, f32[2,2,2,128,256]{4,3,2,1,0:T(8,128)S(1)}) custom-call(s32[2,2]{1,0:T(2,128)S(1)} %copy-done.4, s32[1]{0:T(128)S(6)} %copy.9.refs_1_, bf16[2,2,2,256,256]{4,3,2,1,0:T(8,128)(2,1)S(1)} %copy-done.5, f32[2,256,256]{2,1,0:T(8,128)S(1)} %shard_map.86.refs_3_, f32[2,2,256,256]{3,2,1,0:T(8,128)S(1)} %copy-done.3, ...), custom_call_target="tpu_custom_call" | custom-call | flops 3221225472 | bytes 9437204 | tf_op jit(solution)/shard_map/pallas_call | solution.py:331
  26.0 1.8 %collective-permute-start.7 = (f32[2,2,64,256]{3,2,1,0:T(8,128)S(1)}, f32[2,2,64,256]{3,2,1,0:T(8,128)S(1)}, u32[]{:S(2)}, u32[]{:S(2)}) collective-permute-start(f32[2,2,64,256]{3,2,1,0:T(8,128)S(1)} %slice.120), channel_id=1, source_target_pairs={{0,4},{2,6},{4,0},{6,2},{8,12},{10,14},{12,8},{14,10},{1,5},{3,7},... | collective-permute-start | bytes 786440 | tf_op jit(solution)/shard_map/ppermute | solution.py:364
  27.8 2.3 %collective-permute-done.6 = f32[2,2,64,256]{3,2,1,0:T(8,128)S(1)} collective-permute-done((f32[2,2,64,256]{3,2,1,0:T(8,128)S(1)}, f32[2,2,64,256]{3,2,1,0:T(8,128)S(1)}, u32[]{:S(2)}, u32[]{:S(2)}) %collective-permute-start.6) | collective-permute-done | bytes 262176 | tf_op jit(solution)/shard_map/ppermute | solution.py:364
  30.1 4.7 %collective-permute-done.7 = f32[2,2,64,256]{3,2,1,0:T(8,128)S(1)} collective-permute-done((f32[2,2,64,256]{3,2,1,0:T(8,128)S(1)}, f32[2,2,64,256]{3,2,1,0:T(8,128)S(1)}, u32[]{:S(2)}, u32[]{:S(2)}) %collective-permute-start.7) | collective-permute-done | bytes 262176 | tf_op jit(solution)/shard_map/ppermute | solution.py:364
  36.7 2.2 %collective-permute-start.9 = (f32[1,2,64,256]{3,2,1,0:T(8,128)S(1)}, f32[1,2,64,256]{3,2,1,0:T(8,128)S(1)}, u32[]{:S(2)}, u32[]{:S(2)}) collective-permute-start(f32[1,2,64,256]{3,2,1,0:T(8,128)S(1)} %slice.125), channel_id=1, source_target_pairs={{0,8},{2,10},{4,12},{6,14},{8,0},{10,2},{12,4},{14,6},{1,9},{3,11}... | collective-permute-start | bytes 393224 | tf_op jit(solution)/shard_map/ppermute | solution.py:364
  39.8 2.0 %collective-permute-done.8 = f32[1,2,64,256]{3,2,1,0:T(8,128)S(1)} collective-permute-done((f32[1,2,64,256]{3,2,1,0:T(8,128)S(1)}, f32[1,2,64,256]{3,2,1,0:T(8,128)S(1)}, u32[]{:S(2)}, u32[]{:S(2)}) %collective-permute-start.8) | collective-permute-done | bytes 131104 | tf_op jit(solution)/shard_map/ppermute | solution.py:364
  41.8 2.9 %collective-permute-done.9 = f32[1,2,64,256]{3,2,1,0:T(8,128)S(1)} collective-permute-done((f32[1,2,64,256]{3,2,1,0:T(8,128)S(1)}, f32[1,2,64,256]{3,2,1,0:T(8,128)S(1)}, u32[]{:S(2)}, u32[]{:S(2)}) %collective-permute-start.9) | collective-permute-done | bytes 131104 | tf_op jit(solution)/shard_map/ppermute | solution.py:364
  44.7 2.3 %collective-permute-start.12 = (f32[2,128,256]{2,1,0:T(8,128)S(1)}, f32[2,128,256]{2,1,0:T(8,128)S(1)}, u32[]{:S(2)}, u32[]{:S(2)}) collective-permute-start(f32[2,128,256]{2,1,0:T(8,128)S(1)} %get-tuple-element.73), channel_id=1, source_target_pairs={{0,2},{2,0},{4,6},{6,4},{8,10},{10,8},{12,14},{14,12},{1,3},{3,1},... | collective-permute-start | bytes 786440 | tf_op jit(solution)/shard_map/ppermute | solution.py:354
  48.4 8.2 %collective-permute-done.10 = f32[1,2,64,256]{3,2,1,0:T(8,128)S(1)} collective-permute-done((f32[1,2,64,256]{3,2,1,0:T(8,128)S(1)}, f32[1,2,64,256]{3,2,1,0:T(8,128)S(1)}, u32[]{:S(2)}, u32[]{:S(2)}) %collective-permute-start.10) | collective-permute-done | bytes 131104 | tf_op jit(solution)/shard_map/ppermute | solution.py:364
  57.0 2.8 %collective-permute-start.15 = (f32[1,2,64,256]{3,2,1,0:T(8,128)S(1)}, f32[1,2,64,256]{3,2,1,0:T(8,128)S(1)}, u32[]{:S(2)}, u32[]{:S(2)}) collective-permute-start(f32[1,2,64,256]{3,2,1,0:T(8,128)S(1)} %add.74.refs_5_), channel_id=1, source_target_pairs={{0,4},{2,6},{4,0},{6,2},{8,12},{10,14},{12,8},{14,10},{1,5},{3,7},... | collective-permute-start | bytes 393224 | tf_op jit(solution)/shard_map/ppermute | solution.py:364
  59.8 2.3 %collective-permute-start.16 = (f32[1,2,64,256]{3,2,1,0:T(8,128)S(1)}, f32[1,2,64,256]{3,2,1,0:T(8,128)S(1)}, u32[]{:S(2)}, u32[]{:S(2)}) collective-permute-start(f32[1,2,64,256]{3,2,1,0:T(8,128)S(1)} %add.75.refs_8_), channel_id=1, source_target_pairs={{0,8},{2,10},{4,12},{6,14},{8,0},{10,2},{12,4},{14,6},{1,9},{3,11}... | collective-permute-start | bytes 393224 | tf_op jit(solution)/shard_map/ppermute | solution.py:364
  64.0 4.5 %collective-permute-done.16.refs_9_ = f32[1,2,64,256]{3,2,1,0:T(8,128)S(1)} collective-permute-done((f32[1,2,64,256]{3,2,1,0:T(8,128)S(1)}, f32[1,2,64,256]{3,2,1,0:T(8,128)S(1)}, u32[]{:S(2)}, u32[]{:S(2)}) %collective-permute-start.16) | collective-permute-done | bytes 131104 | tf_op jit(solution)/shard_map/ppermute | solution.py:364
  68.5 2.0 %collective-permute-start.17 = (f32[2,2,64,256]{3,2,1,0:T(8,128)S(1)}, f32[2,2,64,256]{3,2,1,0:T(8,128)S(1)}, u32[]{:S(2)}, u32[]{:S(2)}) collective-permute-start(f32[2,2,64,256]{3,2,1,0:T(8,128)S(1)} %pad_maximum_fusion.1), channel_id=1, source_target_pairs={{0,2},{2,0},{4,6},{6,4},{8,10},{10,8},{12,14},{14,12},{1,3},{3,1},... | collective-permute-start | bytes 786440 | tf_op jit(solution)/shard_map/ppermute | solution.py:364
  70.6 5.8 %collective-permute-done.17.refs_7_ = f32[2,2,64,256]{3,2,1,0:T(8,128)S(1)} collective-permute-done((f32[2,2,64,256]{3,2,1,0:T(8,128)S(1)}, f32[2,2,64,256]{3,2,1,0:T(8,128)S(1)}, u32[]{:S(2)}, u32[]{:S(2)}) %collective-permute-start.17) | collective-permute-done | bytes 262176 | tf_op jit(solution)/shard_map/ppermute | solution.py:364
  78.0 2.1 %shard_map.91 = (f32[2,2,256,256]{3,2,1,0:T(8,128)S(1)}, f32[256,256]{1,0:T(8,128)S(1)}, f32[2,256,256]{2,1,0:T(8,128)S(1)}, f32[2,2,256,256]{3,2,1,0:T(8,128)S(1)}) custom-call(s32[2,2]{1,0:T(2,128)S(1)} %copy-done.4, f32[2,2,128,256]{3,2,1,0:T(8,128)S(1)} %fusion.refs_1_, f32[2,2,128,256]{3,2,1,0:T(8,128)S(1)} %collective-permute-done.14.refs_2_, ...), custom_call_target="tpu_custom_call" | custom-call | flops 3221225472 | bytes 7077904 | tf_op jit(solution)/shard_map/pallas_call | solution.py:331
  80.1 2.0 %shard_map.92 = (f32[2,2,256,256]{3,2,1,0:T(8,128)S(1)}, f32[256,256]{1,0:T(8,128)S(1)}, f32[2,256,256]{2,1,0:T(8,128)S(1)}) custom-call(s32[2,2]{1,0:T(2,128)S(1)} %copy-done.4, f32[2,2,128,256]{3,2,1,0:T(8,128)S(1)} %fusion.refs_1_, f32[2,2,128,256]{3,2,1,0:T(8,128)S(1)} %collective-permute-done.14.refs_2_, ...), custom_call_target="tpu_custom_call" | custom-call | flops 3221225472 | bytes 4980752 | tf_op jit(solution)/shard_map/pallas_call | solution.py:331
  83.9 2.2 %shard_map.93 = (f32[4,2,64,256]{3,2,1,0:T(8,128)S(1)}, f32[2,2,256,256]{3,2,1,0:T(8,128)S(1)}) custom-call(s32[2,2]{1,0:T(2,128)S(1)} %copy-done.4, s32[1]{0:T(128)S(6)} %copy.9.refs_1_, bf16[2,2,2,256,256]{4,3,2,1,0:T(8,128)(2,1)S(1)} %copy-done.5, f32[2,256,256]{2,1,0:T(8,128)S(1)} %shard_map.86.refs_3_, ...), custom_call_target="tpu_custom_call" | custom-call | flops 3221225472 | bytes 8388628 | tf_op jit(solution)/shard_map/pallas_call | solution.py:331
  86.5 2.4 %shard_map.94 = (f32[4,2,64,256]{3,2,1,0:T(8,128)S(1)}, f32[2,2,2,128,256]{4,3,2,1,0:T(8,128)S(1)}) custom-call(s32[2,2]{1,0:T(2,128)S(1)} %copy-done.4, s32[1]{0:T(128)S(6)} %copy.9.refs_1_, bf16[2,2,2,256,256]{4,3,2,1,0:T(8,128)(2,1)S(1)} %copy-done.5, f32[2,256,256]{2,1,0:T(8,128)S(1)} %shard_map.86.refs_3_, ...), custom_call_target="tpu_custom_call" | custom-call | flops 3221225472 | bytes 9437204 | tf_op jit(solution)/shard_map/pallas_call | solution.py:331
  89.4 5.3 %collective-permute-done.22 = f32[2,2,64,256]{3,2,1,0:T(8,128)S(1)} collective-permute-done((f32[2,2,64,256]{3,2,1,0:T(8,128)S(1)}, f32[2,2,64,256]{3,2,1,0:T(8,128)S(1)}, u32[]{:S(2)}, u32[]{:S(2)}) %collective-permute-start.22) | collective-permute-done | bytes 262176 | tf_op jit(solution)/shard_map/ppermute | solution.py:364
  94.8 2.5 %collective-permute-done.23 = f32[2,2,64,256]{3,2,1,0:T(8,128)S(1)} collective-permute-done((f32[2,2,64,256]{3,2,1,0:T(8,128)S(1)}, f32[2,2,64,256]{3,2,1,0:T(8,128)S(1)}, u32[]{:S(2)}, u32[]{:S(2)}) %collective-permute-start.23) | collective-permute-done | bytes 262176 | tf_op jit(solution)/shard_map/ppermute | solution.py:364
  99.8 5.2 %collective-permute-done.24 = f32[1,2,64,256]{3,2,1,0:T(8,128)S(1)} collective-permute-done((f32[1,2,64,256]{3,2,1,0:T(8,128)S(1)}, f32[1,2,64,256]{3,2,1,0:T(8,128)S(1)}, u32[]{:S(2)}, u32[]{:S(2)}) %collective-permute-start.24) | collective-permute-done | bytes 131104 | tf_op jit(solution)/shard_map/ppermute | solution.py:364
  105.0 2.9 %collective-permute-done.25 = f32[1,2,64,256]{3,2,1,0:T(8,128)S(1)} collective-permute-done((f32[1,2,64,256]{3,2,1,0:T(8,128)S(1)}, f32[1,2,64,256]{3,2,1,0:T(8,128)S(1)}, u32[]{:S(2)}, u32[]{:S(2)}) %collective-permute-start.25) | collective-permute-done | bytes 131104 | tf_op jit(solution)/shard_map/ppermute | solution.py:364
  110.1 4.5 %collective-permute-done.26 = f32[1,2,64,256]{3,2,1,0:T(8,128)S(1)} collective-permute-done((f32[1,2,64,256]{3,2,1,0:T(8,128)S(1)}, f32[1,2,64,256]{3,2,1,0:T(8,128)S(1)}, u32[]{:S(2)}, u32[]{:S(2)}) %collective-permute-start.26) | collective-permute-done | bytes 131104 | tf_op jit(solution)/shard_map/ppermute | solution.py:364
  117.6 2.9 %collective-permute-done.31.refs_4_ = f32[1,2,64,256]{3,2,1,0:T(8,128)S(1)} collective-permute-done((f32[1,2,64,256]{3,2,1,0:T(8,128)S(1)}, f32[1,2,64,256]{3,2,1,0:T(8,128)S(1)}, u32[]{:S(2)}, u32[]{:S(2)}) %collective-permute-start.31) | collective-permute-done | bytes 131104 | tf_op jit(solution)/shard_map/ppermute | solution.py:364
  120.5 2.9 %collective-permute-done.32.refs_7_ = f32[1,2,64,256]{3,2,1,0:T(8,128)S(1)} collective-permute-done((f32[1,2,64,256]{3,2,1,0:T(8,128)S(1)}, f32[1,2,64,256]{3,2,1,0:T(8,128)S(1)}, u32[]{:S(2)}, u32[]{:S(2)}) %collective-permute-start.32) | collective-permute-done | bytes 131104 | tf_op jit(solution)/shard_map/ppermute | solution.py:364
  125.2 4.7 %collective-permute-done.33.refs_5_ = f32[2,2,64,256]{3,2,1,0:T(8,128)S(1)} collective-permute-done((f32[2,2,64,256]{3,2,1,0:T(8,128)S(1)}, f32[2,2,64,256]{3,2,1,0:T(8,128)S(1)}, u32[]{:S(2)}, u32[]{:S(2)}) %collective-permute-start.33) | collective-permute-done | bytes 262176 | tf_op jit(solution)/shard_map/ppermute | solution.py:364
  (106 shorter events, 28.4 us)
Async XLA Ops:
  1.7 6.5 %collective-permute-start = (f32[2,128,128]{2,1,0:T(8,128)S(1)}, f32[2,128,128]{2,1,0:T(8,128)S(1)}, u32[]{:S(2)}, u32[]{:S(2)}) collective-permute-start(f32[2,128,128]{2,1,0:T(8,128)S(1)} %get-tuple-element.120), channel_id=1, source_target_pairs={{0,2},{2,0},{4,6},{6,4},{8,10},{10,8},{12,14},{14,12},{1,3},{3,1},... | collective-permute-start | bytes 393224 | tf_op jit(solution)/shard_map/ppermute | solution.py:354
  4.8 3.5 %collective-permute-start.1 = (f32[2,128,128]{2,1,0:T(8,128)S(1)}, f32[2,128,128]{2,1,0:T(8,128)S(1)}, u32[]{:S(2)}, u32[]{:S(2)}) collective-permute-start(f32[2,128,128]{2,1,0:T(8,128)S(1)} %get-tuple-element.121), channel_id=1, source_target_pairs={{2,4},{4,2},{6,8},{8,6},{10,12},{12,10},{3,5},{5,3},{7,9},{9,7},{1... | collective-permute-start | bytes 393224 | tf_op jit(solution)/shard_map/ppermute | solution.py:354
  8.5 2.0 %collective-permute-start.2 = (f32[2,2,128,256]{3,2,1,0:T(8,128)S(1)}, f32[2,2,128,256]{3,2,1,0:T(8,128)S(1)}, u32[]{:S(2)}, u32[]{:S(2)}) collective-permute-start(f32[2,2,128,256]{3,2,1,0:T(8,128)S(1)} %pad_maximum_fusion.refs_1_), channel_id=1, source_target_pairs={{0,1},{1,0},{2,3},{3,2},{4,5},{5,4},{6,7},{7,6},{8,9},{9,8},{10,11... | collective-permute-start | bytes 1572872 | tf_op jit(solution)/shard_map/ppermute | solution.py:345
  18.7 11.3 %collective-permute-start.6 = (f32[2,2,64,256]{3,2,1,0:T(8,128)S(1)}, f32[2,2,64,256]{3,2,1,0:T(8,128)S(1)}, u32[]{:S(2)}, u32[]{:S(2)}) collective-permute-start(f32[2,2,64,256]{3,2,1,0:T(8,128)S(1)} %slice.118), channel_id=1, source_target_pairs={{0,2},{2,0},{4,6},{6,4},{8,10},{10,8},{12,14},{14,12},{1,3},{3,1},... | collective-permute-start | bytes 786440 | tf_op jit(solution)/shard_map/ppermute | solution.py:364
  25.9 8.9 %collective-permute-start.5 = (f32[2,2,128,256]{3,2,1,0:T(8,128)S(1)}, f32[2,2,128,256]{3,2,1,0:T(8,128)S(1)}, u32[]{:S(2)}, u32[]{:S(2)}) collective-permute-start(f32[2,2,128,256]{3,2,1,0:T(8,128)S(1)} %slice_bitcast_fusion.1), channel_id=1, source_target_pairs={{0,1},{1,0},{2,3},{3,2},{4,5},{5,4},{6,7},{7,6},{8,9},{9,8},{10,11... | collective-permute-start | bytes 1572872 | tf_op jit(solution)/shard_map/ppermute | solution.py:345
  26.0 8.8 %collective-permute-start.7 = (f32[2,2,64,256]{3,2,1,0:T(8,128)S(1)}, f32[2,2,64,256]{3,2,1,0:T(8,128)S(1)}, u32[]{:S(2)}, u32[]{:S(2)}) collective-permute-start(f32[2,2,64,256]{3,2,1,0:T(8,128)S(1)} %slice.120), channel_id=1, source_target_pairs={{0,4},{2,6},{4,0},{6,2},{8,12},{10,14},{12,8},{14,10},{1,5},{3,7},... | collective-permute-start | bytes 786440 | tf_op jit(solution)/shard_map/ppermute | solution.py:364
  35.0 6.8 %collective-permute-start.8 = (f32[1,2,64,256]{3,2,1,0:T(8,128)S(1)}, f32[1,2,64,256]{3,2,1,0:T(8,128)S(1)}, u32[]{:S(2)}, u32[]{:S(2)}) collective-permute-start(f32[1,2,64,256]{3,2,1,0:T(8,128)S(1)} %slice.123), channel_id=1, source_target_pairs={{0,4},{2,6},{4,0},{6,2},{8,12},{10,14},{12,8},{14,10},{1,5},{3,7},... | collective-permute-start | bytes 393224 | tf_op jit(solution)/shard_map/ppermute | solution.py:364
  36.7 7.9 %collective-permute-start.9 = (f32[1,2,64,256]{3,2,1,0:T(8,128)S(1)}, f32[1,2,64,256]{3,2,1,0:T(8,128)S(1)}, u32[]{:S(2)}, u32[]{:S(2)}) collective-permute-start(f32[1,2,64,256]{3,2,1,0:T(8,128)S(1)} %slice.125), channel_id=1, source_target_pairs={{0,8},{2,10},{4,12},{6,14},{8,0},{10,2},{12,4},{14,6},{1,9},{3,11}... | collective-permute-start | bytes 393224 | tf_op jit(solution)/shard_map/ppermute | solution.py:364
  38.9 18.1 %collective-permute-start.13 = (f32[2,128,256]{2,1,0:T(8,128)S(1)}, f32[2,128,256]{2,1,0:T(8,128)S(1)}, u32[]{:S(2)}, u32[]{:S(2)}) collective-permute-start(f32[2,128,256]{2,1,0:T(8,128)S(1)} %get-tuple-element.74), channel_id=1, source_target_pairs={{2,4},{4,2},{6,8},{8,6},{10,12},{12,10},{3,5},{5,3},{7,9},{9,7},{1... | collective-permute-start | bytes 786440 | tf_op jit(solution)/shard_map/ppermute | solution.py:354
  44.7 12.3 %collective-permute-start.12 = (f32[2,128,256]{2,1,0:T(8,128)S(1)}, f32[2,128,256]{2,1,0:T(8,128)S(1)}, u32[]{:S(2)}, u32[]{:S(2)}) collective-permute-start(f32[2,128,256]{2,1,0:T(8,128)S(1)} %get-tuple-element.73), channel_id=1, source_target_pairs={{0,2},{2,0},{4,6},{6,4},{8,10},{10,8},{12,14},{14,12},{1,3},{3,1},... | collective-permute-start | bytes 786440 | tf_op jit(solution)/shard_map/ppermute | solution.py:354
  47.0 9.7 %collective-permute-start.10 = (f32[1,2,64,256]{3,2,1,0:T(8,128)S(1)}, f32[1,2,64,256]{3,2,1,0:T(8,128)S(1)}, u32[]{:S(2)}, u32[]{:S(2)}) collective-permute-start(f32[1,2,64,256]{3,2,1,0:T(8,128)S(1)} %slice_add_fusion.7), channel_id=1, source_target_pairs={{0,8},{2,10},{4,12},{6,14},{8,0},{10,2},{12,4},{14,6},{1,9},{3,11}... | collective-permute-start | bytes 393224 | tf_op jit(solution)/shard_map/ppermute | solution.py:364
  48.4 8.6 %collective-permute-start.11 = (f32[1,2,64,256]{3,2,1,0:T(8,128)S(1)}, f32[1,2,64,256]{3,2,1,0:T(8,128)S(1)}, u32[]{:S(2)}, u32[]{:S(2)}) collective-permute-start(f32[1,2,64,256]{3,2,1,0:T(8,128)S(1)} %slice_add_fusion.6), channel_id=1, source_target_pairs={{0,2},{2,0},{4,6},{6,4},{8,10},{10,8},{12,14},{14,12},{1,3},{3,1},... | collective-permute-start | bytes 393224 | tf_op jit(solution)/shard_map/ppermute | solution.py:364
  57.0 7.0 %collective-permute-start.15 = (f32[1,2,64,256]{3,2,1,0:T(8,128)S(1)}, f32[1,2,64,256]{3,2,1,0:T(8,128)S(1)}, u32[]{:S(2)}, u32[]{:S(2)}) collective-permute-start(f32[1,2,64,256]{3,2,1,0:T(8,128)S(1)} %add.74.refs_5_), channel_id=1, source_target_pairs={{0,4},{2,6},{4,0},{6,2},{8,12},{10,14},{12,8},{14,10},{1,5},{3,7},... | collective-permute-start | bytes 393224 | tf_op jit(solution)/shard_map/ppermute | solution.py:364
  59.8 8.7 %collective-permute-start.16 = (f32[1,2,64,256]{3,2,1,0:T(8,128)S(1)}, f32[1,2,64,256]{3,2,1,0:T(8,128)S(1)}, u32[]{:S(2)}, u32[]{:S(2)}) collective-permute-start(f32[1,2,64,256]{3,2,1,0:T(8,128)S(1)} %add.75.refs_8_), channel_id=1, source_target_pairs={{0,8},{2,10},{4,12},{6,14},{8,0},{10,2},{12,4},{14,6},{1,9},{3,11}... | collective-permute-start | bytes 393224 | tf_op jit(solution)/shard_map/ppermute | solution.py:364
  62.2 15.8 %collective-permute-start.14 = (f32[2,2,128,256]{3,2,1,0:T(8,128)S(1)}, f32[2,2,128,256]{3,2,1,0:T(8,128)S(1)}, u32[]{:S(2)}, u32[]{:S(2)}) collective-permute-start(f32[2,2,128,256]{3,2,1,0:T(8,128)S(1)} %fusion.refs_1_), channel_id=1, source_target_pairs={{0,1},{1,0},{2,3},{3,2},{4,5},{5,4},{6,7},{7,6},{8,9},{9,8},{10,11... | collective-permute-start | bytes 1572872 | tf_op jit(solution)/shard_map/ppermute | solution.py:345
  68.5 7.9 %collective-permute-start.17 = (f32[2,2,64,256]{3,2,1,0:T(8,128)S(1)}, f32[2,2,64,256]{3,2,1,0:T(8,128)S(1)}, u32[]{:S(2)}, u32[]{:S(2)}) collective-permute-start(f32[2,2,64,256]{3,2,1,0:T(8,128)S(1)} %pad_maximum_fusion.1), channel_id=1, source_target_pairs={{0,2},{2,0},{4,6},{6,4},{8,10},{10,8},{12,14},{14,12},{1,3},{3,1},... | collective-permute-start | bytes 786440 | tf_op jit(solution)/shard_map/ppermute | solution.py:364
  70.5 7.5 %collective-permute-start.18 = (f32[2,2,64,256]{3,2,1,0:T(8,128)S(1)}, f32[2,2,64,256]{3,2,1,0:T(8,128)S(1)}, u32[]{:S(2)}, u32[]{:S(2)}) collective-permute-start(f32[2,2,64,256]{3,2,1,0:T(8,128)S(1)} %pad_maximum_fusion.2), channel_id=1, source_target_pairs={{0,4},{2,6},{4,0},{6,2},{8,12},{10,14},{12,8},{14,10},{1,5},{3,7},... | collective-permute-start | bytes 786440 | tf_op jit(solution)/shard_map/ppermute | solution.py:364
  80.1 2.7 %collective-permute-start.19 = (f32[256,256]{1,0:T(8,128)S(1)}, f32[256,256]{1,0:T(8,128)S(1)}, u32[]{:S(2)}, u32[]{:S(2)}) collective-permute-start(f32[256,256]{1,0:T(8,128)S(1)} %get-tuple-element.86.refs_7_), channel_id=1, source_target_pairs={{0,1},{1,0},{2,3},{3,2},{4,5},{5,4},{6,7},{7,6},{8,9},{9,8},{10,11... | collective-permute-start | bytes 786440 | tf_op jit(solution)/shard_map/ppermute | solution.py:345
  86.1 8.7 %collective-permute-start.22 = (f32[2,2,64,256]{3,2,1,0:T(8,128)S(1)}, f32[2,2,64,256]{3,2,1,0:T(8,128)S(1)}, u32[]{:S(2)}, u32[]{:S(2)}) collective-permute-start(f32[2,2,64,256]{3,2,1,0:T(8,128)S(1)} %slice.138), channel_id=1, source_target_pairs={{0,2},{2,0},{4,6},{6,4},{8,10},{10,8},{12,14},{14,12},{1,3},{3,1},... | collective-permute-start | bytes 786440 | tf_op jit(solution)/shard_map/ppermute | solution.py:364
  88.9 8.4 %collective-permute-start.23 = (f32[2,2,64,256]{3,2,1,0:T(8,128)S(1)}, f32[2,2,64,256]{3,2,1,0:T(8,128)S(1)}, u32[]{:S(2)}, u32[]{:S(2)}) collective-permute-start(f32[2,2,64,256]{3,2,1,0:T(8,128)S(1)} %slice.140), channel_id=1, source_target_pairs={{0,4},{2,6},{4,0},{6,2},{8,12},{10,14},{12,8},{14,10},{1,5},{3,7},... | collective-permute-start | bytes 786440 | tf_op jit(solution)/shard_map/ppermute | solution.py:364
  89.3 8.0 %collective-permute-start.21 = (f32[2,2,128,256]{3,2,1,0:T(8,128)S(1)}, f32[2,2,128,256]{3,2,1,0:T(8,128)S(1)}, u32[]{:S(2)}, u32[]{:S(2)}) collective-permute-start(f32[2,2,128,256]{3,2,1,0:T(8,128)S(1)} %slice_bitcast_fusion), channel_id=1, source_target_pairs={{0,1},{1,0},{2,3},{3,2},{4,5},{5,4},{6,7},{7,6},{8,9},{9,8},{10,11... | collective-permute-start | bytes 1572872 | tf_op jit(solution)/shard_map/ppermute | solution.py:345
  97.5 7.5 %collective-permute-start.24 = (f32[1,2,64,256]{3,2,1,0:T(8,128)S(1)}, f32[1,2,64,256]{3,2,1,0:T(8,128)S(1)}, u32[]{:S(2)}, u32[]{:S(2)}) collective-permute-start(f32[1,2,64,256]{3,2,1,0:T(8,128)S(1)} %slice.145), channel_id=1, source_target_pairs={{0,4},{2,6},{4,0},{6,2},{8,12},{10,14},{12,8},{14,10},{1,5},{3,7},... | collective-permute-start | bytes 393224 | tf_op jit(solution)/shard_map/ppermute | solution.py:364
  97.9 10.0 %collective-permute-start.25 = (f32[1,2,64,256]{3,2,1,0:T(8,128)S(1)}, f32[1,2,64,256]{3,2,1,0:T(8,128)S(1)}, u32[]{:S(2)}, u32[]{:S(2)}) collective-permute-start(f32[1,2,64,256]{3,2,1,0:T(8,128)S(1)} %slice.147), channel_id=1, source_target_pairs={{0,8},{2,10},{4,12},{6,14},{8,0},{10,2},{12,4},{14,6},{1,9},{3,11}... | collective-permute-start | bytes 393224 | tf_op jit(solution)/shard_map/ppermute | solution.py:364
  99.1 15.6 %collective-permute-start.29 = (f32[2,128,128]{2,1,0:T(8,128)S(1)}, f32[2,128,128]{2,1,0:T(8,128)S(1)}, u32[]{:S(2)}, u32[]{:S(2)}) collective-permute-start(f32[2,128,128]{2,1,0:T(8,128)S(1)} %slice_select_fusion.2), channel_id=1, source_target_pairs={{2,4},{4,2},{6,8},{8,6},{10,12},{12,10},{3,5},{5,3},{7,9},{9,7},{1... | collective-permute-start | bytes 393224 | tf_op jit(solution)/shard_map/ppermute | solution.py:354
  107.9 6.7 %collective-permute-start.26 = (f32[1,2,64,256]{3,2,1,0:T(8,128)S(1)}, f32[1,2,64,256]{3,2,1,0:T(8,128)S(1)}, u32[]{:S(2)}, u32[]{:S(2)}) collective-permute-start(f32[1,2,64,256]{3,2,1,0:T(8,128)S(1)} %slice_add_fusion.5), channel_id=1, source_target_pairs={{0,8},{2,10},{4,12},{6,14},{8,0},{10,2},{12,4},{14,6},{1,9},{3,11}... | collective-permute-start | bytes 393224 | tf_op jit(solution)/shard_map/ppermute | solution.py:364
  108.0 6.6 %collective-permute-start.27 = (f32[1,2,64,256]{3,2,1,0:T(8,128)S(1)}, f32[1,2,64,256]{3,2,1,0:T(8,128)S(1)}, u32[]{:S(2)}, u32[]{:S(2)}) collective-permute-start(f32[1,2,64,256]{3,2,1,0:T(8,128)S(1)} %slice_add_fusion.4), channel_id=1, source_target_pairs={{0,2},{2,0},{4,6},{6,4},{8,10},{10,8},{12,14},{14,12},{1,3},{3,1},... | collective-permute-start | bytes 393224 | tf_op jit(solution)/shard_map/ppermute | solution.py:364
  109.5 5.1 %collective-permute-start.28 = (f32[2,128,128]{2,1,0:T(8,128)S(1)}, f32[2,128,128]{2,1,0:T(8,128)S(1)}, u32[]{:S(2)}, u32[]{:S(2)}) collective-permute-start(f32[2,128,128]{2,1,0:T(8,128)S(1)} %slice_select_fusion.3), channel_id=1, source_target_pairs={{0,2},{2,0},{4,6},{6,4},{8,10},{10,8},{12,14},{14,12},{1,3},{3,1},... | collective-permute-start | bytes 393224 | tf_op jit(solution)/shard_map/ppermute | solution.py:354
  114.7 5.8 %collective-permute-start.31 = (f32[1,2,64,256]{3,2,1,0:T(8,128)S(1)}, f32[1,2,64,256]{3,2,1,0:T(8,128)S(1)}, u32[]{:S(2)}, u32[]{:S(2)}) collective-permute-start(f32[1,2,64,256]{3,2,1,0:T(8,128)S(1)} %add.84.refs_3_), channel_id=1, source_target_pairs={{0,4},{2,6},{4,0},{6,2},{8,12},{10,14},{12,8},{14,10},{1,5},{3,7},... | collective-permute-start | bytes 393224 | tf_op jit(solution)/shard_map/ppermute | solution.py:364
  116.1 7.4 %collective-permute-start.32 = (f32[1,2,64,256]{3,2,1,0:T(8,128)S(1)}, f32[1,2,64,256]{3,2,1,0:T(8,128)S(1)}, u32[]{:S(2)}, u32[]{:S(2)}) collective-permute-start(f32[1,2,64,256]{3,2,1,0:T(8,128)S(1)} %add.85.refs_6_), channel_id=1, source_target_pairs={{0,8},{2,10},{4,12},{6,14},{8,0},{10,2},{12,4},{14,6},{1,9},{3,11}... | collective-permute-start | bytes 393224 | tf_op jit(solution)/shard_map/ppermute | solution.py:364
  117.5 7.7 %collective-permute-start.30 = (f32[2,2,128,128]{3,2,1,0:T(8,128)S(1)}, f32[2,2,128,128]{3,2,1,0:T(8,128)S(1)}, u32[]{:S(2)}, u32[]{:S(2)}) collective-permute-start(f32[2,2,128,128]{3,2,1,0:T(8,128)S(1)} %maximum_add_fusion.refs_0_), channel_id=1, source_target_pairs={{0,1},{1,0},{2,3},{3,2},{4,5},{5,4},{6,7},{7,6},{8,9},{9,8},{10,11... | collective-permute-start | bytes 786440 | tf_op jit(solution)/shard_map/ppermute | solution.py:345
  123.5 6.4 %collective-permute-start.33 = (f32[2,2,64,256]{3,2,1,0:T(8,128)S(1)}, f32[2,2,64,256]{3,2,1,0:T(8,128)S(1)}, u32[]{:S(2)}, u32[]{:S(2)}) collective-permute-start(f32[2,2,64,256]{3,2,1,0:T(8,128)S(1)} %pad_maximum_fusion.3), channel_id=1, source_target_pairs={{0,2},{2,0},{4,6},{6,4},{8,10},{10,8},{12,14},{14,12},{1,3},{3,1},... | collective-permute-start | bytes 786440 | tf_op jit(solution)/shard_map/ppermute | solution.py:364
  125.1 6.4 %collective-permute-start.34 = (f32[2,2,64,256]{3,2,1,0:T(8,128)S(1)}, f32[2,2,64,256]{3,2,1,0:T(8,128)S(1)}, u32[]{:S(2)}, u32[]{:S(2)}) collective-permute-start(f32[2,2,64,256]{3,2,1,0:T(8,128)S(1)} %pad_maximum_fusion.4), channel_id=1, source_target_pairs={{0,4},{2,6},{4,0},{6,2},{8,12},{10,14},{12,8},{14,10},{1,5},{3,7},... | collective-permute-start | bytes 786440 | tf_op jit(solution)/shard_map/ppermute | solution.py:364
  (9 other events, 14.6 us)

commit v13 on v9

--- a/solution.py
+++ b/solution.py
@@ -404,8 +404,6 @@
     for i in reversed(range(HALVINGS)):
         for p, o in zip(pieces, ORDERS):
             p.append(exchange(p[0] if len(p) == 1 else jnp.concatenate(p, 0), o[i], tiles))
-        if i:
-            (pieces,) = together(pieces)
     return pieces, jnp.stack([a + b for a, b in zip(stay, got)])
 
 

time: 129 us -> 130 us (level)
  starting transfers between devices: 40.3 us -> 43.9 us
  waiting for transfers between devices: 63.5 us -> 60.9 us
    ppermute x20, waiting for transfers between devices: 58.7 us -> 56.1 us  [exchange(): return lax.ppermute(x, 'tile', [(s, s ^ 1 << bit) for s in range(tiles)])]
    ppermute x20, starting transfers between devices: 31.5 us -> 33.6 us  [exchange(): return lax.ppermute(x, 'tile', [(s, s ^ 1 << bit) for s in range(tiles)])]
    ppermute x6, starting transfers between devices: 7.24 us -> 8.73 us  [beside(): return lax.ppermute(x, 'tile', pairs)]
where the time goes in v13:
time: 130 us; the launch traced here: 129 us
  waiting for transfers between devices  60.9 us (47%)
  starting transfers between devices  43.9 us (34%)
  Pallas kernels  19.5 us (15%)
  local copies, waits for them, and re-layouts  2.38 us (2%)
  between operations  1.85 us (1%)
    ppermute x20, waiting for transfers between devices, exchange(): return lax.ppermute(x, 'tile', [(s, s ^ 1 << bit) for s in range(tiles)])  56.1 us
    ppermute x20, starting transfers between devices, exchange(): return lax.ppermute(x, 'tile', [(s, s ^ 1 << bit) for s in range(tiles)])  33.6 us
    pallas_call x10, Pallas kernels, call(): pl.pallas_call(kernel, out_shape=[jax.ShapeDtypeStruct(o, f32) for o in o...  19.5 us
    ppermute x6, starting transfers between devices, beside(): return lax.ppermute(x, 'tile', pairs)  8.73 us
    ppermute x6, waiting for transfers between devices, beside(): return lax.ppermute(x, 'tile', pairs)  2.84 us
  transfers between devices with their start and end apart: 35, of which 24 were waited for; matrix products, arithmetic and copies ran while one was open for 1% of the time, Pallas kernels for 6%

profile of v13, /device:TPU:0, one launch (start us, length us, event | category | flops | bytes accessed | tf_op | source)
XLA Modules:
  0.0 129.4 jit_solution(11571225831750781909)
XLA Ops:
  1.7 3.0 %collective-permute-start = (f32[2,128,128]{2,1,0:T(8,128)S(1)}, f32[2,128,128]{2,1,0:T(8,128)S(1)}, u32[]{:S(2)}, u32[]{:S(2)}) collective-permute-start(f32[2,128,128]{2,1,0:T(8,128)S(1)} %get-tuple-element.104), channel_id=1, source_target_pairs={{0,2},{2,0},{4,6},{6,4},{8,10},{10,8},{12,14},{14,12},{1,3},{3,1},... | collective-permute-start | bytes 393224 | tf_op jit(solution)/shard_map/ppermute | solution.py:354
  5.4 2.8 %collective-permute-done = f32[2,128,128]{2,1,0:T(8,128)S(1)} collective-permute-done((f32[2,128,128]{2,1,0:T(8,128)S(1)}, f32[2,128,128]{2,1,0:T(8,128)S(1)}, u32[]{:S(2)}, u32[]{:S(2)}) %collective-permute-start) | collective-permute-done | bytes 131104 | tf_op jit(solution)/shard_map/ppermute | solution.py:354
  10.5 2.0 %shard_map.87 = (f32[2,2,256,256]{3,2,1,0:T(8,128)S(1)}, f32[256,256]{1,0:T(8,128)S(1)}, f32[2,256,256]{2,1,0:T(8,128)S(1)}) custom-call(s32[2,2]{1,0:T(2,128)S(1)} %copy-done.4, f32[2,2,128,256]{3,2,1,0:T(8,128)S(1)} %pad_maximum_fusion.refs_1_, f32[2,2,128,256]{3,2,1,0:T(8,128)S(1)} %collective-permute-done.2.refs_2_, f32[2,2,256,256]{3,2,1,0:T(8,128)S(1)} %copy-done.3, ...), custom_call_target="tpu_custom_call" | custom-call | flops 3221225472 | bytes 4980752 | tf_op jit(solution)/shard_map/pallas_call | solution.py:331
  12.5 2.0 %shard_map.88 = (f32[2,2,256,256]{3,2,1,0:T(8,128)S(1)}, f32[256,256]{1,0:T(8,128)S(1)}, f32[2,256,256]{2,1,0:T(8,128)S(1)}) custom-call(s32[2,2]{1,0:T(2,128)S(1)} %copy-done.4, f32[2,2,128,256]{3,2,1,0:T(8,128)S(1)} %pad_maximum_fusion.refs_1_, f32[2,2,128,256]{3,2,1,0:T(8,128)S(1)} %collective-permute-done.2.refs_2_, f32[2,2,256,256]{3,2,1,0:T(8,128)S(1)} %copy-done.3, ...), custom_call_target="tpu_custom_call" | custom-call | flops 3221225472 | bytes 4980752 | tf_op jit(solution)/shard_map/pallas_call | solution.py:331
  16.5 2.2 %shard_map.89 = (f32[4,2,64,256]{3,2,1,0:T(8,128)S(1)}, f32[2,2,256,256]{3,2,1,0:T(8,128)S(1)}) custom-call(s32[2,2]{1,0:T(2,128)S(1)} %copy-done.4, s32[1]{0:T(128)S(6)} %copy.9.refs_1_, bf16[2,2,2,256,256]{4,3,2,1,0:T(8,128)(2,1)S(1)} %copy-done.5, f32[2,256,256]{2,1,0:T(8,128)S(1)} %shard_map.86.refs_3_, f32[2,2,256,256]{3,2,1,0:T(8,128)S(1)} %copy-done.3, ...), custom_call_target="tpu_custom_call" | custom-call | flops 3221225472 | bytes 8388628 | tf_op jit(solution)/shard_map/pallas_call | solution.py:331
  18.7 4.7 %collective-permute-start.6 = (f32[2,2,64,256]{3,2,1,0:T(8,128)S(1)}, f32[2,2,64,256]{3,2,1,0:T(8,128)S(1)}, u32[]{:S(2)}, u32[]{:S(2)}) collective-permute-start(f32[2,2,64,256]{3,2,1,0:T(8,128)S(1)} %slice.118), channel_id=1, source_target_pairs={{0,2},{2,0},{4,6},{6,4},{8,10},{10,8},{12,14},{14,12},{1,3},{3,1},... | collective-permute-start | bytes 786440 | tf_op jit(solution)/shard_map/ppermute | solution.py:364
  23.4 2.4 %shard_map.90 = (f32[4,2,64,256]{3,2,1,0:T(8,128)S(1)}, f32[2,2,2,128,256]{4,3,2,1,0:T(8,128)S(1)}) custom-call(s32[2,2]{1,0:T(2,128)S(1)} %copy-done.4, s32[1]{0:T(128)S(6)} %copy.9.refs_1_, bf16[2,2,2,256,256]{4,3,2,1,0:T(8,128)(2,1)S(1)} %copy-done.5, f32[2,256,256]{2,1,0:T(8,128)S(1)} %shard_map.86.refs_3_, f32[2,2,256,256]{3,2,1,0:T(8,128)S(1)} %copy-done.3, ...), custom_call_target="tpu_custom_call" | custom-call | flops 3221225472 | bytes 9437204 | tf_op jit(solution)/shard_map/pallas_call | solution.py:331
  26.0 1.8 %collective-permute-start.7 = (f32[2,2,64,256]{3,2,1,0:T(8,128)S(1)}, f32[2,2,64,256]{3,2,1,0:T(8,128)S(1)}, u32[]{:S(2)}, u32[]{:S(2)}) collective-permute-start(f32[2,2,64,256]{3,2,1,0:T(8,128)S(1)} %slice.120), channel_id=1, source_target_pairs={{0,4},{2,6},{4,0},{6,2},{8,12},{10,14},{12,8},{14,10},{1,5},{3,7},... | collective-permute-start | bytes 786440 | tf_op jit(solution)/shard_map/ppermute | solution.py:364
  27.8 2.3 %collective-permute-done.6 = f32[2,2,64,256]{3,2,1,0:T(8,128)S(1)} collective-permute-done((f32[2,2,64,256]{3,2,1,0:T(8,128)S(1)}, f32[2,2,64,256]{3,2,1,0:T(8,128)S(1)}, u32[]{:S(2)}, u32[]{:S(2)}) %collective-permute-start.6) | collective-permute-done | bytes 262176 | tf_op jit(solution)/shard_map/ppermute | solution.py:364
  30.1 4.7 %collective-permute-done.7 = f32[2,2,64,256]{3,2,1,0:T(8,128)S(1)} collective-permute-done((f32[2,2,64,256]{3,2,1,0:T(8,128)S(1)}, f32[2,2,64,256]{3,2,1,0:T(8,128)S(1)}, u32[]{:S(2)}, u32[]{:S(2)}) %collective-permute-start.7) | collective-permute-done | bytes 262176 | tf_op jit(solution)/shard_map/ppermute | solution.py:364
  35.0 1.8 %collective-permute-start.8 = (f32[1,2,64,256]{3,2,1,0:T(8,128)S(1)}, f32[1,2,64,256]{3,2,1,0:T(8,128)S(1)}, u32[]{:S(2)}, u32[]{:S(2)}) collective-permute-start(f32[1,2,64,256]{3,2,1,0:T(8,128)S(1)} %slice.123), channel_id=1, source_target_pairs={{0,4},{2,6},{4,0},{6,2},{8,12},{10,14},{12,8},{14,10},{1,5},{3,7},... | collective-permute-start | bytes 393224 | tf_op jit(solution)/shard_map/ppermute | solution.py:364
  40.2 1.6 %collective-permute-done.9 = f32[1,2,64,256]{3,2,1,0:T(8,128)S(1)} collective-permute-done((f32[1,2,64,256]{3,2,1,0:T(8,128)S(1)}, f32[1,2,64,256]{3,2,1,0:T(8,128)S(1)}, u32[]{:S(2)}, u32[]{:S(2)}) %collective-permute-start.9) | collective-permute-done | bytes 131104 | tf_op jit(solution)/shard_map/ppermute | solution.py:364
  43.4 6.7 %collective-permute-start.10 = (f32[1,2,64,256]{3,2,1,0:T(8,128)S(1)}, f32[1,2,64,256]{3,2,1,0:T(8,128)S(1)}, u32[]{:S(2)}, u32[]{:S(2)}) collective-permute-start(f32[1,2,64,256]{3,2,1,0:T(8,128)S(1)} %slice_add_fusion.7), channel_id=1, source_target_pairs={{0,8},{2,10},{4,12},{6,14},{8,0},{10,2},{12,4},{14,6},{1,9},{3,11}... | collective-permute-start | bytes 393224 | tf_op jit(solution)/shard_map/ppermute | solution.py:364
  50.1 8.1 %collective-permute-done.10 = f32[1,2,64,256]{3,2,1,0:T(8,128)S(1)} collective-permute-done((f32[1,2,64,256]{3,2,1,0:T(8,128)S(1)}, f32[1,2,64,256]{3,2,1,0:T(8,128)S(1)}, u32[]{:S(2)}, u32[]{:S(2)}) %collective-permute-start.10) | collective-permute-done | bytes 131104 | tf_op jit(solution)/shard_map/ppermute | solution.py:364
  61.4 3.4 %collective-permute-done.15.refs_6_ = f32[1,2,64,256]{3,2,1,0:T(8,128)S(1)} collective-permute-done((f32[1,2,64,256]{3,2,1,0:T(8,128)S(1)}, f32[1,2,64,256]{3,2,1,0:T(8,128)S(1)}, u32[]{:S(2)}, u32[]{:S(2)}) %collective-permute-start.15) | collective-permute-done | bytes 131104 | tf_op jit(solution)/shard_map/ppermute | solution.py:364
  66.4 2.1 %collective-permute-start.18 = (f32[2,2,64,256]{3,2,1,0:T(8,128)S(1)}, f32[2,2,64,256]{3,2,1,0:T(8,128)S(1)}, u32[]{:S(2)}, u32[]{:S(2)}) collective-permute-start(f32[2,2,64,256]{3,2,1,0:T(8,128)S(1)} %pad_maximum_fusion.2), channel_id=1, source_target_pairs={{0,4},{2,6},{4,0},{6,2},{8,12},{10,14},{12,8},{14,10},{1,5},{3,7},... | collective-permute-start | bytes 786440 | tf_op jit(solution)/shard_map/ppermute | solution.py:364
  68.5 3.1 %collective-permute-done.16.refs_7_ = f32[2,2,64,256]{3,2,1,0:T(8,128)S(1)} collective-permute-done((f32[2,2,64,256]{3,2,1,0:T(8,128)S(1)}, f32[2,2,64,256]{3,2,1,0:T(8,128)S(1)}, u32[]{:S(2)}, u32[]{:S(2)}) %collective-permute-start.16) | collective-permute-done | bytes 262176 | tf_op jit(solution)/shard_map/ppermute | solution.py:364
  71.6 2.6 %collective-permute-done.18.refs_10_ = f32[2,2,64,256]{3,2,1,0:T(8,128)S(1)} collective-permute-done((f32[2,2,64,256]{3,2,1,0:T(8,128)S(1)}, f32[2,2,64,256]{3,2,1,0:T(8,128)S(1)}, u32[]{:S(2)}, u32[]{:S(2)}) %collective-permute-start.18) | collective-permute-done | bytes 262176 | tf_op jit(solution)/shard_map/ppermute | solution.py:364
  74.2 2.1 %shard_map.91 = (f32[2,2,256,256]{3,2,1,0:T(8,128)S(1)}, f32[256,256]{1,0:T(8,128)S(1)}, f32[2,256,256]{2,1,0:T(8,128)S(1)}, f32[2,2,256,256]{3,2,1,0:T(8,128)S(1)}) custom-call(s32[2,2]{1,0:T(2,128)S(1)} %copy-done.4, f32[2,2,128,256]{3,2,1,0:T(8,128)S(1)} %fusion.refs_1_, f32[2,2,128,256]{3,2,1,0:T(8,128)S(1)} %collective-permute-done.14.refs_2_, ...), custom_call_target="tpu_custom_call" | custom-call | flops 3221225472 | bytes 7077904 | tf_op jit(solution)/shard_map/pallas_call | solution.py:331
  76.4 2.0 %shard_map.92 = (f32[2,2,256,256]{3,2,1,0:T(8,128)S(1)}, f32[256,256]{1,0:T(8,128)S(1)}, f32[2,256,256]{2,1,0:T(8,128)S(1)}) custom-call(s32[2,2]{1,0:T(2,128)S(1)} %copy-done.4, f32[2,2,128,256]{3,2,1,0:T(8,128)S(1)} %fusion.refs_1_, f32[2,2,128,256]{3,2,1,0:T(8,128)S(1)} %collective-permute-done.14.refs_2_, ...), custom_call_target="tpu_custom_call" | custom-call | flops 3221225472 | bytes 4980752 | tf_op jit(solution)/shard_map/pallas_call | solution.py:331
  80.1 2.2 %shard_map.93 = (f32[4,2,64,256]{3,2,1,0:T(8,128)S(1)}, f32[2,2,256,256]{3,2,1,0:T(8,128)S(1)}) custom-call(s32[2,2]{1,0:T(2,128)S(1)} %copy-done.4, s32[1]{0:T(128)S(6)} %copy.9.refs_1_, bf16[2,2,2,256,256]{4,3,2,1,0:T(8,128)(2,1)S(1)} %copy-done.5, f32[2,256,256]{2,1,0:T(8,128)S(1)} %shard_map.86.refs_3_, ...), custom_call_target="tpu_custom_call" | custom-call | flops 3221225472 | bytes 8388628 | tf_op jit(solution)/shard_map/pallas_call | solution.py:331
  83.4 2.4 %shard_map.94 = (f32[4,2,64,256]{3,2,1,0:T(8,128)S(1)}, f32[2,2,2,128,256]{4,3,2,1,0:T(8,128)S(1)}) custom-call(s32[2,2]{1,0:T(2,128)S(1)} %copy-done.4, s32[1]{0:T(128)S(6)} %copy.9.refs_1_, bf16[2,2,2,256,256]{4,3,2,1,0:T(8,128)(2,1)S(1)} %copy-done.5, f32[2,256,256]{2,1,0:T(8,128)S(1)} %shard_map.86.refs_3_, ...), custom_call_target="tpu_custom_call" | custom-call | flops 3221225472 | bytes 9437204 | tf_op jit(solution)/shard_map/pallas_call | solution.py:331
  87.3 3.7 %collective-permute-done.22 = f32[2,2,64,256]{3,2,1,0:T(8,128)S(1)} collective-permute-done((f32[2,2,64,256]{3,2,1,0:T(8,128)S(1)}, f32[2,2,64,256]{3,2,1,0:T(8,128)S(1)}, u32[]{:S(2)}, u32[]{:S(2)}) %collective-permute-start.22) | collective-permute-done | bytes 262176 | tf_op jit(solution)/shard_map/ppermute | solution.py:364
  91.0 3.2 %collective-permute-done.23 = f32[2,2,64,256]{3,2,1,0:T(8,128)S(1)} collective-permute-done((f32[2,2,64,256]{3,2,1,0:T(8,128)S(1)}, f32[2,2,64,256]{3,2,1,0:T(8,128)S(1)}, u32[]{:S(2)}, u32[]{:S(2)}) %collective-permute-start.23) | collective-permute-done | bytes 262176 | tf_op jit(solution)/shard_map/ppermute | solution.py:364
  95.7 1.6 %collective-permute-start.25 = (f32[1,2,64,256]{3,2,1,0:T(8,128)S(1)}, f32[1,2,64,256]{3,2,1,0:T(8,128)S(1)}, u32[]{:S(2)}, u32[]{:S(2)}) collective-permute-start(f32[1,2,64,256]{3,2,1,0:T(8,128)S(1)} %slice.147), channel_id=1, source_target_pairs={{0,2},{2,0},{4,6},{6,4},{8,10},{10,8},{12,14},{14,12},{1,3},{3,1},... | collective-permute-start | bytes 393224 | tf_op jit(solution)/shard_map/ppermute | solution.py:364
  99.5 1.8 %collective-permute-done.25 = f32[1,2,64,256]{3,2,1,0:T(8,128)S(1)} collective-permute-done((f32[1,2,64,256]{3,2,1,0:T(8,128)S(1)}, f32[1,2,64,256]{3,2,1,0:T(8,128)S(1)}, u32[]{:S(2)}, u32[]{:S(2)}) %collective-permute-start.25) | collective-permute-done | bytes 131104 | tf_op jit(solution)/shard_map/ppermute | solution.py:364
  101.3 3.4 %collective-permute-start.26 = (f32[1,2,64,256]{3,2,1,0:T(8,128)S(1)}, f32[1,2,64,256]{3,2,1,0:T(8,128)S(1)}, u32[]{:S(2)}, u32[]{:S(2)}) collective-permute-start(f32[1,2,64,256]{3,2,1,0:T(8,128)S(1)} %slice_add_fusion.5), channel_id=1, source_target_pairs={{0,8},{2,10},{4,12},{6,14},{8,0},{10,2},{12,4},{14,6},{1,9},{3,11}... | collective-permute-start | bytes 393224 | tf_op jit(solution)/shard_map/ppermute | solution.py:364
  104.8 1.9 %collective-permute-start.28 = (f32[2,128,128]{2,1,0:T(8,128)S(1)}, f32[2,128,128]{2,1,0:T(8,128)S(1)}, u32[]{:S(2)}, u32[]{:S(2)}) collective-permute-start(f32[2,128,128]{2,1,0:T(8,128)S(1)} %slice_select_fusion.3), channel_id=1, source_target_pairs={{0,2},{2,0},{4,6},{6,4},{8,10},{10,8},{12,14},{14,12},{1,3},{3,1},... | collective-permute-start | bytes 393224 | tf_op jit(solution)/shard_map/ppermute | solution.py:354
  106.7 6.9 %collective-permute-done.26 = f32[1,2,64,256]{3,2,1,0:T(8,128)S(1)} collective-permute-done((f32[1,2,64,256]{3,2,1,0:T(8,128)S(1)}, f32[1,2,64,256]{3,2,1,0:T(8,128)S(1)}, u32[]{:S(2)}, u32[]{:S(2)}) %collective-permute-start.26) | collective-permute-done | bytes 131104 | tf_op jit(solution)/shard_map/ppermute | solution.py:364
  116.7 3.5 %collective-permute-done.31.refs_4_ = f32[1,2,64,256]{3,2,1,0:T(8,128)S(1)} collective-permute-done((f32[1,2,64,256]{3,2,1,0:T(8,128)S(1)}, f32[1,2,64,256]{3,2,1,0:T(8,128)S(1)}, u32[]{:S(2)}, u32[]{:S(2)}) %collective-permute-start.31) | collective-permute-done | bytes 131104 | tf_op jit(solution)/shard_map/ppermute | solution.py:364
  120.6 3.2 %collective-permute-start.34 = (f32[2,2,64,256]{3,2,1,0:T(8,128)S(1)}, f32[2,2,64,256]{3,2,1,0:T(8,128)S(1)}, u32[]{:S(2)}, u32[]{:S(2)}) collective-permute-start(f32[2,2,64,256]{3,2,1,0:T(8,128)S(1)} %pad_maximum_fusion.4), channel_id=1, source_target_pairs={{0,4},{2,6},{4,0},{6,2},{8,12},{10,14},{12,8},{14,10},{1,5},{3,7},... | collective-permute-start | bytes 786440 | tf_op jit(solution)/shard_map/ppermute | solution.py:364
  123.8 2.9 %collective-permute-done.32.refs_5_ = f32[2,2,64,256]{3,2,1,0:T(8,128)S(1)} collective-permute-done((f32[2,2,64,256]{3,2,1,0:T(8,128)S(1)}, f32[2,2,64,256]{3,2,1,0:T(8,128)S(1)}, u32[]{:S(2)}, u32[]{:S(2)}) %collective-permute-start.32) | collective-permute-done | bytes 262176 | tf_op jit(solution)/shard_map/ppermute | solution.py:364
  (106 shorter events, 29.4 us)
Async XLA Ops:
  1.7 6.5 %collective-permute-start = (f32[2,128,128]{2,1,0:T(8,128)S(1)}, f32[2,128,128]{2,1,0:T(8,128)S(1)}, u32[]{:S(2)}, u32[]{:S(2)}) collective-permute-start(f32[2,128,128]{2,1,0:T(8,128)S(1)} %get-tuple-element.104), channel_id=1, source_target_pairs={{0,2},{2,0},{4,6},{6,4},{8,10},{10,8},{12,14},{14,12},{1,3},{3,1},... | collective-permute-start | bytes 393224 | tf_op jit(solution)/shard_map/ppermute | solution.py:354
  4.8 3.5 %collective-permute-start.1 = (f32[2,128,128]{2,1,0:T(8,128)S(1)}, f32[2,128,128]{2,1,0:T(8,128)S(1)}, u32[]{:S(2)}, u32[]{:S(2)}) collective-permute-start(f32[2,128,128]{2,1,0:T(8,128)S(1)} %get-tuple-element.105), channel_id=1, source_target_pairs={{2,4},{4,2},{6,8},{8,6},{10,12},{12,10},{3,5},{5,3},{7,9},{9,7},{1... | collective-permute-start | bytes 393224 | tf_op jit(solution)/shard_map/ppermute | solution.py:354
  8.5 2.0 %collective-permute-start.2 = (f32[2,2,128,256]{3,2,1,0:T(8,128)S(1)}, f32[2,2,128,256]{3,2,1,0:T(8,128)S(1)}, u32[]{:S(2)}, u32[]{:S(2)}) collective-permute-start(f32[2,2,128,256]{3,2,1,0:T(8,128)S(1)} %pad_maximum_fusion.refs_1_), channel_id=1, source_target_pairs={{0,1},{1,0},{2,3},{3,2},{4,5},{5,4},{6,7},{7,6},{8,9},{9,8},{10,11... | collective-permute-start | bytes 1572872 | tf_op jit(solution)/shard_map/ppermute | solution.py:345
  18.7 11.3 %collective-permute-start.6 = (f32[2,2,64,256]{3,2,1,0:T(8,128)S(1)}, f32[2,2,64,256]{3,2,1,0:T(8,128)S(1)}, u32[]{:S(2)}, u32[]{:S(2)}) collective-permute-start(f32[2,2,64,256]{3,2,1,0:T(8,128)S(1)} %slice.118), channel_id=1, source_target_pairs={{0,2},{2,0},{4,6},{6,4},{8,10},{10,8},{12,14},{14,12},{1,3},{3,1},... | collective-permute-start | bytes 786440 | tf_op jit(solution)/shard_map/ppermute | solution.py:364
  25.9 8.9 %collective-permute-start.5 = (f32[2,2,128,256]{3,2,1,0:T(8,128)S(1)}, f32[2,2,128,256]{3,2,1,0:T(8,128)S(1)}, u32[]{:S(2)}, u32[]{:S(2)}) collective-permute-start(f32[2,2,128,256]{3,2,1,0:T(8,128)S(1)} %slice_bitcast_fusion.1), channel_id=1, source_target_pairs={{0,1},{1,0},{2,3},{3,2},{4,5},{5,4},{6,7},{7,6},{8,9},{9,8},{10,11... | collective-permute-start | bytes 1572872 | tf_op jit(solution)/shard_map/ppermute | solution.py:345
  26.0 8.8 %collective-permute-start.7 = (f32[2,2,64,256]{3,2,1,0:T(8,128)S(1)}, f32[2,2,64,256]{3,2,1,0:T(8,128)S(1)}, u32[]{:S(2)}, u32[]{:S(2)}) collective-permute-start(f32[2,2,64,256]{3,2,1,0:T(8,128)S(1)} %slice.120), channel_id=1, source_target_pairs={{0,4},{2,6},{4,0},{6,2},{8,12},{10,14},{12,8},{14,10},{1,5},{3,7},... | collective-permute-start | bytes 786440 | tf_op jit(solution)/shard_map/ppermute | solution.py:364
  35.0 5.2 %collective-permute-start.8 = (f32[1,2,64,256]{3,2,1,0:T(8,128)S(1)}, f32[1,2,64,256]{3,2,1,0:T(8,128)S(1)}, u32[]{:S(2)}, u32[]{:S(2)}) collective-permute-start(f32[1,2,64,256]{3,2,1,0:T(8,128)S(1)} %slice.123), channel_id=1, source_target_pairs={{0,4},{2,6},{4,0},{6,2},{8,12},{10,14},{12,8},{14,10},{1,5},{3,7},... | collective-permute-start | bytes 393224 | tf_op jit(solution)/shard_map/ppermute | solution.py:364
  36.7 5.0 %collective-permute-start.9 = (f32[1,2,64,256]{3,2,1,0:T(8,128)S(1)}, f32[1,2,64,256]{3,2,1,0:T(8,128)S(1)}, u32[]{:S(2)}, u32[]{:S(2)}) collective-permute-start(f32[1,2,64,256]{3,2,1,0:T(8,128)S(1)} %slice.125), channel_id=1, source_target_pairs={{0,2},{2,0},{4,6},{6,4},{8,10},{10,8},{12,14},{14,12},{1,3},{3,1},... | collective-permute-start | bytes 393224 | tf_op jit(solution)/shard_map/ppermute | solution.py:364
  38.3 21.4 %collective-permute-start.13 = (f32[2,128,256]{2,1,0:T(8,128)S(1)}, f32[2,128,256]{2,1,0:T(8,128)S(1)}, u32[]{:S(2)}, u32[]{:S(2)}) collective-permute-start(f32[2,128,256]{2,1,0:T(8,128)S(1)} %get-tuple-element.66), channel_id=1, source_target_pairs={{2,4},{4,2},{6,8},{8,6},{10,12},{12,10},{3,5},{5,3},{7,9},{9,7},{1... | collective-permute-start | bytes 786440 | tf_op jit(solution)/shard_map/ppermute | solution.py:354
  41.8 17.9 %collective-permute-start.12 = (f32[2,128,256]{2,1,0:T(8,128)S(1)}, f32[2,128,256]{2,1,0:T(8,128)S(1)}, u32[]{:S(2)}, u32[]{:S(2)}) collective-permute-start(f32[2,128,256]{2,1,0:T(8,128)S(1)} %get-tuple-element.65), channel_id=1, source_target_pairs={{0,2},{2,0},{4,6},{6,4},{8,10},{10,8},{12,14},{14,12},{1,3},{3,1},... | collective-permute-start | bytes 786440 | tf_op jit(solution)/shard_map/ppermute | solution.py:354
  43.4 14.9 %collective-permute-start.10 = (f32[1,2,64,256]{3,2,1,0:T(8,128)S(1)}, f32[1,2,64,256]{3,2,1,0:T(8,128)S(1)}, u32[]{:S(2)}, u32[]{:S(2)}) collective-permute-start(f32[1,2,64,256]{3,2,1,0:T(8,128)S(1)} %slice_add_fusion.7), channel_id=1, source_target_pairs={{0,8},{2,10},{4,12},{6,14},{8,0},{10,2},{12,4},{14,6},{1,9},{3,11}... | collective-permute-start | bytes 393224 | tf_op jit(solution)/shard_map/ppermute | solution.py:364
  50.1 9.6 %collective-permute-start.11 = (f32[1,2,64,256]{3,2,1,0:T(8,128)S(1)}, f32[1,2,64,256]{3,2,1,0:T(8,128)S(1)}, u32[]{:S(2)}, u32[]{:S(2)}) collective-permute-start(f32[1,2,64,256]{3,2,1,0:T(8,128)S(1)} %slice_add_fusion.6), channel_id=1, source_target_pairs={{0,8},{2,10},{4,12},{6,14},{8,0},{10,2},{12,4},{14,6},{1,9},{3,11}... | collective-permute-start | bytes 393224 | tf_op jit(solution)/shard_map/ppermute | solution.py:364
  59.7 5.0 %collective-permute-start.15 = (f32[1,2,64,256]{3,2,1,0:T(8,128)S(1)}, f32[1,2,64,256]{3,2,1,0:T(8,128)S(1)}, u32[]{:S(2)}, u32[]{:S(2)}) collective-permute-start(f32[1,2,64,256]{3,2,1,0:T(8,128)S(1)} %add.74.refs_5_), channel_id=1, source_target_pairs={{0,4},{2,6},{4,0},{6,2},{8,12},{10,14},{12,8},{14,10},{1,5},{3,7},... | collective-permute-start | bytes 393224 | tf_op jit(solution)/shard_map/ppermute | solution.py:364
  60.0 14.2 %collective-permute-start.14 = (f32[2,2,128,256]{3,2,1,0:T(8,128)S(1)}, f32[2,2,128,256]{3,2,1,0:T(8,128)S(1)}, u32[]{:S(2)}, u32[]{:S(2)}) collective-permute-start(f32[2,2,128,256]{3,2,1,0:T(8,128)S(1)} %fusion.refs_1_), channel_id=1, source_target_pairs={{0,1},{1,0},{2,3},{3,2},{4,5},{5,4},{6,7},{7,6},{8,9},{9,8},{10,11... | collective-permute-start | bytes 1572872 | tf_op jit(solution)/shard_map/ppermute | solution.py:345
  60.0 6.4 %collective-permute-start.17 = (f32[1,2,64,256]{3,2,1,0:T(8,128)S(1)}, f32[1,2,64,256]{3,2,1,0:T(8,128)S(1)}, u32[]{:S(2)}, u32[]{:S(2)}) collective-permute-start(f32[1,2,64,256]{3,2,1,0:T(8,128)S(1)} %add.75.refs_8_), channel_id=1, source_target_pairs={{0,2},{2,0},{4,6},{6,4},{8,10},{10,8},{12,14},{14,12},{1,3},{3,1},... | collective-permute-start | bytes 393224 | tf_op jit(solution)/shard_map/ppermute | solution.py:364
  64.8 6.8 %collective-permute-start.16 = (f32[2,2,64,256]{3,2,1,0:T(8,128)S(1)}, f32[2,2,64,256]{3,2,1,0:T(8,128)S(1)}, u32[]{:S(2)}, u32[]{:S(2)}) collective-permute-start(f32[2,2,64,256]{3,2,1,0:T(8,128)S(1)} %pad_maximum_fusion.1), channel_id=1, source_target_pairs={{0,2},{2,0},{4,6},{6,4},{8,10},{10,8},{12,14},{14,12},{1,3},{3,1},... | collective-permute-start | bytes 786440 | tf_op jit(solution)/shard_map/ppermute | solution.py:364
  66.4 7.8 %collective-permute-start.18 = (f32[2,2,64,256]{3,2,1,0:T(8,128)S(1)}, f32[2,2,64,256]{3,2,1,0:T(8,128)S(1)}, u32[]{:S(2)}, u32[]{:S(2)}) collective-permute-start(f32[2,2,64,256]{3,2,1,0:T(8,128)S(1)} %pad_maximum_fusion.2), channel_id=1, source_target_pairs={{0,4},{2,6},{4,0},{6,2},{8,12},{10,14},{12,8},{14,10},{1,5},{3,7},... | collective-permute-start | bytes 786440 | tf_op jit(solution)/shard_map/ppermute | solution.py:364
  76.3 2.7 %collective-permute-start.19 = (f32[256,256]{1,0:T(8,128)S(1)}, f32[256,256]{1,0:T(8,128)S(1)}, u32[]{:S(2)}, u32[]{:S(2)}) collective-permute-start(f32[256,256]{1,0:T(8,128)S(1)} %get-tuple-element.74.refs_7_), channel_id=1, source_target_pairs={{0,1},{1,0},{2,3},{3,2},{4,5},{5,4},{6,7},{7,6},{8,9},{9,8},{10,11... | collective-permute-start | bytes 786440 | tf_op jit(solution)/shard_map/ppermute | solution.py:345
  82.3 8.7 %collective-permute-start.22 = (f32[2,2,64,256]{3,2,1,0:T(8,128)S(1)}, f32[2,2,64,256]{3,2,1,0:T(8,128)S(1)}, u32[]{:S(2)}, u32[]{:S(2)}) collective-permute-start(f32[2,2,64,256]{3,2,1,0:T(8,128)S(1)} %slice.138), channel_id=1, source_target_pairs={{0,2},{2,0},{4,6},{6,4},{8,10},{10,8},{12,14},{14,12},{1,3},{3,1},... | collective-permute-start | bytes 786440 | tf_op jit(solution)/shard_map/ppermute | solution.py:364
  85.8 8.4 %collective-permute-start.23 = (f32[2,2,64,256]{3,2,1,0:T(8,128)S(1)}, f32[2,2,64,256]{3,2,1,0:T(8,128)S(1)}, u32[]{:S(2)}, u32[]{:S(2)}) collective-permute-start(f32[2,2,64,256]{3,2,1,0:T(8,128)S(1)} %slice.140), channel_id=1, source_target_pairs={{0,4},{2,6},{4,0},{6,2},{8,12},{10,14},{12,8},{14,10},{1,5},{3,7},... | collective-permute-start | bytes 786440 | tf_op jit(solution)/shard_map/ppermute | solution.py:364
  87.2 7.1 %collective-permute-start.21 = (f32[2,2,128,256]{3,2,1,0:T(8,128)S(1)}, f32[2,2,128,256]{3,2,1,0:T(8,128)S(1)}, u32[]{:S(2)}, u32[]{:S(2)}) collective-permute-start(f32[2,2,128,256]{3,2,1,0:T(8,128)S(1)} %slice_bitcast_fusion), channel_id=1, source_target_pairs={{0,1},{1,0},{2,3},{3,2},{4,5},{5,4},{6,7},{7,6},{8,9},{9,8},{10,11... | collective-permute-start | bytes 1572872 | tf_op jit(solution)/shard_map/ppermute | solution.py:345
  94.4 5.0 %collective-permute-start.24 = (f32[1,2,64,256]{3,2,1,0:T(8,128)S(1)}, f32[1,2,64,256]{3,2,1,0:T(8,128)S(1)}, u32[]{:S(2)}, u32[]{:S(2)}) collective-permute-start(f32[1,2,64,256]{3,2,1,0:T(8,128)S(1)} %slice.145), channel_id=1, source_target_pairs={{0,4},{2,6},{4,0},{6,2},{8,12},{10,14},{12,8},{14,10},{1,5},{3,7},... | collective-permute-start | bytes 393224 | tf_op jit(solution)/shard_map/ppermute | solution.py:364
  95.7 5.6 %collective-permute-start.25 = (f32[1,2,64,256]{3,2,1,0:T(8,128)S(1)}, f32[1,2,64,256]{3,2,1,0:T(8,128)S(1)}, u32[]{:S(2)}, u32[]{:S(2)}) collective-permute-start(f32[1,2,64,256]{3,2,1,0:T(8,128)S(1)} %slice.147), channel_id=1, source_target_pairs={{0,2},{2,0},{4,6},{6,4},{8,10},{10,8},{12,14},{14,12},{1,3},{3,1},... | collective-permute-start | bytes 393224 | tf_op jit(solution)/shard_map/ppermute | solution.py:364
  97.3 17.7 %collective-permute-start.29 = (f32[2,128,128]{2,1,0:T(8,128)S(1)}, f32[2,128,128]{2,1,0:T(8,128)S(1)}, u32[]{:S(2)}, u32[]{:S(2)}) collective-permute-start(f32[2,128,128]{2,1,0:T(8,128)S(1)} %slice_select_fusion.2), channel_id=1, source_target_pairs={{2,4},{4,2},{6,8},{8,6},{10,12},{12,10},{3,5},{5,3},{7,9},{9,7},{1... | collective-permute-start | bytes 393224 | tf_op jit(solution)/shard_map/ppermute | solution.py:354
  101.3 12.4 %collective-permute-start.26 = (f32[1,2,64,256]{3,2,1,0:T(8,128)S(1)}, f32[1,2,64,256]{3,2,1,0:T(8,128)S(1)}, u32[]{:S(2)}, u32[]{:S(2)}) collective-permute-start(f32[1,2,64,256]{3,2,1,0:T(8,128)S(1)} %slice_add_fusion.5), channel_id=1, source_target_pairs={{0,8},{2,10},{4,12},{6,14},{8,0},{10,2},{12,4},{14,6},{1,9},{3,11}... | collective-permute-start | bytes 393224 | tf_op jit(solution)/shard_map/ppermute | solution.py:364
  104.7 10.4 %collective-permute-start.27 = (f32[1,2,64,256]{3,2,1,0:T(8,128)S(1)}, f32[1,2,64,256]{3,2,1,0:T(8,128)S(1)}, u32[]{:S(2)}, u32[]{:S(2)}) collective-permute-start(f32[1,2,64,256]{3,2,1,0:T(8,128)S(1)} %slice_add_fusion.4), channel_id=1, source_target_pairs={{0,8},{2,10},{4,12},{6,14},{8,0},{10,2},{12,4},{14,6},{1,9},{3,11}... | collective-permute-start | bytes 393224 | tf_op jit(solution)/shard_map/ppermute | solution.py:364
  104.8 10.3 %collective-permute-start.28 = (f32[2,128,128]{2,1,0:T(8,128)S(1)}, f32[2,128,128]{2,1,0:T(8,128)S(1)}, u32[]{:S(2)}, u32[]{:S(2)}) collective-permute-start(f32[2,128,128]{2,1,0:T(8,128)S(1)} %slice_select_fusion.3), channel_id=1, source_target_pairs={{0,2},{2,0},{4,6},{6,4},{8,10},{10,8},{12,14},{14,12},{1,3},{3,1},... | collective-permute-start | bytes 393224 | tf_op jit(solution)/shard_map/ppermute | solution.py:354
  115.1 5.0 %collective-permute-start.31 = (f32[1,2,64,256]{3,2,1,0:T(8,128)S(1)}, f32[1,2,64,256]{3,2,1,0:T(8,128)S(1)}, u32[]{:S(2)}, u32[]{:S(2)}) collective-permute-start(f32[1,2,64,256]{3,2,1,0:T(8,128)S(1)} %add.84.refs_3_), channel_id=1, source_target_pairs={{0,4},{2,6},{4,0},{6,2},{8,12},{10,14},{12,8},{14,10},{1,5},{3,7},... | collective-permute-start | bytes 393224 | tf_op jit(solution)/shard_map/ppermute | solution.py:364
  115.2 5.3 %collective-permute-start.33 = (f32[1,2,64,256]{3,2,1,0:T(8,128)S(1)}, f32[1,2,64,256]{3,2,1,0:T(8,128)S(1)}, u32[]{:S(2)}, u32[]{:S(2)}) collective-permute-start(f32[1,2,64,256]{3,2,1,0:T(8,128)S(1)} %add.85.refs_6_), channel_id=1, source_target_pairs={{0,2},{2,0},{4,6},{6,4},{8,10},{10,8},{12,14},{14,12},{1,3},{3,1},... | collective-permute-start | bytes 393224 | tf_op jit(solution)/shard_map/ppermute | solution.py:364
  116.6 7.2 %collective-permute-start.30 = (f32[2,2,128,128]{3,2,1,0:T(8,128)S(1)}, f32[2,2,128,128]{3,2,1,0:T(8,128)S(1)}, u32[]{:S(2)}, u32[]{:S(2)}) collective-permute-start(f32[2,2,128,128]{3,2,1,0:T(8,128)S(1)} %maximum_add_fusion.refs_0_), channel_id=1, source_target_pairs={{0,1},{1,0},{2,3},{3,2},{4,5},{5,4},{6,7},{7,6},{8,9},{9,8},{10,11... | collective-permute-start | bytes 786440 | tf_op jit(solution)/shard_map/ppermute | solution.py:345
  120.2 6.4 %collective-permute-start.32 = (f32[2,2,64,256]{3,2,1,0:T(8,128)S(1)}, f32[2,2,64,256]{3,2,1,0:T(8,128)S(1)}, u32[]{:S(2)}, u32[]{:S(2)}) collective-permute-start(f32[2,2,64,256]{3,2,1,0:T(8,128)S(1)} %pad_maximum_fusion.3), channel_id=1, source_target_pairs={{0,2},{2,0},{4,6},{6,4},{8,10},{10,8},{12,14},{14,12},{1,3},{3,1},... | collective-permute-start | bytes 786440 | tf_op jit(solution)/shard_map/ppermute | solution.py:364
  120.6 7.5 %collective-permute-start.34 = (f32[2,2,64,256]{3,2,1,0:T(8,128)S(1)}, f32[2,2,64,256]{3,2,1,0:T(8,128)S(1)}, u32[]{:S(2)}, u32[]{:S(2)}) collective-permute-start(f32[2,2,64,256]{3,2,1,0:T(8,128)S(1)} %pad_maximum_fusion.4), channel_id=1, source_target_pairs={{0,4},{2,6},{4,0},{6,2},{8,12},{10,14},{12,8},{14,10},{1,5},{3,7},... | collective-permute-start | bytes 786440 | tf_op jit(solution)/shard_map/ppermute | solution.py:364
  (9 other events, 14.6 us)
